TPU v7x, 32 devices: a whole 2x2x4 slice. The times are simulated.
32 devices in a mesh: gx: 4 (over x, core), gy: 4 (over z), gz: 2 (over y).
Axes of the slice: x: 2, y: 2, z: 4, core: 2. Of those that a mesh axis runs over, the one named last changes fastest.
Arguments:
- state: float32 [7, 16, 16, 32, 128], P(None, 'gx', 'gy', 'gz'), may hold values from -6 to 6, as said below
- arms: float32 [3, 16, 16, 32, 128], P(None, 'gx', 'gy', 'gz'), may hold values from -6 to 6
- sphere_frag: int32 [16, 16, 32, 128], P('gx', 'gy', 'gz'), may hold values from 0 to 63
- frag_owner: int32 [2048, 1], P(('gx', 'gy', 'gz')), may hold values from 0 to 31; in each aligned block of 64 rows (0 to 63, 64 to 127, ...) at most 2 rows name the same one
- frag_clump: int32 [2048], P(('gx', 'gy', 'gz')), may hold values from 0 to 47
- tiles: int32 [32, 2048], P(('gx', 'gy', 'gz')), may hold values from 0 to 6911, as said below
- clump_motion: float32 [6, 1536], P(None, ('gx', 'gy', 'gz')), may hold values from -6 to 6
- inv_mass: float32 [1536], P(('gx', 'gy', 'gz')), may hold values from 0.3 to 3
- inv_moment: float32 [1536], P(('gx', 'gy', 'gz')), may hold values from 0.1 to 1
Outputs:
- sphere_next: float32 [6, 16, 16, 32, 128], P(None, 'gx', 'gy', 'gz')
- clump_next: float32 [6, 1536], P(None, ('gx', 'gy', 'gz'))
Inputs may be any that keep to these rules, and one draw needn't show every extreme that they name: `state`: rows 0 to 2 lie in [0, 1), rows 3 to 5 in [-6, 6], row 6 in [0.08, 0.14]. `tiles`: the 2048 codes of one brick are distinct. `frag_owner`: among the 64 fragments of one brick at most 2 name the same owner.
All inputs are finite; a program needn't handle non-finite values.
Results may differ from a plain program's by a relative error of at most 0.0003.
Values sent between devices are 32-bit elements; how exact they have to be, the bound alone decides.
No kernel may reach another device: no remote copies, remote signals or barrier semaphores. Data moves between devices by JAX's collectives and lax.ppermute only.
A program may use at most 64 MiB of HBM per device.

v0:
```python
import jax
import jax.numpy as jnp
from jax import lax
from jax.sharding import PartitionSpec as P

CAP = 2


stiffness = 100.0
damping = 2.0
time_step = 0.01
gravity = 9.81
epsilon_sq = 1e-08


def with_halo(x, sides, width):
    for axis, dim in sides:
        devices, length = (lax.axis_size(axis), x.shape[dim])
        up = [(i, (i + 1) % devices) for i in range(devices)]
        down = [(j, i) for i, j in up]
        last = lax.slice_in_dim(x, length - width, length, axis=dim)
        initial = lax.slice_in_dim(x, 0, width, axis=dim)
        before = lax.ppermute(last, axis, up)
        after = lax.ppermute(initial, axis, down)
        x = jnp.concatenate([before, x, after], axis=dim)
    return x


def cross_rows(first, second):
    return jnp.stack(
        [
            first[1] * second[2] - first[2] * second[1],
            first[2] * second[0] - first[0] * second[2],
            first[0] * second[1] - first[1] * second[0],
        ]
    )


def pair_forces(own_block, neighbor_block, cell_shift):
    separation = [
        neighbor_block[axis_k][:, None, :]
        + cell_shift[axis_k][:, None, None]
        - own_block[axis_k][:, :, None]
        for axis_k in range(3)
    ]
    distance = jnp.sqrt(
        separation[0] * separation[0]
        + separation[1] * separation[1]
        + separation[2] * separation[2]
        + epsilon_sq
    )
    radius_own = own_block[6][:, :, None]
    radius_other = neighbor_block[6][:, None, :]
    distinct = (own_block[7][:, :, None] != neighbor_block[7][:, None, :]).astype(jnp.float32)
    intersection = jnp.maximum(radius_own + radius_other - distance, 0.0) * distinct
    reduced = radius_own * radius_other / (radius_own + radius_other)
    closing = (
        sum(
            (
                (neighbor_block[3 + axis_k][:, None, :] - own_block[3 + axis_k][:, :, None])
                * separation[axis_k]
                for axis_k in range(3)
            )
        )
        / distance
    )
    magnitude = (
        stiffness * jnp.sqrt(reduced) * intersection * jnp.sqrt(intersection)
        - damping * jnp.sqrt(reduced * intersection) * closing
    )
    factor = magnitude / distance
    return jnp.stack([-jnp.sum(factor * separation[axis_k], axis=2) for axis_k in range(3)])


def advance(motion, sums, inv_mass, inv_moment):
    pull = jnp.array([0.0, 0.0, gravity], jnp.float32)[:, None]
    velocity = motion[0:3] + time_step * (sums[0:3] * inv_mass[None, :] - pull)
    spin = motion[3:6] + time_step * sums[3:6] * inv_moment[None, :]
    return jnp.concatenate([velocity, spin], axis=0)


def move_spheres(state, arms, motion):
    velocity = motion[0:3]
    spin = motion[3:6]
    half = 0.5 * time_step * spin
    turned = cross_rows(half, arms)
    twice = cross_rows(half, turned)
    scale = 2.0 / (1.0 + half[0] * half[0] + half[1] * half[1] + half[2] * half[2])
    new_arm = arms + scale * (turned + twice)
    position = state[0:3] + time_step * velocity + (new_arm - arms)
    moving = velocity + cross_rows(spin, new_arm)
    return jnp.concatenate([position, moving], axis=0)


def local(
    state, arms, sphere_frag, frag_owner, frag_clump, tiles, clump_motion, inv_mass, inv_moment
):
    cells_x, cells_y, cells_z = (state.shape[1], state.shape[2], state.shape[3])
    slots = state.shape[4]
    cell_count = cells_x * cells_y * cells_z
    owned = inv_mass.shape[0]
    held = frag_clump.shape[0]
    size_x = lax.axis_size("gx")
    size_y = lax.axis_size("gy")
    size_z = lax.axis_size("gz")
    bricks = size_x * size_y * size_z
    owner = frag_owner[:, 0]
    frag_key = (owner * owned + frag_clump).astype(jnp.float32)
    sphere_key = frag_key[sphere_frag]
    full = jnp.concatenate([state, sphere_key[None]], axis=0)
    padded = with_halo(full, (("gx", 1), ("gy", 2), ("gz", 3)), 1)
    span_y = cells_y + 2
    span_z = cells_z + 2
    padded = padded.reshape(8, (cells_x + 2) * span_y * span_z, slots)
    codes = tiles[0]
    block = 64

    def accumulate(total, block_codes):
        own_cell = block_codes // 27
        offset = block_codes % 27
        step_x = offset // 9 - 1
        step_y = offset // 3 % 3 - 1
        step_z = offset % 3 - 1
        cell_x = own_cell // (cells_y * cells_z) + 1
        cell_y = own_cell // cells_z % cells_y + 1
        cell_z = own_cell % cells_z + 1
        own_pad = (cell_x * span_y + cell_y) * span_z + cell_z
        other_pad = ((cell_x + step_x) * span_y + cell_y + step_y) * span_z + cell_z + step_z
        cell_shift = jnp.stack([step_x, step_y, step_z]).astype(jnp.float32)
        forces = pair_forces(
            jnp.take(padded, own_pad, axis=1), jnp.take(padded, other_pad, axis=1), cell_shift
        )
        return (total.at[:, own_cell].add(forces), None)

    force, unused = lax.scan(
        accumulate, jnp.zeros((3, cell_count, slots), jnp.float32), codes.reshape(-1, block)
    )
    lever = arms.reshape(3, cell_count, slots)
    torque = cross_rows(lever, force)
    loads = jnp.concatenate([force, torque], axis=0).reshape(6, -1)
    frag_sums = jax.ops.segment_sum(loads.T, sphere_frag.reshape(-1), num_segments=held).T
    hits = (owner[:, None] == jnp.arange(bricks, dtype=jnp.int32)[None, :]).astype(jnp.int32)
    rank = jnp.sum((jnp.cumsum(hits, axis=0) - hits) * hits, axis=1)
    slot_index = owner * CAP + rank
    payload = jnp.concatenate([frag_sums, (frag_clump + 1).astype(jnp.float32)[None]], axis=0)
    outbox = jnp.zeros((7, bricks * CAP), jnp.float32).at[:, slot_index].set(payload)
    inbox = lax.all_to_all(outbox, ("gx", "gy", "gz"), split_axis=1, concat_axis=1, tiled=True)
    labels = (jnp.arange(owned, dtype=jnp.int32) + 1).astype(jnp.float32)
    which = (inbox[6][:, None] == labels[None, :]).astype(jnp.float32)
    clump_sums = jnp.dot(
        inbox[0:6], which, precision=lax.Precision.HIGHEST, preferred_element_type=jnp.float32
    )
    clump_next = advance(clump_motion, clump_sums, inv_mass, inv_moment)
    column = jnp.clip(inbox[6].astype(jnp.int32) - 1, 0, owned - 1)
    reply = jnp.take(clump_next, column, axis=1)
    answer = lax.all_to_all(reply, ("gx", "gy", "gz"), split_axis=1, concat_axis=1, tiled=True)
    frag_motion = jnp.take(answer, slot_index, axis=1)
    sphere_motion = jnp.take(frag_motion, sphere_frag, axis=1)
    sphere_next = move_spheres(state, arms, sphere_motion)
    return (sphere_next, clump_next)


def solution(mesh):
    return jax.shard_map(
        local,
        mesh=mesh,
        in_specs=(
            P(None, "gx", "gy", "gz", None),
            P(None, "gx", "gy", "gz", None),
            P("gx", "gy", "gz", None),
            P(("gx", "gy", "gz"), None),
            P(("gx", "gy", "gz")),
            P(("gx", "gy", "gz"), None),
            P(None, ("gx", "gy", "gz")),
            P(("gx", "gy", "gz")),
            P(("gx", "gy", "gz")),
        ),
        out_specs=(P(None, "gx", "gy", "gz", None), P(None, ("gx", "gy", "gz"))),
        check_vma=False,
    )
```

profile of v0, /device:TPU:0, one launch (start us, length us, event | category | flops | bytes accessed | tf_op | source)
XLA Modules:
  0.0 1378.7 jit_solution(7658812386687172491)
XLA Ops:
  4.0 193.9 %gather_fusion.2 = f32[32768]{0:T(1024)S(1)} fusion(f32[64]{0:T(128)S(1)} %get-tuple-element.181, s32[32768]{0:T(1024)S(1)} %broadcast_clamp_fusion), kind=kCustom, calls=%fused_computation.2 | custom fusion | bytes 393216 | tf_op jit(solution)/shard_map/gather | solution.py:109
  239.5 765.3 %while.13 = (s32[]{:T(128)}, f32[3,256,128]{2,0,1:T(4,128)S(1)}, s32[32,64]{1,0:T(8,128)S(1)}, f32[8,648,128]{2,0,1:T(8,128)}, s32[]{:T(128)}) while((s32[]{:T(128)}, f32[3,256,128]{2,0,1:T(4,128)S(1)}, s32[32,64]{1,0:T(8,128)S(1)}, f32[8,648,128]{2,0,1:T(8,128)}, s32[]{:T(128)}) %tuple.103), condition=%wide.region_7.9_spmd, body=%wide.region_2.0_spmd.sunk | while | flops 41136192 | bytes 4869185 | solution.py:135
  245.2 15.3 %fusion.67 = (f32[64,128]{1,0:T(8,128)S(1)}, f32[64,128]{1,0:T(8,128)S(1)}, f32[64,128]{1,0:T(8,128)S(1)}) fusion(f32[64,128]{1,0:T(8,128)S(1)} %bitcast.202, f32[64,128]{1,0:T(8,128)S(1)} %broadcast_add_fusion.5, f32[64,128]{1,0:T(8,128)S(1)} %bitcast.197, f32[64,128]{1,0:T(8,128)S(1)} %bitcast.192, f32[64,128]{1,0:T(8,128)S(1)} %bitcast.198, ...), kind=kLoop, calls=%fused_computation.32.clone.1 | loop fusion | flops 40869888 | bytes 622592 | tf_op jit(solution)/shard_map/while/body/eval_jaxpr/reduce_sum | solution.py:72
  269.2 15.3 %fusion.67 = (f32[64,128]{1,0:T(8,128)S(1)}, f32[64,128]{1,0:T(8,128)S(1)}, f32[64,128]{1,0:T(8,128)S(1)}) fusion(f32[64,128]{1,0:T(8,128)S(1)} %bitcast.202, f32[64,128]{1,0:T(8,128)S(1)} %broadcast_add_fusion.5, f32[64,128]{1,0:T(8,128)S(1)} %bitcast.197, f32[64,128]{1,0:T(8,128)S(1)} %bitcast.192, f32[64,128]{1,0:T(8,128)S(1)} %bitcast.198, ...), kind=kLoop, calls=%fused_computation.32.clone.1 | loop fusion | flops 40869888 | bytes 622592 | tf_op jit(solution)/shard_map/while/body/eval_jaxpr/reduce_sum | solution.py:72
  293.1 15.3 %fusion.67 = (f32[64,128]{1,0:T(8,128)S(1)}, f32[64,128]{1,0:T(8,128)S(1)}, f32[64,128]{1,0:T(8,128)S(1)}) fusion(f32[64,128]{1,0:T(8,128)S(1)} %bitcast.202, f32[64,128]{1,0:T(8,128)S(1)} %broadcast_add_fusion.5, f32[64,128]{1,0:T(8,128)S(1)} %bitcast.197, f32[64,128]{1,0:T(8,128)S(1)} %bitcast.192, f32[64,128]{1,0:T(8,128)S(1)} %bitcast.198, ...), kind=kLoop, calls=%fused_computation.32.clone.1 | loop fusion | flops 40869888 | bytes 622592 | tf_op jit(solution)/shard_map/while/body/eval_jaxpr/reduce_sum | solution.py:72
  340.9 15.3 %fusion.67 = (f32[64,128]{1,0:T(8,128)S(1)}, f32[64,128]{1,0:T(8,128)S(1)}, f32[64,128]{1,0:T(8,128)S(1)}) fusion(f32[64,128]{1,0:T(8,128)S(1)} %bitcast.202, f32[64,128]{1,0:T(8,128)S(1)} %broadcast_add_fusion.5, f32[64,128]{1,0:T(8,128)S(1)} %bitcast.197, f32[64,128]{1,0:T(8,128)S(1)} %bitcast.192, f32[64,128]{1,0:T(8,128)S(1)} %bitcast.198, ...), kind=kLoop, calls=%fused_computation.32.clone.1 | loop fusion | flops 40869888 | bytes 622592 | tf_op jit(solution)/shard_map/while/body/eval_jaxpr/reduce_sum | solution.py:72
  436.5 15.3 %fusion.67 = (f32[64,128]{1,0:T(8,128)S(1)}, f32[64,128]{1,0:T(8,128)S(1)}, f32[64,128]{1,0:T(8,128)S(1)}) fusion(f32[64,128]{1,0:T(8,128)S(1)} %bitcast.202, f32[64,128]{1,0:T(8,128)S(1)} %broadcast_add_fusion.5, f32[64,128]{1,0:T(8,128)S(1)} %bitcast.197, f32[64,128]{1,0:T(8,128)S(1)} %bitcast.192, f32[64,128]{1,0:T(8,128)S(1)} %bitcast.198, ...), kind=kLoop, calls=%fused_computation.32.clone.1 | loop fusion | flops 40869888 | bytes 622592 | tf_op jit(solution)/shard_map/while/body/eval_jaxpr/reduce_sum | solution.py:72
  460.5 15.3 %fusion.67 = (f32[64,128]{1,0:T(8,128)S(1)}, f32[64,128]{1,0:T(8,128)S(1)}, f32[64,128]{1,0:T(8,128)S(1)}) fusion(f32[64,128]{1,0:T(8,128)S(1)} %bitcast.202, f32[64,128]{1,0:T(8,128)S(1)} %broadcast_add_fusion.5, f32[64,128]{1,0:T(8,128)S(1)} %bitcast.197, f32[64,128]{1,0:T(8,128)S(1)} %bitcast.192, f32[64,128]{1,0:T(8,128)S(1)} %bitcast.198, ...), kind=kLoop, calls=%fused_computation.32.clone.1 | loop fusion | flops 40869888 | bytes 622592 | tf_op jit(solution)/shard_map/while/body/eval_jaxpr/reduce_sum | solution.py:72
  484.4 15.3 %fusion.67 = (f32[64,128]{1,0:T(8,128)S(1)}, f32[64,128]{1,0:T(8,128)S(1)}, f32[64,128]{1,0:T(8,128)S(1)}) fusion(f32[64,128]{1,0:T(8,128)S(1)} %bitcast.202, f32[64,128]{1,0:T(8,128)S(1)} %broadcast_add_fusion.5, f32[64,128]{1,0:T(8,128)S(1)} %bitcast.197, f32[64,128]{1,0:T(8,128)S(1)} %bitcast.192, f32[64,128]{1,0:T(8,128)S(1)} %bitcast.198, ...), kind=kLoop, calls=%fused_computation.32.clone.1 | loop fusion | flops 40869888 | bytes 622592 | tf_op jit(solution)/shard_map/while/body/eval_jaxpr/reduce_sum | solution.py:72
  532.2 15.3 %fusion.67 = (f32[64,128]{1,0:T(8,128)S(1)}, f32[64,128]{1,0:T(8,128)S(1)}, f32[64,128]{1,0:T(8,128)S(1)}) fusion(f32[64,128]{1,0:T(8,128)S(1)} %bitcast.202, f32[64,128]{1,0:T(8,128)S(1)} %broadcast_add_fusion.5, f32[64,128]{1,0:T(8,128)S(1)} %bitcast.197, f32[64,128]{1,0:T(8,128)S(1)} %bitcast.192, f32[64,128]{1,0:T(8,128)S(1)} %bitcast.198, ...), kind=kLoop, calls=%fused_computation.32.clone.1 | loop fusion | flops 40869888 | bytes 622592 | tf_op jit(solution)/shard_map/while/body/eval_jaxpr/reduce_sum | solution.py:72
  556.1 15.3 %fusion.67 = (f32[64,128]{1,0:T(8,128)S(1)}, f32[64,128]{1,0:T(8,128)S(1)}, f32[64,128]{1,0:T(8,128)S(1)}) fusion(f32[64,128]{1,0:T(8,128)S(1)} %bitcast.202, f32[64,128]{1,0:T(8,128)S(1)} %broadcast_add_fusion.5, f32[64,128]{1,0:T(8,128)S(1)} %bitcast.197, f32[64,128]{1,0:T(8,128)S(1)} %bitcast.192, f32[64,128]{1,0:T(8,128)S(1)} %bitcast.198, ...), kind=kLoop, calls=%fused_computation.32.clone.1 | loop fusion | flops 40869888 | bytes 622592 | tf_op jit(solution)/shard_map/while/body/eval_jaxpr/reduce_sum | solution.py:72
  604.0 15.3 %fusion.67 = (f32[64,128]{1,0:T(8,128)S(1)}, f32[64,128]{1,0:T(8,128)S(1)}, f32[64,128]{1,0:T(8,128)S(1)}) fusion(f32[64,128]{1,0:T(8,128)S(1)} %bitcast.202, f32[64,128]{1,0:T(8,128)S(1)} %broadcast_add_fusion.5, f32[64,128]{1,0:T(8,128)S(1)} %bitcast.197, f32[64,128]{1,0:T(8,128)S(1)} %bitcast.192, f32[64,128]{1,0:T(8,128)S(1)} %bitcast.198, ...), kind=kLoop, calls=%fused_computation.32.clone.1 | loop fusion | flops 40869888 | bytes 622592 | tf_op jit(solution)/shard_map/while/body/eval_jaxpr/reduce_sum | solution.py:72
  699.6 15.3 %fusion.67 = (f32[64,128]{1,0:T(8,128)S(1)}, f32[64,128]{1,0:T(8,128)S(1)}, f32[64,128]{1,0:T(8,128)S(1)}) fusion(f32[64,128]{1,0:T(8,128)S(1)} %bitcast.202, f32[64,128]{1,0:T(8,128)S(1)} %broadcast_add_fusion.5, f32[64,128]{1,0:T(8,128)S(1)} %bitcast.197, f32[64,128]{1,0:T(8,128)S(1)} %bitcast.192, f32[64,128]{1,0:T(8,128)S(1)} %bitcast.198, ...), kind=kLoop, calls=%fused_computation.32.clone.1 | loop fusion | flops 40869888 | bytes 622592 | tf_op jit(solution)/shard_map/while/body/eval_jaxpr/reduce_sum | solution.py:72
  723.5 15.3 %fusion.67 = (f32[64,128]{1,0:T(8,128)S(1)}, f32[64,128]{1,0:T(8,128)S(1)}, f32[64,128]{1,0:T(8,128)S(1)}) fusion(f32[64,128]{1,0:T(8,128)S(1)} %bitcast.202, f32[64,128]{1,0:T(8,128)S(1)} %broadcast_add_fusion.5, f32[64,128]{1,0:T(8,128)S(1)} %bitcast.197, f32[64,128]{1,0:T(8,128)S(1)} %bitcast.192, f32[64,128]{1,0:T(8,128)S(1)} %bitcast.198, ...), kind=kLoop, calls=%fused_computation.32.clone.1 | loop fusion | flops 40869888 | bytes 622592 | tf_op jit(solution)/shard_map/while/body/eval_jaxpr/reduce_sum | solution.py:72
  771.4 15.3 %fusion.67 = (f32[64,128]{1,0:T(8,128)S(1)}, f32[64,128]{1,0:T(8,128)S(1)}, f32[64,128]{1,0:T(8,128)S(1)}) fusion(f32[64,128]{1,0:T(8,128)S(1)} %bitcast.202, f32[64,128]{1,0:T(8,128)S(1)} %broadcast_add_fusion.5, f32[64,128]{1,0:T(8,128)S(1)} %bitcast.197, f32[64,128]{1,0:T(8,128)S(1)} %bitcast.192, f32[64,128]{1,0:T(8,128)S(1)} %bitcast.198, ...), kind=kLoop, calls=%fused_computation.32.clone.1 | loop fusion | flops 40869888 | bytes 622592 | tf_op jit(solution)/shard_map/while/body/eval_jaxpr/reduce_sum | solution.py:72
  795.3 15.3 %fusion.67 = (f32[64,128]{1,0:T(8,128)S(1)}, f32[64,128]{1,0:T(8,128)S(1)}, f32[64,128]{1,0:T(8,128)S(1)}) fusion(f32[64,128]{1,0:T(8,128)S(1)} %bitcast.202, f32[64,128]{1,0:T(8,128)S(1)} %broadcast_add_fusion.5, f32[64,128]{1,0:T(8,128)S(1)} %bitcast.197, f32[64,128]{1,0:T(8,128)S(1)} %bitcast.192, f32[64,128]{1,0:T(8,128)S(1)} %bitcast.198, ...), kind=kLoop, calls=%fused_computation.32.clone.1 | loop fusion | flops 40869888 | bytes 622592 | tf_op jit(solution)/shard_map/while/body/eval_jaxpr/reduce_sum | solution.py:72
  819.2 15.3 %fusion.67 = (f32[64,128]{1,0:T(8,128)S(1)}, f32[64,128]{1,0:T(8,128)S(1)}, f32[64,128]{1,0:T(8,128)S(1)}) fusion(f32[64,128]{1,0:T(8,128)S(1)} %bitcast.202, f32[64,128]{1,0:T(8,128)S(1)} %broadcast_add_fusion.5, f32[64,128]{1,0:T(8,128)S(1)} %bitcast.197, f32[64,128]{1,0:T(8,128)S(1)} %bitcast.192, f32[64,128]{1,0:T(8,128)S(1)} %bitcast.198, ...), kind=kLoop, calls=%fused_computation.32.clone.1 | loop fusion | flops 40869888 | bytes 622592 | tf_op jit(solution)/shard_map/while/body/eval_jaxpr/reduce_sum | solution.py:72
  843.1 15.3 %fusion.67 = (f32[64,128]{1,0:T(8,128)S(1)}, f32[64,128]{1,0:T(8,128)S(1)}, f32[64,128]{1,0:T(8,128)S(1)}) fusion(f32[64,128]{1,0:T(8,128)S(1)} %bitcast.202, f32[64,128]{1,0:T(8,128)S(1)} %broadcast_add_fusion.5, f32[64,128]{1,0:T(8,128)S(1)} %bitcast.197, f32[64,128]{1,0:T(8,128)S(1)} %bitcast.192, f32[64,128]{1,0:T(8,128)S(1)} %bitcast.198, ...), kind=kLoop, calls=%fused_computation.32.clone.1 | loop fusion | flops 40869888 | bytes 622592 | tf_op jit(solution)/shard_map/while/body/eval_jaxpr/reduce_sum | solution.py:72
  867.0 15.3 %fusion.67 = (f32[64,128]{1,0:T(8,128)S(1)}, f32[64,128]{1,0:T(8,128)S(1)}, f32[64,128]{1,0:T(8,128)S(1)}) fusion(f32[64,128]{1,0:T(8,128)S(1)} %bitcast.202, f32[64,128]{1,0:T(8,128)S(1)} %broadcast_add_fusion.5, f32[64,128]{1,0:T(8,128)S(1)} %bitcast.197, f32[64,128]{1,0:T(8,128)S(1)} %bitcast.192, f32[64,128]{1,0:T(8,128)S(1)} %bitcast.198, ...), kind=kLoop, calls=%fused_computation.32.clone.1 | loop fusion | flops 40869888 | bytes 622592 | tf_op jit(solution)/shard_map/while/body/eval_jaxpr/reduce_sum | solution.py:72
  914.8 15.3 %fusion.67 = (f32[64,128]{1,0:T(8,128)S(1)}, f32[64,128]{1,0:T(8,128)S(1)}, f32[64,128]{1,0:T(8,128)S(1)}) fusion(f32[64,128]{1,0:T(8,128)S(1)} %bitcast.202, f32[64,128]{1,0:T(8,128)S(1)} %broadcast_add_fusion.5, f32[64,128]{1,0:T(8,128)S(1)} %bitcast.197, f32[64,128]{1,0:T(8,128)S(1)} %bitcast.192, f32[64,128]{1,0:T(8,128)S(1)} %bitcast.198, ...), kind=kLoop, calls=%fused_computation.32.clone.1 | loop fusion | flops 40869888 | bytes 622592 | tf_op jit(solution)/shard_map/while/body/eval_jaxpr/reduce_sum | solution.py:72
  938.8 15.3 %fusion.67 = (f32[64,128]{1,0:T(8,128)S(1)}, f32[64,128]{1,0:T(8,128)S(1)}, f32[64,128]{1,0:T(8,128)S(1)}) fusion(f32[64,128]{1,0:T(8,128)S(1)} %bitcast.202, f32[64,128]{1,0:T(8,128)S(1)} %broadcast_add_fusion.5, f32[64,128]{1,0:T(8,128)S(1)} %bitcast.197, f32[64,128]{1,0:T(8,128)S(1)} %bitcast.192, f32[64,128]{1,0:T(8,128)S(1)} %bitcast.198, ...), kind=kLoop, calls=%fused_computation.32.clone.1 | loop fusion | flops 40869888 | bytes 622592 | tf_op jit(solution)/shard_map/while/body/eval_jaxpr/reduce_sum | solution.py:72
  986.6 15.3 %fusion.67 = (f32[64,128]{1,0:T(8,128)S(1)}, f32[64,128]{1,0:T(8,128)S(1)}, f32[64,128]{1,0:T(8,128)S(1)}) fusion(f32[64,128]{1,0:T(8,128)S(1)} %bitcast.202, f32[64,128]{1,0:T(8,128)S(1)} %broadcast_add_fusion.5, f32[64,128]{1,0:T(8,128)S(1)} %bitcast.197, f32[64,128]{1,0:T(8,128)S(1)} %bitcast.192, f32[64,128]{1,0:T(8,128)S(1)} %bitcast.198, ...), kind=kLoop, calls=%fused_computation.32.clone.1 | loop fusion | flops 40869888 | bytes 622592 | tf_op jit(solution)/shard_map/while/body/eval_jaxpr/reduce_sum | solution.py:72
  1014.4 216.3 %scatter_custom_fusion.1 = f32[64,6]{1,0:T(8,128)S(1)} fusion(s32[32768]{0:T(1024)S(1)} %bitcast.204, f32[32768,6]{1,0:T(8,128)} %copy.76, f32[]{:T(128)} %constant.266.clone.1), kind=kCustom, calls=%fused_computation.148 | custom fusion | flops 196608 | bytes 2048 | tf_op jit(solution)/shard_map/scatter-add | solution.py:141
  1257.0 109.0 %gather_fusion.5 = f32[32768,6]{1,0:T(8,128)} fusion(f32[6,64]{0,1:T(8,128)S(1)} %select_bitcast_fusion.3, s32[32768]{0:T(1024)S(1)} %broadcast_clamp_fusion), kind=kCustom, calls=%fused_computation.5 | custom fusion | bytes 1703936 | tf_op jit(solution)/shard_map/jit(_take)/gather | solution.py:158
  (871 shorter events, 547.9 us)
Async XLA Ops:
  4.0 196.5 %copy-start.3 = (s32[64,1]{0,1:T(1,128)S(1)}, s32[64,1]{0,1:T(1,128)}, u32[]{:S(2)}) copy-start(s32[64,1]{0,1:T(1,128)} %param.17) | copy-start | bytes 772
  4.0 197.4 %copy-start.4 = (s32[1,2048]{1,0:T(1,128)S(1)}, s32[1,2048]{1,0:T(1,128)}, u32[]{:S(2)}) copy-start(s32[1,2048]{1,0:T(1,128)} %param.19) | copy-start | bytes 24580
  4.0 198.2 %copy-start.1 = (s32[4,4,16,128]{3,2,1,0:T(8,128)S(1)}, s32[4,4,16,128]{3,2,1,0:T(8,128)}, u32[]{:S(2)}) copy-start(s32[4,4,16,128]{3,2,1,0:T(8,128)} %param.16) | copy-start | bytes 393220
  197.9 13.3 copy-start
  197.9 33.1 %copy-start.8 = (f32[48]{0:T(128)S(1)}, f32[48]{0:T(128)}, u32[]{:S(2)}) copy-start(f32[48]{0:T(128)} %param.22) | copy-start | bytes 580
  198.0 6.6 collective-permute-start
  198.5 8.6 collective-permute-start.1
  207.2 13.9 %collective-permute-start.2 = (f32[8,6,1,16,128]{4,0,3,2,1:T(8,128)S(1)}, f32[8,6,1,16,128]{4,0,3,2,1:T(8,128)S(1)}, u32[]{:S(2)}, u32[]{:S(2)}) collective-permute-start(f32[8,6,1,16,128]{4,0,3,2,1:T(8,128)S(1)} %get-tuple-element.163), channel_id=1, source_target_pairs={{0,2},{2,4},{4,6},{6,0},{1,3},{3,5},{5,7},{7,1},{8,10},{10,12},{12... | collective-permute-start | bytes 1179656 | tf_op jit(solution)/shard_map/ppermute | solution.py:23
  208.9 20.0 %collective-permute-start.3 = (f32[8,6,1,16,128]{4,0,3,2,1:T(8,128)S(1)}, f32[8,6,1,16,128]{4,0,3,2,1:T(8,128)S(1)}, u32[]{:S(2)}, u32[]{:S(2)}) collective-permute-start(f32[8,6,1,16,128]{4,0,3,2,1:T(8,128)S(1)} %get-tuple-element.164), channel_id=1, source_target_pairs={{2,0},{4,2},{6,4},{0,6},{3,1},{5,3},{7,5},{1,7},{10,8},{12,10},{14... | collective-permute-start | bytes 1179656 | tf_op jit(solution)/shard_map/ppermute | solution.py:24
  228.9 6.8 collective-permute-start.4
  230.5 7.1 collective-permute-start.5
  1005.4 239.3 %copy-start.5 = (f32[6,48]{1,0:T(8,128)S(1)}, f32[6,48]{1,0:T(8,128)}, u32[]{:S(2)}) copy-start(f32[6,48]{1,0:T(8,128)} %param.20) | copy-start | bytes 3460
  1005.4 239.3 %copy-start.6 = (f32[48]{0:T(128)S(1)}, f32[48]{0:T(128)}, u32[]{:S(2)}) copy-start(f32[48]{0:T(128)} %param.21) | copy-start | bytes 580
  1005.4 239.3 %copy-start.7 = (f32[3]{0:T(128)S(1)}, f32[3]{0:T(128)}, u32[]{:S(2)}) copy-start(f32[3]{0:T(128)} %constant.281) | copy-start | bytes 40
  1232.2 11.8 all-to-all-start
  1244.8 131.3 %copy-start.2 = (f32[6,48]{1,0:T(8,128)}, f32[6,48]{1,0:T(8,128)S(1)}, u32[]{:S(2)}) copy-start(f32[6,48]{1,0:T(8,128)S(1)} %pad_maximum_fusion.14) | copy-start | bytes 3460
  1246.5 9.8 all-to-all-start.1
where the time goes:
time: 1380 us
  other arithmetic  821 us (59%)
  local copies, waits for them, and re-layouts  492 us (36%)
  waiting for transfers between devices  43.6 us (3%)
  starting transfers between devices  15.7 us (1%)
    reduce_sum x32, other arithmetic, pair_forces(): jnp.sum(factor * separation[axis_k], axis=2)  488 us
    scatter-add x1, other arithmetic, local(): jax.ops.segment_sum(loads.T, sphere_frag.reshape(-1), num_segments=held)  216 us
    gather x1, local copies, waits for them, and re-layouts, local(): sphere_key = frag_key[sphere_frag]  194 us
    gather x2, local copies, waits for them, and re-layouts, local(): sphere_motion = jnp.take(frag_motion, sphere_frag, axis=1)  119 us
    scatter-add x32, other arithmetic, accumulate(): return (total.at[:, own_cell].add(forces), None)  87.6 us
    gather x32, local copies, waits for them, and re-layouts, accumulate(): jnp.take(padded, other_pad, axis=1)  75 us
    gather x32, local copies, waits for them, and re-layouts, accumulate(): jnp.take(padded, own_pad, axis=1)  75 us
  transfers between devices with their start and end apart: 8, of which 8 were waited for; matrix products, arithmetic and copies ran while one was open for 0% of the time, Pallas kernels for 0%

commit v1 on v0

v1 whole, which is shorter than its diff:
```python
import functools

import jax
import jax.numpy as jnp
from jax import lax
from jax.experimental import pallas as pl
from jax.experimental.pallas import tpu as pltpu
from jax.sharding import PartitionSpec as P

stiffness = 100.0
damping = 2.0
time_step = 0.01
gravity = 9.81
epsilon_sq = 1e-08
radius_top = 0.14

GROUP = 32
GROUP_BITS = GROUP.bit_length() - 1
UNITS = 4
VMEM = 56 * 1024 * 1024


def lanes_of(values, index):
    return jnp.take_along_axis(values, index, axis=1, mode="promise_in_bounds")


def split_rows(values):
    high = values.astype(jnp.bfloat16).astype(jnp.float32)
    rest = values - high
    middle = rest.astype(jnp.bfloat16).astype(jnp.float32)
    low = rest - middle
    return jnp.concatenate([high, middle, low], axis=0).astype(jnp.bfloat16)


def joined_rows(stacked):
    rows = stacked.shape[0] // 3
    return stacked[0:rows] + stacked[rows : 2 * rows] + stacked[2 * rows :]


def dot_lanes(first, second):
    return lax.dot_general(
        first, second, (((1,), (1,)), ((), ())), preferred_element_type=jnp.float32
    )


def with_halo(x, sides, width):
    for axis, dim in sides:
        devices, length = (lax.axis_size(axis), x.shape[dim])
        up = [(i, (i + 1) % devices) for i in range(devices)]
        down = [(j, i) for i, j in up]
        last = lax.slice_in_dim(x, length - width, length, axis=dim)
        initial = lax.slice_in_dim(x, 0, width, axis=dim)
        before = lax.ppermute(last, axis, up)
        after = lax.ppermute(initial, axis, down)
        x = jnp.concatenate([before, x, after], axis=dim)
    return x


def pack_kernel(state_ref, frag_ref, key_ref, out_ref):
    cells = frag_ref.shape[0]
    for comp in range(7):
        out_ref[:, comp, :] = state_ref[comp]
    keys = jnp.broadcast_to(key_ref[0:1, :], (8, key_ref.shape[1]))
    for block in range(cells // 8):
        rows = pl.ds(block * 8, 8)
        out_ref[rows, 7, :] = lanes_of(keys, frag_ref[rows, :])


def list_kernel(near_smem, need_smem, table_ref, slots_ref, count_ref, class_ref, member_ref):
    tiles = slots_ref.shape[0]
    lanes = slots_ref.shape[1]
    radius = table_ref[:, 6, :] + (radius_top + 1e-5)
    classes = jnp.zeros(class_ref.shape, jnp.int32)
    for axis in range(3):
        place = table_ref[:, axis, :]
        classes = classes | jnp.where(place < radius, 1 << (2 * axis), 0)
        classes = classes | jnp.where(place > 1.0 - radius, 2 << (2 * axis), 0)
    class_ref[...] = classes

    def copy_rows(block, unused):
        for unit in range(8):
            tile = block * 8 + unit
            need = need_smem[tile]
            row = class_ref[pl.ds(near_smem[tile], 1), :]
            member_ref[pl.ds(tile, 1), :] = jnp.where((row & need) == need, 1, 0)
        return unused

    lax.fori_loop(0, tiles // 8, copy_rows, 0)

    before = lax.broadcasted_iota(jnp.int32, (lanes, lanes), 0)
    after = lax.broadcasted_iota(jnp.int32, (lanes, lanes), 1)
    earlier = (before < after).astype(jnp.bfloat16)
    ones = jnp.ones((8, lanes), jnp.bfloat16)
    step_rows = 64

    def compact(block, unused):
        rows = pl.ds(pl.multiple_of(block * step_rows, step_rows), step_rows)
        member = member_ref[rows, :]
        flags = member.astype(jnp.float32).astype(jnp.bfloat16)
        rank = jnp.dot(flags, earlier, preferred_element_type=jnp.float32)
        slot = lax.broadcasted_iota(jnp.int32, (step_rows, lanes), 1)
        moves = slot - rank.astype(jnp.int32)
        word = jnp.where(member != 0, slot + lanes * moves, 0)
        bit = 1
        while bit < lanes:
            keep = jnp.where((word & (bit * lanes)) != 0, 0, word)
            gone = word ^ keep
            word = keep | pltpu.roll(gone, lanes - bit, 1)
            bit *= 2
        slots_ref[rows, :] = word & (lanes - 1)
        return unused

    lax.fori_loop(0, tiles // step_rows, compact, 0)
    for block in range(tiles // lanes):
        flags = member_ref[pl.ds(block * lanes, lanes), :].astype(jnp.float32).astype(jnp.bfloat16)
        count_ref[:, pl.ds(block * lanes, lanes)] = dot_lanes(ones, flags).astype(jnp.int32)


def force_kernel(
    near_smem,
    shift_smem,
    own_smem,
    first_smem,
    count_smem,
    place_smem,
    table_ref,
    slots_ref,
    shift_ref,
    arms_ref,
    frag_ref,
    out_ref,
    list_ref,
    turned_ref,
    force_ref,
    loads_ref,
    cell_smem,
):
    tiles = slots_ref.shape[0]
    lanes = slots_ref.shape[1]
    cells = frag_ref.shape[0]
    held = out_ref.shape[1]
    lane_bits = lanes.bit_length() - 1
    lane = lax.broadcasted_iota(jnp.int32, (8, lanes), 1)
    row = lax.broadcasted_iota(jnp.int32, (8, lanes), 0)
    absent = jnp.where(row == 6, -10.0, 0.0)

    force_ref[...] = jnp.zeros(force_ref.shape, jnp.float32)

    def fill(block, carry):
        end, last_chunk, last_new, last_held = carry
        for unit in range(8):
            tile = block * 8 + unit
            align = first_smem[tile]
            own = own_smem[tile]
            start = (end + align) & ~align
            amount = count_smem[0, tile]
            chunk = start >> lane_bits
            offset = start & (lanes - 1)
            for piece in range(lanes // GROUP + 1):
                cell_smem[(start >> GROUP_BITS) + piece] = own
            slots = jnp.broadcast_to(slots_ref[pl.ds(tile, 1), :], (8, lanes))
            slots = pltpu.roll(slots, offset, 1)
            found = lanes_of(table_ref[near_smem[tile]], slots) + shift_ref[shift_smem[tile]]
            new = jnp.where(((lane - offset) & (lanes - 1)) < amount, found, absent)
            held_row = jnp.where(chunk != last_chunk, last_new, last_held)
            held_row = jnp.where(lane >= offset, new, held_row)
            new = jnp.where(lane >= offset, absent, new)
            list_ref[pl.ds(pl.multiple_of(chunk * 8, 8), 8), :] = held_row
            list_ref[pl.ds(pl.multiple_of(chunk * 8 + 8, 8), 8), :] = new
            end, last_chunk, last_new, last_held = start + amount, chunk, new, held_row
        return end, last_chunk, last_new, last_held

    start = (jnp.int32(0), jnp.int32(0), absent, absent)
    end = lax.fori_loop(0, tiles // 8, fill, start)[0]
    groups = (end + GROUP - 1) >> GROUP_BITS
    for extra in range(UNITS):
        cell_smem[groups + extra] = cells

    def turn(block, unused):
        rows = pl.ds(pl.multiple_of(block * lanes, lanes), lanes)
        turned_ref[rows, :] = list_ref[rows, :].T
        return unused

    lax.fori_loop(0, (end + 16 * lanes - 1) >> (lane_bits + 4), turn, 0)

    def pairs(step, unused):
        totals = []
        for unit in range(UNITS):
            group = step * UNITS + unit
            cell = cell_smem[group]
            own = place_smem[cell]
            begin = group * GROUP
            chunk = begin >> lane_bits
            at = (chunk >> 4) * lanes + (begin & (lanes - 1))
            block = turned_ref[pl.ds(pl.multiple_of(at, GROUP), GROUP), :]
            column = (chunk & 15) * 8
            other = [
                lanes_of(block, jnp.full((GROUP, lanes), column + comp, jnp.int32))
                for comp in range(8)
            ]
            mine = [table_ref[own, pl.ds(comp, 1), :] for comp in range(8)]
            apart = [other[axis] - mine[axis] for axis in range(3)]
            square = apart[0] * apart[0] + apart[1] * apart[1] + apart[2] * apart[2] + epsilon_sq
            inverse = lax.rsqrt(square)
            reach = other[6] + mine[6]
            overlap = jnp.maximum(reach - square * inverse, 0.0)
            overlap = jnp.where(other[7] != mine[7], overlap, 0.0)
            closing = (
                (other[3] - mine[3]) * apart[0]
                + (other[4] - mine[4]) * apart[1]
                + (other[5] - mine[5]) * apart[2]
            )
            scaled = overlap * (other[6] * mine[6])
            root = scaled * lax.rsqrt(jnp.maximum(scaled * reach, 1e-30))
            factor = (
                root * inverse * (stiffness / damping * overlap - closing * inverse)
            )
            totals.append(
                (
                    cell,
                    [
                        jnp.sum((factor * apart[axis]).reshape(GROUP // 8, 8, lanes), axis=0)
                        for axis in range(3)
                    ],
                )
            )
        for cell, parts in totals:
            for axis in range(3):
                force_ref[axis, cell] += parts[axis]
        return unused

    lax.fori_loop(0, lax.div(groups + (UNITS - 1), UNITS), pairs, 0)

    label = lax.broadcasted_iota(jnp.int32, (held, lanes), 0)

    def gather_sums(block, total):
        rows = pl.ds(pl.multiple_of(block * 8, 8), 8)
        force = [-damping * jnp.sum(force_ref[axis, rows], axis=1) for axis in range(3)]
        lever = [arms_ref[axis, rows, :] for axis in range(3)]
        torque = [
            lever[1] * force[2] - lever[2] * force[1],
            lever[2] * force[0] - lever[0] * force[2],
            lever[0] * force[1] - lever[1] * force[0],
        ]
        loads = force + torque + [jnp.zeros_like(force[0])] * 2
        for comp in range(8):
            loads_ref[:, comp, :] = loads[comp]
        frags = frag_ref[rows, :]
        for unit in range(8):
            hits = (frags[unit : unit + 1, :] == label).astype(jnp.float32).astype(jnp.bfloat16)
            total = total + dot_lanes(split_rows(loads_ref[unit]), hits)
        return total

    total = lax.fori_loop(0, cells // 8, gather_sums, jnp.zeros((24, held), jnp.float32))
    out_ref[...] = joined_rows(total)


def move_kernel(
    owned, target_ref, fixed_ref, sums_ref, state_ref, arms_ref, frag_ref, spheres_ref, clumps_ref
):
    bricks, _, held = sums_ref.shape
    lanes = frag_ref.shape[1]
    cells = frag_ref.shape[0]
    targets = jnp.broadcast_to(target_ref[...], (lanes, held))
    lane = lax.broadcasted_iota(jnp.int32, (1, held), 1)

    def match(brick, carry):
        sums, base = carry
        fixed = fixed_ref[brick]
        hits = (targets == fixed[8:9, :]).astype(jnp.float32).astype(jnp.bfloat16)
        sums = sums + dot_lanes(split_rows(sums_ref[brick]), hits)
        number = jnp.where(lane < owned, brick * owned + lane, -1).astype(jnp.float32)
        hits = (targets == number).astype(jnp.float32).astype(jnp.bfloat16)
        base = base + dot_lanes(split_rows(fixed[0:8, :]), hits)
        return sums, base

    zero = jnp.zeros((24, lanes), jnp.float32)
    sums, base = lax.fori_loop(0, bricks, match, (zero, zero))
    sums = joined_rows(sums)
    base = joined_rows(base)
    rows = []
    for axis in range(3):
        pull = gravity if axis == 2 else 0.0
        rows.append(
            base[axis : axis + 1]
            + time_step * (sums[axis : axis + 1] * base[6:7] - pull)
        )
    for axis in range(3, 6):
        rows.append(base[axis : axis + 1] + time_step * sums[axis : axis + 1] * base[7:8])
    for comp in range(6):
        clumps_ref[comp : comp + 1, :] = rows[comp]
    wide = [jnp.broadcast_to(value, (8, lanes)) for value in rows]

    def cross(first, second):
        return [
            first[1] * second[2] - first[2] * second[1],
            first[2] * second[0] - first[0] * second[2],
            first[0] * second[1] - first[1] * second[0],
        ]

    def move(block, unused):
        at = pl.ds(pl.multiple_of(block * 8, 8), 8)
        index = frag_ref[at, :] + (lanes - held)
        motion = [lanes_of(value, index) for value in wide]
        velocity, spin = motion[0:3], motion[3:6]
        arm = [arms_ref[axis, at, :] for axis in range(3)]
        half = [0.5 * time_step * value for value in spin]
        turned = cross(half, arm)
        twice = cross(half, turned)
        scale = 2.0 / (1.0 + half[0] * half[0] + half[1] * half[1] + half[2] * half[2])
        change = [scale * (turned[axis] + twice[axis]) for axis in range(3)]
        new_arm = [arm[axis] + change[axis] for axis in range(3)]
        swing = cross(spin, new_arm)
        for axis in range(3):
            spheres_ref[axis, at, :] = (
                state_ref[axis, at, :] + time_step * velocity[axis] + (new_arm[axis] - arm[axis])
            )
            spheres_ref[3 + axis, at, :] = velocity[axis] + swing[axis]
        return unused

    lax.fori_loop(0, cells // 8, move, 0)


def local(
    state, arms, sphere_frag, frag_owner, frag_clump, tiles, clump_motion, inv_mass, inv_moment
):
    cells_x, cells_y, cells_z = (state.shape[1], state.shape[2], state.shape[3])
    lanes = state.shape[4]
    cells = cells_x * cells_y * cells_z
    owned = inv_mass.shape[0]
    held = frag_clump.shape[0]
    names = ("gx", "gy", "gz")
    vmem = pl.BlockSpec(memory_space=pltpu.VMEM)
    smem = pl.BlockSpec(memory_space=pltpu.SMEM)
    params = pltpu.CompilerParams(vmem_limit_bytes=VMEM)

    frag_key = (frag_owner[:, 0] * owned + frag_clump).astype(jnp.float32)
    flat_state = state.reshape(7, cells, lanes)
    flat_arms = arms.reshape(3, cells, lanes)
    flat_frag = sphere_frag.reshape(cells, lanes)

    fixed = jnp.concatenate(
        [
            jnp.pad(
                jnp.concatenate([clump_motion, inv_mass[None], inv_moment[None]], axis=0),
                ((0, 0), (0, held - owned)),
            ),
            frag_key[None],
            jnp.zeros((7, held), jnp.float32),
        ],
        axis=0,
    )
    fixed = lax.all_gather(fixed, names, axis=0, tiled=False)

    table = pl.pallas_call(
        pack_kernel,
        out_shape=jax.ShapeDtypeStruct((cells, 8, lanes), jnp.float32),
        in_specs=[vmem] * 3,
        out_specs=vmem,
        compiler_params=params,
    )(flat_state, flat_frag, jnp.pad(frag_key, (0, lanes - held))[None])
    padded = with_halo(
        table.reshape(cells_x, cells_y, cells_z, 8, lanes), (("gx", 0), ("gy", 1), ("gz", 2)), 1
    )
    span_y, span_z = (cells_y + 2, cells_z + 2)
    span = (cells_x + 2) * span_y * span_z
    padded = padded.reshape(span, 8, lanes)

    codes = jnp.sort(tiles[0])
    total = codes.shape[0]
    own = codes // 27
    offset = codes % 27
    steps = (offset // 9 - 1, offset // 3 % 3 - 1, offset % 3 - 1)

    def pad_place(cell):
        x = cell // (cells_y * cells_z) + 1
        y = cell // cells_z % cells_y + 1
        z = cell % cells_z + 1
        return (x * span_y + y) * span_z + z

    near = pad_place(own) + (steps[0] * span_y + steps[1]) * span_z + steps[2]
    need = sum(
        jnp.where(steps[axis] == 1, 1, jnp.where(steps[axis] == -1, 2, 0)) << (2 * axis)
        for axis in range(3)
    )
    first = jnp.where(own != jnp.roll(own, 1), GROUP - 1, 0).at[0].set(GROUP - 1)
    place = pad_place(jnp.arange(cells + 1, dtype=jnp.int32) % cells)
    kinds = jnp.arange(27, dtype=jnp.int32)
    moves = jnp.stack([kinds // 9 - 1, kinds // 3 % 3 - 1, kinds % 3 - 1], axis=1)
    shift = jnp.pad(moves.astype(jnp.float32), ((0, 0), (0, 5)))
    shift = jnp.broadcast_to(shift[:, :, None], (27, 8, lanes))

    slots, count = pl.pallas_call(
        list_kernel,
        out_shape=(
            jax.ShapeDtypeStruct((total, lanes), jnp.int32),
            jax.ShapeDtypeStruct((8, total), jnp.int32),
        ),
        in_specs=[smem, smem, vmem],
        out_specs=(vmem, vmem),
        scratch_shapes=[
            pltpu.VMEM((span, lanes), jnp.int32),
            pltpu.VMEM((total, lanes), jnp.int32),
        ],
        compiler_params=params,
    )(near, need, padded)

    chunks = total + cells * GROUP // lanes + 2
    chunks = -(-chunks // 16) * 16
    sums = pl.pallas_call(
        force_kernel,
        out_shape=jax.ShapeDtypeStruct((8, held), jnp.float32),
        in_specs=[smem] * 6 + [vmem] * 5,
        out_specs=vmem,
        scratch_shapes=[
            pltpu.VMEM((chunks * 8, lanes), jnp.float32),
            pltpu.VMEM((chunks * 8, lanes), jnp.float32),
            pltpu.VMEM((3, cells + 8, 8, lanes), jnp.float32),
            pltpu.VMEM((8, 8, lanes), jnp.float32),
            pltpu.SMEM((chunks * (lanes // GROUP) + 16,), jnp.int32),
        ],
        compiler_params=params,
    )(near, offset, own, first, count[0:1], place, padded, slots, shift, flat_arms, flat_frag)

    sums = lax.all_gather(sums, names, axis=0, tiled=False)

    brick = lax.axis_index(names)
    mine = jnp.where(
        jnp.arange(lanes - held) < owned, brick * owned + jnp.arange(lanes - held), -2
    ).astype(jnp.float32)
    target = jnp.concatenate([mine, frag_key])[:, None]
    spheres, clumps = pl.pallas_call(
        functools.partial(move_kernel, owned),
        out_shape=(
            jax.ShapeDtypeStruct((6, cells, lanes), jnp.float32),
            jax.ShapeDtypeStruct((6, lanes), jnp.float32),
        ),
        in_specs=[vmem] * 6,
        out_specs=(vmem, vmem),
        compiler_params=params,
    )(target, fixed, sums, flat_state, flat_arms, flat_frag)
    return (spheres.reshape((6,) + state.shape[1:]), clumps[:, :owned])


def solution(mesh):
    return jax.shard_map(
        local,
        mesh=mesh,
        in_specs=(
            P(None, "gx", "gy", "gz", None),
            P(None, "gx", "gy", "gz", None),
            P("gx", "gy", "gz", None),
            P(("gx", "gy", "gz"), None),
            P(("gx", "gy", "gz")),
            P(("gx", "gy", "gz"), None),
            P(None, ("gx", "gy", "gz")),
            P(("gx", "gy", "gz")),
            P(("gx", "gy", "gz")),
        ),
        out_specs=(P(None, "gx", "gy", "gz", None), P(None, ("gx", "gy", "gz"))),
        check_vma=False,
    )
```

time: 1380 us -> 379 us (0.27)
  other arithmetic: 821 us -> 11.1 us
  local copies, waits for them, and re-layouts: 492 us -> 4.87 us
  Pallas kernels: 0 us -> 193 us
  blocking collectives: 0 us -> 141 us
  waiting for transfers between devices: 43.6 us -> 15.9 us
    reduce_sum x33 -> x0, other arithmetic: 489 us -> none  [the longest x32 488 us: pair_forces(): jnp.sum(factor * separation[axis_k], axis=2)]
    gather x69 -> x0, local copies, waits for them, and re-layouts: 464 us -> none  [the longest x1 194 us: local(): sphere_key = frag_key[sphere_frag]]
    scatter-add x33 -> x0, other arithmetic: 304 us -> none  [the longest x1 216 us: local(): jax.ops.segment_sum(loads.T, sphere_frag.reshape(-1), num_segments=held)]
    pallas_call x0 -> x4, Pallas kernels: none -> 193 us  [the longest x1 151 us: local(): pl.pallas_call(force_kernel, out_shape=jax.ShapeDtypeStruct((8, held), jn...]
    all_gather x0 -> x2, blocking collectives: none -> 141 us  [the longest x1 71.3 us: local(): fixed = lax.all_gather(fixed, names, axis=0, tiled=False)]
    all_to_all x2 -> x0, waiting for transfers between devices: 14.3 us -> none  [the longest x1 7.17 us: local(): lax.all_to_all(outbox, ('gx', 'gy', 'gz'), split_axis=1, concat_axis=1, t...]
  transfers between devices with their start and end apart: 8 -> 6, of which waited for: 8 -> 2; matrix products, arithmetic and copies ran while one was open for 0% -> 2% of each run, Pallas kernels for 0% -> 0%
where the time goes in v1:
time: 379 us; the launch traced here: 376 us
  Pallas kernels  193 us (51%)
  blocking collectives  141 us (37%)
  waiting for transfers between devices  15.9 us (4%)
  other arithmetic  11.1 us (3%)
  starting transfers between devices  9.06 us (2%)
  local copies, waits for them, and re-layouts  4.87 us (1%)
    pallas_call x1, Pallas kernels, local(): pl.pallas_call(force_kernel, out_shape=jax.ShapeDtypeStruct((8, held), jn...  151 us
    all_gather x1, blocking collectives, local(): fixed = lax.all_gather(fixed, names, axis=0, tiled=False)  71.3 us
    all_gather x1, blocking collectives, local(): sums = lax.all_gather(sums, names, axis=0, tiled=False)  69.3 us
    pallas_call x1, Pallas kernels, local(): pl.pallas_call(list_kernel, out_shape=(jax.ShapeDtypeStruct((total, lanes...  29.2 us
    pallas_call x1, Pallas kernels, local(): pl.pallas_call(functools.partial(move_kernel, owned), out_shape=(jax.Shap...  10.3 us
    ppermute x3, waiting for transfers between devices, with_halo(): before = lax.ppermute(last, axis, up)  8.87 us
  transfers between devices with their start and end apart: 6, of which 2 were waited for; matrix products, arithmetic and copies ran while one was open for 2% of the time, Pallas kernels for 0%

profile of v1, /device:TPU:0, one launch (start us, length us, event | category | flops | bytes accessed | tf_op | source)
XLA Modules:
  0.0 375.6 jit_solution(14863608788978069835)
XLA Ops:
  0.6 0.7 fusion.38
  1.3 0.5 pad_bitcast_fusion
  1.8 2.9 shard_map.104
  4.8 1.2 fusion.40
  6.4 2.0 collective-permute-start.1
  8.5 5.0 %sort.15 = (s32[2048]{0:T(1024)S(1)}, s32[2048]{0:T(1024)}) sort(s32[2048]{0:T(1024)S(1)} %bitcast.41, s32[2048]{0:T(1024)S(1)} %iota.26), dimensions={0}, to_apply=%region_0.1 | sort | flops 22528 | bytes 32768 | tf_op jit(solution)/shard_map/jit(sort)/sort | solution.py:369
  13.5 0.6 slice.60
  14.1 1.3 shift-left_add_fusion
  15.4 1.1 pad_maximum_fusion.3
  16.5 2.4 collective-permute-start.2
  18.9 2.1 collective-permute-start.3
  21.1 0.7 copy.13.target_ref
  22.0 8.9 %collective-permute-done.2 = f32[6,1,16,8,128]{4,3,2,1,0:T(8,128)S(1)} collective-permute-done((f32[6,1,16,8,128]{4,3,2,1,0:T(8,128)S(1)}, f32[6,1,16,8,128]{4,3,2,1,0:T(8,128)S(1)}, u32[]{:S(2)}, u32[]{:S(2)}) %collective-permute-start.2) | collective-permute-done | bytes 393248 | tf_op jit(solution)/shard_map/ppermute | solution.py:53
  30.9 7.0 %collective-permute-done.3 = f32[6,1,16,8,128]{4,3,2,1,0:T(8,128)S(1)} collective-permute-done((f32[6,1,16,8,128]{4,3,2,1,0:T(8,128)S(1)}, f32[6,1,16,8,128]{4,3,2,1,0:T(8,128)S(1)}, u32[]{:S(2)}, u32[]{:S(2)}) %collective-permute-start.3) | collective-permute-done | bytes 393248 | tf_op jit(solution)/shard_map/ppermute | solution.py:54
  37.9 1.6 collective-permute-start.4
  40.0 71.3 %all-gather = f32[512,64]{1,0:T(8,128)} all-gather(f32[16,64]{1,0:T(8,128)S(1)} %maximum_maximum_fusion), channel_id=2, replica_groups=mesh['gx'=4,'gy'=4,'gz'=2] {'gx','gy','gz'}, dimensions={0}, use_global_device_ids=true | all-gather | bytes 135168 | tf_op jit(solution)/shard_map/all_gather | solution.py:353
  111.3 0.6 fusion.25.place_smem
  112.0 1.7 pad_maximum_fusion
  113.7 29.2 %shard_map.105 = (s32[2048,128]{1,0:T(8,128)}, s32[8,2048]{1,0:T(8,128)}) custom-call(s32[2048]{0:T(1024)} %get-tuple-element.33.near_smem, s32[2048]{0:T(1024)} %get-tuple-element.31.need_smem, f32[648,8,128]{2,1,0:T(8,128)} %bitcast.24), custom_call_target="tpu_custom_call" | custom-call | tf_op jit(solution)/shard_map/pallas_call | solution.py:393
  142.9 1.4 slice.58.count_smem
  144.3 0.7 broadcast_in_dim.55.shift_ref
  145.1 150.9 %shard_map.106 = f32[8,64]{1,0:T(8,128)} custom-call(s32[2048]{0:T(1024)} %get-tuple-element.33.near_smem, s32[2048]{0:T(1024)} %get-tuple-element.34.shift_smem, s32[2048]{0:T(1024)} %copy-done.1, s32[2048]{0:T(1024)} %copy-done.2, s32[1,2048]{1,0:T(1,128)} %slice.58.count_smem, s32[257]{0:T(512)} %fusion.25.place_smem, f32[648,8,128]{2,1,0:T(8,128)} %bitcast.25, ...), custom_call_target="tpu_custom_call" | custom-call | tf_op jit(solution)/shard_map/pallas_call | solution.py:410
  296.0 69.3 %all-gather.1 = f32[256,64]{1,0:T(8,128)} all-gather(f32[8,64]{1,0:T(8,128)} %shard_map.106), channel_id=3, replica_groups=mesh['gx'=4,'gy'=4,'gz'=2] {'gx','gy','gz'}, dimensions={0}, use_global_device_ids=true | all-gather | bytes 67584 | tf_op jit(solution)/shard_map/all_gather | solution.py:425
  365.3 10.3 %shard_map.107 = (f32[6,256,128]{2,1,0:T(8,128)}, f32[6,128]{1,0:T(8,128)}) custom-call(f32[128,1]{1,0:T(8,128)} %copy.13.target_ref, f32[32,16,64]{2,1,0:T(8,128)} %bitcast.36, f32[32,8,64]{2,1,0:T(8,128)} %bitcast.37, f32[7,256,128]{2,1,0:T(8,128)} %bitcast.30, f32[3,256,128]{2,1,0:T(8,128)} %bitcast.32, s32[256,128]{1,0:T(8,128)} %bitcast.35), custom_call_target="tpu_custom_call" | custom-call | tf_op jit(solution)/shard_map/pallas_call | solution.py:432
  (33 shorter events, 1.4 us)
Async XLA Ops:
  0.6 7.8 %copy-start.3 = (s32[1,2048]{1,0:T(1,128)S(1)}, s32[1,2048]{1,0:T(1,128)}, u32[]{:S(2)}) copy-start(s32[1,2048]{1,0:T(1,128)} %param.16) | copy-start | bytes 24580
  1.8 20.1 %copy-start.4 = (f32[6,48]{1,0:T(8,128)S(1)}, f32[6,48]{1,0:T(8,128)}, u32[]{:S(2)}) copy-start(f32[6,48]{1,0:T(8,128)} %param.17) | copy-start | bytes 3460
  1.8 20.1 %copy-start.5 = (f32[48]{0:T(128)S(1)}, f32[48]{0:T(128)}, u32[]{:S(2)}) copy-start(f32[48]{0:T(128)} %param.19) | copy-start | bytes 580
  1.8 20.1 %copy-start.6 = (f32[48]{0:T(128)S(1)}, f32[48]{0:T(128)}, u32[]{:S(2)}) copy-start(f32[48]{0:T(128)} %param.18) | copy-start | bytes 580
  4.8 33.2 %copy-start = (f32[256,8,128]{2,1,0:T(8,128)S(1)}, f32[256,8,128]{2,1,0:T(8,128)}, u32[]{:S(2)}) copy-start(f32[256,8,128]{2,1,0:T(8,128)} %shard_map.104) | copy-start | bytes 3145732
  5.9 9.5 %collective-permute-start = (f32[1,4,16,8,128]{4,3,2,1,0:T(8,128)S(1)}, f32[1,4,16,8,128]{4,3,2,1,0:T(8,128)S(1)}, u32[]{:S(2)}, u32[]{:S(2)}) collective-permute-start(f32[1,4,16,8,128]{4,3,2,1,0:T(8,128)S(1)} %bitcast.39), channel_id=1, source_target_pairs={{0,8},{8,16},{16,24},{24,0},{1,9},{9,17},{17,25},{25,1},{2,10},{10... | collective-permute-start | bytes 786440 | tf_op jit(solution)/shard_map/ppermute | solution.py:53
  6.4 9.0 %collective-permute-start.1 = (f32[1,4,16,8,128]{4,3,2,1,0:T(8,128)S(1)}, f32[1,4,16,8,128]{4,3,2,1,0:T(8,128)S(1)}, u32[]{:S(2)}, u32[]{:S(2)}) collective-permute-start(f32[1,4,16,8,128]{4,3,2,1,0:T(8,128)S(1)} %bitcast.38), channel_id=1, source_target_pairs={{8,0},{16,8},{24,16},{0,24},{9,1},{17,9},{25,17},{1,25},{10,2},{18... | collective-permute-start | bytes 786440 | tf_op jit(solution)/shard_map/ppermute | solution.py:54
  13.5 97.8 %copy-start.1 = (s32[2048]{0:T(1024)}, s32[2048]{0:T(1024)S(1)}, u32[]{:S(2)}) copy-start(s32[2048]{0:T(1024)S(1)} %add_select_fusion.9.own_smem) | copy-start | bytes 24580
  16.5 14.4 %collective-permute-start.2 = (f32[6,1,16,8,128]{4,3,2,1,0:T(8,128)S(1)}, f32[6,1,16,8,128]{4,3,2,1,0:T(8,128)S(1)}, u32[]{:S(2)}, u32[]{:S(2)}) collective-permute-start(f32[6,1,16,8,128]{4,3,2,1,0:T(8,128)S(1)} %get-tuple-element.27), channel_id=1, source_target_pairs={{0,2},{2,4},{4,6},{6,0},{1,3},{3,5},{5,7},{7,1},{8,10},{10,12},{12... | collective-permute-start | bytes 1179656 | tf_op jit(solution)/shard_map/ppermute | solution.py:53
  18.9 19.0 %collective-permute-start.3 = (f32[6,1,16,8,128]{4,3,2,1,0:T(8,128)S(1)}, f32[6,1,16,8,128]{4,3,2,1,0:T(8,128)S(1)}, u32[]{:S(2)}, u32[]{:S(2)}) collective-permute-start(f32[6,1,16,8,128]{4,3,2,1,0:T(8,128)S(1)} %get-tuple-element.28), channel_id=1, source_target_pairs={{2,0},{4,2},{6,4},{0,6},{3,1},{5,3},{7,5},{1,7},{10,8},{12,10},{14... | collective-permute-start | bytes 1179656 | tf_op jit(solution)/shard_map/ppermute | solution.py:54
  21.8 91.8 %copy-start.2 = (s32[2048]{0:T(1024)}, s32[2048]{0:T(1024)S(1)}, u32[]{:S(2)}) copy-start(s32[2048]{0:T(1024)S(1)} %constant_dynamic-update-slice_fusion.first_smem) | copy-start | bytes 24580
  37.9 74.0 %collective-permute-start.4 = (f32[6,6,1,8,128]{4,3,2,1,0:T(8,128)S(1)}, f32[6,6,1,8,128]{4,3,2,1,0:T(8,128)S(1)}, u32[]{:S(2)}, u32[]{:S(2)}) collective-permute-start(f32[6,6,1,8,128]{4,3,2,1,0:T(8,128)S(1)} %get-tuple-element.25), channel_id=1, source_target_pairs={{0,1},{1,0},{2,3},{3,2},{4,5},{5,4},{6,7},{7,6},{8,9},{9,8},{10,11... | collective-permute-start | bytes 442376 | tf_op jit(solution)/shard_map/ppermute | solution.py:53
  39.5 72.4 %collective-permute-start.5 = (f32[6,6,1,8,128]{4,3,2,1,0:T(8,128)S(1)}, f32[6,6,1,8,128]{4,3,2,1,0:T(8,128)S(1)}, u32[]{:S(2)}, u32[]{:S(2)}) collective-permute-start(f32[6,6,1,8,128]{4,3,2,1,0:T(8,128)S(1)} %get-tuple-element.26), channel_id=1, source_target_pairs={{1,0},{0,1},{3,2},{2,3},{5,4},{4,5},{7,6},{6,7},{9,8},{8,9},{11,10... | collective-permute-start | bytes 442376 | tf_op jit(solution)/shard_map/ppermute | solution.py:54

commit v2 on v1

--- a/solution.py
+++ b/solution.py
@@ -41,6 +41,12 @@
     return lax.dot_general(
         first, second, (((1,), (1,)), ((), ())), preferred_element_type=jnp.float32
     )
+
+
+def everywhere(x, names):
+    devices = lax.axis_size(names)
+    copies = jnp.broadcast_to(x[None], (devices,) + x.shape)
+    return lax.all_to_all(copies, names, split_axis=0, concat_axis=0, tiled=True)
 
 
 def with_halo(x, sides, width):
@@ -69,10 +75,15 @@
 def list_kernel(near_smem, need_smem, table_ref, slots_ref, count_ref, class_ref, member_ref):
     tiles = slots_ref.shape[0]
     lanes = slots_ref.shape[1]
-    radius = table_ref[:, 6, :] + (radius_top + 1e-5)
+    span = class_ref.shape[0]
+
+    def plane(comp):
+        return table_ref[pl.ds(comp, span, stride=8), :]
+
+    radius = plane(6) + (radius_top + 1e-5)
     classes = jnp.zeros(class_ref.shape, jnp.int32)
     for axis in range(3):
-        place = table_ref[:, axis, :]
+        place = plane(axis)
         classes = classes | jnp.where(place < radius, 1 << (2 * axis), 0)
         classes = classes | jnp.where(place > 1.0 - radius, 2 << (2 * axis), 0)
     class_ref[...] = classes
@@ -91,7 +102,7 @@
     after = lax.broadcasted_iota(jnp.int32, (lanes, lanes), 1)
     earlier = (before < after).astype(jnp.bfloat16)
     ones = jnp.ones((8, lanes), jnp.bfloat16)
-    step_rows = 64
+    step_rows = 256
 
     def compact(block, unused):
         rows = pl.ds(pl.multiple_of(block * step_rows, step_rows), step_rows)
@@ -116,36 +127,16 @@
         count_ref[:, pl.ds(block * lanes, lanes)] = dot_lanes(ones, flags).astype(jnp.int32)
 
 
-def force_kernel(
-    near_smem,
-    shift_smem,
-    own_smem,
-    first_smem,
-    count_smem,
-    place_smem,
-    table_ref,
-    slots_ref,
-    shift_ref,
-    arms_ref,
-    frag_ref,
-    out_ref,
-    list_ref,
-    turned_ref,
-    force_ref,
-    loads_ref,
-    cell_smem,
+def fill_kernel(
+    near_smem, shift_smem, own_smem, first_smem, count_smem, table_ref, slots_ref, shift_ref,
+    turned_ref, cell_smem, groups_smem, list_ref,
 ):
     tiles = slots_ref.shape[0]
     lanes = slots_ref.shape[1]
-    cells = frag_ref.shape[0]
-    held = out_ref.shape[1]
     lane_bits = lanes.bit_length() - 1
     lane = lax.broadcasted_iota(jnp.int32, (8, lanes), 1)
     row = lax.broadcasted_iota(jnp.int32, (8, lanes), 0)
     absent = jnp.where(row == 6, -10.0, 0.0)
-
-    force_ref[...] = jnp.zeros(force_ref.shape, jnp.float32)
-
     def fill(block, carry):
         end, last_chunk, last_new, last_held = carry
         for unit in range(8):
@@ -174,7 +165,8 @@
     end = lax.fori_loop(0, tiles // 8, fill, start)[0]
     groups = (end + GROUP - 1) >> GROUP_BITS
     for extra in range(UNITS):
-        cell_smem[groups + extra] = cells
+        cell_smem[groups + extra] = -1
+    groups_smem[0] = groups
 
     def turn(block, unused):
         rows = pl.ds(pl.multiple_of(block * lanes, lanes), lanes)
@@ -182,13 +174,22 @@
         return unused
 
     lax.fori_loop(0, (end + 16 * lanes - 1) >> (lane_bits + 4), turn, 0)
+
+
+def pair_kernel(cell_smem, groups_smem, place_smem, table_ref, turned_ref, force_ref):
+    lanes = table_ref.shape[2]
+    lane_bits = lanes.bit_length() - 1
+    cells = place_smem.shape[0]
+    groups = groups_smem[0]
+    force_ref[...] = jnp.zeros(force_ref.shape, jnp.float32)
 
     def pairs(step, unused):
         totals = []
         for unit in range(UNITS):
             group = step * UNITS + unit
             cell = cell_smem[group]
-            own = place_smem[cell]
+            target = jnp.where(cell < 0, cells, cell)
+            own = place_smem[jnp.maximum(cell, 0)]
             begin = group * GROUP
             chunk = begin >> lane_bits
             at = (chunk >> 4) * lanes + (begin & (lanes - 1))
@@ -217,7 +218,7 @@
             )
             totals.append(
                 (
-                    cell,
+                    target,
                     [
                         jnp.sum((factor * apart[axis]).reshape(GROUP // 8, 8, lanes), axis=0)
                         for axis in range(3)
@@ -231,6 +232,10 @@
 
     lax.fori_loop(0, lax.div(groups + (UNITS - 1), UNITS), pairs, 0)
 
+
+def sums_kernel(force_ref, arms_ref, frag_ref, out_ref, loads_ref):
+    cells, lanes = frag_ref.shape
+    held = out_ref.shape[1]
     label = lax.broadcasted_iota(jnp.int32, (held, lanes), 0)
 
     def gather_sums(block, total):
@@ -255,29 +260,44 @@
     out_ref[...] = joined_rows(total)
 
 
+def add_over(bricks, dots, rows, lanes):
+    def step(block, total):
+        parts = [dots(block * 8 + unit) for unit in range(8)]
+        while len(parts) > 1:
+            parts = [first + second for first, second in zip(parts[::2], parts[1::2])]
+        return total + parts[0]
+
+    return joined_rows(lax.fori_loop(0, bricks // 8, step, jnp.zeros((rows, lanes), jnp.float32)))
+
+
+def base_kernel(owned, target_ref, fixed_ref, base_ref):
+    bricks, _, held = fixed_ref.shape
+    lanes = target_ref.shape[0]
+    targets = jnp.broadcast_to(target_ref[...], (lanes, held))
+    lane = lax.broadcasted_iota(jnp.int32, (1, held), 1)
+
+    def dots(brick):
+        number = jnp.where(lane < owned, brick * owned + lane, -1).astype(jnp.float32)
+        hits = (targets == number).astype(jnp.float32).astype(jnp.bfloat16)
+        return dot_lanes(split_rows(fixed_ref[brick, 0:8, :]), hits)
+
+    base_ref[...] = add_over(bricks, dots, 24, lanes)
+
+
 def move_kernel(
-    owned, target_ref, fixed_ref, sums_ref, state_ref, arms_ref, frag_ref, spheres_ref, clumps_ref
+    target_ref, fixed_ref, base_ref, sums_ref, state_ref, arms_ref, frag_ref, spheres_ref, clumps_ref
 ):
     bricks, _, held = sums_ref.shape
     lanes = frag_ref.shape[1]
     cells = frag_ref.shape[0]
     targets = jnp.broadcast_to(target_ref[...], (lanes, held))
-    lane = lax.broadcasted_iota(jnp.int32, (1, held), 1)
-
-    def match(brick, carry):
-        sums, base = carry
-        fixed = fixed_ref[brick]
-        hits = (targets == fixed[8:9, :]).astype(jnp.float32).astype(jnp.bfloat16)
-        sums = sums + dot_lanes(split_rows(sums_ref[brick]), hits)
-        number = jnp.where(lane < owned, brick * owned + lane, -1).astype(jnp.float32)
-        hits = (targets == number).astype(jnp.float32).astype(jnp.bfloat16)
-        base = base + dot_lanes(split_rows(fixed[0:8, :]), hits)
-        return sums, base
-
-    zero = jnp.zeros((24, lanes), jnp.float32)
-    sums, base = lax.fori_loop(0, bricks, match, (zero, zero))
-    sums = joined_rows(sums)
-    base = joined_rows(base)
+
+    def dots(brick):
+        hits = (targets == fixed_ref[brick, 8:9, :]).astype(jnp.float32).astype(jnp.bfloat16)
+        return dot_lanes(split_rows(sums_ref[brick]), hits)
+
+    sums = add_over(bricks, dots, 24, lanes)
+    base = base_ref[...]
     rows = []
     for axis in range(3):
         pull = gravity if axis == 2 else 0.0
@@ -289,7 +309,8 @@
         rows.append(base[axis : axis + 1] + time_step * sums[axis : axis + 1] * base[7:8])
     for comp in range(6):
         clumps_ref[comp : comp + 1, :] = rows[comp]
-    wide = [jnp.broadcast_to(value, (8, lanes)) for value in rows]
+    tall = 32
+    wide = [jnp.broadcast_to(value, (tall, lanes)) for value in rows]
 
     def cross(first, second):
         return [
@@ -299,7 +320,7 @@
         ]
 
     def move(block, unused):
-        at = pl.ds(pl.multiple_of(block * 8, 8), 8)
+        at = pl.ds(pl.multiple_of(block * tall, tall), tall)
         index = frag_ref[at, :] + (lanes - held)
         motion = [lanes_of(value, index) for value in wide]
         velocity, spin = motion[0:3], motion[3:6]
@@ -318,7 +339,7 @@
             spheres_ref[3 + axis, at, :] = velocity[axis] + swing[axis]
         return unused
 
-    lax.fori_loop(0, cells // 8, move, 0)
+    lax.fori_loop(0, cells // tall, move, 0)
 
 
 def local(
@@ -350,7 +371,7 @@
         ],
         axis=0,
     )
-    fixed = lax.all_gather(fixed, names, axis=0, tiled=False)
+    fixed = everywhere(fixed, names)
 
     table = pl.pallas_call(
         pack_kernel,
@@ -384,7 +405,7 @@
         for axis in range(3)
     )
     first = jnp.where(own != jnp.roll(own, 1), GROUP - 1, 0).at[0].set(GROUP - 1)
-    place = pad_place(jnp.arange(cells + 1, dtype=jnp.int32) % cells)
+    place = pad_place(jnp.arange(cells, dtype=jnp.int32))
     kinds = jnp.arange(27, dtype=jnp.int32)
     moves = jnp.stack([kinds // 9 - 1, kinds // 3 % 3 - 1, kinds % 3 - 1], axis=1)
     shift = jnp.pad(moves.astype(jnp.float32), ((0, 0), (0, 5)))
@@ -403,42 +424,62 @@
             pltpu.VMEM((total, lanes), jnp.int32),
         ],
         compiler_params=params,
-    )(near, need, padded)
+    )(near, need, padded.reshape(span * 8, lanes))
 
     chunks = total + cells * GROUP // lanes + 2
     chunks = -(-chunks // 16) * 16
+    turned, cell_of, groups = pl.pallas_call(
+        fill_kernel,
+        out_shape=(
+            jax.ShapeDtypeStruct((chunks * 8, lanes), jnp.float32),
+            jax.ShapeDtypeStruct((chunks * (lanes // GROUP) + 16,), jnp.int32),
+            jax.ShapeDtypeStruct((1,), jnp.int32),
+        ),
+        in_specs=[smem] * 5 + [vmem] * 3,
+        out_specs=(vmem, smem, smem),
+        scratch_shapes=[pltpu.VMEM((chunks * 8, lanes), jnp.float32)],
+        compiler_params=params,
+    )(near, offset, own, first, count[0:1], padded, slots, shift)
+    force = pl.pallas_call(
+        pair_kernel,
+        out_shape=jax.ShapeDtypeStruct((3, cells + 8, 8, lanes), jnp.float32),
+        in_specs=[smem] * 3 + [vmem] * 2,
+        out_specs=vmem,
+        compiler_params=params,
+    )(cell_of, groups, place, padded, turned)
     sums = pl.pallas_call(
-        force_kernel,
+        sums_kernel,
         out_shape=jax.ShapeDtypeStruct((8, held), jnp.float32),
-        in_specs=[smem] * 6 + [vmem] * 5,
+        in_specs=[vmem] * 3,
         out_specs=vmem,
-        scratch_shapes=[
-            pltpu.VMEM((chunks * 8, lanes), jnp.float32),
-            pltpu.VMEM((chunks * 8, lanes), jnp.float32),
-            pltpu.VMEM((3, cells + 8, 8, lanes), jnp.float32),
-            pltpu.VMEM((8, 8, lanes), jnp.float32),
-            pltpu.SMEM((chunks * (lanes // GROUP) + 16,), jnp.int32),
-        ],
-        compiler_params=params,
-    )(near, offset, own, first, count[0:1], place, padded, slots, shift, flat_arms, flat_frag)
-
-    sums = lax.all_gather(sums, names, axis=0, tiled=False)
+        scratch_shapes=[pltpu.VMEM((8, 8, lanes), jnp.float32)],
+        compiler_params=params,
+    )(force, flat_arms, flat_frag)
+
+    sums = everywhere(sums, names)
 
     brick = lax.axis_index(names)
     mine = jnp.where(
         jnp.arange(lanes - held) < owned, brick * owned + jnp.arange(lanes - held), -2
     ).astype(jnp.float32)
     target = jnp.concatenate([mine, frag_key])[:, None]
+    base = pl.pallas_call(
+        functools.partial(base_kernel, owned),
+        out_shape=jax.ShapeDtypeStruct((8, lanes), jnp.float32),
+        in_specs=[vmem] * 2,
+        out_specs=vmem,
+        compiler_params=params,
+    )(target, fixed)
     spheres, clumps = pl.pallas_call(
-        functools.partial(move_kernel, owned),
+        move_kernel,
         out_shape=(
             jax.ShapeDtypeStruct((6, cells, lanes), jnp.float32),
             jax.ShapeDtypeStruct((6, lanes), jnp.float32),
         ),
-        in_specs=[vmem] * 6,
+        in_specs=[vmem] * 7,
         out_specs=(vmem, vmem),
         compiler_params=params,
-    )(target, fixed, sums, flat_state, flat_arms, flat_frag)
+    )(target, fixed, base, sums, flat_state, flat_arms, flat_frag)
     return (spheres.reshape((6,) + state.shape[1:]), clumps[:, :owned])
 
 

time: 379 us -> 253 us (0.67); the launches traced: 376 us -> 254 us
  blocking collectives: 141 us -> 0 us
  starting transfers between devices: 9.06 us -> 24 us
  Pallas kernels: 193 us -> 185 us
  waiting for transfers between devices: 15.9 us -> 22.7 us
  local copies, waits for them, and re-layouts: 4.87 us -> 9.19 us
    all_gather x2 -> x0, blocking collectives: 141 us -> none  [the longest x1 71.3 us: local(): fixed = lax.all_gather(fixed, names, axis=0, tiled=False)]
    pallas_call x1, Pallas kernels: 29.2 us -> 12.5 us  [local(): pl.pallas_call(list_kernel, out_shape=(jax.ShapeDtypeStruct((total, lanes...]
    all_to_all x0 -> x2, starting transfers between devices: none -> 15.6 us  [everywhere(): lax.all_to_all(copies, names, split_axis=0, concat_axis=0, tiled=True)]
    pallas_call x2 -> x5, Pallas kernels: 161 us -> 170 us  [the longest x1 100 us: local(): pl.pallas_call(pair_kernel, out_shape=jax.ShapeDtypeStruct((3, cells + 8,...]
  transfers between devices with their start and end apart: 6 -> 8, of which waited for: 2 -> 5; matrix products, arithmetic and copies ran while one was open for 2% -> 7% of each run, Pallas kernels for 0% -> 70%
where the time goes in v2:
time: 253 us; the launch traced here: 254 us
  Pallas kernels  185 us (73%)
  starting transfers between devices  24 us (9%)
  waiting for transfers between devices  22.7 us (9%)
  other arithmetic  11.8 us (5%)
  local copies, waits for them, and re-layouts  9.19 us (4%)
    pallas_call x1, Pallas kernels, local(): pl.pallas_call(pair_kernel, out_shape=jax.ShapeDtypeStruct((3, cells + 8,...  100 us
    pallas_call x1, Pallas kernels, local(): pl.pallas_call(fill_kernel, out_shape=(jax.ShapeDtypeStruct((chunks * 8,...  52.6 us
    all_to_all x2, starting transfers between devices, everywhere(): lax.all_to_all(copies, names, split_axis=0, concat_axis=0, tiled=True)  15.6 us
    pallas_call x1, Pallas kernels, local(): pl.pallas_call(list_kernel, out_shape=(jax.ShapeDtypeStruct((total, lanes...  12.5 us
    ppermute x3, waiting for transfers between devices, with_halo(): before = lax.ppermute(last, axis, up)  12.1 us
    pallas_call x1, Pallas kernels, local(): pl.pallas_call(sums_kernel, out_shape=jax.ShapeDtypeStruct((8, held), jnp...  9.81 us
    ppermute x3, waiting for transfers between devices, with_halo(): after = lax.ppermute(initial, axis, down)  9.04 us
  transfers between devices with their start and end apart: 8, of which 5 were waited for; matrix products, arithmetic and copies ran while one was open for 7% of the time, Pallas kernels for 70%

profile of v2, /device:TPU:0, one launch (start us, length us, event | category | flops | bytes accessed | tf_op | source)
XLA Modules:
  0.0 253.8 jit_solution(16737677938667456784)
XLA Ops:
  1.9 2.9 %shard_map.105 = f32[256,8,128]{2,1,0:T(8,128)} custom-call(f32[7,256,128]{2,1,0:T(8,128)} %bitcast.29, s32[256,128]{1,0:T(8,128)} %bitcast.33, f32[1,128]{1,0:T(1,128)} %get-tuple-element.41.key_ref), custom_call_target="tpu_custom_call" | custom-call | tf_op jit(solution)/shard_map/pallas_call | solution.py:376
  4.8 1.2 fusion.37
  6.4 2.0 collective-permute-start.1
  9.4 6.6 %all-to-all-start = ((f32[32,1,1024]{2,1,0:T(1,128)}), f32[32,1,1024]{2,1,0:T(1,128)S(1)}, u32[]{:S(2)}, u32[]{:S(2)}) async-start(f32[32,1,1024]{2,1,0:T(1,128)} %reshape.157), calls=%async_computation | async-start | bytes 262144 | tf_op jit(solution)/shard_map/all_to_all | solution.py:49
  16.1 5.0 %sort.15 = (s32[2048]{0:T(1024)S(1)}, s32[2048]{0:T(1024)}) sort(s32[2048]{0:T(1024)S(1)} %bitcast.39, s32[2048]{0:T(1024)S(1)} %iota.26), dimensions={0}, to_apply=%region_0.1 | sort | flops 22528 | bytes 32768 | tf_op jit(solution)/shard_map/jit(sort)/sort | solution.py:390
  21.2 1.8 collective-permute-start.2
  23.0 2.1 collective-permute-start.3
  25.7 1.3 shift-left_add_fusion
  27.0 8.1 %collective-permute-done.2 = f32[6,1,16,8,128]{4,3,2,1,0:T(8,128)S(1)} collective-permute-done((f32[6,1,16,8,128]{4,3,2,1,0:T(8,128)S(1)}, f32[6,1,16,8,128]{4,3,2,1,0:T(8,128)S(1)}, u32[]{:S(2)}, u32[]{:S(2)}) %collective-permute-start.2) | collective-permute-done | bytes 393248 | tf_op jit(solution)/shard_map/ppermute | solution.py:59
  35.1 7.3 %collective-permute-done.3 = f32[6,1,16,8,128]{4,3,2,1,0:T(8,128)S(1)} collective-permute-done((f32[6,1,16,8,128]{4,3,2,1,0:T(8,128)S(1)}, f32[6,1,16,8,128]{4,3,2,1,0:T(8,128)S(1)}, u32[]{:S(2)}, u32[]{:S(2)}) %collective-permute-start.3) | collective-permute-done | bytes 393248 | tf_op jit(solution)/shard_map/ppermute | solution.py:60
  42.4 1.5 collective-permute-start.4
  45.2 4.0 %collective-permute-done.4 = f32[6,6,1,8,128]{4,3,2,1,0:T(8,128)S(1)} collective-permute-done((f32[6,6,1,8,128]{4,3,2,1,0:T(8,128)S(1)}, f32[6,6,1,8,128]{4,3,2,1,0:T(8,128)S(1)}, u32[]{:S(2)}, u32[]{:S(2)}) %collective-permute-start.4) | collective-permute-done | bytes 147488 | tf_op jit(solution)/shard_map/ppermute | solution.py:59
  49.2 1.7 collective-permute-done.5
  51.0 1.7 pad_maximum_fusion
  52.7 12.5 %shard_map.106 = (s32[2048,128]{1,0:T(8,128)}, s32[8,2048]{1,0:T(8,128)}) custom-call(s32[2048]{0:T(1024)} %get-tuple-element.39.near_smem, s32[2048]{0:T(1024)} %get-tuple-element.37.need_smem, f32[5184,128]{1,0:T(8,128)} %bitcast.23), custom_call_target="tpu_custom_call" | custom-call | tf_op jit(solution)/shard_map/pallas_call | solution.py:414
  65.2 1.4 slice.58.count_smem
  67.4 52.6 %shard_map.107 = (f32[17024,128]{1,0:T(8,128)}, s32[8528]{0:T(1024)}, s32[1]{0:T(128)}) custom-call(s32[2048]{0:T(1024)} %get-tuple-element.39.near_smem, s32[2048]{0:T(1024)} %get-tuple-element.40.shift_smem, s32[2048]{0:T(1024)} %copy-done.1, s32[2048]{0:T(1024)} %copy-done.2, s32[1,2048]{1,0:T(1,128)} %slice.58.count_smem, f32[648,8,128]{2,1,0:T(8,128)} %bitcast.24, ...), custom_call_target="tpu_custom_call" | custom-call | tf_op jit(solution)/shard_map/pallas_call | solution.py:431
  120.0 100.2 %shard_map.108.force_ref = f32[3,264,8,128]{3,2,1,0:T(8,128)} custom-call(s32[8528]{0:T(1024)} %get-tuple-element.26.cell_smem, s32[1]{0:T(128)} %get-tuple-element.27.groups_smem, s32[256]{0:T(256)} %fusion.23.place_smem, f32[648,8,128]{2,1,0:T(8,128)} %bitcast.25, f32[17024,128]{1,0:T(8,128)} %get-tuple-element.28.turned_ref), custom_call_target="tpu_custom_call" | custom-call | tf_op jit(solution)/shard_map/pallas_call | solution.py:443
  220.1 9.8 %shard_map.109 = f32[8,64]{1,0:T(8,128)} custom-call(f32[3,264,8,128]{3,2,1,0:T(8,128)} %shard_map.108.force_ref, f32[3,256,128]{2,1,0:T(8,128)} %bitcast.31, s32[256,128]{1,0:T(8,128)} %bitcast.34), custom_call_target="tpu_custom_call" | custom-call | tf_op jit(solution)/shard_map/pallas_call | solution.py:450
  231.4 9.0 %all-to-all-start.1 = ((f32[32,1,512]{2,1,0:T(1,128)}), f32[32,1,512]{2,1,0:T(1,128)S(1)}, u32[]{:S(2)}, u32[]{:S(2)}) async-start(f32[32,1,512]{2,1,0:T(1,128)} %reshape.159), calls=%async_computation.1 | async-start | bytes 131072 | tf_op jit(solution)/shard_map/all_to_all | solution.py:49
  241.6 0.9 reduce.2
  243.4 2.7 %shard_map.104.base_ref = f32[8,128]{1,0:T(8,128)} custom-call(f32[128,1]{1,0:T(8,128)} %copy.15.target_ref, f32[32,16,64]{2,1,0:T(8,128)} %reshape.158.fixed_ref), custom_call_target="tpu_custom_call" | custom-call | tf_op jit(solution)/shard_map/pallas_call | solution.py:466
  246.1 1.6 all-to-all-done.1
  249.2 4.6 %shard_map.110 = (f32[6,256,128]{2,1,0:T(8,128)}, f32[6,128]{1,0:T(8,128)}) custom-call(f32[128,1]{1,0:T(8,128)} %copy.15.target_ref, f32[32,16,64]{2,1,0:T(8,128)} %reshape.158.fixed_ref, f32[8,128]{1,0:T(8,128)} %shard_map.104.base_ref, f32[32,8,64]{2,1,0:T(8,128)} %reshape.160.sums_ref, f32[7,256,128]{2,1,0:T(8,128)} %bitcast.30, ...), custom_call_target="tpu_custom_call" | custom-call | tf_op jit(solution)/shard_map/pallas_call | solution.py:473
  (47 shorter events, 10.5 us)
Async XLA Ops:
  0.6 7.9 %copy-start.6 = (f32[48]{0:T(128)S(1)}, f32[48]{0:T(128)}, u32[]{:S(2)}) copy-start(f32[48]{0:T(128)} %param.18) | copy-start | bytes 580
  0.6 7.9 %copy-start.5 = (f32[48]{0:T(128)S(1)}, f32[48]{0:T(128)}, u32[]{:S(2)}) copy-start(f32[48]{0:T(128)} %param.19) | copy-start | bytes 580
  0.7 7.8 %copy-start.4 = (f32[6,48]{1,0:T(8,128)S(1)}, f32[6,48]{1,0:T(8,128)}, u32[]{:S(2)}) copy-start(f32[6,48]{1,0:T(8,128)} %param.17) | copy-start | bytes 3460
  0.7 15.4 %copy-start.3 = (s32[1,2048]{1,0:T(1,128)S(1)}, s32[1,2048]{1,0:T(1,128)}, u32[]{:S(2)}) copy-start(s32[1,2048]{1,0:T(1,128)} %param.16) | copy-start | bytes 24580
  4.8 16.4 %copy-start = (f32[256,8,128]{2,1,0:T(8,128)S(1)}, f32[256,8,128]{2,1,0:T(8,128)}, u32[]{:S(2)}) copy-start(f32[256,8,128]{2,1,0:T(8,128)} %shard_map.105) | copy-start | bytes 3145732
  5.9 15.2 %collective-permute-start = (f32[1,4,16,8,128]{4,3,2,1,0:T(8,128)S(1)}, f32[1,4,16,8,128]{4,3,2,1,0:T(8,128)S(1)}, u32[]{:S(2)}, u32[]{:S(2)}) collective-permute-start(f32[1,4,16,8,128]{4,3,2,1,0:T(8,128)S(1)} %bitcast.37), channel_id=1, source_target_pairs={{0,8},{8,16},{16,24},{24,0},{1,9},{9,17},{17,25},{25,1},{2,10},{10... | collective-permute-start | bytes 786440 | tf_op jit(solution)/shard_map/ppermute | solution.py:59
  6.4 14.7 %collective-permute-start.1 = (f32[1,4,16,8,128]{4,3,2,1,0:T(8,128)S(1)}, f32[1,4,16,8,128]{4,3,2,1,0:T(8,128)S(1)}, u32[]{:S(2)}, u32[]{:S(2)}) collective-permute-start(f32[1,4,16,8,128]{4,3,2,1,0:T(8,128)S(1)} %bitcast.36), channel_id=1, source_target_pairs={{8,0},{16,8},{24,16},{0,24},{9,1},{17,9},{25,17},{1,25},{10,2},{18... | collective-permute-start | bytes 786440 | tf_op jit(solution)/shard_map/ppermute | solution.py:60
  9.4 222.0 %all-to-all-start = ((f32[32,1,1024]{2,1,0:T(1,128)}), f32[32,1,1024]{2,1,0:T(1,128)S(1)}, u32[]{:S(2)}, u32[]{:S(2)}) async-start(f32[32,1,1024]{2,1,0:T(1,128)} %reshape.157), calls=%async_computation | async-start | bytes 262144 | tf_op jit(solution)/shard_map/all_to_all | solution.py:49
  21.1 31.6 %copy-start.1 = (s32[2048]{0:T(1024)}, s32[2048]{0:T(1024)S(1)}, u32[]{:S(2)}) copy-start(s32[2048]{0:T(1024)S(1)} %add_select_fusion.9.own_smem) | copy-start | bytes 24580
  21.2 13.8 %collective-permute-start.2 = (f32[6,1,16,8,128]{4,3,2,1,0:T(8,128)S(1)}, f32[6,1,16,8,128]{4,3,2,1,0:T(8,128)S(1)}, u32[]{:S(2)}, u32[]{:S(2)}) collective-permute-start(f32[6,1,16,8,128]{4,3,2,1,0:T(8,128)S(1)} %get-tuple-element.33), channel_id=1, source_target_pairs={{0,2},{2,4},{4,6},{6,0},{1,3},{3,5},{5,7},{7,1},{8,10},{10,12},{12... | collective-permute-start | bytes 1179656 | tf_op jit(solution)/shard_map/ppermute | solution.py:59
  23.0 19.3 %collective-permute-start.3 = (f32[6,1,16,8,128]{4,3,2,1,0:T(8,128)S(1)}, f32[6,1,16,8,128]{4,3,2,1,0:T(8,128)S(1)}, u32[]{:S(2)}, u32[]{:S(2)}) collective-permute-start(f32[6,1,16,8,128]{4,3,2,1,0:T(8,128)S(1)} %get-tuple-element.34), channel_id=1, source_target_pairs={{2,0},{4,2},{6,4},{0,6},{3,1},{5,3},{7,5},{1,7},{10,8},{12,10},{14... | collective-permute-start | bytes 1179656 | tf_op jit(solution)/shard_map/ppermute | solution.py:60
  42.4 6.8 %collective-permute-start.4 = (f32[6,6,1,8,128]{4,3,2,1,0:T(8,128)S(1)}, f32[6,6,1,8,128]{4,3,2,1,0:T(8,128)S(1)}, u32[]{:S(2)}, u32[]{:S(2)}) collective-permute-start(f32[6,6,1,8,128]{4,3,2,1,0:T(8,128)S(1)} %get-tuple-element.31), channel_id=1, source_target_pairs={{0,1},{1,0},{2,3},{3,2},{4,5},{5,4},{6,7},{7,6},{8,9},{9,8},{10,11... | collective-permute-start | bytes 442376 | tf_op jit(solution)/shard_map/ppermute | solution.py:59
  43.9 7.0 %collective-permute-start.5 = (f32[6,6,1,8,128]{4,3,2,1,0:T(8,128)S(1)}, f32[6,6,1,8,128]{4,3,2,1,0:T(8,128)S(1)}, u32[]{:S(2)}, u32[]{:S(2)}) collective-permute-start(f32[6,6,1,8,128]{4,3,2,1,0:T(8,128)S(1)} %get-tuple-element.32), channel_id=1, source_target_pairs={{1,0},{0,1},{3,2},{2,3},{5,4},{4,5},{7,6},{6,7},{9,8},{8,9},{11,10... | collective-permute-start | bytes 442376 | tf_op jit(solution)/shard_map/ppermute | solution.py:60
  45.2 7.5 %copy-start.2 = (s32[2048]{0:T(1024)}, s32[2048]{0:T(1024)S(1)}, u32[]{:S(2)}) copy-start(s32[2048]{0:T(1024)S(1)} %constant_dynamic-update-slice_fusion.first_smem) | copy-start | bytes 24580
  231.4 16.3 %all-to-all-start.1 = ((f32[32,1,512]{2,1,0:T(1,128)}), f32[32,1,512]{2,1,0:T(1,128)S(1)}, u32[]{:S(2)}, u32[]{:S(2)}) async-start(f32[32,1,512]{2,1,0:T(1,128)} %reshape.159), calls=%async_computation.1 | async-start | bytes 131072 | tf_op jit(solution)/shard_map/all_to_all | solution.py:49

commit v3 on v2

--- a/solution.py
+++ b/solution.py
@@ -16,6 +16,7 @@
 
 GROUP = 32
 GROUP_BITS = GROUP.bit_length() - 1
+FILL = 16
 UNITS = 4
 VMEM = 56 * 1024 * 1024
 
@@ -72,133 +73,143 @@
         out_ref[rows, 7, :] = lanes_of(keys, frag_ref[rows, :])
 
 
-def list_kernel(near_smem, need_smem, table_ref, slots_ref, count_ref, class_ref, member_ref):
-    tiles = slots_ref.shape[0]
-    lanes = slots_ref.shape[1]
-    span = class_ref.shape[0]
+def list_kernel(near_ref, need_ref, table_ref, slots_ref, count_ref, class_ref):
+    tiles, lanes = slots_ref.shape
+    span = table_ref.shape[0] // 8
+    padded = class_ref.shape[0]
 
     def plane(comp):
         return table_ref[pl.ds(comp, span, stride=8), :]
 
     radius = plane(6) + (radius_top + 1e-5)
-    classes = jnp.zeros(class_ref.shape, jnp.int32)
+    classes = jnp.zeros((span, lanes), jnp.float32)
     for axis in range(3):
         place = plane(axis)
-        classes = classes | jnp.where(place < radius, 1 << (2 * axis), 0)
-        classes = classes | jnp.where(place > 1.0 - radius, 2 << (2 * axis), 0)
-    class_ref[...] = classes
-
-    def copy_rows(block, unused):
-        for unit in range(8):
-            tile = block * 8 + unit
-            need = need_smem[tile]
-            row = class_ref[pl.ds(near_smem[tile], 1), :]
-            member_ref[pl.ds(tile, 1), :] = jnp.where((row & need) == need, 1, 0)
-        return unused
-
-    lax.fori_loop(0, tiles // 8, copy_rows, 0)
-
-    before = lax.broadcasted_iota(jnp.int32, (lanes, lanes), 0)
-    after = lax.broadcasted_iota(jnp.int32, (lanes, lanes), 1)
-    earlier = (before < after).astype(jnp.bfloat16)
+        classes = classes + jnp.where(place < radius, 1.0 * (1 << (2 * axis)), 0.0)
+        classes = classes + jnp.where(place > 1.0 - radius, 1.0 * (2 << (2 * axis)), 0.0)
+    class_ref[pl.ds(span // 8 * 8, padded - span // 8 * 8), :] = jnp.zeros(
+        (padded - span // 8 * 8, lanes), jnp.float32
+    )
+    class_ref[pl.ds(0, span), :] = classes
+    codes = jnp.concatenate(
+        [class_ref[pl.ds(at, lanes), :].T for at in range(0, padded, lanes)], axis=1
+    ).astype(jnp.bfloat16)
+    before = lax.broadcasted_iota(jnp.int32, (lanes, lanes), 1)
+    after = lax.broadcasted_iota(jnp.int32, (lanes, lanes), 0)
+    earlier = (before < after).astype(jnp.float32).astype(jnp.bfloat16)
     ones = jnp.ones((8, lanes), jnp.bfloat16)
-    step_rows = 256
+    wide = 256
 
     def compact(block, unused):
-        rows = pl.ds(pl.multiple_of(block * step_rows, step_rows), step_rows)
-        member = member_ref[rows, :]
+        at = pl.ds(pl.multiple_of(block * wide, wide), wide)
+        cell = lax.broadcasted_iota(jnp.int32, (padded, wide), 0)
+        hits = (cell == near_ref[:, at]).astype(jnp.float32).astype(jnp.bfloat16)
+        found = jnp.dot(codes, hits, preferred_element_type=jnp.float32).astype(jnp.int32)
+        need = need_ref[:, at]
+        member = (found & need) == need
         flags = member.astype(jnp.float32).astype(jnp.bfloat16)
-        rank = jnp.dot(flags, earlier, preferred_element_type=jnp.float32)
-        slot = lax.broadcasted_iota(jnp.int32, (step_rows, lanes), 1)
+        count_ref[:, at] = jnp.dot(ones, flags, preferred_element_type=jnp.float32).astype(jnp.int32)
+        rank = jnp.dot(earlier, flags, preferred_element_type=jnp.float32)
+        slot = lax.broadcasted_iota(jnp.int32, (lanes, wide), 0)
         moves = slot - rank.astype(jnp.int32)
-        word = jnp.where(member != 0, slot + lanes * moves, 0)
+        word = jnp.where(member, slot + lanes * moves, 0)
         bit = 1
         while bit < lanes:
             keep = jnp.where((word & (bit * lanes)) != 0, 0, word)
             gone = word ^ keep
-            word = keep | pltpu.roll(gone, lanes - bit, 1)
+            word = keep | jnp.concatenate([gone[bit:], gone[:bit]], axis=0)
             bit *= 2
-        slots_ref[rows, :] = word & (lanes - 1)
+        word = word & (lanes - 1)
+        for part in range(wide // lanes):
+            rows = pl.ds(pl.multiple_of(block * wide + part * lanes, lanes), lanes)
+            slots_ref[rows, :] = word[:, part * lanes : (part + 1) * lanes].T
         return unused
 
-    lax.fori_loop(0, tiles // step_rows, compact, 0)
-    for block in range(tiles // lanes):
-        flags = member_ref[pl.ds(block * lanes, lanes), :].astype(jnp.float32).astype(jnp.bfloat16)
-        count_ref[:, pl.ds(block * lanes, lanes)] = dot_lanes(ones, flags).astype(jnp.int32)
+    lax.fori_loop(0, tiles // wide, compact, 0)
 
 
 def fill_kernel(
     near_smem, shift_smem, own_smem, first_smem, count_smem, table_ref, slots_ref, shift_ref,
-    turned_ref, cell_smem, groups_smem, list_ref,
+    turned_ref, cell_smem, until_smem, groups_smem, list_ref,
 ):
-    tiles = slots_ref.shape[0]
-    lanes = slots_ref.shape[1]
+    tiles, lanes = slots_ref.shape
+    cells = cell_smem.shape[0] - 8
     lane_bits = lanes.bit_length() - 1
     lane = lax.broadcasted_iota(jnp.int32, (8, lanes), 1)
     row = lax.broadcasted_iota(jnp.int32, (8, lanes), 0)
     absent = jnp.where(row == 6, -10.0, 0.0)
+
     def fill(block, carry):
-        end, last_chunk, last_new, last_held = carry
-        for unit in range(8):
-            tile = block * 8 + unit
-            align = first_smem[tile]
-            own = own_smem[tile]
+        end, entry, last_chunk, last_new, last_held = carry
+        units = range(FILL)
+        first = [first_smem[block * FILL + unit] for unit in units]
+        own = [own_smem[block * FILL + unit] for unit in units]
+        near = [near_smem[block * FILL + unit] for unit in units]
+        shift = [shift_smem[block * FILL + unit] for unit in units]
+        amounts = [count_smem[0, block * FILL + unit] for unit in units]
+        starts, ends, entries = [], [], []
+        for unit in units:
+            align = first[unit] * (GROUP - 1)
             start = (end + align) & ~align
-            amount = count_smem[0, tile]
-            chunk = start >> lane_bits
-            offset = start & (lanes - 1)
-            for piece in range(lanes // GROUP + 1):
-                cell_smem[(start >> GROUP_BITS) + piece] = own
-            slots = jnp.broadcast_to(slots_ref[pl.ds(tile, 1), :], (8, lanes))
-            slots = pltpu.roll(slots, offset, 1)
-            found = lanes_of(table_ref[near_smem[tile]], slots) + shift_ref[shift_smem[tile]]
-            new = jnp.where(((lane - offset) & (lanes - 1)) < amount, found, absent)
+            end = start + jnp.maximum(amounts[unit], first[unit])
+            entry = entry + first[unit]
+            starts.append(start)
+            ends.append(end)
+            entries.append(entry)
+        found = []
+        for unit in units:
+            slots = jnp.broadcast_to(slots_ref[pl.ds(block * FILL + unit, 1), :], (8, lanes))
+            slots = pltpu.roll(slots, starts[unit] & (lanes - 1), 1)
+            found.append(lanes_of(table_ref[near[unit]], slots) + shift_ref[shift[unit]])
+        for unit in units:
+            chunk = starts[unit] >> lane_bits
+            offset = starts[unit] & (lanes - 1)
+            new = jnp.where(((lane - offset) & (lanes - 1)) < amounts[unit], found[unit], absent)
             held_row = jnp.where(chunk != last_chunk, last_new, last_held)
             held_row = jnp.where(lane >= offset, new, held_row)
             new = jnp.where(lane >= offset, absent, new)
-            list_ref[pl.ds(pl.multiple_of(chunk * 8, 8), 8), :] = held_row
-            list_ref[pl.ds(pl.multiple_of(chunk * 8 + 8, 8), 8), :] = new
-            end, last_chunk, last_new, last_held = start + amount, chunk, new, held_row
-        return end, last_chunk, last_new, last_held
-
-    start = (jnp.int32(0), jnp.int32(0), absent, absent)
-    end = lax.fori_loop(0, tiles // 8, fill, start)[0]
-    groups = (end + GROUP - 1) >> GROUP_BITS
-    for extra in range(UNITS):
-        cell_smem[groups + extra] = -1
-    groups_smem[0] = groups
+            list_ref[chunk] = held_row
+            list_ref[chunk + 1] = new
+            last_chunk, last_new, last_held = chunk, new, held_row
+        for unit in units:
+            cell_smem[entries[unit]] = own[unit]
+            until_smem[entries[unit]] = (ends[unit] + (GROUP - 1)) >> GROUP_BITS
+        return end, entry, last_chunk, last_new, last_held
+
+    start = (jnp.int32(0), jnp.int32(-1), jnp.int32(0), absent, absent)
+    end, entry = lax.fori_loop(0, tiles // FILL, fill, start)[0:2]
+    groups_smem[0] = (end + (GROUP - 1)) >> GROUP_BITS
+    cell_smem[entry + 1] = cells
+    until_smem[entry + 1] = 1 << 30
 
     def turn(block, unused):
         rows = pl.ds(pl.multiple_of(block * lanes, lanes), lanes)
-        turned_ref[rows, :] = list_ref[rows, :].T
+        chunks = pl.ds(pl.multiple_of(block * 16, 16), 16)
+        turned_ref[rows, :] = list_ref[chunks].reshape(lanes, lanes).T
         return unused
 
     lax.fori_loop(0, (end + 16 * lanes - 1) >> (lane_bits + 4), turn, 0)
 
 
-def pair_kernel(cell_smem, groups_smem, place_smem, table_ref, turned_ref, force_ref):
+def pair_kernel(cell_smem, until_smem, groups_smem, place_smem, table_ref, turned_ref, force_ref):
     lanes = table_ref.shape[2]
     lane_bits = lanes.bit_length() - 1
-    cells = place_smem.shape[0]
     groups = groups_smem[0]
     force_ref[...] = jnp.zeros(force_ref.shape, jnp.float32)
 
-    def pairs(step, unused):
+    def pairs(step, entry):
         totals = []
         for unit in range(UNITS):
             group = step * UNITS + unit
-            cell = cell_smem[group]
-            target = jnp.where(cell < 0, cells, cell)
-            own = place_smem[jnp.maximum(cell, 0)]
+            entry = entry + jnp.where(group >= until_smem[entry], 1, 0)
+            cell = cell_smem[entry]
+            own = place_smem[cell]
             begin = group * GROUP
             chunk = begin >> lane_bits
             at = (chunk >> 4) * lanes + (begin & (lanes - 1))
             block = turned_ref[pl.ds(pl.multiple_of(at, GROUP), GROUP), :]
-            column = (chunk & 15) * 8
-            other = [
-                lanes_of(block, jnp.full((GROUP, lanes), column + comp, jnp.int32))
-                for comp in range(8)
-            ]
+            block = pltpu.roll(block, (lanes - (chunk & 15) * 8) & (lanes - 1), 1)
+            other = [block[:, comp : comp + 1] for comp in range(8)]
             mine = [table_ref[own, pl.ds(comp, 1), :] for comp in range(8)]
             apart = [other[axis] - mine[axis] for axis in range(3)]
             square = apart[0] * apart[0] + apart[1] * apart[1] + apart[2] * apart[2] + epsilon_sq
@@ -218,7 +229,7 @@
             )
             totals.append(
                 (
-                    target,
+                    cell,
                     [
                         jnp.sum((factor * apart[axis]).reshape(GROUP // 8, 8, lanes), axis=0)
                         for axis in range(3)
@@ -228,7 +239,7 @@
         for cell, parts in totals:
             for axis in range(3):
                 force_ref[axis, cell] += parts[axis]
-        return unused
+        return entry
 
     lax.fori_loop(0, lax.div(groups + (UNITS - 1), UNITS), pairs, 0)
 
@@ -404,8 +415,8 @@
         jnp.where(steps[axis] == 1, 1, jnp.where(steps[axis] == -1, 2, 0)) << (2 * axis)
         for axis in range(3)
     )
-    first = jnp.where(own != jnp.roll(own, 1), GROUP - 1, 0).at[0].set(GROUP - 1)
-    place = pad_place(jnp.arange(cells, dtype=jnp.int32))
+    first = jnp.concatenate([jnp.ones((1,), jnp.int32), (own[1:] != own[:-1]).astype(jnp.int32)])
+    place = pad_place(jnp.arange(cells + 1, dtype=jnp.int32) % cells)
     kinds = jnp.arange(27, dtype=jnp.int32)
     moves = jnp.stack([kinds // 9 - 1, kinds // 3 % 3 - 1, kinds % 3 - 1], axis=1)
     shift = jnp.pad(moves.astype(jnp.float32), ((0, 0), (0, 5)))
@@ -417,36 +428,34 @@
             jax.ShapeDtypeStruct((total, lanes), jnp.int32),
             jax.ShapeDtypeStruct((8, total), jnp.int32),
         ),
-        in_specs=[smem, smem, vmem],
+        in_specs=[vmem] * 3,
         out_specs=(vmem, vmem),
-        scratch_shapes=[
-            pltpu.VMEM((span, lanes), jnp.int32),
-            pltpu.VMEM((total, lanes), jnp.int32),
-        ],
-        compiler_params=params,
-    )(near, need, padded.reshape(span * 8, lanes))
+        scratch_shapes=[pltpu.VMEM((-(-span // lanes) * lanes, lanes), jnp.float32)],
+        compiler_params=params,
+    )(near[None], need[None], padded.reshape(span * 8, lanes))
 
     chunks = total + cells * GROUP // lanes + 2
     chunks = -(-chunks // 16) * 16
-    turned, cell_of, groups = pl.pallas_call(
+    turned, cell_of, until, groups = pl.pallas_call(
         fill_kernel,
         out_shape=(
             jax.ShapeDtypeStruct((chunks * 8, lanes), jnp.float32),
-            jax.ShapeDtypeStruct((chunks * (lanes // GROUP) + 16,), jnp.int32),
+            jax.ShapeDtypeStruct((cells + 8,), jnp.int32),
+            jax.ShapeDtypeStruct((cells + 8,), jnp.int32),
             jax.ShapeDtypeStruct((1,), jnp.int32),
         ),
         in_specs=[smem] * 5 + [vmem] * 3,
-        out_specs=(vmem, smem, smem),
-        scratch_shapes=[pltpu.VMEM((chunks * 8, lanes), jnp.float32)],
+        out_specs=(vmem, smem, smem, smem),
+        scratch_shapes=[pltpu.VMEM((chunks, 8, lanes), jnp.float32)],
         compiler_params=params,
     )(near, offset, own, first, count[0:1], padded, slots, shift)
     force = pl.pallas_call(
         pair_kernel,
         out_shape=jax.ShapeDtypeStruct((3, cells + 8, 8, lanes), jnp.float32),
-        in_specs=[smem] * 3 + [vmem] * 2,
+        in_specs=[smem] * 4 + [vmem] * 2,
         out_specs=vmem,
         compiler_params=params,
-    )(cell_of, groups, place, padded, turned)
+    )(cell_of, until, groups, place, padded, turned)
     sums = pl.pallas_call(
         sums_kernel,
         out_shape=jax.ShapeDtypeStruct((8, held), jnp.float32),

time: 253 us -> 280 us (1.11)
  Pallas kernels: 185 us -> 213 us
    pallas_call x1, Pallas kernels: 100 us -> 145 us  [local(): pl.pallas_call(pair_kernel, out_shape=jax.ShapeDtypeStruct((3, cells + 8,...]
    pallas_call x1, Pallas kernels: 52.6 us -> 39.6 us  [local(): pl.pallas_call(fill_kernel, out_shape=(jax.ShapeDtypeStruct((chunks * 8,...]
    pallas_call x1, Pallas kernels: 12.5 us -> 8.67 us  [local(): pl.pallas_call(list_kernel, out_shape=(jax.ShapeDtypeStruct((total, lanes...]
  transfers between devices with their start and end apart: 8 -> 8, of which waited for: 5 -> 5; matrix products, arithmetic and copies ran while one was open for 7% -> 6% of each run, Pallas kernels for 70% -> 73%
where the time goes in v3:
time: 280 us; the launch traced here: 281 us
  Pallas kernels  213 us (76%)
  waiting for transfers between devices  24.4 us (9%)
  starting transfers between devices  22 us (8%)
  other arithmetic  11.9 us (4%)
  local copies, waits for them, and re-layouts  8.65 us (3%)
    pallas_call x1, Pallas kernels, local(): pl.pallas_call(pair_kernel, out_shape=jax.ShapeDtypeStruct((3, cells + 8,...  145 us
    pallas_call x1, Pallas kernels, local(): pl.pallas_call(fill_kernel, out_shape=(jax.ShapeDtypeStruct((chunks * 8,...  39.6 us
    ppermute x3, waiting for transfers between devices, with_halo(): before = lax.ppermute(last, axis, up)  13.8 us
    all_to_all x2, starting transfers between devices, everywhere(): lax.all_to_all(copies, names, split_axis=0, concat_axis=0, tiled=True)  13.6 us
    pallas_call x1, Pallas kernels, local(): pl.pallas_call(sums_kernel, out_shape=jax.ShapeDtypeStruct((8, held), jnp...  9.81 us
    ppermute x3, waiting for transfers between devices, with_halo(): after = lax.ppermute(initial, axis, down)  9.04 us
    pallas_call x1, Pallas kernels, local(): pl.pallas_call(list_kernel, out_shape=(jax.ShapeDtypeStruct((total, lanes...  8.67 us
  transfers between devices with their start and end apart: 8, of which 5 were waited for; matrix products, arithmetic and copies ran while one was open for 6% of the time, Pallas kernels for 73%

profile of v3, /device:TPU:0, one launch (start us, length us, event | category | flops | bytes accessed | tf_op | source)
XLA Modules:
  0.0 281.1 jit_solution(10914448338401307180)
XLA Ops:
  1.9 2.9 %shard_map.105 = f32[256,8,128]{2,1,0:T(8,128)} custom-call(f32[7,256,128]{2,1,0:T(8,128)} %bitcast.30, s32[256,128]{1,0:T(8,128)} %bitcast.34, f32[1,128]{1,0:T(1,128)} %get-tuple-element.31.key_ref), custom_call_target="tpu_custom_call" | custom-call | tf_op jit(solution)/shard_map/pallas_call | solution.py:387
  4.8 1.2 fusion.39
  6.4 2.0 collective-permute-start.1
  8.6 0.8 reshape.134
  9.4 6.6 %all-to-all-start = ((f32[32,1,1024]{2,1,0:T(1,128)}), f32[32,1,1024]{2,1,0:T(1,128)S(1)}, u32[]{:S(2)}, u32[]{:S(2)}) async-start(f32[32,1,1024]{2,1,0:T(1,128)} %reshape.134), calls=%async_computation | async-start | bytes 262144 | tf_op jit(solution)/shard_map/all_to_all | solution.py:50
  16.7 5.0 %sort.15 = (s32[2048]{0:T(1024)S(1)}, s32[2048]{0:T(1024)}) sort(s32[2048]{0:T(1024)S(1)} %bitcast.41, s32[2048]{0:T(1024)S(1)} %iota.26), dimensions={0}, to_apply=%region_0.1 | sort | flops 22528 | bytes 32768 | tf_op jit(solution)/shard_map/jit(sort)/sort | solution.py:401
  22.4 1.8 collective-permute-start.2
  24.3 2.1 collective-permute-start.3
  27.1 9.2 %collective-permute-done.2 = f32[6,1,16,8,128]{4,3,2,1,0:T(8,128)S(1)} collective-permute-done((f32[6,1,16,8,128]{4,3,2,1,0:T(8,128)S(1)}, f32[6,1,16,8,128]{4,3,2,1,0:T(8,128)S(1)}, u32[]{:S(2)}, u32[]{:S(2)}) %collective-permute-start.2) | collective-permute-done | bytes 393248 | tf_op jit(solution)/shard_map/ppermute | solution.py:60
  36.3 7.3 %collective-permute-done.3 = f32[6,1,16,8,128]{4,3,2,1,0:T(8,128)S(1)} collective-permute-done((f32[6,1,16,8,128]{4,3,2,1,0:T(8,128)S(1)}, f32[6,1,16,8,128]{4,3,2,1,0:T(8,128)S(1)}, u32[]{:S(2)}, u32[]{:S(2)}) %collective-permute-start.3) | collective-permute-done | bytes 393248 | tf_op jit(solution)/shard_map/ppermute | solution.py:61
  43.6 1.5 collective-permute-start.4
  45.8 4.6 %collective-permute-done.4 = f32[6,6,1,8,128]{4,3,2,1,0:T(8,128)S(1)} collective-permute-done((f32[6,6,1,8,128]{4,3,2,1,0:T(8,128)S(1)}, f32[6,6,1,8,128]{4,3,2,1,0:T(8,128)S(1)}, u32[]{:S(2)}, u32[]{:S(2)}) %collective-permute-start.4) | collective-permute-done | bytes 147488 | tf_op jit(solution)/shard_map/ppermute | solution.py:60
  50.4 1.7 collective-permute-done.5
  52.2 1.7 pad_maximum_fusion
  53.9 8.7 %shard_map.106 = (s32[2048,128]{1,0:T(8,128)}, s32[8,2048]{1,0:T(8,128)}) custom-call(s32[1,2048]{1,0:T(1,128)} %bitcast.39, s32[1,2048]{1,0:T(1,128)} %bitcast.40, f32[5184,128]{1,0:T(8,128)} %bitcast.24), custom_call_target="tpu_custom_call" | custom-call | tf_op jit(solution)/shard_map/pallas_call | solution.py:425
  62.6 1.4 slice.46.count_smem
  64.8 39.6 %shard_map.107 = (f32[17024,128]{1,0:T(8,128)}, s32[264]{0:T(512)}, s32[264]{0:T(512)}, s32[1]{0:T(128)}) custom-call(s32[2048]{0:T(1024)} %get-tuple-element.28.near_smem, s32[2048]{0:T(1024)} %get-tuple-element.29.shift_smem, s32[2048]{0:T(1024)} %copy-done.1, s32[2048]{0:T(1024)} %add_convert_fusion.first_smem, s32[1,2048]{1,0:T(1,128)} %slice.46.count_smem, ...), custom_call_target="tpu_custom_call" | custom-call | tf_op jit(solution)/shard_map/pallas_call | solution.py:439
  104.4 145.0 %shard_map.108.force_ref = f32[3,264,8,128]{3,2,1,0:T(8,128)} custom-call(s32[264]{0:T(512)} %get-tuple-element.15.cell_smem, s32[264]{0:T(512)} %get-tuple-element.16.until_smem, s32[1]{0:T(128)} %get-tuple-element.17.groups_smem, s32[257]{0:T(512)} %fusion.24.place_smem, f32[648,8,128]{2,1,0:T(8,128)} %bitcast.26, f32[17024,128]{1,0:T(8,128)} %get-tuple-element.18.turned_ref), custom_call_target="tpu_custom_call" | custom-call | tf_op jit(solution)/shard_map/pallas_call | solution.py:452
  249.4 9.8 %shard_map.109 = f32[8,64]{1,0:T(8,128)} custom-call(f32[3,264,8,128]{3,2,1,0:T(8,128)} %shard_map.108.force_ref, f32[3,256,128]{2,1,0:T(8,128)} %bitcast.32, s32[256,128]{1,0:T(8,128)} %bitcast.35), custom_call_target="tpu_custom_call" | custom-call | tf_op jit(solution)/shard_map/pallas_call | solution.py:459
  260.7 7.0 %all-to-all-start.1 = ((f32[32,1,512]{2,1,0:T(1,128)}), f32[32,1,512]{2,1,0:T(1,128)S(1)}, u32[]{:S(2)}, u32[]{:S(2)}) async-start(f32[32,1,512]{2,1,0:T(1,128)} %reshape.136), calls=%async_computation.1 | async-start | bytes 131072 | tf_op jit(solution)/shard_map/all_to_all | solution.py:50
  268.9 0.9 reduce
  270.7 2.7 shard_map.104.base_ref
  273.4 1.5 all-to-all-done.1
  276.5 4.6 %shard_map.110 = (f32[6,256,128]{2,1,0:T(8,128)}, f32[6,128]{1,0:T(8,128)}) custom-call(f32[128,1]{1,0:T(8,128)} %copy.15.target_ref, f32[32,16,64]{2,1,0:T(8,128)} %reshape.135.fixed_ref, f32[8,128]{1,0:T(8,128)} %shard_map.104.base_ref, f32[32,8,64]{2,1,0:T(8,128)} %reshape.137.sums_ref, f32[7,256,128]{2,1,0:T(8,128)} %bitcast.31, ...), custom_call_target="tpu_custom_call" | custom-call | tf_op jit(solution)/shard_map/pallas_call | solution.py:482
  (44 shorter events, 10.5 us)
Async XLA Ops:
  0.6 7.9 %copy-start.5 = (f32[48]{0:T(128)S(1)}, f32[48]{0:T(128)}, u32[]{:S(2)}) copy-start(f32[48]{0:T(128)} %param.16) | copy-start | bytes 580
  0.6 7.9 %copy-start.4 = (f32[48]{0:T(128)S(1)}, f32[48]{0:T(128)}, u32[]{:S(2)}) copy-start(f32[48]{0:T(128)} %param.17) | copy-start | bytes 580
  0.7 7.8 %copy-start.3 = (f32[6,48]{1,0:T(8,128)S(1)}, f32[6,48]{1,0:T(8,128)}, u32[]{:S(2)}) copy-start(f32[6,48]{1,0:T(8,128)} %param.15) | copy-start | bytes 3460
  0.7 16.0 %copy-start.2 = (s32[1,2048]{1,0:T(1,128)S(1)}, s32[1,2048]{1,0:T(1,128)}, u32[]{:S(2)}) copy-start(s32[1,2048]{1,0:T(1,128)} %param.14) | copy-start | bytes 24580
  4.8 17.6 %copy-start = (f32[256,8,128]{2,1,0:T(8,128)S(1)}, f32[256,8,128]{2,1,0:T(8,128)}, u32[]{:S(2)}) copy-start(f32[256,8,128]{2,1,0:T(8,128)} %shard_map.105) | copy-start | bytes 3145732
  5.9 16.4 %collective-permute-start = (f32[1,4,16,8,128]{4,3,2,1,0:T(8,128)S(1)}, f32[1,4,16,8,128]{4,3,2,1,0:T(8,128)S(1)}, u32[]{:S(2)}, u32[]{:S(2)}) collective-permute-start(f32[1,4,16,8,128]{4,3,2,1,0:T(8,128)S(1)} %bitcast.38), channel_id=1, source_target_pairs={{0,8},{8,16},{16,24},{24,0},{1,9},{9,17},{17,25},{25,1},{2,10},{10... | collective-permute-start | bytes 786440 | tf_op jit(solution)/shard_map/ppermute | solution.py:60
  6.4 15.9 %collective-permute-start.1 = (f32[1,4,16,8,128]{4,3,2,1,0:T(8,128)S(1)}, f32[1,4,16,8,128]{4,3,2,1,0:T(8,128)S(1)}, u32[]{:S(2)}, u32[]{:S(2)}) collective-permute-start(f32[1,4,16,8,128]{4,3,2,1,0:T(8,128)S(1)} %bitcast.37), channel_id=1, source_target_pairs={{8,0},{16,8},{24,16},{0,24},{9,1},{17,9},{25,17},{1,25},{10,2},{18... | collective-permute-start | bytes 786440 | tf_op jit(solution)/shard_map/ppermute | solution.py:61
  9.4 251.3 %all-to-all-start = ((f32[32,1,1024]{2,1,0:T(1,128)}), f32[32,1,1024]{2,1,0:T(1,128)S(1)}, u32[]{:S(2)}, u32[]{:S(2)}) async-start(f32[32,1,1024]{2,1,0:T(1,128)} %reshape.134), calls=%async_computation | async-start | bytes 262144 | tf_op jit(solution)/shard_map/all_to_all | solution.py:50
  22.4 31.6 %copy-start.1 = (s32[2048]{0:T(1024)}, s32[2048]{0:T(1024)S(1)}, u32[]{:S(2)}) copy-start(s32[2048]{0:T(1024)S(1)} %get-tuple-element.30.own_smem) | copy-start | bytes 24580
  22.4 13.8 %collective-permute-start.2 = (f32[6,1,16,8,128]{4,3,2,1,0:T(8,128)S(1)}, f32[6,1,16,8,128]{4,3,2,1,0:T(8,128)S(1)}, u32[]{:S(2)}, u32[]{:S(2)}) collective-permute-start(f32[6,1,16,8,128]{4,3,2,1,0:T(8,128)S(1)} %get-tuple-element.23), channel_id=1, source_target_pairs={{0,2},{2,4},{4,6},{6,0},{1,3},{3,5},{5,7},{7,1},{8,10},{10,12},{12... | collective-permute-start | bytes 1179656 | tf_op jit(solution)/shard_map/ppermute | solution.py:60
  24.3 19.3 %collective-permute-start.3 = (f32[6,1,16,8,128]{4,3,2,1,0:T(8,128)S(1)}, f32[6,1,16,8,128]{4,3,2,1,0:T(8,128)S(1)}, u32[]{:S(2)}, u32[]{:S(2)}) collective-permute-start(f32[6,1,16,8,128]{4,3,2,1,0:T(8,128)S(1)} %get-tuple-element.24), channel_id=1, source_target_pairs={{2,0},{4,2},{6,4},{0,6},{3,1},{5,3},{7,5},{1,7},{10,8},{12,10},{14... | collective-permute-start | bytes 1179656 | tf_op jit(solution)/shard_map/ppermute | solution.py:61
  43.6 6.8 %collective-permute-start.4 = (f32[6,6,1,8,128]{4,3,2,1,0:T(8,128)S(1)}, f32[6,6,1,8,128]{4,3,2,1,0:T(8,128)S(1)}, u32[]{:S(2)}, u32[]{:S(2)}) collective-permute-start(f32[6,6,1,8,128]{4,3,2,1,0:T(8,128)S(1)} %get-tuple-element.21), channel_id=1, source_target_pairs={{0,1},{1,0},{2,3},{3,2},{4,5},{5,4},{6,7},{7,6},{8,9},{9,8},{10,11... | collective-permute-start | bytes 442376 | tf_op jit(solution)/shard_map/ppermute | solution.py:60
  45.1 7.0 %collective-permute-start.5 = (f32[6,6,1,8,128]{4,3,2,1,0:T(8,128)S(1)}, f32[6,6,1,8,128]{4,3,2,1,0:T(8,128)S(1)}, u32[]{:S(2)}, u32[]{:S(2)}) collective-permute-start(f32[6,6,1,8,128]{4,3,2,1,0:T(8,128)S(1)} %get-tuple-element.22), channel_id=1, source_target_pairs={{1,0},{0,1},{3,2},{2,3},{5,4},{4,5},{7,6},{6,7},{9,8},{8,9},{11,10... | collective-permute-start | bytes 442376 | tf_op jit(solution)/shard_map/ppermute | solution.py:61
  260.7 14.2 %all-to-all-start.1 = ((f32[32,1,512]{2,1,0:T(1,128)}), f32[32,1,512]{2,1,0:T(1,128)S(1)}, u32[]{:S(2)}, u32[]{:S(2)}) async-start(f32[32,1,512]{2,1,0:T(1,128)} %reshape.136), calls=%async_computation.1 | async-start | bytes 131072 | tf_op jit(solution)/shard_map/all_to_all | solution.py:50

commit v4 on v3

--- a/solution.py
+++ b/solution.py
@@ -15,9 +15,8 @@
 radius_top = 0.14
 
 GROUP = 32
-GROUP_BITS = GROUP.bit_length() - 1
 FILL = 16
-UNITS = 4
+SPREAD = 2
 VMEM = 56 * 1024 * 1024
 
 
@@ -73,13 +72,26 @@
         out_ref[rows, 7, :] = lanes_of(keys, frag_ref[rows, :])
 
 
-def list_kernel(near_ref, need_ref, table_ref, slots_ref, count_ref, class_ref):
+def list_kernel(
+    near_ref, need_ref, own_ref, table_ref, slots_ref, where_ref, cell_ref, class_ref, member_ref, count_ref
+):
     tiles, lanes = slots_ref.shape
     span = table_ref.shape[0] // 8
     padded = class_ref.shape[0]
+    cells = count_ref.shape[0]
+    wide = 256
 
     def plane(comp):
         return table_ref[pl.ds(comp, span, stride=8), :]
+
+    def flag(value):
+        return value.astype(jnp.float32).astype(jnp.bfloat16)
+
+    def dot(first, second):
+        return jnp.dot(first, second, preferred_element_type=jnp.float32)
+
+    def ramp(shape, axis):
+        return lax.broadcasted_iota(jnp.int32, shape, axis)
 
     radius = plane(6) + (radius_top + 1e-5)
     classes = jnp.zeros((span, lanes), jnp.float32)
@@ -94,25 +106,62 @@
     codes = jnp.concatenate(
         [class_ref[pl.ds(at, lanes), :].T for at in range(0, padded, lanes)], axis=1
     ).astype(jnp.bfloat16)
-    before = lax.broadcasted_iota(jnp.int32, (lanes, lanes), 1)
-    after = lax.broadcasted_iota(jnp.int32, (lanes, lanes), 0)
-    earlier = (before < after).astype(jnp.float32).astype(jnp.bfloat16)
-    ones = jnp.ones((8, lanes), jnp.bfloat16)
-    wide = 256
-
-    def compact(block, unused):
+    ones = jnp.ones((lanes, lanes), jnp.bfloat16)
+    count_ref[...] = jnp.zeros(count_ref.shape, jnp.float32)
+
+    def choose(block, unused):
         at = pl.ds(pl.multiple_of(block * wide, wide), wide)
-        cell = lax.broadcasted_iota(jnp.int32, (padded, wide), 0)
-        hits = (cell == near_ref[:, at]).astype(jnp.float32).astype(jnp.bfloat16)
-        found = jnp.dot(codes, hits, preferred_element_type=jnp.float32).astype(jnp.int32)
+        hits = flag(ramp((padded, wide), 0) == near_ref[:, at])
+        found = dot(codes, hits).astype(jnp.int32)
         need = need_ref[:, at]
-        member = (found & need) == need
-        flags = member.astype(jnp.float32).astype(jnp.bfloat16)
-        count_ref[:, at] = jnp.dot(ones, flags, preferred_element_type=jnp.float32).astype(jnp.int32)
-        rank = jnp.dot(earlier, flags, preferred_element_type=jnp.float32)
-        slot = lax.broadcasted_iota(jnp.int32, (lanes, wide), 0)
-        moves = slot - rank.astype(jnp.int32)
-        word = jnp.where(member, slot + lanes * moves, 0)
+        member = ((found & need) == need).astype(jnp.float32)
+        member_ref[:, at] = member
+        count = dot(ones, member.astype(jnp.bfloat16))
+        mine = flag(ramp((cells, wide), 0) == own_ref[:, at])
+        count_ref[...] += dot_lanes(mine, count.astype(jnp.bfloat16))
+        return unused
+
+    lax.fori_loop(0, tiles // wide, choose, 0)
+
+    held = count_ref[...]
+    high = jnp.floor(held * (1.0 / lanes))
+    low = held - lanes * high
+    taken = jnp.floor((held + (GROUP - 1)) * (1.0 / GROUP))
+    upto = flag(ramp((cells, cells), 1) <= ramp((cells, cells), 0))
+    ends = dot(upto, taken.astype(jnp.bfloat16))
+    cell_ones = jnp.ones((8, cells), jnp.bfloat16)
+    group_blocks = cell_ref.shape[1] // lanes - 1
+
+    def name_groups(block, unused):
+        group = (ramp((cells, lanes), 1) + block * lanes).astype(jnp.float32)
+        over = dot(cell_ones, flag(ends <= group))
+        at = pl.ds(pl.multiple_of(block * lanes, lanes), lanes)
+        cell_ref[:, at] = over[0:1].astype(jnp.int32)
+        return unused
+
+    lax.fori_loop(0, group_blocks, name_groups, 0)
+    cell_ref[:, pl.ds(group_blocks * lanes, lanes)] = ends[cells - 1 : cells].astype(jnp.int32)
+    before_cell = jnp.concatenate(
+        [value.T[0:8] for value in (taken, high, low)], axis=0
+    ).astype(jnp.bfloat16)
+
+    earlier = flag(ramp((lanes, lanes), 1) < ramp((lanes, lanes), 0))
+    earlier_tile = flag(ramp((wide, wide), 0) < ramp((wide, wide), 1))
+
+    def place(block, done):
+        at = pl.ds(pl.multiple_of(block * wide, wide), wide)
+        member = member_ref[:, at]
+        flags = member.astype(jnp.bfloat16)
+        count = dot(ones, flags)
+        lower = flag(ramp((cells, wide), 0) < own_ref[:, at])
+        before = dot(before_cell, lower)
+        so_far = dot(count[0:8].astype(jnp.bfloat16), earlier_tile) + done
+        start = (GROUP * before[0:8] + so_far - (lanes * before[8:16] + before[16:24]))
+        start = start.astype(jnp.int32)[0:1]
+        where_ref[:, at] = start * 256 + count[0:1].astype(jnp.int32)
+        rank = dot(earlier, flags)
+        slot = ramp((lanes, wide), 0)
+        word = jnp.where(member > 0.0, slot + lanes * (slot - rank.astype(jnp.int32)), 0)
         bit = 1
         while bit < lanes:
             keep = jnp.where((word & (bit * lanes)) != 0, 0, word)
@@ -120,97 +169,89 @@
             word = keep | jnp.concatenate([gone[bit:], gone[:bit]], axis=0)
             bit *= 2
         word = word & (lanes - 1)
+        turn = jnp.broadcast_to(start, (lanes, wide))
+        bit = 1
+        while bit < lanes:
+            moved = jnp.concatenate([word[lanes - bit :], word[: lanes - bit]], axis=0)
+            word = jnp.where((turn & bit) != 0, moved, word)
+            bit *= 2
         for part in range(wide // lanes):
             rows = pl.ds(pl.multiple_of(block * wide + part * lanes, lanes), lanes)
             slots_ref[rows, :] = word[:, part * lanes : (part + 1) * lanes].T
-        return unused
-
-    lax.fori_loop(0, tiles // wide, compact, 0)
-
-
-def fill_kernel(
-    near_smem, shift_smem, own_smem, first_smem, count_smem, table_ref, slots_ref, shift_ref,
-    turned_ref, cell_smem, until_smem, groups_smem, list_ref,
-):
+        total = jnp.sum(count[0:8], axis=1, keepdims=True)
+        return done + total
+
+    lax.fori_loop(0, tiles // wide, place, jnp.zeros((8, 1), jnp.float32))
+
+
+def fill_kernel(where_smem, near_smem, table_ref, slots_ref, shift_ref, list_ref):
     tiles, lanes = slots_ref.shape
-    cells = cell_smem.shape[0] - 8
     lane_bits = lanes.bit_length() - 1
     lane = lax.broadcasted_iota(jnp.int32, (8, lanes), 1)
     row = lax.broadcasted_iota(jnp.int32, (8, lanes), 0)
     absent = jnp.where(row == 6, -10.0, 0.0)
 
     def fill(block, carry):
-        end, entry, last_chunk, last_new, last_held = carry
+        last_chunk, last_new, last_held = carry
         units = range(FILL)
-        first = [first_smem[block * FILL + unit] for unit in units]
-        own = [own_smem[block * FILL + unit] for unit in units]
+        where = [where_smem[0, block * FILL + unit] for unit in units]
         near = [near_smem[block * FILL + unit] for unit in units]
-        shift = [shift_smem[block * FILL + unit] for unit in units]
-        amounts = [count_smem[0, block * FILL + unit] for unit in units]
-        starts, ends, entries = [], [], []
-        for unit in units:
-            align = first[unit] * (GROUP - 1)
-            start = (end + align) & ~align
-            end = start + jnp.maximum(amounts[unit], first[unit])
-            entry = entry + first[unit]
-            starts.append(start)
-            ends.append(end)
-            entries.append(entry)
         found = []
         for unit in units:
-            slots = jnp.broadcast_to(slots_ref[pl.ds(block * FILL + unit, 1), :], (8, lanes))
-            slots = pltpu.roll(slots, starts[unit] & (lanes - 1), 1)
-            found.append(lanes_of(table_ref[near[unit]], slots) + shift_ref[shift[unit]])
+            slots = slots_ref[pl.ds(block * FILL + unit, 8, stride=0), :]
+            cell = table_ref[near[unit] >> 5]
+            found.append(lanes_of(cell, slots) + shift_ref[near[unit] & 31])
         for unit in units:
-            chunk = starts[unit] >> lane_bits
-            offset = starts[unit] & (lanes - 1)
-            new = jnp.where(((lane - offset) & (lanes - 1)) < amounts[unit], found[unit], absent)
+            amount = where[unit] & 255
+            chunk = where[unit] >> (8 + lane_bits)
+            offset = (where[unit] >> 8) & (lanes - 1)
+            new = jnp.where(((lane - offset) & (lanes - 1)) < amount, found[unit], absent)
             held_row = jnp.where(chunk != last_chunk, last_new, last_held)
             held_row = jnp.where(lane >= offset, new, held_row)
             new = jnp.where(lane >= offset, absent, new)
             list_ref[chunk] = held_row
             list_ref[chunk + 1] = new
             last_chunk, last_new, last_held = chunk, new, held_row
-        for unit in units:
-            cell_smem[entries[unit]] = own[unit]
-            until_smem[entries[unit]] = (ends[unit] + (GROUP - 1)) >> GROUP_BITS
-        return end, entry, last_chunk, last_new, last_held
-
-    start = (jnp.int32(0), jnp.int32(-1), jnp.int32(0), absent, absent)
-    end, entry = lax.fori_loop(0, tiles // FILL, fill, start)[0:2]
-    groups_smem[0] = (end + (GROUP - 1)) >> GROUP_BITS
-    cell_smem[entry + 1] = cells
-    until_smem[entry + 1] = 1 << 30
-
-    def turn(block, unused):
-        rows = pl.ds(pl.multiple_of(block * lanes, lanes), lanes)
-        chunks = pl.ds(pl.multiple_of(block * 16, 16), 16)
-        turned_ref[rows, :] = list_ref[chunks].reshape(lanes, lanes).T
-        return unused
-
-    lax.fori_loop(0, (end + 16 * lanes - 1) >> (lane_bits + 4), turn, 0)
-
-
-def pair_kernel(cell_smem, until_smem, groups_smem, place_smem, table_ref, turned_ref, force_ref):
-    lanes = table_ref.shape[2]
-    lane_bits = lanes.bit_length() - 1
-    groups = groups_smem[0]
+        return last_chunk, last_new, last_held
+
+    lax.fori_loop(0, tiles // FILL, fill, (jnp.int32(0), absent, absent))
+
+
+def pair_kernel(cell_smem, place_smem, table_ref, list_ref, force_ref, even_ref, odd_ref):
+    lanes = table_ref.shape[1]
+    rows = even_ref.shape[0]
+    chunks = rows // lanes
+    units = rows // GROUP
+    groups = cell_smem[0, cell_smem.shape[1] - lanes]
     force_ref[...] = jnp.zeros(force_ref.shape, jnp.float32)
-
-    def pairs(step, entry):
+    part = lax.broadcasted_iota(jnp.int32, (32, 8 * lanes), 0)
+    comp = lax.broadcasted_iota(jnp.int32, (32, 8 * lanes), 1) // lanes
+    weights = jnp.where((part < 24) & (part % 8 == comp), 1.0, 0.0).astype(jnp.bfloat16)
+
+    def spread(step, out_ref):
+        turned = []
+        for piece in range(chunks):
+            values = list_ref[step * chunks + piece]
+            high = values.astype(jnp.bfloat16).astype(jnp.float32)
+            rest = values - high
+            middle = rest.astype(jnp.bfloat16).astype(jnp.float32)
+            parts = jnp.concatenate([high, middle, rest - middle, jnp.zeros_like(values)], axis=0)
+            turned.append(parts.T.astype(jnp.bfloat16))
+        turned = jnp.concatenate(turned, axis=0)
+        out_ref[...] = jnp.dot(turned, weights, preferred_element_type=jnp.float32)
+
+    def pairs(step, wide_ref):
         totals = []
-        for unit in range(UNITS):
-            group = step * UNITS + unit
-            entry = entry + jnp.where(group >= until_smem[entry], 1, 0)
-            cell = cell_smem[entry]
-            own = place_smem[cell]
-            begin = group * GROUP
-            chunk = begin >> lane_bits
-            at = (chunk >> 4) * lanes + (begin & (lanes - 1))
-            block = turned_ref[pl.ds(pl.multiple_of(at, GROUP), GROUP), :]
-            block = pltpu.roll(block, (lanes - (chunk & 15) * 8) & (lanes - 1), 1)
-            other = [block[:, comp : comp + 1] for comp in range(8)]
-            mine = [table_ref[own, pl.ds(comp, 1), :] for comp in range(8)]
+        for unit in range(units):
+            cell = cell_smem[0, step * units + unit]
+            own = place_smem[cell] * 8
+            other = [
+                wide_ref[pl.ds(unit * GROUP, GROUP), pl.ds(value * lanes, lanes)].reshape(
+                    GROUP // 8, 8, lanes
+                )
+                for value in range(8)
+            ]
+            mine = [table_ref[pl.ds(own + value, 8, stride=0), :][None] for value in range(8)]
             apart = [other[axis] - mine[axis] for axis in range(3)]
             square = apart[0] * apart[0] + apart[1] * apart[1] + apart[2] * apart[2] + epsilon_sq
             inverse = lax.rsqrt(square)
@@ -224,33 +265,32 @@
             )
             scaled = overlap * (other[6] * mine[6])
             root = scaled * lax.rsqrt(jnp.maximum(scaled * reach, 1e-30))
-            factor = (
-                root * inverse * (stiffness / damping * overlap - closing * inverse)
-            )
-            totals.append(
-                (
-                    cell,
-                    [
-                        jnp.sum((factor * apart[axis]).reshape(GROUP // 8, 8, lanes), axis=0)
-                        for axis in range(3)
-                    ],
-                )
-            )
+            factor = root * inverse * (stiffness / damping * overlap - closing * inverse)
+            totals.append((cell, [jnp.sum(factor * apart[axis], axis=0) for axis in range(3)]))
         for cell, parts in totals:
             for axis in range(3):
                 force_ref[axis, cell] += parts[axis]
-        return entry
-
-    lax.fori_loop(0, lax.div(groups + (UNITS - 1), UNITS), pairs, 0)
+
+    spread(0, even_ref)
+
+    def both(step, unused):
+        spread(2 * step + 1, odd_ref)
+        pairs(2 * step, even_ref)
+        spread(2 * step + 2, even_ref)
+        pairs(2 * step + 1, odd_ref)
+        return unused
+
+    lax.fori_loop(0, lax.div(groups + (2 * units - 1), 2 * units), both, 0)
 
 
 def sums_kernel(force_ref, arms_ref, frag_ref, out_ref, loads_ref):
     cells, lanes = frag_ref.shape
     held = out_ref.shape[1]
+    tall = loads_ref.shape[0]
     label = lax.broadcasted_iota(jnp.int32, (held, lanes), 0)
 
     def gather_sums(block, total):
-        rows = pl.ds(pl.multiple_of(block * 8, 8), 8)
+        rows = pl.ds(pl.multiple_of(block * tall, tall), tall)
         force = [-damping * jnp.sum(force_ref[axis, rows], axis=1) for axis in range(3)]
         lever = [arms_ref[axis, rows, :] for axis in range(3)]
         torque = [
@@ -262,12 +302,14 @@
         for comp in range(8):
             loads_ref[:, comp, :] = loads[comp]
         frags = frag_ref[rows, :]
-        for unit in range(8):
-            hits = (frags[unit : unit + 1, :] == label).astype(jnp.float32).astype(jnp.bfloat16)
-            total = total + dot_lanes(split_rows(loads_ref[unit]), hits)
-        return total
-
-    total = lax.fori_loop(0, cells // 8, gather_sums, jnp.zeros((24, held), jnp.float32))
+        hits = [
+            (frags[unit : unit + 1, :] == label).astype(jnp.float32).astype(jnp.bfloat16)
+            for unit in range(tall)
+        ]
+        values = [split_rows(loads_ref[unit]) for unit in range(tall)]
+        return total + dot_lanes(jnp.concatenate(values, axis=1), jnp.concatenate(hits, axis=1))
+
+    total = lax.fori_loop(0, cells // tall, gather_sums, jnp.zeros((24, held), jnp.float32))
     out_ref[...] = joined_rows(total)
 
 
@@ -397,6 +439,7 @@
     span_y, span_z = (cells_y + 2, cells_z + 2)
     span = (cells_x + 2) * span_y * span_z
     padded = padded.reshape(span, 8, lanes)
+    flat = padded.reshape(span * 8, lanes)
 
     codes = jnp.sort(tiles[0])
     total = codes.shape[0]
@@ -415,53 +458,51 @@
         jnp.where(steps[axis] == 1, 1, jnp.where(steps[axis] == -1, 2, 0)) << (2 * axis)
         for axis in range(3)
     )
-    first = jnp.concatenate([jnp.ones((1,), jnp.int32), (own[1:] != own[:-1]).astype(jnp.int32)])
     place = pad_place(jnp.arange(cells + 1, dtype=jnp.int32) % cells)
     kinds = jnp.arange(27, dtype=jnp.int32)
     moves = jnp.stack([kinds // 9 - 1, kinds // 3 % 3 - 1, kinds % 3 - 1], axis=1)
     shift = jnp.pad(moves.astype(jnp.float32), ((0, 0), (0, 5)))
     shift = jnp.broadcast_to(shift[:, :, None], (27, 8, lanes))
 
-    slots, count = pl.pallas_call(
+    chunks = -(-(total + cells * GROUP // lanes) // 16) * 16 + 8
+    group_top = chunks * (lanes // GROUP)
+    slots, where, cell_of = pl.pallas_call(
         list_kernel,
         out_shape=(
             jax.ShapeDtypeStruct((total, lanes), jnp.int32),
-            jax.ShapeDtypeStruct((8, total), jnp.int32),
+            jax.ShapeDtypeStruct((1, total), jnp.int32),
+            jax.ShapeDtypeStruct((1, -(-group_top // lanes) * lanes + lanes), jnp.int32),
         ),
-        in_specs=[vmem] * 3,
-        out_specs=(vmem, vmem),
-        scratch_shapes=[pltpu.VMEM((-(-span // lanes) * lanes, lanes), jnp.float32)],
-        compiler_params=params,
-    )(near[None], need[None], padded.reshape(span * 8, lanes))
-
-    chunks = total + cells * GROUP // lanes + 2
-    chunks = -(-chunks // 16) * 16
-    turned, cell_of, until, groups = pl.pallas_call(
+        in_specs=[vmem] * 4,
+        out_specs=(vmem, vmem, vmem),
+        scratch_shapes=[
+            pltpu.VMEM((-(-span // lanes) * lanes, lanes), jnp.float32),
+            pltpu.VMEM((lanes, total), jnp.float32),
+            pltpu.VMEM((cells, lanes), jnp.float32),
+        ],
+        compiler_params=params,
+    )(near[None], need[None], own[None], flat)
+    lists = pl.pallas_call(
         fill_kernel,
-        out_shape=(
-            jax.ShapeDtypeStruct((chunks * 8, lanes), jnp.float32),
-            jax.ShapeDtypeStruct((cells + 8,), jnp.int32),
-            jax.ShapeDtypeStruct((cells + 8,), jnp.int32),
-            jax.ShapeDtypeStruct((1,), jnp.int32),
-        ),
-        in_specs=[smem] * 5 + [vmem] * 3,
-        out_specs=(vmem, smem, smem, smem),
-        scratch_shapes=[pltpu.VMEM((chunks, 8, lanes), jnp.float32)],
-        compiler_params=params,
-    )(near, offset, own, first, count[0:1], padded, slots, shift)
+        out_shape=jax.ShapeDtypeStruct((chunks, 8, lanes), jnp.float32),
+        in_specs=[smem] * 2 + [vmem] * 3,
+        out_specs=vmem,
+        compiler_params=params,
+    )(where, near * 32 + offset, padded, slots, shift)
     force = pl.pallas_call(
         pair_kernel,
         out_shape=jax.ShapeDtypeStruct((3, cells + 8, 8, lanes), jnp.float32),
-        in_specs=[smem] * 4 + [vmem] * 2,
+        in_specs=[smem] * 2 + [vmem] * 2,
         out_specs=vmem,
-        compiler_params=params,
-    )(cell_of, until, groups, place, padded, turned)
+        scratch_shapes=[pltpu.VMEM((SPREAD * lanes, 8 * lanes), jnp.float32)] * 2,
+        compiler_params=params,
+    )(cell_of, place, flat, lists)
     sums = pl.pallas_call(
         sums_kernel,
         out_shape=jax.ShapeDtypeStruct((8, held), jnp.float32),
         in_specs=[vmem] * 3,
         out_specs=vmem,
-        scratch_shapes=[pltpu.VMEM((8, 8, lanes), jnp.float32)],
+        scratch_shapes=[pltpu.VMEM((16, 8, lanes), jnp.float32)],
         compiler_params=params,
     )(force, flat_arms, flat_frag)
 

time: 280 us -> 176 us (0.63)
  Pallas kernels: 213 us -> 116 us
  waiting for transfers between devices: 24.4 us -> 19.9 us
    pallas_call x1, Pallas kernels: 145 us -> 56.1 us  [local(): pl.pallas_call(pair_kernel, out_shape=jax.ShapeDtypeStruct((3, cells + 8,...]
    pallas_call x1, Pallas kernels: 39.6 us -> 20 us  [local(): pl.pallas_call(fill_kernel, out_shape=jax.ShapeDtypeStruct((chunks, 8, la...]
    pallas_call x1, Pallas kernels: 8.67 us -> 22 us  [local(): pl.pallas_call(list_kernel, out_shape=(jax.ShapeDtypeStruct((total, lanes...]
    ppermute x3, waiting for transfers between devices: 13.8 us -> 10 us  [with_halo(): before = lax.ppermute(last, axis, up)]
  transfers between devices with their start and end apart: 8 -> 8, of which waited for: 5 -> 5; matrix products, arithmetic and copies ran while one was open for 6% -> 8% of each run, Pallas kernels for 73% -> 61%
where the time goes in v4:
time: 176 us
  Pallas kernels  116 us (66%)
  starting transfers between devices  21.2 us (12%)
  waiting for transfers between devices  19.9 us (11%)
  other arithmetic  11.2 us (6%)
  local copies, waits for them, and re-layouts  7.21 us (4%)
    pallas_call x1, Pallas kernels, local(): pl.pallas_call(pair_kernel, out_shape=jax.ShapeDtypeStruct((3, cells + 8,...  56.1 us
    pallas_call x1, Pallas kernels, local(): pl.pallas_call(list_kernel, out_shape=(jax.ShapeDtypeStruct((total, lanes...  22 us
    pallas_call x1, Pallas kernels, local(): pl.pallas_call(fill_kernel, out_shape=jax.ShapeDtypeStruct((chunks, 8, la...  20 us
    all_to_all x2, starting transfers between devices, everywhere(): lax.all_to_all(copies, names, split_axis=0, concat_axis=0, tiled=True)  12.8 us
    ppermute x3, waiting for transfers between devices, with_halo(): before = lax.ppermute(last, axis, up)  10 us
    ppermute x3, waiting for transfers between devices, with_halo(): after = lax.ppermute(initial, axis, down)  8.29 us
    pallas_call x1, Pallas kernels, local(): pl.pallas_call(sums_kernel, out_shape=jax.ShapeDtypeStruct((8, held), jnp...  7.21 us
    sort x1, other arithmetic, local(): codes = jnp.sort(tiles[0])  5.03 us
  transfers between devices with their start and end apart: 8, of which 5 were waited for; matrix products, arithmetic and copies ran while one was open for 8% of the time, Pallas kernels for 61%

profile of v4, /device:TPU:0, one launch (start us, length us, event | category | flops | bytes accessed | tf_op | source)
XLA Modules:
  0.0 175.8 jit_solution(5678354335873896200)
XLA Ops:
  1.9 2.9 %shard_map.105 = f32[256,8,128]{2,1,0:T(8,128)} custom-call(f32[7,256,128]{2,1,0:T(8,128)} %bitcast.31, s32[256,128]{1,0:T(8,128)} %bitcast.35, f32[1,128]{1,0:T(1,128)} %get-tuple-element.27.key_ref), custom_call_target="tpu_custom_call" | custom-call | tf_op jit(solution)/shard_map/pallas_call | solution.py:429
  4.7 1.2 fusion.40
  6.4 2.0 %collective-permute-start.1 = (f32[1,4,16,8,128]{4,3,2,1,0:T(8,128)S(1)}, f32[1,4,16,8,128]{4,3,2,1,0:T(8,128)S(1)}, u32[]{:S(2)}, u32[]{:S(2)}) collective-permute-start(f32[1,4,16,8,128]{4,3,2,1,0:T(8,128)S(1)} %bitcast.38), channel_id=1, source_target_pairs={{8,0},{16,8},{24,16},{0,24},{9,1},{17,9},{25,17},{1,25},{10,2},{18... | collective-permute-start | bytes 786440 | tf_op jit(solution)/shard_map/ppermute | solution.py:60
  8.6 0.8 reshape.134
  9.4 6.6 %all-to-all-start = ((f32[32,1,1024]{2,1,0:T(1,128)}), f32[32,1,1024]{2,1,0:T(1,128)S(1)}, u32[]{:S(2)}, u32[]{:S(2)}) async-start(f32[32,1,1024]{2,1,0:T(1,128)} %reshape.134), calls=%async_computation | async-start | bytes 262144 | tf_op jit(solution)/shard_map/all_to_all | solution.py:49
  16.1 1.8 %collective-permute-start.2 = (f32[6,1,16,8,128]{4,3,2,1,0:T(8,128)S(1)}, f32[6,1,16,8,128]{4,3,2,1,0:T(8,128)S(1)}, u32[]{:S(2)}, u32[]{:S(2)}) collective-permute-start(f32[6,1,16,8,128]{4,3,2,1,0:T(8,128)S(1)} %get-tuple-element.19), channel_id=1, source_target_pairs={{0,2},{2,4},{4,6},{6,0},{1,3},{3,5},{5,7},{7,1},{8,10},{10,12},{12... | collective-permute-start | bytes 1179656 | tf_op jit(solution)/shard_map/ppermute | solution.py:59
  18.0 2.1 %collective-permute-start.3 = (f32[6,1,16,8,128]{4,3,2,1,0:T(8,128)S(1)}, f32[6,1,16,8,128]{4,3,2,1,0:T(8,128)S(1)}, u32[]{:S(2)}, u32[]{:S(2)}) collective-permute-start(f32[6,1,16,8,128]{4,3,2,1,0:T(8,128)S(1)} %get-tuple-element.20), channel_id=1, source_target_pairs={{2,0},{4,2},{6,4},{0,6},{3,1},{5,3},{7,5},{1,7},{10,8},{12,10},{14... | collective-permute-start | bytes 1179656 | tf_op jit(solution)/shard_map/ppermute | solution.py:60
  20.1 5.0 %sort.15 = (s32[2048]{0:T(1024)S(1)}, s32[2048]{0:T(1024)}) sort(s32[2048]{0:T(1024)S(1)} %bitcast.43, s32[2048]{0:T(1024)S(1)} %iota.26), dimensions={0}, to_apply=%region_0.1 | sort | flops 22528 | bytes 32768 | tf_op jit(solution)/shard_map/jit(sort)/sort | solution.py:444
  26.4 5.4 %collective-permute-done.2 = f32[6,1,16,8,128]{4,3,2,1,0:T(8,128)S(1)} collective-permute-done((f32[6,1,16,8,128]{4,3,2,1,0:T(8,128)S(1)}, f32[6,1,16,8,128]{4,3,2,1,0:T(8,128)S(1)}, u32[]{:S(2)}, u32[]{:S(2)}) %collective-permute-start.2) | collective-permute-done | bytes 393248 | tf_op jit(solution)/shard_map/ppermute | solution.py:59
  31.8 6.6 %collective-permute-done.3 = f32[6,1,16,8,128]{4,3,2,1,0:T(8,128)S(1)} collective-permute-done((f32[6,1,16,8,128]{4,3,2,1,0:T(8,128)S(1)}, f32[6,1,16,8,128]{4,3,2,1,0:T(8,128)S(1)}, u32[]{:S(2)}, u32[]{:S(2)}) %collective-permute-start.3) | collective-permute-done | bytes 393248 | tf_op jit(solution)/shard_map/ppermute | solution.py:60
  38.4 1.5 collective-permute-start.4
  40.7 4.6 %collective-permute-done.4 = f32[6,6,1,8,128]{4,3,2,1,0:T(8,128)S(1)} collective-permute-done((f32[6,6,1,8,128]{4,3,2,1,0:T(8,128)S(1)}, f32[6,6,1,8,128]{4,3,2,1,0:T(8,128)S(1)}, u32[]{:S(2)}, u32[]{:S(2)}) %collective-permute-start.4) | collective-permute-done | bytes 147488 | tf_op jit(solution)/shard_map/ppermute | solution.py:59
  45.3 1.7 collective-permute-done.5
  46.9 1.8 %pad_maximum_fusion = f32[6,6,18,8,128]{4,3,2,1,0:T(8,128)} fusion(f32[6,6,1,8,128]{4,3,2,1,0:T(8,128)S(1)} %collective-permute-done.5, f32[6,1,16,8,128]{4,3,2,1,0:T(8,128)S(1)} %collective-permute-done.3, f32[1,4,16,8,128]{4,3,2,1,0:T(8,128)S(1)} %collective-permute-done.1, f32[4,4,16,8,128]{4,3,2,1,0:T(8,128)S(1)} %bitcast.30, ...), kind=kLoop, calls=%fused_computation | loop fusion | flops 3981312 | bytes 5308416 | tf_op jit(solution)/shard_map/concatenate | solution.py:61
  48.7 22.0 %shard_map.106 = (s32[2048,128]{1,0:T(8,128)}, s32[1,2048]{1,0:T(1,128)}, s32[1,8704]{1,0:T(1,128)}) custom-call(s32[1,2048]{1,0:T(1,128)} %bitcast.42, s32[1,2048]{1,0:T(1,128)} %bitcast.41, s32[1,2048]{1,0:T(1,128)} %bitcast.40, f32[5184,128]{1,0:T(8,128)} %bitcast.25), custom_call_target="tpu_custom_call" | custom-call | tf_op jit(solution)/shard_map/pallas_call | solution.py:469
  71.4 20.0 %shard_map.107.list_ref = f32[2120,8,128]{2,1,0:T(8,128)} custom-call(s32[1,2048]{1,0:T(1,128)} %get-tuple-element.11.where_smem, s32[2048]{0:T(1024)} %get-tuple-element.25.near_smem, f32[648,8,128]{2,1,0:T(8,128)} %bitcast.26, s32[2048,128]{1,0:T(8,128)} %get-tuple-element.12.slots_ref, f32[27,8,128]{2,1,0:T(8,128)} %broadcast_in_dim.75.shift_ref), custom_call_target="tpu_custom_call" | custom-call | tf_op jit(solution)/shard_map/pallas_call | solution.py:485
  91.5 56.1 %shard_map.108.force_ref = f32[3,264,8,128]{3,2,1,0:T(8,128)} custom-call(s32[1,8704]{1,0:T(1,128)} %get-tuple-element.10.cell_smem, s32[257]{0:T(512)} %fusion.24.place_smem, f32[5184,128]{1,0:T(8,128)} %bitcast.27, f32[2120,8,128]{2,1,0:T(8,128)} %shard_map.107.list_ref), custom_call_target="tpu_custom_call" | custom-call | tf_op jit(solution)/shard_map/pallas_call | solution.py:492
  147.6 7.2 %shard_map.109 = f32[8,64]{1,0:T(8,128)} custom-call(f32[3,264,8,128]{3,2,1,0:T(8,128)} %shard_map.108.force_ref, f32[3,256,128]{2,1,0:T(8,128)} %bitcast.33, s32[256,128]{1,0:T(8,128)} %bitcast.36), custom_call_target="tpu_custom_call" | custom-call | tf_op jit(solution)/shard_map/pallas_call | solution.py:500
  156.3 6.2 %all-to-all-start.1 = ((f32[32,1,512]{2,1,0:T(1,128)}), f32[32,1,512]{2,1,0:T(1,128)S(1)}, u32[]{:S(2)}, u32[]{:S(2)}) async-start(f32[32,1,512]{2,1,0:T(1,128)} %reshape.136), calls=%async_computation.1 | async-start | bytes 131072 | tf_op jit(solution)/shard_map/all_to_all | solution.py:49
  163.7 0.9 reduce
  164.6 0.8 reshape.135.fixed_ref
  165.5 2.7 %shard_map.104.base_ref = f32[8,128]{1,0:T(8,128)} custom-call(f32[128,1]{1,0:T(8,128)} %copy.15.target_ref, f32[32,16,64]{2,1,0:T(8,128)} %reshape.135.fixed_ref), custom_call_target="tpu_custom_call" | custom-call | tf_op jit(solution)/shard_map/pallas_call | solution.py:516
  168.2 1.6 all-to-all-done.1
  171.3 4.6 %shard_map.110 = (f32[6,256,128]{2,1,0:T(8,128)}, f32[6,128]{1,0:T(8,128)}) custom-call(f32[128,1]{1,0:T(8,128)} %copy.15.target_ref, f32[32,16,64]{2,1,0:T(8,128)} %reshape.135.fixed_ref, f32[8,128]{1,0:T(8,128)} %shard_map.104.base_ref, f32[32,8,64]{2,1,0:T(8,128)} %reshape.137.sums_ref, f32[7,256,128]{2,1,0:T(8,128)} %bitcast.32, ...), custom_call_target="tpu_custom_call" | custom-call | tf_op jit(solution)/shard_map/pallas_call | solution.py:523
  (39 shorter events, 9.0 us)
Async XLA Ops:
  0.6 7.8 %copy-start.4 = (f32[48]{0:T(128)S(1)}, f32[48]{0:T(128)}, u32[]{:S(2)}) copy-start(f32[48]{0:T(128)} %param.16) | copy-start | bytes 580
  0.6 7.8 %copy-start.3 = (f32[48]{0:T(128)S(1)}, f32[48]{0:T(128)}, u32[]{:S(2)}) copy-start(f32[48]{0:T(128)} %param.17) | copy-start | bytes 580
  0.7 7.8 %copy-start.2 = (f32[6,48]{1,0:T(8,128)S(1)}, f32[6,48]{1,0:T(8,128)}, u32[]{:S(2)}) copy-start(f32[6,48]{1,0:T(8,128)} %param.15) | copy-start | bytes 3460
  4.7 11.3 %copy-start = (f32[256,8,128]{2,1,0:T(8,128)S(1)}, f32[256,8,128]{2,1,0:T(8,128)}, u32[]{:S(2)}) copy-start(f32[256,8,128]{2,1,0:T(8,128)} %shard_map.105) | copy-start | bytes 3145732
  4.7 15.3 %copy-start.1 = (s32[1,2048]{1,0:T(1,128)S(1)}, s32[1,2048]{1,0:T(1,128)}, u32[]{:S(2)}) copy-start(s32[1,2048]{1,0:T(1,128)} %param.14) | copy-start | bytes 24580
  5.9 10.2 %collective-permute-start = (f32[1,4,16,8,128]{4,3,2,1,0:T(8,128)S(1)}, f32[1,4,16,8,128]{4,3,2,1,0:T(8,128)S(1)}, u32[]{:S(2)}, u32[]{:S(2)}) collective-permute-start(f32[1,4,16,8,128]{4,3,2,1,0:T(8,128)S(1)} %bitcast.39), channel_id=1, source_target_pairs={{0,8},{8,16},{16,24},{24,0},{1,9},{9,17},{17,25},{25,1},{2,10},{10... | collective-permute-start | bytes 786440 | tf_op jit(solution)/shard_map/ppermute | solution.py:59
  6.4 9.7 %collective-permute-start.1 = (f32[1,4,16,8,128]{4,3,2,1,0:T(8,128)S(1)}, f32[1,4,16,8,128]{4,3,2,1,0:T(8,128)S(1)}, u32[]{:S(2)}, u32[]{:S(2)}) collective-permute-start(f32[1,4,16,8,128]{4,3,2,1,0:T(8,128)S(1)} %bitcast.38), channel_id=1, source_target_pairs={{8,0},{16,8},{24,16},{0,24},{9,1},{17,9},{25,17},{1,25},{10,2},{18... | collective-permute-start | bytes 786440 | tf_op jit(solution)/shard_map/ppermute | solution.py:60
  9.4 146.8 %all-to-all-start = ((f32[32,1,1024]{2,1,0:T(1,128)}), f32[32,1,1024]{2,1,0:T(1,128)S(1)}, u32[]{:S(2)}, u32[]{:S(2)}) async-start(f32[32,1,1024]{2,1,0:T(1,128)} %reshape.134), calls=%async_computation | async-start | bytes 262144 | tf_op jit(solution)/shard_map/all_to_all | solution.py:49
  16.1 15.6 %collective-permute-start.2 = (f32[6,1,16,8,128]{4,3,2,1,0:T(8,128)S(1)}, f32[6,1,16,8,128]{4,3,2,1,0:T(8,128)S(1)}, u32[]{:S(2)}, u32[]{:S(2)}) collective-permute-start(f32[6,1,16,8,128]{4,3,2,1,0:T(8,128)S(1)} %get-tuple-element.19), channel_id=1, source_target_pairs={{0,2},{2,4},{4,6},{6,0},{1,3},{3,5},{5,7},{7,1},{8,10},{10,12},{12... | collective-permute-start | bytes 1179656 | tf_op jit(solution)/shard_map/ppermute | solution.py:59
  18.0 20.4 %collective-permute-start.3 = (f32[6,1,16,8,128]{4,3,2,1,0:T(8,128)S(1)}, f32[6,1,16,8,128]{4,3,2,1,0:T(8,128)S(1)}, u32[]{:S(2)}, u32[]{:S(2)}) collective-permute-start(f32[6,1,16,8,128]{4,3,2,1,0:T(8,128)S(1)} %get-tuple-element.20), channel_id=1, source_target_pairs={{2,0},{4,2},{6,4},{0,6},{3,1},{5,3},{7,5},{1,7},{10,8},{12,10},{14... | collective-permute-start | bytes 1179656 | tf_op jit(solution)/shard_map/ppermute | solution.py:60
  38.4 6.8 %collective-permute-start.4 = (f32[6,6,1,8,128]{4,3,2,1,0:T(8,128)S(1)}, f32[6,6,1,8,128]{4,3,2,1,0:T(8,128)S(1)}, u32[]{:S(2)}, u32[]{:S(2)}) collective-permute-start(f32[6,6,1,8,128]{4,3,2,1,0:T(8,128)S(1)} %get-tuple-element.17), channel_id=1, source_target_pairs={{0,1},{1,0},{2,3},{3,2},{4,5},{5,4},{6,7},{7,6},{8,9},{9,8},{10,11... | collective-permute-start | bytes 442376 | tf_op jit(solution)/shard_map/ppermute | solution.py:59
  39.9 7.0 %collective-permute-start.5 = (f32[6,6,1,8,128]{4,3,2,1,0:T(8,128)S(1)}, f32[6,6,1,8,128]{4,3,2,1,0:T(8,128)S(1)}, u32[]{:S(2)}, u32[]{:S(2)}) collective-permute-start(f32[6,6,1,8,128]{4,3,2,1,0:T(8,128)S(1)} %get-tuple-element.18), channel_id=1, source_target_pairs={{1,0},{0,1},{3,2},{2,3},{5,4},{4,5},{7,6},{6,7},{9,8},{8,9},{11,10... | collective-permute-start | bytes 442376 | tf_op jit(solution)/shard_map/ppermute | solution.py:60
  156.3 13.5 %all-to-all-start.1 = ((f32[32,1,512]{2,1,0:T(1,128)}), f32[32,1,512]{2,1,0:T(1,128)S(1)}, u32[]{:S(2)}, u32[]{:S(2)}) async-start(f32[32,1,512]{2,1,0:T(1,128)} %reshape.136), calls=%async_computation.1 | async-start | bytes 131072 | tf_op jit(solution)/shard_map/all_to_all | solution.py:49

commit v5 on v4

v5 whole, which is shorter than its diff:
```python
import functools

import jax
import jax.numpy as jnp
from jax import lax
from jax.experimental import pallas as pl
from jax.experimental.pallas import tpu as pltpu
from jax.sharding import PartitionSpec as P

stiffness = 100.0
damping = 2.0
time_step = 0.01
gravity = 9.81
epsilon_sq = 1e-08
radius_top = 0.14

GROUP = 32
FILL = 16
SPREAD = 2
VMEM = 56 * 1024 * 1024


def lanes_of(values, index):
    return jnp.take_along_axis(values, index, axis=1, mode="promise_in_bounds")


def split_rows(values):
    high = values.astype(jnp.bfloat16).astype(jnp.float32)
    rest = values - high
    middle = rest.astype(jnp.bfloat16).astype(jnp.float32)
    low = rest - middle
    return jnp.concatenate([high, middle, low], axis=0).astype(jnp.bfloat16)


def joined_rows(stacked):
    rows = stacked.shape[0] // 3
    return stacked[0:rows] + stacked[rows : 2 * rows] + stacked[2 * rows :]


def dot_lanes(first, second):
    return lax.dot_general(
        first, second, (((1,), (1,)), ((), ())), preferred_element_type=jnp.float32
    )


def exchange(last, initial, axis):
    devices = lax.axis_size(axis)
    up = [(i, (i + 1) % devices) for i in range(devices)]
    down = [(j, i) for i, j in up]
    return lax.ppermute(last, axis, up), lax.ppermute(initial, axis, down)


def pack_kernel(state_ref, frag_ref, key_ref, out_ref):
    cells = frag_ref.shape[0]
    for comp in range(7):
        out_ref[:, comp, :] = state_ref[comp]
    keys = jnp.broadcast_to(key_ref[0:1, :], (8, key_ref.shape[1]))
    for block in range(cells // 8):
        rows = pl.ds(block * 8, 8)
        out_ref[rows, 7, :] = lanes_of(keys, frag_ref[rows, :])


def list_kernel(
    amount_smem, near_ref, need_ref, own_ref, table_ref, slots_ref, where_ref, cell_ref, class_ref, member_ref, count_ref
):
    tiles, lanes = slots_ref.shape
    span = table_ref.shape[0] // 8
    padded = class_ref.shape[0]
    cells = count_ref.shape[0]
    wide = 256

    def plane(comp):
        return table_ref[pl.ds(comp, span, stride=8), :]

    def flag(value):
        return value.astype(jnp.float32).astype(jnp.bfloat16)

    def dot(first, second):
        return jnp.dot(first, second, preferred_element_type=jnp.float32)

    def ramp(shape, axis):
        return lax.broadcasted_iota(jnp.int32, shape, axis)

    radius = plane(6) + (radius_top + 1e-5)
    classes = jnp.zeros((span, lanes), jnp.float32)
    for axis in range(3):
        place = plane(axis)
        classes = classes + jnp.where(place < radius, 1.0 * (1 << (2 * axis)), 0.0)
        classes = classes + jnp.where(place > 1.0 - radius, 1.0 * (2 << (2 * axis)), 0.0)
    class_ref[...] = jnp.zeros(class_ref.shape, jnp.float32)
    class_ref[pl.ds(0, span), :] = classes
    codes = jnp.concatenate(
        [class_ref[pl.ds(at, lanes), :].T for at in range(0, padded, lanes)], axis=1
    ).astype(jnp.bfloat16)
    ones = jnp.ones((lanes, lanes), jnp.bfloat16)
    count_ref[...] = jnp.zeros(count_ref.shape, jnp.float32)

    pair = 2 * wide
    blocks = lax.div(amount_smem[0] + (pair - 1), pair)

    def choose(block, unused):
        held = []
        for half in range(2):
            at = pl.ds(pl.multiple_of(block * pair + half * wide, wide), wide)
            hits = flag(ramp((padded, wide), 0) == near_ref[:, at])
            found = dot(codes, hits).astype(jnp.int32)
            need = need_ref[:, at]
            member = ((found & need) == need).astype(jnp.float32)
            member_ref[:, at] = member
            count = dot(ones, member.astype(jnp.bfloat16))
            mine = flag(ramp((cells, wide), 0) == own_ref[:, at])
            held.append(dot_lanes(mine, count.astype(jnp.bfloat16)))
        count_ref[...] += held[0] + held[1]
        return unused

    lax.fori_loop(0, blocks, choose, 0)

    held = count_ref[...]
    high = jnp.floor(held * (1.0 / lanes))
    low = held - lanes * high
    taken = jnp.floor((held + (GROUP - 1)) * (1.0 / GROUP))
    upto = flag(ramp((cells, cells), 1) <= ramp((cells, cells), 0))
    ends = dot(upto, taken.astype(jnp.bfloat16))
    cell_ones = jnp.ones((8, cells), jnp.bfloat16)
    group_blocks = cell_ref.shape[1] // lanes - 1

    def name_groups(block, unused):
        group = (ramp((cells, lanes), 1) + block * lanes).astype(jnp.float32)
        over = dot(cell_ones, flag(ends <= group))
        at = pl.ds(pl.multiple_of(block * lanes, lanes), lanes)
        cell_ref[:, at] = over[0:1].astype(jnp.int32)
        return unused

    used = jnp.max(ends).astype(jnp.int32)
    needed = jnp.minimum((used >> (lanes.bit_length() - 1)) + 2, group_blocks)
    lax.fori_loop(0, needed, name_groups, 0)
    cell_ref[:, pl.ds(group_blocks * lanes, lanes)] = ends[cells - 1 : cells].astype(jnp.int32)
    before_cell = jnp.concatenate(
        [value.T[0:8] for value in (taken, high, low)], axis=0
    ).astype(jnp.bfloat16)

    earlier = flag(ramp((lanes, lanes), 1) < ramp((lanes, lanes), 0))
    earlier_tile = flag(ramp((wide, wide), 0) < ramp((wide, wide), 1))

    def place(block, done):
        for half in range(2):
            at = pl.ds(pl.multiple_of(block * pair + half * wide, wide), wide)
            flags = member_ref[:, at].astype(jnp.bfloat16)
            count = dot(ones, flags)
            lower = flag(ramp((cells, wide), 0) < own_ref[:, at])
            before = dot(before_cell, lower)
            so_far = dot(count[0:8].astype(jnp.bfloat16), earlier_tile) + done
            start = GROUP * before[0:8] + so_far - (lanes * before[8:16] + before[16:24])
            start = start.astype(jnp.int32)[0:1]
            where_ref[:, at] = start * 256 + count[0:1].astype(jnp.int32)
            rank = dot(earlier, flags)
            slot = ramp((lanes, wide), 0)
            moves = slot - rank.astype(jnp.int32)
            word = jnp.where(member_ref[:, at] > 0.0, slot + lanes * moves, 0)
            bit = 1
            while bit < lanes:
                keep = jnp.where((word & (bit * lanes)) != 0, 0, word)
                gone = word ^ keep
                word = keep | jnp.concatenate([gone[bit:], gone[:bit]], axis=0)
                bit *= 2
            word = word & (lanes - 1)
            turn = jnp.broadcast_to(start, (lanes, wide))
            bit = 1
            while bit < lanes:
                moved = jnp.concatenate([word[lanes - bit :], word[: lanes - bit]], axis=0)
                word = jnp.where((turn & bit) != 0, moved, word)
                bit *= 2
            for part in range(wide // lanes):
                first = block * pair + half * wide + part * lanes
                rows = pl.ds(pl.multiple_of(first, lanes), lanes)
                slots_ref[rows, :] = word[:, part * lanes : (part + 1) * lanes].T
            done = done + jnp.sum(count[0:8], axis=1, keepdims=True)
        return done

    lax.fori_loop(0, blocks, place, jnp.zeros((8, 1), jnp.float32))


def fill_lists(amount, where_smem, near_smem, table_ref, slots_ref, shift_ref, list_ref):
    tiles, lanes = slots_ref.shape
    lane_bits = lanes.bit_length() - 1
    lane = lax.broadcasted_iota(jnp.int32, (8, lanes), 1)
    row = lax.broadcasted_iota(jnp.int32, (8, lanes), 0)
    absent = jnp.where(row == 6, -10.0, 0.0)

    def fill(block, carry):
        last_chunk, last_new, last_held = carry
        units = range(FILL)
        where = [where_smem[0, block * FILL + unit] for unit in units]
        near = [near_smem[block * FILL + unit] for unit in units]
        found = []
        for unit in units:
            slots = slots_ref[pl.ds(block * FILL + unit, 8, stride=0), :]
            cell = table_ref[near[unit] >> 5]
            found.append(lanes_of(cell, slots) + shift_ref[near[unit] & 31])
        for unit in units:
            amount = where[unit] & 255
            chunk = where[unit] >> (8 + lane_bits)
            offset = (where[unit] >> 8) & (lanes - 1)
            new = jnp.where(((lane - offset) & (lanes - 1)) < amount, found[unit], absent)
            held_row = jnp.where(chunk != last_chunk, last_new, last_held)
            held_row = jnp.where(lane >= offset, new, held_row)
            new = jnp.where(lane >= offset, absent, new)
            list_ref[chunk] = held_row
            list_ref[chunk + 1] = new
            last_chunk, last_new, last_held = chunk, new, held_row
        return last_chunk, last_new, last_held

    blocks = lax.div(amount + (FILL - 1), FILL)
    lax.fori_loop(0, blocks, fill, (jnp.int32(0), absent, absent))


def pair_forces(cell_smem, table_ref, list_ref, force_ref, even_ref, odd_ref):
    lanes = table_ref.shape[1]
    cells = table_ref.shape[0] // 8
    rows = even_ref.shape[0]
    chunks = rows // lanes
    units = rows // GROUP
    groups = cell_smem[0, cell_smem.shape[1] - lanes]
    force_ref[...] = jnp.zeros(force_ref.shape, jnp.float32)
    part = lax.broadcasted_iota(jnp.int32, (32, 8 * lanes), 0)
    comp = lax.broadcasted_iota(jnp.int32, (32, 8 * lanes), 1) // lanes
    weights = jnp.where((part < 24) & (part % 8 == comp), 1.0, 0.0).astype(jnp.bfloat16)

    def spread(step, out_ref):
        turned = []
        for piece in range(chunks):
            values = list_ref[step * chunks + piece]
            high = values.astype(jnp.bfloat16).astype(jnp.float32)
            rest = values - high
            middle = rest.astype(jnp.bfloat16).astype(jnp.float32)
            parts = jnp.concatenate([high, middle, rest - middle, jnp.zeros_like(values)], axis=0)
            turned.append(parts.T.astype(jnp.bfloat16))
        turned = jnp.concatenate(turned, axis=0)
        out_ref[...] = jnp.dot(turned, weights, preferred_element_type=jnp.float32)

    def pairs(step, wide_ref, carry):
        last, running = carry
        for unit in range(units):
            cell = cell_smem[0, step * units + unit]
            own = jnp.minimum(cell, cells - 1) * 8
            other = [
                wide_ref[pl.ds(unit * GROUP, GROUP), pl.ds(value * lanes, lanes)].reshape(
                    GROUP // 8, 8, lanes
                )
                for value in range(8)
            ]
            mine = [table_ref[pl.ds(own + value, 8, stride=0), :][None] for value in range(8)]
            apart = [other[axis] - mine[axis] for axis in range(3)]
            square = apart[0] * apart[0] + apart[1] * apart[1] + apart[2] * apart[2] + epsilon_sq
            inverse = lax.rsqrt(square)
            reach = other[6] + mine[6]
            overlap = jnp.maximum(reach - square * inverse, 0.0)
            overlap = jnp.where(other[7] != mine[7], overlap, 0.0)
            closing = (
                (other[3] - mine[3]) * apart[0]
                + (other[4] - mine[4]) * apart[1]
                + (other[5] - mine[5]) * apart[2]
            )
            scaled = overlap * (other[6] * mine[6])
            root = scaled * lax.rsqrt(jnp.maximum(scaled * reach, 1e-30))
            factor = root * inverse * (stiffness / damping * overlap - closing * inverse)
            running = [
                jnp.sum(factor * apart[axis], axis=0)
                + jnp.where(cell == last, running[axis], 0.0)
                for axis in range(3)
            ]
            last = cell
            for axis in range(3):
                force_ref[cell, axis] = running[axis]
        return last, running

    spread(0, even_ref)

    def both(step, carry):
        spread(2 * step + 1, odd_ref)
        carry = pairs(2 * step, even_ref, carry)
        spread(2 * step + 2, even_ref)
        return pairs(2 * step + 1, odd_ref, carry)

    zero = jnp.zeros((8, lanes), jnp.float32)
    steps = lax.div(groups + (2 * units - 1), 2 * units)
    lax.fori_loop(0, steps, both, (jnp.int32(-1), [zero] * 3))


def inner_kernel(
    amount_smem, where_smem, near_smem, cell_smem, table_ref, slots_ref, shift_ref,
    force_ref, list_ref, even_ref, odd_ref,
):
    cells = table_ref.shape[0]
    fill_lists(amount_smem[0], where_smem, near_smem, table_ref, slots_ref, shift_ref, list_ref)
    flat = table_ref.reshape(cells * 8, table_ref.shape[2])
    pair_forces(cell_smem, flat, list_ref, force_ref, even_ref, odd_ref)


def outer_kernel(
    amount_smem, where_smem, near_smem, cell_smem, table_ref, halo_ref, slots_ref, shift_ref,
    inner_ref, arms_ref, frag_ref, fixed_ref, out_ref, list_ref, even_ref, odd_ref, force_ref, loads_ref,
):
    held = fixed_ref.shape[1] // 2
    fill_lists(amount_smem[0], where_smem, near_smem, halo_ref, slots_ref, shift_ref, list_ref)
    pair_forces(cell_smem, table_ref, list_ref, force_ref, even_ref, odd_ref)
    sums = fragment_sums(inner_ref, force_ref, arms_ref, frag_ref, loads_ref, held)
    out = fixed_ref[...] + jnp.concatenate([sums, jnp.zeros_like(sums)], axis=1)
    for brick in range(out_ref.shape[0]):
        out_ref[brick] = out


def fragment_sums(inner_ref, outer_ref, arms_ref, frag_ref, loads_ref, held):
    cells, lanes = frag_ref.shape
    tall = loads_ref.shape[0]
    label = lax.broadcasted_iota(jnp.int32, (held, lanes), 0)

    def gather_sums(block, total):
        rows = pl.ds(pl.multiple_of(block * tall, tall), tall)
        force = [
            -damping * jnp.sum(inner_ref[rows, axis] + outer_ref[rows, axis], axis=1)
            for axis in range(3)
        ]
        lever = [arms_ref[axis, rows, :] for axis in range(3)]
        torque = [
            lever[1] * force[2] - lever[2] * force[1],
            lever[2] * force[0] - lever[0] * force[2],
            lever[0] * force[1] - lever[1] * force[0],
        ]
        loads = force + torque + [jnp.zeros_like(force[0])] * 2
        for comp in range(8):
            loads_ref[:, comp, :] = loads[comp]
        frags = frag_ref[rows, :]
        hits = [
            (frags[unit : unit + 1, :] == label).astype(jnp.float32).astype(jnp.bfloat16)
            for unit in range(tall)
        ]
        values = [split_rows(loads_ref[unit]) for unit in range(tall)]
        return total + dot_lanes(jnp.concatenate(values, axis=1), jnp.concatenate(hits, axis=1))

    total = lax.fori_loop(0, cells // tall, gather_sums, jnp.zeros((24, held), jnp.float32))
    return joined_rows(total)


def move_kernel(
    owned, target_ref, known_ref, state_ref, arms_ref, frag_ref, spheres_ref, clumps_ref
):
    bricks, _, lanes = known_ref.shape
    held = lanes // 2
    cells = frag_ref.shape[0]
    targets = jnp.broadcast_to(target_ref[...], (lanes, lanes))
    lane = lax.broadcasted_iota(jnp.int32, (1, lanes), 1)

    def match(block, carry):
        sums, base = carry
        for unit in range(8):
            brick = block * 8 + unit
            known = known_ref[brick]
            values = split_rows(known)
            key = jnp.where(lane < held, known[6:7], -1.0)
            number = jnp.where(
                (lane >= held) & (lane < held + owned), brick * owned + lane - held, -1
            ).astype(jnp.float32)
            sums = sums + dot_lanes(values, (targets == key).astype(jnp.float32).astype(jnp.bfloat16))
            base = base + dot_lanes(values, (targets == number).astype(jnp.float32).astype(jnp.bfloat16))
        return sums, base

    zero = jnp.zeros((24, lanes), jnp.float32)
    sums, base = lax.fori_loop(0, bricks // 8, match, (zero, zero))
    sums = joined_rows(sums)
    base = joined_rows(base)
    rows = []
    for axis in range(3):
        pull = gravity if axis == 2 else 0.0
        rows.append(
            base[axis : axis + 1]
            + time_step * (sums[axis : axis + 1] * base[6:7] - pull)
        )
    for axis in range(3, 6):
        rows.append(base[axis : axis + 1] + time_step * sums[axis : axis + 1] * base[7:8])
    for comp in range(6):
        clumps_ref[comp : comp + 1, :] = rows[comp]
    tall = 32
    wide = [jnp.broadcast_to(value, (tall, lanes)) for value in rows]

    def cross(first, second):
        return [
            first[1] * second[2] - first[2] * second[1],
            first[2] * second[0] - first[0] * second[2],
            first[0] * second[1] - first[1] * second[0],
        ]

    def move(block, unused):
        at = pl.ds(pl.multiple_of(block * tall, tall), tall)
        index = frag_ref[at, :] + (lanes - held)
        motion = [lanes_of(value, index) for value in wide]
        velocity, spin = motion[0:3], motion[3:6]
        arm = [arms_ref[axis, at, :] for axis in range(3)]
        half = [0.5 * time_step * value for value in spin]
        turned = cross(half, arm)
        twice = cross(half, turned)
        scale = 2.0 / (1.0 + half[0] * half[0] + half[1] * half[1] + half[2] * half[2])
        change = [scale * (turned[axis] + twice[axis]) for axis in range(3)]
        new_arm = [arm[axis] + change[axis] for axis in range(3)]
        swing = cross(spin, new_arm)
        for axis in range(3):
            spheres_ref[axis, at, :] = (
                state_ref[axis, at, :] + time_step * velocity[axis] + (new_arm[axis] - arm[axis])
            )
            spheres_ref[3 + axis, at, :] = velocity[axis] + swing[axis]
        return unused

    lax.fori_loop(0, cells // tall, move, 0)


def local(
    state, arms, sphere_frag, frag_owner, frag_clump, tiles, clump_motion, inv_mass, inv_moment
):
    cells_x, cells_y, cells_z = (state.shape[1], state.shape[2], state.shape[3])
    lanes = state.shape[4]
    cells = cells_x * cells_y * cells_z
    owned = inv_mass.shape[0]
    held = frag_clump.shape[0]
    names = ("gx", "gy", "gz")
    vmem = pl.BlockSpec(memory_space=pltpu.VMEM)
    smem = pl.BlockSpec(memory_space=pltpu.SMEM)
    params = pltpu.CompilerParams(vmem_limit_bytes=VMEM)

    frag_key = (frag_owner[:, 0] * owned + frag_clump).astype(jnp.float32)
    flat_state = state.reshape(7, cells, lanes)
    flat_arms = arms.reshape(3, cells, lanes)
    flat_frag = sphere_frag.reshape(cells, lanes)

    fixed = jnp.concatenate(
        [
            jnp.concatenate([jnp.zeros((6, held)), frag_key[None], jnp.zeros((1, held))], axis=0),
            jnp.concatenate([clump_motion, inv_mass[None], inv_moment[None]], axis=0),
            jnp.zeros((8, lanes - held - owned)),
        ],
        axis=1,
    )

    table = pl.pallas_call(
        pack_kernel,
        out_shape=jax.ShapeDtypeStruct((cells, 8, lanes), jnp.float32),
        in_specs=[vmem] * 3,
        out_specs=vmem,
        compiler_params=params,
    )(flat_state, flat_frag, jnp.pad(frag_key, (0, lanes - held))[None])
    grid = table.reshape(cells_x, cells_y, cells_z, 8, lanes)
    z_before, z_after = exchange(grid[:, :, -1:], grid[:, :, :1], "gz")

    kinds = jnp.arange(27, dtype=jnp.int32)
    moves = jnp.stack([kinds // 9 - 1, kinds // 3 % 3 - 1, kinds % 3 - 1], axis=1)
    shift = jnp.pad(moves.astype(jnp.float32), ((0, 0), (0, 5)))
    shift = jnp.broadcast_to(shift[:, :, None], (27, 8, lanes))

    outside = 1 << 20
    span_z = cells_z + 2
    starts = [0, cells_x * cells_y, 2 * cells_x * cells_y]
    starts += [starts[-1] + cells_y * span_z, starts[-1] + 2 * cells_y * span_z]
    starts += [starts[-1] + (cells_x + 2) * span_z]

    def decode(codes):
        own, offset = (codes // 27, codes % 27)
        steps = (offset // 9 - 1, offset // 3 % 3 - 1, offset % 3 - 1)
        x = own // (cells_y * cells_z) + steps[0]
        y = own // cells_z % cells_y + steps[1]
        z = own % cells_z + steps[2]
        need = sum(
            jnp.where(steps[axis] == 1, 1, jnp.where(steps[axis] == -1, 2, 0)) << (2 * axis)
            for axis in range(3)
        )
        return own, offset, need, x, y, z

    def inside(x, y, z):
        inner = (x >= 0) & (x < cells_x) & (y >= 0) & (y < cells_y)
        return inner & (z >= 0) & (z < cells_z)

    codes = tiles[0]
    total = codes.shape[0]
    codes = jnp.sort(codes + jnp.where(inside(*decode(codes)[3:]), 0, outside))
    inner_amount = jnp.sum((codes < outside).astype(jnp.int32))
    order = jnp.arange(total, dtype=jnp.int32)

    def listed(codes, amount, want_inside):
        own, offset, need, x, y, z = decode(codes & (outside - 1))
        if want_inside:
            near = (x * cells_y + y) * cells_z + z
        else:
            in_y = jnp.where(y < 0, starts[4], starts[5]) + (x + 1) * span_z + z + 1
            in_x = jnp.where(x < 0, starts[2], starts[3]) + y * span_z + z + 1
            in_z = jnp.where(z < 0, starts[0], starts[1]) + x * cells_y + y
            near = jnp.where(
                (y < 0) | (y >= cells_y), in_y, jnp.where((x < 0) | (x >= cells_x), in_x, in_z)
            )
        live = order < amount
        near = jnp.where(live, near, 0)
        return (
            near,
            near * 32 + jnp.where(live, offset, 0),
            jnp.where(live, need, 64),
            jnp.where(live, own, cells),
        )

    chunks = -(-(total + cells * GROUP // lanes) // 16) * 16 + 8
    group_top = chunks * (lanes // GROUP)

    def lists(near, need, own, amount, source):
        span = source.shape[0]
        return pl.pallas_call(
            list_kernel,
            out_shape=(
                jax.ShapeDtypeStruct((total, lanes), jnp.int32),
                jax.ShapeDtypeStruct((1, total), jnp.int32),
                jax.ShapeDtypeStruct((1, -(-group_top // lanes) * lanes + lanes), jnp.int32),
            ),
            in_specs=[smem] + [vmem] * 4,
            out_specs=(vmem, vmem, vmem),
            scratch_shapes=[
                pltpu.VMEM((-(-span // lanes) * lanes, lanes), jnp.float32),
                pltpu.VMEM((lanes, total), jnp.float32),
                pltpu.VMEM((cells, lanes), jnp.float32),
            ],
            compiler_params=params,
        )(amount[None], near[None], need[None], own[None], source.reshape(span * 8, lanes))

    force_shape = (cells + 8, 3, 8, lanes)
    scratch = [
        pltpu.VMEM((chunks, 8, lanes), jnp.float32),
        pltpu.VMEM((SPREAD * lanes, 8 * lanes), jnp.float32),
        pltpu.VMEM((SPREAD * lanes, 8 * lanes), jnp.float32),
    ]

    near, word, need, own = listed(codes, inner_amount, True)
    z_before, z_after, near, need, own = lax.optimization_barrier(
        (z_before, z_after, near, need, own)
    )
    x_before, x_after = exchange(
        jnp.concatenate([z_before[-1:], grid[-1:], z_after[-1:]], axis=2),
        jnp.concatenate([z_before[:1], grid[:1], z_after[:1]], axis=2),
        "gx",
    )
    slots, where, cell_of = lists(near, need, own, inner_amount, table)
    x_before, x_after, slots, where, cell_of = lax.optimization_barrier(
        (x_before, x_after, slots, where, cell_of)
    )

    def face(at):
        middle = jnp.concatenate([z_before[:, at], grid[:, at], z_after[:, at]], axis=2)
        return jnp.concatenate([x_before[:, at], middle, x_after[:, at]], axis=0)

    y_before, y_after = exchange(face(slice(-1, None)), face(slice(0, 1)), "gy")
    inner = pl.pallas_call(
        inner_kernel,
        out_shape=jax.ShapeDtypeStruct(force_shape, jnp.float32),
        in_specs=[smem] * 4 + [vmem] * 3,
        out_specs=vmem,
        scratch_shapes=scratch,
        compiler_params=params,
    )(inner_amount[None], where, word, cell_of, table, slots, shift)

    outer_amount = total - inner_amount
    codes = lax.dynamic_slice(jnp.concatenate([codes, codes]), (inner_amount,), (total,))
    near, word, need, own = listed(codes, outer_amount, False)
    halo = jnp.concatenate(
        [
            part.reshape(-1, 8, lanes)
            for part in (z_before, z_after, x_before, x_after, y_before, y_after)
        ],
        axis=0,
    )
    slots, where, cell_of = lists(near, need, own, outer_amount, halo)
    bricks = lax.axis_size(names)
    known = pl.pallas_call(
        outer_kernel,
        out_shape=jax.ShapeDtypeStruct((bricks, 8, lanes), jnp.float32),
        in_specs=[smem] * 4 + [vmem] * 8,
        out_specs=vmem,
        scratch_shapes=scratch
        + [pltpu.VMEM(force_shape, jnp.float32), pltpu.VMEM((16, 8, lanes), jnp.float32)],
        compiler_params=params,
    )(
        outer_amount[None],
        where,
        word,
        cell_of,
        table.reshape(cells * 8, lanes),
        halo,
        slots,
        shift,
        inner,
        flat_arms,
        flat_frag,
        fixed,
    )
    known = lax.all_to_all(known, names, split_axis=0, concat_axis=0, tiled=True)

    brick = lax.axis_index(names)
    mine = jnp.where(
        jnp.arange(lanes - held) < owned, brick * owned + jnp.arange(lanes - held), -2
    ).astype(jnp.float32)
    target = jnp.concatenate([mine, frag_key])[:, None]
    spheres, clumps = pl.pallas_call(
        functools.partial(move_kernel, owned),
        out_shape=(
            jax.ShapeDtypeStruct((6, cells, lanes), jnp.float32),
            jax.ShapeDtypeStruct((6, lanes), jnp.float32),
        ),
        in_specs=[vmem] * 5,
        out_specs=(vmem, vmem),
        compiler_params=params,
    )(target, known, flat_state, flat_arms, flat_frag)
    return (spheres.reshape((6,) + state.shape[1:]), clumps[:, :owned])


def solution(mesh):
    return jax.shard_map(
        local,
        mesh=mesh,
        in_specs=(
            P(None, "gx", "gy", "gz", None),
            P(None, "gx", "gy", "gz", None),
            P("gx", "gy", "gz", None),
            P(("gx", "gy", "gz"), None),
            P(("gx", "gy", "gz")),
            P(("gx", "gy", "gz"), None),
            P(None, ("gx", "gy", "gz")),
            P(("gx", "gy", "gz")),
            P(("gx", "gy", "gz")),
        ),
        out_specs=(P(None, "gx", "gy", "gz", None), P(None, ("gx", "gy", "gz"))),
        check_vma=False,
    )
```

time: 176 us -> 145 us (0.82)
  waiting for transfers between devices: 19.9 us -> 7.03 us
  Pallas kernels: 116 us -> 105 us
  starting transfers between devices: 21.2 us -> 14.7 us
  between operations: 0.79 us -> 3.09 us
    ppermute x6, waiting for transfers between devices: 18.3 us -> 0.02 us  [exchange(): return (lax.ppermute(last, axis, up), lax.ppermute(initial, axis, down))]
    pallas_call x6 -> x5, Pallas kernels: 113 us -> 102 us  [the longest x1 54.2 us: local(): pl.pallas_call(inner_kernel, out_shape=jax.ShapeDtypeStruct(force_shape,...]
    all_to_all x2 -> x1, starting transfers between devices: 12.8 us -> 5.61 us  [local(): lax.all_to_all(known, names, split_axis=0, concat_axis=0, tiled=True)]
    all_to_all x2 -> x1, waiting for transfers between devices: 1.55 us -> 7.01 us  [local(): lax.all_to_all(known, names, split_axis=0, concat_axis=0, tiled=True)]
  transfers between devices with their start and end apart: 8 -> 7, of which waited for: 5 -> 1; matrix products, arithmetic and copies ran while one was open for 8% -> 8% of each run, Pallas kernels for 61% -> 44%
where the time goes in v5:
time: 145 us
  Pallas kernels  105 us (72%)
  starting transfers between devices  14.7 us (10%)
  other arithmetic  9.66 us (7%)
  waiting for transfers between devices  7.03 us (5%)
  local copies, waits for them, and re-layouts  5.77 us (4%)
  between operations  3.09 us (2%)
    pallas_call x1, Pallas kernels, local(): pl.pallas_call(inner_kernel, out_shape=jax.ShapeDtypeStruct(force_shape,...  54.2 us
    pallas_call x1, Pallas kernels, local(): pl.pallas_call(outer_kernel, out_shape=jax.ShapeDtypeStruct((bricks, 8, l...  25.9 us
    pallas_call x2, Pallas kernels, lists(): pl.pallas_call(list_kernel, out_shape=(jax.ShapeDtypeStruct((total, lanes...  16.6 us
    ppermute x6, starting transfers between devices, exchange(): return (lax.ppermute(last, axis, up), lax.ppermute(initial, axis, down))  9.1 us
    all_to_all x1, waiting for transfers between devices, local(): lax.all_to_all(known, names, split_axis=0, concat_axis=0, tiled=True)  7.01 us
    all_to_all x1, starting transfers between devices, local(): lax.all_to_all(known, names, split_axis=0, concat_axis=0, tiled=True)  5.61 us
    sort x1, other arithmetic, local(): codes = jnp.sort(codes + jnp.where(inside(*decode(codes)[3:]), 0, outside))  5.04 us
    pallas_call x1, Pallas kernels, local(): pl.pallas_call(functools.partial(move_kernel, owned), out_shape=(jax.Shap...  5.03 us
  transfers between devices with their start and end apart: 7, of which 1 were waited for; matrix products, arithmetic and copies ran while one was open for 8% of the time, Pallas kernels for 44%

profile of v5, /device:TPU:0, one launch (start us, length us, event | category | flops | bytes accessed | tf_op | source)
XLA Modules:
  0.0 144.9 jit_solution(13708704654672733208)
XLA Ops:
  0.6 0.7 fusion.51
  1.8 2.9 %shard_map.104.table_ref = f32[256,8,128]{2,1,0:T(8,128)} custom-call(f32[7,256,128]{2,1,0:T(8,128)} %bitcast.49, s32[256,128]{1,0:T(8,128)} %bitcast.53, f32[1,128]{1,0:T(1,128)} %get-tuple-element.73.key_ref), custom_call_target="tpu_custom_call" | custom-call | tf_op jit(solution)/shard_map/pallas_call | solution.py:443
  4.8 1.0 fusion.56
  5.8 3.0 %collective-permute-start = (f32[4,4,1,8,128]{4,3,2,0,1:T(8,128)S(1)}, f32[4,4,1,8,128]{4,3,2,0,1:T(8,128)S(1)}, u32[]{:S(2)}, u32[]{:S(2)}) collective-permute-start(f32[4,4,1,8,128]{4,3,2,0,1:T(8,128)S(1)} %copy.30), channel_id=1, source_target_pairs={{0,1},{1,0},{2,3},{3,2},{4,5},{5,4},{6,7},{7,6},{8,9},{9,8},{10,11... | collective-permute-start | bytes 196616 | tf_op jit(solution)/shard_map/ppermute | solution.py:50
  8.9 1.1 fusion.55
  10.1 5.0 %sort.15 = (s32[2048]{0:T(1024)S(1)}, s32[2048]{0:T(1024)}) sort(s32[2048]{0:T(1024)S(1)} %select_add_fusion.2, s32[2048]{0:T(1024)S(1)} %iota.28), dimensions={0}, to_apply=%region_0.1 | sort | flops 22528 | bytes 32768 | tf_op jit(solution)/shard_map/jit(sort)/sort | solution.py:482
  15.2 0.6 convert_reduce_fusion
  17.9 1.3 select_add_fusion
  19.2 0.6 fusion.35
  20.0 0.7 maximum_maximum_fusion.fixed_ref
  21.0 1.8 %collective-permute-start.3 = (f32[1,4,18,8,128]{4,3,2,0,1:T(8,128)S(1)}, f32[1,4,18,8,128]{4,3,2,0,1:T(8,128)S(1)}, u32[]{:S(2)}, u32[]{:S(2)}) collective-permute-start(f32[1,4,18,8,128]{4,3,2,0,1:T(8,128)S(1)} %pad_maximum_fusion.3), channel_id=1, source_target_pairs={{8,0},{16,8},{24,16},{0,24},{9,1},{17,9},{25,17},{1,25},{10,2},{18... | collective-permute-start | bytes 884744 | tf_op jit(solution)/shard_map/ppermute | solution.py:50
  22.8 9.5 %shard_map.105 = (s32[2048,128]{1,0:T(8,128)}, s32[1,2048]{1,0:T(1,128)}, s32[1,8704]{1,0:T(1,128)}) custom-call(s32[1]{0:T(128)} %bitcast.17.amount_smem, s32[1,2048]{1,0:T(1,128)} %bitcast.67, s32[1,2048]{1,0:T(1,128)} %bitcast.68, s32[1,2048]{1,0:T(1,128)} %bitcast.69, f32[2048,128]{1,0:T(8,128)} %bitcast.45), custom_call_target="tpu_custom_call" | custom-call | tf_op jit(solution)/shard_map/pallas_call | solution.py:511
  32.4 2.1 %collective-permute-start.4 = (f32[6,1,18,8,128]{4,3,2,0,1:T(8,128)S(1)}, f32[6,1,18,8,128]{4,3,2,0,1:T(8,128)S(1)}, u32[]{:S(2)}, u32[]{:S(2)}) collective-permute-start(f32[6,1,18,8,128]{4,3,2,0,1:T(8,128)S(1)} %pad_maximum_fusion), channel_id=1, source_target_pairs={{0,2},{2,4},{4,6},{6,0},{1,3},{3,5},{5,7},{7,1},{8,10},{10,12},{12... | collective-permute-start | bytes 1327112 | tf_op jit(solution)/shard_map/ppermute | solution.py:50
  34.5 2.1 %collective-permute-start.5 = (f32[6,1,18,8,128]{4,3,2,0,1:T(8,128)S(1)}, f32[6,1,18,8,128]{4,3,2,0,1:T(8,128)S(1)}, u32[]{:S(2)}, u32[]{:S(2)}) collective-permute-start(f32[6,1,18,8,128]{4,3,2,0,1:T(8,128)S(1)} %pad_maximum_fusion.1), channel_id=1, source_target_pairs={{2,0},{4,2},{6,4},{0,6},{3,1},{5,3},{7,5},{1,7},{10,8},{12,10},{14... | collective-permute-start | bytes 1327112 | tf_op jit(solution)/shard_map/ppermute | solution.py:50
  36.6 0.7 broadcast_in_dim.131.shift_ref
  37.3 54.2 %shard_map.107.inner_ref = f32[264,3,8,128]{3,2,1,0:T(8,128)} custom-call(s32[1]{0:T(128)} %bitcast.17.amount_smem, s32[1,2048]{1,0:T(1,128)} %get-tuple-element.36.where_smem, s32[2048]{0:T(1024)} %get-tuple-element.41.near_smem, s32[1,8704]{1,0:T(1,128)} %get-tuple-element.37.cell_smem, f32[256,8,128]{2,1,0:T(8,128)} %shard_map.104.table_ref, ...), custom_call_target="tpu_custom_call" | custom-call | tf_op jit(solution)/shard_map/pallas_call | solution.py:554
  91.6 1.2 copy-done.1
  92.8 7.1 %shard_map.106 = (s32[2048,128]{1,0:T(8,128)}, s32[1,2048]{1,0:T(1,128)}, s32[1,8704]{1,0:T(1,128)}) custom-call(s32[1]{0:T(128)} %bitcast.3.amount_smem, s32[1,2048]{1,0:T(1,128)} %bitcast.66, s32[1,2048]{1,0:T(1,128)} %bitcast.65, s32[1,2048]{1,0:T(1,128)} %bitcast.64, f32[3136,128]{1,0:T(8,128)} %bitcast.48), custom_call_target="tpu_custom_call" | custom-call | tf_op jit(solution)/shard_map/pallas_call | solution.py:511
  99.9 25.9 %shard_map.108 = f32[32,8,128]{2,1,0:T(8,128)} custom-call(s32[1]{0:T(128)} %bitcast.3.amount_smem, s32[1,2048]{1,0:T(1,128)} %get-tuple-element.33.where_smem, s32[2048]{0:T(1024)} %get-tuple-element.68.near_smem, s32[1,8704]{1,0:T(1,128)} %get-tuple-element.34.cell_smem, f32[2048,128]{1,0:T(8,128)} %bitcast.46, f32[392,8,128]{2,1,0:T(8,128)} %copy-done.1, ...), custom_call_target="tpu_custom_call" | custom-call | tf_op jit(solution)/shard_map/pallas_call | solution.py:575
  125.8 5.6 %all-to-all-start = ((f32[32,8,128]{2,1,0:T(8,128)}), f32[32,8,128]{2,1,0:T(8,128)S(1)}, u32[]{:S(2)}, u32[]{:S(2)}) async-start(f32[32,8,128]{2,1,0:T(8,128)} %shard_map.108), calls=%async_computation | async-start | bytes 262144 | tf_op jit(solution)/shard_map/all_to_all | solution.py:597
  131.5 0.7 copy.29.target_ref
  132.2 7.0 %all-to-all-done.known_ref = f32[32,8,128]{2,1,0:T(8,128)S(1)} async-done(((f32[32,8,128]{2,1,0:T(8,128)}), f32[32,8,128]{2,1,0:T(8,128)S(1)}, u32[]{:S(2)}, u32[]{:S(2)}) %all-to-all-start) | async-done | bytes 131104 | tf_op jit(solution)/shard_map/all_to_all | solution.py:597
  139.2 0.6 copy-done.2
  139.8 5.0 %shard_map.109 = (f32[6,256,128]{2,1,0:T(8,128)}, f32[6,128]{1,0:T(8,128)}) custom-call(f32[128,1]{1,0:T(8,128)} %copy.29.target_ref, f32[32,8,128]{2,1,0:T(8,128)} %copy-done.2, f32[7,256,128]{2,1,0:T(8,128)} %bitcast.50, f32[3,256,128]{2,1,0:T(8,128)} %bitcast.52, s32[256,128]{1,0:T(8,128)} %bitcast.55), custom_call_target="tpu_custom_call" | custom-call | tf_op jit(solution)/shard_map/pallas_call | solution.py:604
  (53 shorter events, 1.3 us)
Async XLA Ops:
  4.7 5.2 %copy-start = (f32[256,8,128]{2,1,0:T(8,128)S(1)}, f32[256,8,128]{2,1,0:T(8,128)}, u32[]{:S(2)}) copy-start(f32[256,8,128]{2,1,0:T(8,128)} %shard_map.104.table_ref) | copy-start | bytes 3145732
  4.7 5.3 %copy-start.3 = (s32[1,2048]{1,0:T(1,128)S(1)}, s32[1,2048]{1,0:T(1,128)}, u32[]{:S(2)}) copy-start(s32[1,2048]{1,0:T(1,128)} %param.14) | copy-start | bytes 24580
  4.7 15.2 %copy-start.4 = (f32[6,48]{1,0:T(8,128)S(1)}, f32[6,48]{1,0:T(8,128)}, u32[]{:S(2)}) copy-start(f32[6,48]{1,0:T(8,128)} %param.15) | copy-start | bytes 3460
  4.7 15.2 %copy-start.5 = (f32[48]{0:T(128)S(1)}, f32[48]{0:T(128)}, u32[]{:S(2)}) copy-start(f32[48]{0:T(128)} %param.17) | copy-start | bytes 580
  4.8 15.2 %copy-start.6 = (f32[48]{0:T(128)S(1)}, f32[48]{0:T(128)}, u32[]{:S(2)}) copy-start(f32[48]{0:T(128)} %param.16) | copy-start | bytes 580
  5.8 15.0 %collective-permute-start = (f32[4,4,1,8,128]{4,3,2,0,1:T(8,128)S(1)}, f32[4,4,1,8,128]{4,3,2,0,1:T(8,128)S(1)}, u32[]{:S(2)}, u32[]{:S(2)}) collective-permute-start(f32[4,4,1,8,128]{4,3,2,0,1:T(8,128)S(1)} %copy.30), channel_id=1, source_target_pairs={{0,1},{1,0},{2,3},{3,2},{4,5},{5,4},{6,7},{7,6},{8,9},{9,8},{10,11... | collective-permute-start | bytes 196616 | tf_op jit(solution)/shard_map/ppermute | solution.py:50
  8.8 12.0 %collective-permute-start.1 = (f32[4,4,1,8,128]{4,3,2,0,1:T(8,128)S(1)}, f32[4,4,1,8,128]{4,3,2,0,1:T(8,128)S(1)}, u32[]{:S(2)}, u32[]{:S(2)}) collective-permute-start(f32[4,4,1,8,128]{4,3,2,0,1:T(8,128)S(1)} %copy.31), channel_id=1, source_target_pairs={{1,0},{0,1},{3,2},{2,3},{5,4},{4,5},{7,6},{6,7},{9,8},{8,9},{11,10... | collective-permute-start | bytes 196616 | tf_op jit(solution)/shard_map/ppermute | solution.py:50
  20.9 11.4 %collective-permute-start.2 = (f32[1,4,18,8,128]{4,3,2,0,1:T(8,128)S(1)}, f32[1,4,18,8,128]{4,3,2,0,1:T(8,128)S(1)}, u32[]{:S(2)}, u32[]{:S(2)}) collective-permute-start(f32[1,4,18,8,128]{4,3,2,0,1:T(8,128)S(1)} %pad_maximum_fusion.2), channel_id=1, source_target_pairs={{0,8},{8,16},{16,24},{24,0},{1,9},{9,17},{17,25},{25,1},{2,10},{10... | collective-permute-start | bytes 884744 | tf_op jit(solution)/shard_map/ppermute | solution.py:50
  21.0 11.3 %collective-permute-start.3 = (f32[1,4,18,8,128]{4,3,2,0,1:T(8,128)S(1)}, f32[1,4,18,8,128]{4,3,2,0,1:T(8,128)S(1)}, u32[]{:S(2)}, u32[]{:S(2)}) collective-permute-start(f32[1,4,18,8,128]{4,3,2,0,1:T(8,128)S(1)} %pad_maximum_fusion.3), channel_id=1, source_target_pairs={{8,0},{16,8},{24,16},{0,24},{9,1},{17,9},{25,17},{1,25},{10,2},{18... | collective-permute-start | bytes 884744 | tf_op jit(solution)/shard_map/ppermute | solution.py:50
  32.4 59.2 %collective-permute-start.4 = (f32[6,1,18,8,128]{4,3,2,0,1:T(8,128)S(1)}, f32[6,1,18,8,128]{4,3,2,0,1:T(8,128)S(1)}, u32[]{:S(2)}, u32[]{:S(2)}) collective-permute-start(f32[6,1,18,8,128]{4,3,2,0,1:T(8,128)S(1)} %pad_maximum_fusion), channel_id=1, source_target_pairs={{0,2},{2,4},{4,6},{6,0},{1,3},{3,5},{5,7},{7,1},{8,10},{10,12},{12... | collective-permute-start | bytes 1327112 | tf_op jit(solution)/shard_map/ppermute | solution.py:50
  34.5 57.1 %collective-permute-start.5 = (f32[6,1,18,8,128]{4,3,2,0,1:T(8,128)S(1)}, f32[6,1,18,8,128]{4,3,2,0,1:T(8,128)S(1)}, u32[]{:S(2)}, u32[]{:S(2)}) collective-permute-start(f32[6,1,18,8,128]{4,3,2,0,1:T(8,128)S(1)} %pad_maximum_fusion.1), channel_id=1, source_target_pairs={{2,0},{4,2},{6,4},{0,6},{3,1},{5,3},{7,5},{1,7},{10,8},{12,10},{14... | collective-permute-start | bytes 1327112 | tf_op jit(solution)/shard_map/ppermute | solution.py:50
  91.6 1.2 copy-start.1
  125.8 13.4 %all-to-all-start = ((f32[32,8,128]{2,1,0:T(8,128)}), f32[32,8,128]{2,1,0:T(8,128)S(1)}, u32[]{:S(2)}, u32[]{:S(2)}) async-start(f32[32,8,128]{2,1,0:T(8,128)} %shard_map.108), calls=%async_computation | async-start | bytes 262144 | tf_op jit(solution)/shard_map/all_to_all | solution.py:597
  139.2 0.6 copy-start.2

commit v6 on v5

--- a/solution.py
+++ b/solution.py
@@ -15,8 +15,8 @@
 radius_top = 0.14
 
 GROUP = 32
-FILL = 16
-SPREAD = 2
+FILL = 32
+SPREAD = 4
 VMEM = 56 * 1024 * 1024
 
 
@@ -234,7 +234,7 @@
             rest = values - high
             middle = rest.astype(jnp.bfloat16).astype(jnp.float32)
             parts = jnp.concatenate([high, middle, rest - middle, jnp.zeros_like(values)], axis=0)
-            turned.append(parts.T.astype(jnp.bfloat16))
+            turned.append(parts.astype(jnp.bfloat16).T)
         turned = jnp.concatenate(turned, axis=0)
         out_ref[...] = jnp.dot(turned, weights, preferred_element_type=jnp.float32)
 
@@ -503,7 +503,7 @@
             jnp.where(live, own, cells),
         )
 
-    chunks = -(-(total + cells * GROUP // lanes) // 16) * 16 + 8
+    chunks = total + cells * GROUP // lanes + 3 * SPREAD
     group_top = chunks * (lanes // GROUP)
 
     def lists(near, need, own, amount, source):

time: 145 us -> 136 us (0.938)
  Pallas kernels: 105 us -> 95.4 us
    pallas_call x1, Pallas kernels: 54.2 us -> 47.1 us  [local(): pl.pallas_call(inner_kernel, out_shape=jax.ShapeDtypeStruct(force_shape,...]
    pallas_call x1, Pallas kernels: 25.9 us -> 23.8 us  [local(): pl.pallas_call(outer_kernel, out_shape=jax.ShapeDtypeStruct((bricks, 8, l...]
  transfers between devices with their start and end apart: 7 -> 7, of which waited for: 1 -> 1; matrix products, arithmetic and copies ran while one was open for 8% -> 8% of each run, Pallas kernels for 44% -> 42%
where the time goes in v6:
time: 136 us
  Pallas kernels  95.4 us (70%)
  starting transfers between devices  14.7 us (11%)
  other arithmetic  9.66 us (7%)
  waiting for transfers between devices  7.03 us (5%)
  local copies, waits for them, and re-layouts  5.77 us (4%)
  between operations  3.09 us (2%)
    pallas_call x1, Pallas kernels, local(): pl.pallas_call(inner_kernel, out_shape=jax.ShapeDtypeStruct(force_shape,...  47.1 us
    pallas_call x1, Pallas kernels, local(): pl.pallas_call(outer_kernel, out_shape=jax.ShapeDtypeStruct((bricks, 8, l...  23.8 us
    pallas_call x2, Pallas kernels, lists(): pl.pallas_call(list_kernel, out_shape=(jax.ShapeDtypeStruct((total, lanes...  16.6 us
    ppermute x6, starting transfers between devices, exchange(): return (lax.ppermute(last, axis, up), lax.ppermute(initial, axis, down))  9.1 us
    all_to_all x1, waiting for transfers between devices, local(): lax.all_to_all(known, names, split_axis=0, concat_axis=0, tiled=True)  7.01 us
    all_to_all x1, starting transfers between devices, local(): lax.all_to_all(known, names, split_axis=0, concat_axis=0, tiled=True)  5.55 us
    sort x1, other arithmetic, local(): codes = jnp.sort(codes + jnp.where(inside(*decode(codes)[3:]), 0, outside))  5.04 us
    pallas_call x1, Pallas kernels, local(): pl.pallas_call(functools.partial(move_kernel, owned), out_shape=(jax.Shap...  5.03 us
  transfers between devices with their start and end apart: 7, of which 1 were waited for; matrix products, arithmetic and copies ran while one was open for 8% of the time, Pallas kernels for 42%

profile of v6, /device:TPU:0, one launch (start us, length us, event | category | flops | bytes accessed | tf_op | source)
XLA Modules:
  0.0 135.6 jit_solution(2750001319545912497)
XLA Ops:
  0.6 0.7 fusion.51
  1.8 2.9 %shard_map.104.table_ref = f32[256,8,128]{2,1,0:T(8,128)} custom-call(f32[7,256,128]{2,1,0:T(8,128)} %bitcast.49, s32[256,128]{1,0:T(8,128)} %bitcast.53, f32[1,128]{1,0:T(1,128)} %get-tuple-element.73.key_ref), custom_call_target="tpu_custom_call" | custom-call | tf_op jit(solution)/shard_map/pallas_call | solution.py:443
  4.8 1.0 fusion.56
  5.8 3.0 %collective-permute-start = (f32[4,4,1,8,128]{4,3,2,0,1:T(8,128)S(1)}, f32[4,4,1,8,128]{4,3,2,0,1:T(8,128)S(1)}, u32[]{:S(2)}, u32[]{:S(2)}) collective-permute-start(f32[4,4,1,8,128]{4,3,2,0,1:T(8,128)S(1)} %copy.30), channel_id=1, source_target_pairs={{0,1},{1,0},{2,3},{3,2},{4,5},{5,4},{6,7},{7,6},{8,9},{9,8},{10,11... | collective-permute-start | bytes 196616 | tf_op jit(solution)/shard_map/ppermute | solution.py:50
  8.9 1.1 fusion.55
  10.1 5.0 %sort.15 = (s32[2048]{0:T(1024)S(1)}, s32[2048]{0:T(1024)}) sort(s32[2048]{0:T(1024)S(1)} %select_add_fusion.2, s32[2048]{0:T(1024)S(1)} %iota.28), dimensions={0}, to_apply=%region_0.1 | sort | flops 22528 | bytes 32768 | tf_op jit(solution)/shard_map/jit(sort)/sort | solution.py:482
  15.2 0.6 convert_reduce_fusion
  17.9 1.3 select_add_fusion
  19.2 0.6 fusion.35
  20.0 0.7 maximum_maximum_fusion.fixed_ref
  21.0 1.8 %collective-permute-start.3 = (f32[1,4,18,8,128]{4,3,2,0,1:T(8,128)S(1)}, f32[1,4,18,8,128]{4,3,2,0,1:T(8,128)S(1)}, u32[]{:S(2)}, u32[]{:S(2)}) collective-permute-start(f32[1,4,18,8,128]{4,3,2,0,1:T(8,128)S(1)} %pad_maximum_fusion.3), channel_id=1, source_target_pairs={{8,0},{16,8},{24,16},{0,24},{9,1},{17,9},{25,17},{1,25},{10,2},{18... | collective-permute-start | bytes 884744 | tf_op jit(solution)/shard_map/ppermute | solution.py:50
  22.8 9.5 %shard_map.105 = (s32[2048,128]{1,0:T(8,128)}, s32[1,2048]{1,0:T(1,128)}, s32[1,8704]{1,0:T(1,128)}) custom-call(s32[1]{0:T(128)} %bitcast.17.amount_smem, s32[1,2048]{1,0:T(1,128)} %bitcast.67, s32[1,2048]{1,0:T(1,128)} %bitcast.68, s32[1,2048]{1,0:T(1,128)} %bitcast.69, f32[2048,128]{1,0:T(8,128)} %bitcast.45), custom_call_target="tpu_custom_call" | custom-call | tf_op jit(solution)/shard_map/pallas_call | solution.py:511
  32.4 2.1 %collective-permute-start.4 = (f32[6,1,18,8,128]{4,3,2,0,1:T(8,128)S(1)}, f32[6,1,18,8,128]{4,3,2,0,1:T(8,128)S(1)}, u32[]{:S(2)}, u32[]{:S(2)}) collective-permute-start(f32[6,1,18,8,128]{4,3,2,0,1:T(8,128)S(1)} %pad_maximum_fusion), channel_id=1, source_target_pairs={{0,2},{2,4},{4,6},{6,0},{1,3},{3,5},{5,7},{7,1},{8,10},{10,12},{12... | collective-permute-start | bytes 1327112 | tf_op jit(solution)/shard_map/ppermute | solution.py:50
  34.5 2.1 %collective-permute-start.5 = (f32[6,1,18,8,128]{4,3,2,0,1:T(8,128)S(1)}, f32[6,1,18,8,128]{4,3,2,0,1:T(8,128)S(1)}, u32[]{:S(2)}, u32[]{:S(2)}) collective-permute-start(f32[6,1,18,8,128]{4,3,2,0,1:T(8,128)S(1)} %pad_maximum_fusion.1), channel_id=1, source_target_pairs={{2,0},{4,2},{6,4},{0,6},{3,1},{5,3},{7,5},{1,7},{10,8},{12,10},{14... | collective-permute-start | bytes 1327112 | tf_op jit(solution)/shard_map/ppermute | solution.py:50
  36.6 0.7 broadcast_in_dim.131.shift_ref
  37.3 47.1 %shard_map.107.inner_ref = f32[264,3,8,128]{3,2,1,0:T(8,128)} custom-call(s32[1]{0:T(128)} %bitcast.17.amount_smem, s32[1,2048]{1,0:T(1,128)} %get-tuple-element.36.where_smem, s32[2048]{0:T(1024)} %get-tuple-element.41.near_smem, s32[1,8704]{1,0:T(1,128)} %get-tuple-element.37.cell_smem, f32[256,8,128]{2,1,0:T(8,128)} %shard_map.104.table_ref, ...), custom_call_target="tpu_custom_call" | custom-call | tf_op jit(solution)/shard_map/pallas_call | solution.py:554
  84.5 1.2 copy-done.1
  85.7 7.1 %shard_map.106 = (s32[2048,128]{1,0:T(8,128)}, s32[1,2048]{1,0:T(1,128)}, s32[1,8704]{1,0:T(1,128)}) custom-call(s32[1]{0:T(128)} %bitcast.3.amount_smem, s32[1,2048]{1,0:T(1,128)} %bitcast.66, s32[1,2048]{1,0:T(1,128)} %bitcast.65, s32[1,2048]{1,0:T(1,128)} %bitcast.64, f32[3136,128]{1,0:T(8,128)} %bitcast.48), custom_call_target="tpu_custom_call" | custom-call | tf_op jit(solution)/shard_map/pallas_call | solution.py:511
  92.8 23.8 %shard_map.108 = f32[32,8,128]{2,1,0:T(8,128)} custom-call(s32[1]{0:T(128)} %bitcast.3.amount_smem, s32[1,2048]{1,0:T(1,128)} %get-tuple-element.33.where_smem, s32[2048]{0:T(1024)} %get-tuple-element.68.near_smem, s32[1,8704]{1,0:T(1,128)} %get-tuple-element.34.cell_smem, f32[2048,128]{1,0:T(8,128)} %bitcast.46, f32[392,8,128]{2,1,0:T(8,128)} %copy-done.1, ...), custom_call_target="tpu_custom_call" | custom-call | tf_op jit(solution)/shard_map/pallas_call | solution.py:575
  116.6 5.6 %all-to-all-start = ((f32[32,8,128]{2,1,0:T(8,128)}), f32[32,8,128]{2,1,0:T(8,128)S(1)}, u32[]{:S(2)}, u32[]{:S(2)}) async-start(f32[32,8,128]{2,1,0:T(8,128)} %shard_map.108), calls=%async_computation | async-start | bytes 262144 | tf_op jit(solution)/shard_map/all_to_all | solution.py:597
  122.2 0.7 copy.29.target_ref
  122.9 7.0 %all-to-all-done.known_ref = f32[32,8,128]{2,1,0:T(8,128)S(1)} async-done(((f32[32,8,128]{2,1,0:T(8,128)}), f32[32,8,128]{2,1,0:T(8,128)S(1)}, u32[]{:S(2)}, u32[]{:S(2)}) %all-to-all-start) | async-done | bytes 131104 | tf_op jit(solution)/shard_map/all_to_all | solution.py:597
  129.9 0.6 copy-done.2
  130.6 5.0 %shard_map.109 = (f32[6,256,128]{2,1,0:T(8,128)}, f32[6,128]{1,0:T(8,128)}) custom-call(f32[128,1]{1,0:T(8,128)} %copy.29.target_ref, f32[32,8,128]{2,1,0:T(8,128)} %copy-done.2, f32[7,256,128]{2,1,0:T(8,128)} %bitcast.50, f32[3,256,128]{2,1,0:T(8,128)} %bitcast.52, s32[256,128]{1,0:T(8,128)} %bitcast.55), custom_call_target="tpu_custom_call" | custom-call | tf_op jit(solution)/shard_map/pallas_call | solution.py:604
  (53 shorter events, 1.3 us)
Async XLA Ops:
  4.7 5.2 %copy-start = (f32[256,8,128]{2,1,0:T(8,128)S(1)}, f32[256,8,128]{2,1,0:T(8,128)}, u32[]{:S(2)}) copy-start(f32[256,8,128]{2,1,0:T(8,128)} %shard_map.104.table_ref) | copy-start | bytes 3145732
  4.7 5.3 %copy-start.3 = (s32[1,2048]{1,0:T(1,128)S(1)}, s32[1,2048]{1,0:T(1,128)}, u32[]{:S(2)}) copy-start(s32[1,2048]{1,0:T(1,128)} %param.14) | copy-start | bytes 24580
  4.7 15.2 %copy-start.4 = (f32[6,48]{1,0:T(8,128)S(1)}, f32[6,48]{1,0:T(8,128)}, u32[]{:S(2)}) copy-start(f32[6,48]{1,0:T(8,128)} %param.15) | copy-start | bytes 3460
  4.7 15.2 %copy-start.5 = (f32[48]{0:T(128)S(1)}, f32[48]{0:T(128)}, u32[]{:S(2)}) copy-start(f32[48]{0:T(128)} %param.17) | copy-start | bytes 580
  4.8 15.2 %copy-start.6 = (f32[48]{0:T(128)S(1)}, f32[48]{0:T(128)}, u32[]{:S(2)}) copy-start(f32[48]{0:T(128)} %param.16) | copy-start | bytes 580
  5.8 15.0 %collective-permute-start = (f32[4,4,1,8,128]{4,3,2,0,1:T(8,128)S(1)}, f32[4,4,1,8,128]{4,3,2,0,1:T(8,128)S(1)}, u32[]{:S(2)}, u32[]{:S(2)}) collective-permute-start(f32[4,4,1,8,128]{4,3,2,0,1:T(8,128)S(1)} %copy.30), channel_id=1, source_target_pairs={{0,1},{1,0},{2,3},{3,2},{4,5},{5,4},{6,7},{7,6},{8,9},{9,8},{10,11... | collective-permute-start | bytes 196616 | tf_op jit(solution)/shard_map/ppermute | solution.py:50
  8.8 12.0 %collective-permute-start.1 = (f32[4,4,1,8,128]{4,3,2,0,1:T(8,128)S(1)}, f32[4,4,1,8,128]{4,3,2,0,1:T(8,128)S(1)}, u32[]{:S(2)}, u32[]{:S(2)}) collective-permute-start(f32[4,4,1,8,128]{4,3,2,0,1:T(8,128)S(1)} %copy.31), channel_id=1, source_target_pairs={{1,0},{0,1},{3,2},{2,3},{5,4},{4,5},{7,6},{6,7},{9,8},{8,9},{11,10... | collective-permute-start | bytes 196616 | tf_op jit(solution)/shard_map/ppermute | solution.py:50
  20.9 11.4 %collective-permute-start.2 = (f32[1,4,18,8,128]{4,3,2,0,1:T(8,128)S(1)}, f32[1,4,18,8,128]{4,3,2,0,1:T(8,128)S(1)}, u32[]{:S(2)}, u32[]{:S(2)}) collective-permute-start(f32[1,4,18,8,128]{4,3,2,0,1:T(8,128)S(1)} %pad_maximum_fusion.2), channel_id=1, source_target_pairs={{0,8},{8,16},{16,24},{24,0},{1,9},{9,17},{17,25},{25,1},{2,10},{10... | collective-permute-start | bytes 884744 | tf_op jit(solution)/shard_map/ppermute | solution.py:50
  21.0 11.3 %collective-permute-start.3 = (f32[1,4,18,8,128]{4,3,2,0,1:T(8,128)S(1)}, f32[1,4,18,8,128]{4,3,2,0,1:T(8,128)S(1)}, u32[]{:S(2)}, u32[]{:S(2)}) collective-permute-start(f32[1,4,18,8,128]{4,3,2,0,1:T(8,128)S(1)} %pad_maximum_fusion.3), channel_id=1, source_target_pairs={{8,0},{16,8},{24,16},{0,24},{9,1},{17,9},{25,17},{1,25},{10,2},{18... | collective-permute-start | bytes 884744 | tf_op jit(solution)/shard_map/ppermute | solution.py:50
  32.4 52.1 %collective-permute-start.4 = (f32[6,1,18,8,128]{4,3,2,0,1:T(8,128)S(1)}, f32[6,1,18,8,128]{4,3,2,0,1:T(8,128)S(1)}, u32[]{:S(2)}, u32[]{:S(2)}) collective-permute-start(f32[6,1,18,8,128]{4,3,2,0,1:T(8,128)S(1)} %pad_maximum_fusion), channel_id=1, source_target_pairs={{0,2},{2,4},{4,6},{6,0},{1,3},{3,5},{5,7},{7,1},{8,10},{10,12},{12... | collective-permute-start | bytes 1327112 | tf_op jit(solution)/shard_map/ppermute | solution.py:50
  34.5 50.0 %collective-permute-start.5 = (f32[6,1,18,8,128]{4,3,2,0,1:T(8,128)S(1)}, f32[6,1,18,8,128]{4,3,2,0,1:T(8,128)S(1)}, u32[]{:S(2)}, u32[]{:S(2)}) collective-permute-start(f32[6,1,18,8,128]{4,3,2,0,1:T(8,128)S(1)} %pad_maximum_fusion.1), channel_id=1, source_target_pairs={{2,0},{4,2},{6,4},{0,6},{3,1},{5,3},{7,5},{1,7},{10,8},{12,10},{14... | collective-permute-start | bytes 1327112 | tf_op jit(solution)/shard_map/ppermute | solution.py:50
  84.5 1.2 copy-start.1
  116.6 13.3 %all-to-all-start = ((f32[32,8,128]{2,1,0:T(8,128)}), f32[32,8,128]{2,1,0:T(8,128)S(1)}, u32[]{:S(2)}, u32[]{:S(2)}) async-start(f32[32,8,128]{2,1,0:T(8,128)} %shard_map.108), calls=%async_computation | async-start | bytes 262144 | tf_op jit(solution)/shard_map/all_to_all | solution.py:597
  129.9 0.6 copy-start.2

commit v7 on v6

--- a/solution.py
+++ b/solution.py
@@ -16,6 +16,7 @@
 
 GROUP = 32
 FILL = 32
+SPREAD_VALUES = 6
 SPREAD = 4
 VMEM = 56 * 1024 * 1024
 
@@ -186,6 +187,9 @@
     lane = lax.broadcasted_iota(jnp.int32, (8, lanes), 1)
     row = lax.broadcasted_iota(jnp.int32, (8, lanes), 0)
     absent = jnp.where(row == 6, -10.0, 0.0)
+    for kind in range(27):
+        steps = (kind // 9 - 1.0, kind // 3 % 3 - 1.0, kind % 3 - 1.0)
+        shift_ref[kind] = sum(jnp.where(row == axis, steps[axis], 0.0) for axis in range(3))
 
     def fill(block, carry):
         last_chunk, last_new, last_held = carry
@@ -214,7 +218,7 @@
     lax.fori_loop(0, blocks, fill, (jnp.int32(0), absent, absent))
 
 
-def pair_forces(cell_smem, table_ref, list_ref, force_ref, even_ref, odd_ref):
+def pair_forces(cell_smem, table_ref, list_ref, force_ref, even_ref, odd_ref, turned_ref):
     lanes = table_ref.shape[1]
     cells = table_ref.shape[0] // 8
     rows = even_ref.shape[0]
@@ -222,8 +226,9 @@
     units = rows // GROUP
     groups = cell_smem[0, cell_smem.shape[1] - lanes]
     force_ref[...] = jnp.zeros(force_ref.shape, jnp.float32)
-    part = lax.broadcasted_iota(jnp.int32, (32, 8 * lanes), 0)
-    comp = lax.broadcasted_iota(jnp.int32, (32, 8 * lanes), 1) // lanes
+    spread_count = even_ref.shape[1] // lanes
+    part = lax.broadcasted_iota(jnp.int32, (32, spread_count * lanes), 0)
+    comp = lax.broadcasted_iota(jnp.int32, (32, spread_count * lanes), 1) // lanes
     weights = jnp.where((part < 24) & (part % 8 == comp), 1.0, 0.0).astype(jnp.bfloat16)
 
     def spread(step, out_ref):
@@ -247,8 +252,14 @@
                 wide_ref[pl.ds(unit * GROUP, GROUP), pl.ds(value * lanes, lanes)].reshape(
                     GROUP // 8, 8, lanes
                 )
-                for value in range(8)
+                for value in range(spread_count)
             ]
+            chunk = step * chunks + unit // (lanes // GROUP)
+            at = (chunk >> 4) * lanes + unit % (lanes // GROUP) * GROUP
+            turned = turned_ref[pl.ds(pl.multiple_of(at, GROUP), GROUP), :]
+            for value in range(spread_count, 8):
+                column = jnp.full((GROUP, lanes), (chunk & 15) * 8 + value, jnp.int32)
+                other.append(lanes_of(turned, column).reshape(GROUP // 8, 8, lanes))
             mine = [table_ref[pl.ds(own + value, 8, stride=0), :][None] for value in range(8)]
             apart = [other[axis] - mine[axis] for axis in range(3)]
             square = apart[0] * apart[0] + apart[1] * apart[1] + apart[2] * apart[2] + epsilon_sq
@@ -274,6 +285,14 @@
                 force_ref[cell, axis] = running[axis]
         return last, running
 
+    def turn(block, unused):
+        rows = pl.ds(pl.multiple_of(block * lanes, lanes), lanes)
+        some = pl.ds(pl.multiple_of(block * 16, 16), 16)
+        turned_ref[rows, :] = list_ref[some].reshape(lanes, lanes).T
+        return unused
+
+    group_bits = (16 * lanes // GROUP).bit_length() - 1
+    lax.fori_loop(0, (groups >> group_bits) + 1, turn, 0)
     spread(0, even_ref)
 
     def both(step, carry):
@@ -288,22 +307,23 @@
 
 
 def inner_kernel(
-    amount_smem, where_smem, near_smem, cell_smem, table_ref, slots_ref, shift_ref,
-    force_ref, list_ref, even_ref, odd_ref,
+    amount_smem, where_smem, near_smem, cell_smem, table_ref, slots_ref,
+    force_ref, list_ref, even_ref, odd_ref, turned_ref, shift_ref,
 ):
     cells = table_ref.shape[0]
     fill_lists(amount_smem[0], where_smem, near_smem, table_ref, slots_ref, shift_ref, list_ref)
     flat = table_ref.reshape(cells * 8, table_ref.shape[2])
-    pair_forces(cell_smem, flat, list_ref, force_ref, even_ref, odd_ref)
+    pair_forces(cell_smem, flat, list_ref, force_ref, even_ref, odd_ref, turned_ref)
 
 
 def outer_kernel(
-    amount_smem, where_smem, near_smem, cell_smem, table_ref, halo_ref, slots_ref, shift_ref,
-    inner_ref, arms_ref, frag_ref, fixed_ref, out_ref, list_ref, even_ref, odd_ref, force_ref, loads_ref,
+    amount_smem, where_smem, near_smem, cell_smem, table_ref, halo_ref, slots_ref,
+    inner_ref, arms_ref, frag_ref, fixed_ref, out_ref, list_ref, even_ref, odd_ref, turned_ref,
+    shift_ref, force_ref, loads_ref,
 ):
     held = fixed_ref.shape[1] // 2
     fill_lists(amount_smem[0], where_smem, near_smem, halo_ref, slots_ref, shift_ref, list_ref)
-    pair_forces(cell_smem, table_ref, list_ref, force_ref, even_ref, odd_ref)
+    pair_forces(cell_smem, table_ref, list_ref, force_ref, even_ref, odd_ref, turned_ref)
     sums = fragment_sums(inner_ref, force_ref, arms_ref, frag_ref, loads_ref, held)
     out = fixed_ref[...] + jnp.concatenate([sums, jnp.zeros_like(sums)], axis=1)
     for brick in range(out_ref.shape[0]):
@@ -450,11 +470,6 @@
     grid = table.reshape(cells_x, cells_y, cells_z, 8, lanes)
     z_before, z_after = exchange(grid[:, :, -1:], grid[:, :, :1], "gz")
 
-    kinds = jnp.arange(27, dtype=jnp.int32)
-    moves = jnp.stack([kinds // 9 - 1, kinds // 3 % 3 - 1, kinds % 3 - 1], axis=1)
-    shift = jnp.pad(moves.astype(jnp.float32), ((0, 0), (0, 5)))
-    shift = jnp.broadcast_to(shift[:, :, None], (27, 8, lanes))
-
     outside = 1 << 20
     span_z = cells_z + 2
     starts = [0, cells_x * cells_y, 2 * cells_x * cells_y]
@@ -503,7 +518,7 @@
             jnp.where(live, own, cells),
         )
 
-    chunks = total + cells * GROUP // lanes + 3 * SPREAD
+    chunks = -(-(total + cells * GROUP // lanes + 3 * SPREAD) // 16) * 16
     group_top = chunks * (lanes // GROUP)
 
     def lists(near, need, own, amount, source):
@@ -528,8 +543,10 @@
     force_shape = (cells + 8, 3, 8, lanes)
     scratch = [
         pltpu.VMEM((chunks, 8, lanes), jnp.float32),
-        pltpu.VMEM((SPREAD * lanes, 8 * lanes), jnp.float32),
-        pltpu.VMEM((SPREAD * lanes, 8 * lanes), jnp.float32),
+        pltpu.VMEM((SPREAD * lanes, SPREAD_VALUES * lanes), jnp.float32),
+        pltpu.VMEM((SPREAD * lanes, SPREAD_VALUES * lanes), jnp.float32),
+        pltpu.VMEM((chunks * 8, lanes), jnp.float32),
+        pltpu.VMEM((27, 8, lanes), jnp.float32),
     ]
 
     near, word, need, own = listed(codes, inner_amount, True)
@@ -554,11 +571,11 @@
     inner = pl.pallas_call(
         inner_kernel,
         out_shape=jax.ShapeDtypeStruct(force_shape, jnp.float32),
-        in_specs=[smem] * 4 + [vmem] * 3,
+        in_specs=[smem] * 4 + [vmem] * 2,
         out_specs=vmem,
         scratch_shapes=scratch,
         compiler_params=params,
-    )(inner_amount[None], where, word, cell_of, table, slots, shift)
+    )(inner_amount[None], where, word, cell_of, table, slots)
 
     outer_amount = total - inner_amount
     codes = lax.dynamic_slice(jnp.concatenate([codes, codes]), (inner_amount,), (total,))
@@ -575,7 +592,7 @@
     known = pl.pallas_call(
         outer_kernel,
         out_shape=jax.ShapeDtypeStruct((bricks, 8, lanes), jnp.float32),
-        in_specs=[smem] * 4 + [vmem] * 8,
+        in_specs=[smem] * 4 + [vmem] * 7,
         out_specs=vmem,
         scratch_shapes=scratch
         + [pltpu.VMEM(force_shape, jnp.float32), pltpu.VMEM((16, 8, lanes), jnp.float32)],
@@ -588,7 +605,6 @@
         table.reshape(cells * 8, lanes),
         halo,
         slots,
-        shift,
         inner,
         flat_arms,
         flat_frag,

time: 136 us -> 137 us (level)
  transfers between devices with their start and end apart: 7 -> 7, of which waited for: 1 -> 1; matrix products, arithmetic and copies ran while one was open for 8% -> 8% of each run, Pallas kernels for 42% -> 41%
where the time goes in v7:
time: 137 us; the launch traced here: 136 us
  Pallas kernels  96.4 us (70%)
  starting transfers between devices  14.5 us (11%)
  other arithmetic  9.82 us (7%)
  waiting for transfers between devices  7.02 us (5%)
  local copies, waits for them, and re-layouts  4.93 us (4%)
  between operations  3.44 us (3%)
    pallas_call x1, Pallas kernels, local(): pl.pallas_call(inner_kernel, out_shape=jax.ShapeDtypeStruct(force_shape,...  46.7 us
    pallas_call x1, Pallas kernels, local(): pl.pallas_call(outer_kernel, out_shape=jax.ShapeDtypeStruct((bricks, 8, l...  25 us
    pallas_call x2, Pallas kernels, lists(): pl.pallas_call(list_kernel, out_shape=(jax.ShapeDtypeStruct((total, lanes...  16.7 us
    ppermute x6, starting transfers between devices, exchange(): return (lax.ppermute(last, axis, up), lax.ppermute(initial, axis, down))  9.1 us
    all_to_all x1, waiting for transfers between devices, local(): lax.all_to_all(known, names, split_axis=0, concat_axis=0, tiled=True)  7 us
    all_to_all x1, starting transfers between devices, local(): lax.all_to_all(known, names, split_axis=0, concat_axis=0, tiled=True)  5.41 us
    sort x1, other arithmetic, local(): codes = jnp.sort(codes + jnp.where(inside(*decode(codes)[3:]), 0, outside))  5.04 us
    pallas_call x1, Pallas kernels, local(): pl.pallas_call(functools.partial(move_kernel, owned), out_shape=(jax.Shap...  5.03 us
  transfers between devices with their start and end apart: 7, of which 1 were waited for; matrix products, arithmetic and copies ran while one was open for 8% of the time, Pallas kernels for 41%

profile of v7, /device:TPU:0, one launch (start us, length us, event | category | flops | bytes accessed | tf_op | source)
XLA Modules:
  0.0 136.1 jit_solution(16326069626631394915)
XLA Ops:
  0.6 0.7 fusion.47
  1.3 0.5 pad_bitcast_fusion
  1.8 2.9 %shard_map.104.table_ref = f32[256,8,128]{2,1,0:T(8,128)} custom-call(f32[7,256,128]{2,1,0:T(8,128)} %bitcast.49, s32[256,128]{1,0:T(8,128)} %bitcast.53, f32[1,128]{1,0:T(1,128)} %get-tuple-element.73.key_ref), custom_call_target="tpu_custom_call" | custom-call | tf_op jit(solution)/shard_map/pallas_call | solution.py:463
  4.8 1.0 fusion.52
  5.8 3.0 %collective-permute-start = (f32[4,4,1,8,128]{4,3,2,0,1:T(8,128)S(1)}, f32[4,4,1,8,128]{4,3,2,0,1:T(8,128)S(1)}, u32[]{:S(2)}, u32[]{:S(2)}) collective-permute-start(f32[4,4,1,8,128]{4,3,2,0,1:T(8,128)S(1)} %copy.20), channel_id=1, source_target_pairs={{0,1},{1,0},{2,3},{3,2},{4,5},{5,4},{6,7},{7,6},{8,9},{9,8},{10,11... | collective-permute-start | bytes 196616 | tf_op jit(solution)/shard_map/ppermute | solution.py:51
  8.9 1.1 fusion.51
  10.1 5.0 %sort.15 = (s32[2048]{0:T(1024)S(1)}, s32[2048]{0:T(1024)}) sort(s32[2048]{0:T(1024)S(1)} %select_add_fusion.2, s32[2048]{0:T(1024)S(1)} %iota.16), dimensions={0}, to_apply=%region_0.1 | sort | flops 22528 | bytes 32768 | tf_op jit(solution)/shard_map/jit(sort)/sort | solution.py:497
  15.1 0.7 convert_reduce_fusion
  18.4 1.4 %select_add_fusion = (s32[2048]{0:T(1024)}, s32[2048]{0:T(1024)}, s32[2048]{0:T(1024)}, s32[2048]{0:T(1024)}, s32[2048]{0:T(1024)}, /*index=5*/s32[2048]{0:T(1024)}, s32[2048]{0:T(1024)S(1)}) fusion(s32[]{:T(128)} %convert_reduce_fusion, s32[2048]{0:T(1024)S(1)} %get-tuple-element.22, s32[]{:T(128)S(6)} %select_n.211, s32[]{:T(128)} %sub.100), kind=kLoop, calls=%fused_computation.99 | loop fusion | flops 458752 | bytes 65548 | tf_op jit(solution)/shard_map/add | solution.py:516
  19.8 0.6 fusion.35
  20.5 0.7 maximum_maximum_fusion.fixed_ref
  21.4 1.8 %collective-permute-start.3 = (f32[1,4,18,8,128]{4,3,2,0,1:T(8,128)S(1)}, f32[1,4,18,8,128]{4,3,2,0,1:T(8,128)S(1)}, u32[]{:S(2)}, u32[]{:S(2)}) collective-permute-start(f32[1,4,18,8,128]{4,3,2,0,1:T(8,128)S(1)} %pad_maximum_fusion.3), channel_id=1, source_target_pairs={{8,0},{16,8},{24,16},{0,24},{9,1},{17,9},{25,17},{1,25},{10,2},{18... | collective-permute-start | bytes 884744 | tf_op jit(solution)/shard_map/ppermute | solution.py:51
  23.2 9.6 %shard_map.105 = (s32[2048,128]{1,0:T(8,128)}, s32[1,2048]{1,0:T(1,128)}, s32[1,8704]{1,0:T(1,128)}) custom-call(s32[1]{0:T(128)} %bitcast.17.amount_smem, s32[1,2048]{1,0:T(1,128)} %bitcast.67, s32[1,2048]{1,0:T(1,128)} %bitcast.68, s32[1,2048]{1,0:T(1,128)} %bitcast.69, f32[2048,128]{1,0:T(8,128)} %bitcast.45), custom_call_target="tpu_custom_call" | custom-call | tf_op jit(solution)/shard_map/pallas_call | solution.py:526
  32.9 2.1 %collective-permute-start.4 = (f32[6,1,18,8,128]{4,3,2,0,1:T(8,128)S(1)}, f32[6,1,18,8,128]{4,3,2,0,1:T(8,128)S(1)}, u32[]{:S(2)}, u32[]{:S(2)}) collective-permute-start(f32[6,1,18,8,128]{4,3,2,0,1:T(8,128)S(1)} %pad_maximum_fusion), channel_id=1, source_target_pairs={{0,2},{2,4},{4,6},{6,0},{1,3},{3,5},{5,7},{7,1},{8,10},{10,12},{12... | collective-permute-start | bytes 1327112 | tf_op jit(solution)/shard_map/ppermute | solution.py:51
  35.0 2.1 %collective-permute-start.5 = (f32[6,1,18,8,128]{4,3,2,0,1:T(8,128)S(1)}, f32[6,1,18,8,128]{4,3,2,0,1:T(8,128)S(1)}, u32[]{:S(2)}, u32[]{:S(2)}) collective-permute-start(f32[6,1,18,8,128]{4,3,2,0,1:T(8,128)S(1)} %pad_maximum_fusion.1), channel_id=1, source_target_pairs={{2,0},{4,2},{6,4},{0,6},{3,1},{5,3},{7,5},{1,7},{10,8},{12,10},{14... | collective-permute-start | bytes 1327112 | tf_op jit(solution)/shard_map/ppermute | solution.py:51
  37.1 46.7 %shard_map.107.inner_ref = f32[264,3,8,128]{3,2,1,0:T(8,128)} custom-call(s32[1]{0:T(128)} %bitcast.17.amount_smem, s32[1,2048]{1,0:T(1,128)} %get-tuple-element.36.where_smem, s32[2048]{0:T(1024)} %get-tuple-element.41.near_smem, s32[1,8704]{1,0:T(1,128)} %get-tuple-element.37.cell_smem, f32[256,8,128]{2,1,0:T(8,128)} %shard_map.104.table_ref, ...), custom_call_target="tpu_custom_call" | custom-call | tf_op jit(solution)/shard_map/pallas_call | solution.py:571
  84.0 1.2 copy-done.1
  85.1 7.1 %shard_map.106 = (s32[2048,128]{1,0:T(8,128)}, s32[1,2048]{1,0:T(1,128)}, s32[1,8704]{1,0:T(1,128)}) custom-call(s32[1]{0:T(128)} %bitcast.3.amount_smem, s32[1,2048]{1,0:T(1,128)} %bitcast.66, s32[1,2048]{1,0:T(1,128)} %bitcast.65, s32[1,2048]{1,0:T(1,128)} %bitcast.64, f32[3136,128]{1,0:T(8,128)} %bitcast.48), custom_call_target="tpu_custom_call" | custom-call | tf_op jit(solution)/shard_map/pallas_call | solution.py:526
  92.2 25.0 %shard_map.108 = f32[32,8,128]{2,1,0:T(8,128)} custom-call(s32[1]{0:T(128)} %bitcast.3.amount_smem, s32[1,2048]{1,0:T(1,128)} %get-tuple-element.33.where_smem, s32[2048]{0:T(1024)} %get-tuple-element.68.near_smem, s32[1,8704]{1,0:T(1,128)} %get-tuple-element.34.cell_smem, f32[2048,128]{1,0:T(8,128)} %bitcast.46, f32[392,8,128]{2,1,0:T(8,128)} %copy-done.1, ...), custom_call_target="tpu_custom_call" | custom-call | tf_op jit(solution)/shard_map/pallas_call | solution.py:592
  117.3 5.4 %all-to-all-start = ((f32[32,8,128]{2,1,0:T(8,128)}), f32[32,8,128]{2,1,0:T(8,128)S(1)}, u32[]{:S(2)}, u32[]{:S(2)}) async-start(f32[32,8,128]{2,1,0:T(8,128)} %shard_map.108), calls=%async_computation | async-start | bytes 262144 | tf_op jit(solution)/shard_map/all_to_all | solution.py:613
  122.7 0.7 copy.19.target_ref
  123.4 7.0 %all-to-all-done.known_ref = f32[32,8,128]{2,1,0:T(8,128)S(1)} async-done(((f32[32,8,128]{2,1,0:T(8,128)}), f32[32,8,128]{2,1,0:T(8,128)S(1)}, u32[]{:S(2)}, u32[]{:S(2)}) %all-to-all-start) | async-done | bytes 131104 | tf_op jit(solution)/shard_map/all_to_all | solution.py:613
  130.4 0.6 copy-done.2
  131.1 5.0 %shard_map.109 = (f32[6,256,128]{2,1,0:T(8,128)}, f32[6,128]{1,0:T(8,128)}) custom-call(f32[128,1]{1,0:T(8,128)} %copy.19.target_ref, f32[32,8,128]{2,1,0:T(8,128)} %copy-done.2, f32[7,256,128]{2,1,0:T(8,128)} %bitcast.50, f32[3,256,128]{2,1,0:T(8,128)} %bitcast.52, s32[256,128]{1,0:T(8,128)} %bitcast.55), custom_call_target="tpu_custom_call" | custom-call | tf_op jit(solution)/shard_map/pallas_call | solution.py:620
  (47 shorter events, 0.7 us)
Async XLA Ops:
  4.7 5.2 %copy-start = (f32[256,8,128]{2,1,0:T(8,128)S(1)}, f32[256,8,128]{2,1,0:T(8,128)}, u32[]{:S(2)}) copy-start(f32[256,8,128]{2,1,0:T(8,128)} %shard_map.104.table_ref) | copy-start | bytes 3145732
  4.8 5.3 %copy-start.3 = (s32[1,2048]{1,0:T(1,128)S(1)}, s32[1,2048]{1,0:T(1,128)}, u32[]{:S(2)}) copy-start(s32[1,2048]{1,0:T(1,128)} %param.14) | copy-start | bytes 24580
  4.8 15.7 %copy-start.4 = (f32[6,48]{1,0:T(8,128)S(1)}, f32[6,48]{1,0:T(8,128)}, u32[]{:S(2)}) copy-start(f32[6,48]{1,0:T(8,128)} %param.15) | copy-start | bytes 3460
  4.8 15.7 %copy-start.5 = (f32[48]{0:T(128)S(1)}, f32[48]{0:T(128)}, u32[]{:S(2)}) copy-start(f32[48]{0:T(128)} %param.17) | copy-start | bytes 580
  4.8 15.7 %copy-start.6 = (f32[48]{0:T(128)S(1)}, f32[48]{0:T(128)}, u32[]{:S(2)}) copy-start(f32[48]{0:T(128)} %param.16) | copy-start | bytes 580
  5.8 15.4 %collective-permute-start = (f32[4,4,1,8,128]{4,3,2,0,1:T(8,128)S(1)}, f32[4,4,1,8,128]{4,3,2,0,1:T(8,128)S(1)}, u32[]{:S(2)}, u32[]{:S(2)}) collective-permute-start(f32[4,4,1,8,128]{4,3,2,0,1:T(8,128)S(1)} %copy.20), channel_id=1, source_target_pairs={{0,1},{1,0},{2,3},{3,2},{4,5},{5,4},{6,7},{7,6},{8,9},{9,8},{10,11... | collective-permute-start | bytes 196616 | tf_op jit(solution)/shard_map/ppermute | solution.py:51
  8.8 12.4 %collective-permute-start.1 = (f32[4,4,1,8,128]{4,3,2,0,1:T(8,128)S(1)}, f32[4,4,1,8,128]{4,3,2,0,1:T(8,128)S(1)}, u32[]{:S(2)}, u32[]{:S(2)}) collective-permute-start(f32[4,4,1,8,128]{4,3,2,0,1:T(8,128)S(1)} %copy.21), channel_id=1, source_target_pairs={{1,0},{0,1},{3,2},{2,3},{5,4},{4,5},{7,6},{6,7},{9,8},{8,9},{11,10... | collective-permute-start | bytes 196616 | tf_op jit(solution)/shard_map/ppermute | solution.py:51
  21.3 11.5 %collective-permute-start.2 = (f32[1,4,18,8,128]{4,3,2,0,1:T(8,128)S(1)}, f32[1,4,18,8,128]{4,3,2,0,1:T(8,128)S(1)}, u32[]{:S(2)}, u32[]{:S(2)}) collective-permute-start(f32[1,4,18,8,128]{4,3,2,0,1:T(8,128)S(1)} %pad_maximum_fusion.2), channel_id=1, source_target_pairs={{0,8},{8,16},{16,24},{24,0},{1,9},{9,17},{17,25},{25,1},{2,10},{10... | collective-permute-start | bytes 884744 | tf_op jit(solution)/shard_map/ppermute | solution.py:51
  21.4 11.4 %collective-permute-start.3 = (f32[1,4,18,8,128]{4,3,2,0,1:T(8,128)S(1)}, f32[1,4,18,8,128]{4,3,2,0,1:T(8,128)S(1)}, u32[]{:S(2)}, u32[]{:S(2)}) collective-permute-start(f32[1,4,18,8,128]{4,3,2,0,1:T(8,128)S(1)} %pad_maximum_fusion.3), channel_id=1, source_target_pairs={{8,0},{16,8},{24,16},{0,24},{9,1},{17,9},{25,17},{1,25},{10,2},{18... | collective-permute-start | bytes 884744 | tf_op jit(solution)/shard_map/ppermute | solution.py:51
  32.9 51.0 %collective-permute-start.4 = (f32[6,1,18,8,128]{4,3,2,0,1:T(8,128)S(1)}, f32[6,1,18,8,128]{4,3,2,0,1:T(8,128)S(1)}, u32[]{:S(2)}, u32[]{:S(2)}) collective-permute-start(f32[6,1,18,8,128]{4,3,2,0,1:T(8,128)S(1)} %pad_maximum_fusion), channel_id=1, source_target_pairs={{0,2},{2,4},{4,6},{6,0},{1,3},{3,5},{5,7},{7,1},{8,10},{10,12},{12... | collective-permute-start | bytes 1327112 | tf_op jit(solution)/shard_map/ppermute | solution.py:51
  35.0 48.9 %collective-permute-start.5 = (f32[6,1,18,8,128]{4,3,2,0,1:T(8,128)S(1)}, f32[6,1,18,8,128]{4,3,2,0,1:T(8,128)S(1)}, u32[]{:S(2)}, u32[]{:S(2)}) collective-permute-start(f32[6,1,18,8,128]{4,3,2,0,1:T(8,128)S(1)} %pad_maximum_fusion.1), channel_id=1, source_target_pairs={{2,0},{4,2},{6,4},{0,6},{3,1},{5,3},{7,5},{1,7},{10,8},{12,10},{14... | collective-permute-start | bytes 1327112 | tf_op jit(solution)/shard_map/ppermute | solution.py:51
  83.9 1.2 copy-start.1
  117.3 13.2 %all-to-all-start = ((f32[32,8,128]{2,1,0:T(8,128)}), f32[32,8,128]{2,1,0:T(8,128)S(1)}, u32[]{:S(2)}, u32[]{:S(2)}) async-start(f32[32,8,128]{2,1,0:T(8,128)} %shard_map.108), calls=%async_computation | async-start | bytes 262144 | tf_op jit(solution)/shard_map/all_to_all | solution.py:613
  130.4 0.6 copy-start.2

commit v8 on v6

--- a/solution.py
+++ b/solution.py
@@ -186,6 +186,9 @@
     lane = lax.broadcasted_iota(jnp.int32, (8, lanes), 1)
     row = lax.broadcasted_iota(jnp.int32, (8, lanes), 0)
     absent = jnp.where(row == 6, -10.0, 0.0)
+    for kind in range(27):
+        steps = (kind // 9 - 1.0, kind // 3 % 3 - 1.0, kind % 3 - 1.0)
+        shift_ref[kind] = sum(jnp.where(row == axis, steps[axis], 0.0) for axis in range(3))
 
     def fill(block, carry):
         last_chunk, last_new, last_held = carry
@@ -225,62 +228,67 @@
     part = lax.broadcasted_iota(jnp.int32, (32, 8 * lanes), 0)
     comp = lax.broadcasted_iota(jnp.int32, (32, 8 * lanes), 1) // lanes
     weights = jnp.where((part < 24) & (part % 8 == comp), 1.0, 0.0).astype(jnp.bfloat16)
-
-    def spread(step, out_ref):
-        turned = []
+    column = 2 * lanes
+
+    def turned(step):
+        pieces = []
         for piece in range(chunks):
             values = list_ref[step * chunks + piece]
             high = values.astype(jnp.bfloat16).astype(jnp.float32)
             rest = values - high
             middle = rest.astype(jnp.bfloat16).astype(jnp.float32)
             parts = jnp.concatenate([high, middle, rest - middle, jnp.zeros_like(values)], axis=0)
-            turned.append(parts.astype(jnp.bfloat16).T)
-        turned = jnp.concatenate(turned, axis=0)
-        out_ref[...] = jnp.dot(turned, weights, preferred_element_type=jnp.float32)
-
-    def pairs(step, wide_ref, carry):
+            pieces.append(parts.astype(jnp.bfloat16).T)
+        return jnp.concatenate(pieces, axis=0)
+
+    def spread(rows_in, at, out_ref):
+        out_ref[:, at : at + column] = jnp.dot(
+            rows_in, weights[:, at : at + column], preferred_element_type=jnp.float32
+        )
+
+    def block_force(wide_ref, row, mine):
+        other = [wide_ref[pl.ds(row, 8), pl.ds(value * lanes, lanes)] for value in range(8)]
+        apart = [other[axis] - mine[axis] for axis in range(3)]
+        square = apart[0] * apart[0] + apart[1] * apart[1] + apart[2] * apart[2] + epsilon_sq
+        inverse = lax.rsqrt(square)
+        reach = other[6] + mine[6]
+        overlap = jnp.maximum(reach - square * inverse, 0.0)
+        overlap = jnp.where(other[7] != mine[7], overlap, 0.0)
+        closing = (
+            (other[3] - mine[3]) * apart[0]
+            + (other[4] - mine[4]) * apart[1]
+            + (other[5] - mine[5]) * apart[2]
+        )
+        scaled = overlap * (other[6] * mine[6])
+        root = scaled * lax.rsqrt(jnp.maximum(scaled * reach, 1e-30))
+        factor = root * inverse * (stiffness / damping * overlap - closing * inverse)
+        return [factor * apart[axis] for axis in range(3)]
+
+    def pairs(step, wide_ref, next_ref, carry):
         last, running = carry
+        rows_in = turned(step + 1)
         for unit in range(units):
+            if unit % (units // 4) == 0:
+                spread(rows_in, unit // (units // 4) * column, next_ref)
             cell = cell_smem[0, step * units + unit]
             own = jnp.minimum(cell, cells - 1) * 8
-            other = [
-                wide_ref[pl.ds(unit * GROUP, GROUP), pl.ds(value * lanes, lanes)].reshape(
-                    GROUP // 8, 8, lanes
-                )
-                for value in range(8)
-            ]
-            mine = [table_ref[pl.ds(own + value, 8, stride=0), :][None] for value in range(8)]
-            apart = [other[axis] - mine[axis] for axis in range(3)]
-            square = apart[0] * apart[0] + apart[1] * apart[1] + apart[2] * apart[2] + epsilon_sq
-            inverse = lax.rsqrt(square)
-            reach = other[6] + mine[6]
-            overlap = jnp.maximum(reach - square * inverse, 0.0)
-            overlap = jnp.where(other[7] != mine[7], overlap, 0.0)
-            closing = (
-                (other[3] - mine[3]) * apart[0]
-                + (other[4] - mine[4]) * apart[1]
-                + (other[5] - mine[5]) * apart[2]
-            )
-            scaled = overlap * (other[6] * mine[6])
-            root = scaled * lax.rsqrt(jnp.maximum(scaled * reach, 1e-30))
-            factor = root * inverse * (stiffness / damping * overlap - closing * inverse)
-            running = [
-                jnp.sum(factor * apart[axis], axis=0)
-                + jnp.where(cell == last, running[axis], 0.0)
-                for axis in range(3)
-            ]
+            mine = [table_ref[pl.ds(own + value, 8, stride=0), :] for value in range(8)]
+            running = [jnp.where(cell == last, running[axis], 0.0) for axis in range(3)]
+            for block in range(GROUP // 8):
+                force = block_force(wide_ref, unit * GROUP + block * 8, mine)
+                running = [running[axis] + force[axis] for axis in range(3)]
             last = cell
             for axis in range(3):
                 force_ref[cell, axis] = running[axis]
         return last, running
 
-    spread(0, even_ref)
+    first = turned(0)
+    for at in range(0, 8 * lanes, column):
+        spread(first, at, even_ref)
 
     def both(step, carry):
-        spread(2 * step + 1, odd_ref)
-        carry = pairs(2 * step, even_ref, carry)
-        spread(2 * step + 2, even_ref)
-        return pairs(2 * step + 1, odd_ref, carry)
+        carry = pairs(2 * step, even_ref, odd_ref, carry)
+        return pairs(2 * step + 1, odd_ref, even_ref, carry)
 
     zero = jnp.zeros((8, lanes), jnp.float32)
     steps = lax.div(groups + (2 * units - 1), 2 * units)
@@ -288,8 +296,8 @@
 
 
 def inner_kernel(
-    amount_smem, where_smem, near_smem, cell_smem, table_ref, slots_ref, shift_ref,
-    force_ref, list_ref, even_ref, odd_ref,
+    amount_smem, where_smem, near_smem, cell_smem, table_ref, slots_ref,
+    force_ref, list_ref, even_ref, odd_ref, shift_ref,
 ):
     cells = table_ref.shape[0]
     fill_lists(amount_smem[0], where_smem, near_smem, table_ref, slots_ref, shift_ref, list_ref)
@@ -298,8 +306,9 @@
 
 
 def outer_kernel(
-    amount_smem, where_smem, near_smem, cell_smem, table_ref, halo_ref, slots_ref, shift_ref,
-    inner_ref, arms_ref, frag_ref, fixed_ref, out_ref, list_ref, even_ref, odd_ref, force_ref, loads_ref,
+    amount_smem, where_smem, near_smem, cell_smem, table_ref, halo_ref, slots_ref,
+    inner_ref, arms_ref, frag_ref, fixed_ref, out_ref, list_ref, even_ref, odd_ref,
+    shift_ref, force_ref, loads_ref,
 ):
     held = fixed_ref.shape[1] // 2
     fill_lists(amount_smem[0], where_smem, near_smem, halo_ref, slots_ref, shift_ref, list_ref)
@@ -450,11 +459,6 @@
     grid = table.reshape(cells_x, cells_y, cells_z, 8, lanes)
     z_before, z_after = exchange(grid[:, :, -1:], grid[:, :, :1], "gz")
 
-    kinds = jnp.arange(27, dtype=jnp.int32)
-    moves = jnp.stack([kinds // 9 - 1, kinds // 3 % 3 - 1, kinds % 3 - 1], axis=1)
-    shift = jnp.pad(moves.astype(jnp.float32), ((0, 0), (0, 5)))
-    shift = jnp.broadcast_to(shift[:, :, None], (27, 8, lanes))
-
     outside = 1 << 20
     span_z = cells_z + 2
     starts = [0, cells_x * cells_y, 2 * cells_x * cells_y]
@@ -503,7 +507,7 @@
             jnp.where(live, own, cells),
         )
 
-    chunks = total + cells * GROUP // lanes + 3 * SPREAD
+    chunks = -(-(total + cells * GROUP // lanes + 3 * SPREAD) // 16) * 16
     group_top = chunks * (lanes // GROUP)
 
     def lists(near, need, own, amount, source):
@@ -530,6 +534,7 @@
         pltpu.VMEM((chunks, 8, lanes), jnp.float32),
         pltpu.VMEM((SPREAD * lanes, 8 * lanes), jnp.float32),
         pltpu.VMEM((SPREAD * lanes, 8 * lanes), jnp.float32),
+        pltpu.VMEM((27, 8, lanes), jnp.float32),
     ]
 
     near, word, need, own = listed(codes, inner_amount, True)
@@ -554,11 +559,11 @@
     inner = pl.pallas_call(
         inner_kernel,
         out_shape=jax.ShapeDtypeStruct(force_shape, jnp.float32),
-        in_specs=[smem] * 4 + [vmem] * 3,
+        in_specs=[smem] * 4 + [vmem] * 2,
         out_specs=vmem,
         scratch_shapes=scratch,
         compiler_params=params,
-    )(inner_amount[None], where, word, cell_of, table, slots, shift)
+    )(inner_amount[None], where, word, cell_of, table, slots)
 
     outer_amount = total - inner_amount
     codes = lax.dynamic_slice(jnp.concatenate([codes, codes]), (inner_amount,), (total,))
@@ -575,7 +580,7 @@
     known = pl.pallas_call(
         outer_kernel,
         out_shape=jax.ShapeDtypeStruct((bricks, 8, lanes), jnp.float32),
-        in_specs=[smem] * 4 + [vmem] * 8,
+        in_specs=[smem] * 4 + [vmem] * 7,
         out_specs=vmem,
         scratch_shapes=scratch
         + [pltpu.VMEM(force_shape, jnp.float32), pltpu.VMEM((16, 8, lanes), jnp.float32)],
@@ -588,7 +593,6 @@
         table.reshape(cells * 8, lanes),
         halo,
         slots,
-        shift,
         inner,
         flat_arms,
         flat_frag,

time: 136 us -> 138 us (1.015)
  starting transfers between devices: 14.7 us -> 16.9 us
    all_to_all x1, starting transfers between devices: 5.55 us -> 7.77 us  [local(): lax.all_to_all(known, names, split_axis=0, concat_axis=0, tiled=True)]
  transfers between devices with their start and end apart: 7 -> 7, of which waited for: 1 -> 1; matrix products, arithmetic and copies ran while one was open for 8% -> 8% of each run, Pallas kernels for 42% -> 41%
where the time goes in v8:
time: 138 us; the launch traced here: 139 us
  Pallas kernels  96.7 us (70%)
  starting transfers between devices  16.9 us (12%)
  other arithmetic  9.82 us (7%)
  waiting for transfers between devices  7.02 us (5%)
  local copies, waits for them, and re-layouts  4.93 us (4%)
  between operations  3.44 us (2%)
    pallas_call x1, Pallas kernels, local(): pl.pallas_call(inner_kernel, out_shape=jax.ShapeDtypeStruct(force_shape,...  47.9 us
    pallas_call x1, Pallas kernels, local(): pl.pallas_call(outer_kernel, out_shape=jax.ShapeDtypeStruct((bricks, 8, l...  24.2 us
    pallas_call x2, Pallas kernels, lists(): pl.pallas_call(list_kernel, out_shape=(jax.ShapeDtypeStruct((total, lanes...  16.7 us
    ppermute x6, starting transfers between devices, exchange(): return (lax.ppermute(last, axis, up), lax.ppermute(initial, axis, down))  9.1 us
    all_to_all x1, starting transfers between devices, local(): lax.all_to_all(known, names, split_axis=0, concat_axis=0, tiled=True)  7.77 us
    all_to_all x1, waiting for transfers between devices, local(): lax.all_to_all(known, names, split_axis=0, concat_axis=0, tiled=True)  7 us
    sort x1, other arithmetic, local(): codes = jnp.sort(codes + jnp.where(inside(*decode(codes)[3:]), 0, outside))  5.04 us
    pallas_call x1, Pallas kernels, local(): pl.pallas_call(functools.partial(move_kernel, owned), out_shape=(jax.Shap...  5.03 us
  transfers between devices with their start and end apart: 7, of which 1 were waited for; matrix products, arithmetic and copies ran while one was open for 8% of the time, Pallas kernels for 41%

profile of v8, /device:TPU:0, one launch (start us, length us, event | category | flops | bytes accessed | tf_op | source)
XLA Modules:
  0.0 138.8 jit_solution(4789271255354158177)
XLA Ops:
  0.6 0.7 fusion.47
  1.3 0.5 pad_bitcast_fusion
  1.8 2.9 %shard_map.104.table_ref = f32[256,8,128]{2,1,0:T(8,128)} custom-call(f32[7,256,128]{2,1,0:T(8,128)} %bitcast.49, s32[256,128]{1,0:T(8,128)} %bitcast.53, f32[1,128]{1,0:T(1,128)} %get-tuple-element.73.key_ref), custom_call_target="tpu_custom_call" | custom-call | tf_op jit(solution)/shard_map/pallas_call | solution.py:452
  4.8 1.0 fusion.52
  5.8 3.0 %collective-permute-start = (f32[4,4,1,8,128]{4,3,2,0,1:T(8,128)S(1)}, f32[4,4,1,8,128]{4,3,2,0,1:T(8,128)S(1)}, u32[]{:S(2)}, u32[]{:S(2)}) collective-permute-start(f32[4,4,1,8,128]{4,3,2,0,1:T(8,128)S(1)} %copy.20), channel_id=1, source_target_pairs={{0,1},{1,0},{2,3},{3,2},{4,5},{5,4},{6,7},{7,6},{8,9},{9,8},{10,11... | collective-permute-start | bytes 196616 | tf_op jit(solution)/shard_map/ppermute | solution.py:50
  8.9 1.1 fusion.51
  10.1 5.0 %sort.15 = (s32[2048]{0:T(1024)S(1)}, s32[2048]{0:T(1024)}) sort(s32[2048]{0:T(1024)S(1)} %select_add_fusion.2, s32[2048]{0:T(1024)S(1)} %iota.16), dimensions={0}, to_apply=%region_0.1 | sort | flops 22528 | bytes 32768 | tf_op jit(solution)/shard_map/jit(sort)/sort | solution.py:486
  15.1 0.7 convert_reduce_fusion
  18.4 1.4 select_add_fusion
  19.8 0.6 fusion.35
  20.5 0.7 maximum_maximum_fusion.fixed_ref
  21.4 1.8 %collective-permute-start.3 = (f32[1,4,18,8,128]{4,3,2,0,1:T(8,128)S(1)}, f32[1,4,18,8,128]{4,3,2,0,1:T(8,128)S(1)}, u32[]{:S(2)}, u32[]{:S(2)}) collective-permute-start(f32[1,4,18,8,128]{4,3,2,0,1:T(8,128)S(1)} %pad_maximum_fusion.3), channel_id=1, source_target_pairs={{8,0},{16,8},{24,16},{0,24},{9,1},{17,9},{25,17},{1,25},{10,2},{18... | collective-permute-start | bytes 884744 | tf_op jit(solution)/shard_map/ppermute | solution.py:50
  23.2 9.6 %shard_map.105 = (s32[2048,128]{1,0:T(8,128)}, s32[1,2048]{1,0:T(1,128)}, s32[1,8704]{1,0:T(1,128)}) custom-call(s32[1]{0:T(128)} %bitcast.17.amount_smem, s32[1,2048]{1,0:T(1,128)} %bitcast.67, s32[1,2048]{1,0:T(1,128)} %bitcast.68, s32[1,2048]{1,0:T(1,128)} %bitcast.69, f32[2048,128]{1,0:T(8,128)} %bitcast.45), custom_call_target="tpu_custom_call" | custom-call | tf_op jit(solution)/shard_map/pallas_call | solution.py:515
  32.9 2.1 %collective-permute-start.4 = (f32[6,1,18,8,128]{4,3,2,0,1:T(8,128)S(1)}, f32[6,1,18,8,128]{4,3,2,0,1:T(8,128)S(1)}, u32[]{:S(2)}, u32[]{:S(2)}) collective-permute-start(f32[6,1,18,8,128]{4,3,2,0,1:T(8,128)S(1)} %pad_maximum_fusion), channel_id=1, source_target_pairs={{0,2},{2,4},{4,6},{6,0},{1,3},{3,5},{5,7},{7,1},{8,10},{10,12},{12... | collective-permute-start | bytes 1327112 | tf_op jit(solution)/shard_map/ppermute | solution.py:50
  35.0 2.1 %collective-permute-start.5 = (f32[6,1,18,8,128]{4,3,2,0,1:T(8,128)S(1)}, f32[6,1,18,8,128]{4,3,2,0,1:T(8,128)S(1)}, u32[]{:S(2)}, u32[]{:S(2)}) collective-permute-start(f32[6,1,18,8,128]{4,3,2,0,1:T(8,128)S(1)} %pad_maximum_fusion.1), channel_id=1, source_target_pairs={{2,0},{4,2},{6,4},{0,6},{3,1},{5,3},{7,5},{1,7},{10,8},{12,10},{14... | collective-permute-start | bytes 1327112 | tf_op jit(solution)/shard_map/ppermute | solution.py:50
  37.1 47.9 %shard_map.107.inner_ref = f32[264,3,8,128]{3,2,1,0:T(8,128)} custom-call(s32[1]{0:T(128)} %bitcast.17.amount_smem, s32[1,2048]{1,0:T(1,128)} %get-tuple-element.36.where_smem, s32[2048]{0:T(1024)} %get-tuple-element.41.near_smem, s32[1,8704]{1,0:T(1,128)} %get-tuple-element.37.cell_smem, f32[256,8,128]{2,1,0:T(8,128)} %shard_map.104.table_ref, ...), custom_call_target="tpu_custom_call" | custom-call | tf_op jit(solution)/shard_map/pallas_call | solution.py:559
  85.1 1.2 copy-done.1
  86.3 7.1 %shard_map.106 = (s32[2048,128]{1,0:T(8,128)}, s32[1,2048]{1,0:T(1,128)}, s32[1,8704]{1,0:T(1,128)}) custom-call(s32[1]{0:T(128)} %bitcast.3.amount_smem, s32[1,2048]{1,0:T(1,128)} %bitcast.66, s32[1,2048]{1,0:T(1,128)} %bitcast.65, s32[1,2048]{1,0:T(1,128)} %bitcast.64, f32[3136,128]{1,0:T(8,128)} %bitcast.48), custom_call_target="tpu_custom_call" | custom-call | tf_op jit(solution)/shard_map/pallas_call | solution.py:515
  93.4 24.2 %shard_map.108 = f32[32,8,128]{2,1,0:T(8,128)} custom-call(s32[1]{0:T(128)} %bitcast.3.amount_smem, s32[1,2048]{1,0:T(1,128)} %get-tuple-element.33.where_smem, s32[2048]{0:T(1024)} %get-tuple-element.68.near_smem, s32[1,8704]{1,0:T(1,128)} %get-tuple-element.34.cell_smem, f32[2048,128]{1,0:T(8,128)} %bitcast.46, f32[392,8,128]{2,1,0:T(8,128)} %copy-done.1, ...), custom_call_target="tpu_custom_call" | custom-call | tf_op jit(solution)/shard_map/pallas_call | solution.py:580
  117.6 7.8 %all-to-all-start = ((f32[32,8,128]{2,1,0:T(8,128)}), f32[32,8,128]{2,1,0:T(8,128)S(1)}, u32[]{:S(2)}, u32[]{:S(2)}) async-start(f32[32,8,128]{2,1,0:T(8,128)} %shard_map.108), calls=%async_computation | async-start | bytes 262144 | tf_op jit(solution)/shard_map/all_to_all | solution.py:601
  125.3 0.7 copy.19.target_ref
  126.1 7.0 %all-to-all-done.known_ref = f32[32,8,128]{2,1,0:T(8,128)S(1)} async-done(((f32[32,8,128]{2,1,0:T(8,128)}), f32[32,8,128]{2,1,0:T(8,128)S(1)}, u32[]{:S(2)}, u32[]{:S(2)}) %all-to-all-start) | async-done | bytes 131104 | tf_op jit(solution)/shard_map/all_to_all | solution.py:601
  133.1 0.6 copy-done.2
  133.7 5.0 %shard_map.109 = (f32[6,256,128]{2,1,0:T(8,128)}, f32[6,128]{1,0:T(8,128)}) custom-call(f32[128,1]{1,0:T(8,128)} %copy.19.target_ref, f32[32,8,128]{2,1,0:T(8,128)} %copy-done.2, f32[7,256,128]{2,1,0:T(8,128)} %bitcast.50, f32[3,256,128]{2,1,0:T(8,128)} %bitcast.52, s32[256,128]{1,0:T(8,128)} %bitcast.55), custom_call_target="tpu_custom_call" | custom-call | tf_op jit(solution)/shard_map/pallas_call | solution.py:608
  (47 shorter events, 0.7 us)
Async XLA Ops:
  4.7 5.2 %copy-start = (f32[256,8,128]{2,1,0:T(8,128)S(1)}, f32[256,8,128]{2,1,0:T(8,128)}, u32[]{:S(2)}) copy-start(f32[256,8,128]{2,1,0:T(8,128)} %shard_map.104.table_ref) | copy-start | bytes 3145732
  4.8 5.3 %copy-start.3 = (s32[1,2048]{1,0:T(1,128)S(1)}, s32[1,2048]{1,0:T(1,128)}, u32[]{:S(2)}) copy-start(s32[1,2048]{1,0:T(1,128)} %param.14) | copy-start | bytes 24580
  4.8 15.7 %copy-start.4 = (f32[6,48]{1,0:T(8,128)S(1)}, f32[6,48]{1,0:T(8,128)}, u32[]{:S(2)}) copy-start(f32[6,48]{1,0:T(8,128)} %param.15) | copy-start | bytes 3460
  4.8 15.7 %copy-start.5 = (f32[48]{0:T(128)S(1)}, f32[48]{0:T(128)}, u32[]{:S(2)}) copy-start(f32[48]{0:T(128)} %param.17) | copy-start | bytes 580
  4.8 15.7 %copy-start.6 = (f32[48]{0:T(128)S(1)}, f32[48]{0:T(128)}, u32[]{:S(2)}) copy-start(f32[48]{0:T(128)} %param.16) | copy-start | bytes 580
  5.8 15.4 %collective-permute-start = (f32[4,4,1,8,128]{4,3,2,0,1:T(8,128)S(1)}, f32[4,4,1,8,128]{4,3,2,0,1:T(8,128)S(1)}, u32[]{:S(2)}, u32[]{:S(2)}) collective-permute-start(f32[4,4,1,8,128]{4,3,2,0,1:T(8,128)S(1)} %copy.20), channel_id=1, source_target_pairs={{0,1},{1,0},{2,3},{3,2},{4,5},{5,4},{6,7},{7,6},{8,9},{9,8},{10,11... | collective-permute-start | bytes 196616 | tf_op jit(solution)/shard_map/ppermute | solution.py:50
  8.8 12.4 %collective-permute-start.1 = (f32[4,4,1,8,128]{4,3,2,0,1:T(8,128)S(1)}, f32[4,4,1,8,128]{4,3,2,0,1:T(8,128)S(1)}, u32[]{:S(2)}, u32[]{:S(2)}) collective-permute-start(f32[4,4,1,8,128]{4,3,2,0,1:T(8,128)S(1)} %copy.21), channel_id=1, source_target_pairs={{1,0},{0,1},{3,2},{2,3},{5,4},{4,5},{7,6},{6,7},{9,8},{8,9},{11,10... | collective-permute-start | bytes 196616 | tf_op jit(solution)/shard_map/ppermute | solution.py:50
  21.3 11.5 %collective-permute-start.2 = (f32[1,4,18,8,128]{4,3,2,0,1:T(8,128)S(1)}, f32[1,4,18,8,128]{4,3,2,0,1:T(8,128)S(1)}, u32[]{:S(2)}, u32[]{:S(2)}) collective-permute-start(f32[1,4,18,8,128]{4,3,2,0,1:T(8,128)S(1)} %pad_maximum_fusion.2), channel_id=1, source_target_pairs={{0,8},{8,16},{16,24},{24,0},{1,9},{9,17},{17,25},{25,1},{2,10},{10... | collective-permute-start | bytes 884744 | tf_op jit(solution)/shard_map/ppermute | solution.py:50
  21.4 11.4 %collective-permute-start.3 = (f32[1,4,18,8,128]{4,3,2,0,1:T(8,128)S(1)}, f32[1,4,18,8,128]{4,3,2,0,1:T(8,128)S(1)}, u32[]{:S(2)}, u32[]{:S(2)}) collective-permute-start(f32[1,4,18,8,128]{4,3,2,0,1:T(8,128)S(1)} %pad_maximum_fusion.3), channel_id=1, source_target_pairs={{8,0},{16,8},{24,16},{0,24},{9,1},{17,9},{25,17},{1,25},{10,2},{18... | collective-permute-start | bytes 884744 | tf_op jit(solution)/shard_map/ppermute | solution.py:50
  32.9 52.1 %collective-permute-start.4 = (f32[6,1,18,8,128]{4,3,2,0,1:T(8,128)S(1)}, f32[6,1,18,8,128]{4,3,2,0,1:T(8,128)S(1)}, u32[]{:S(2)}, u32[]{:S(2)}) collective-permute-start(f32[6,1,18,8,128]{4,3,2,0,1:T(8,128)S(1)} %pad_maximum_fusion), channel_id=1, source_target_pairs={{0,2},{2,4},{4,6},{6,0},{1,3},{3,5},{5,7},{7,1},{8,10},{10,12},{12... | collective-permute-start | bytes 1327112 | tf_op jit(solution)/shard_map/ppermute | solution.py:50
  35.0 50.1 %collective-permute-start.5 = (f32[6,1,18,8,128]{4,3,2,0,1:T(8,128)S(1)}, f32[6,1,18,8,128]{4,3,2,0,1:T(8,128)S(1)}, u32[]{:S(2)}, u32[]{:S(2)}) collective-permute-start(f32[6,1,18,8,128]{4,3,2,0,1:T(8,128)S(1)} %pad_maximum_fusion.1), channel_id=1, source_target_pairs={{2,0},{4,2},{6,4},{0,6},{3,1},{5,3},{7,5},{1,7},{10,8},{12,10},{14... | collective-permute-start | bytes 1327112 | tf_op jit(solution)/shard_map/ppermute | solution.py:50
  85.1 1.2 copy-start.1
  117.6 15.5 %all-to-all-start = ((f32[32,8,128]{2,1,0:T(8,128)}), f32[32,8,128]{2,1,0:T(8,128)S(1)}, u32[]{:S(2)}, u32[]{:S(2)}) async-start(f32[32,8,128]{2,1,0:T(8,128)} %shard_map.108), calls=%async_computation | async-start | bytes 262144 | tf_op jit(solution)/shard_map/all_to_all | solution.py:601
  133.1 0.6 copy-start.2

commit v9 on v8

--- a/solution.py
+++ b/solution.py
@@ -14,8 +14,9 @@
 epsilon_sq = 1e-08
 radius_top = 0.14
 
-GROUP = 32
+GROUP = 16
 FILL = 32
+SLACK = 256
 SPREAD = 4
 VMEM = 56 * 1024 * 1024
 
@@ -60,17 +61,20 @@
         out_ref[rows, 7, :] = lanes_of(keys, frag_ref[rows, :])
 
 
-def list_kernel(
-    amount_smem, near_ref, need_ref, own_ref, table_ref, slots_ref, where_ref, cell_ref, class_ref, member_ref, count_ref
+def list_tiles(
+    amount, near_of, sizes, code_ref, table_ref, slots_ref, where_ref, word_ref, cell_ref,
+    class_ref, member_ref, count_ref, near_ref, need_ref, own_ref,
 ):
     tiles, lanes = slots_ref.shape
-    span = table_ref.shape[0] // 8
+    span = table_ref.shape[0]
     padded = class_ref.shape[0]
     cells = count_ref.shape[0]
     wide = 256
+    parts = 4
+    flat = table_ref.reshape(span * 8, lanes)
 
     def plane(comp):
-        return table_ref[pl.ds(comp, span, stride=8), :]
+        return flat[pl.ds(comp, span, stride=8), :]
 
     def flag(value):
         return value.astype(jnp.float32).astype(jnp.bfloat16)
@@ -80,6 +84,31 @@
 
     def ramp(shape, axis):
         return lax.broadcasted_iota(jnp.int32, shape, axis)
+
+    def over(value, by):
+        return jnp.floor((value.astype(jnp.float32) + 0.5) * (1.0 / by)).astype(jnp.int32)
+
+    code = code_ref[...]
+    own = over(code, 27)
+    kind = code - 27 * own
+    step_x = over(kind, 9)
+    step_y = over(kind, 3) - 3 * step_x
+    steps = (step_x - 1, step_y - 1, kind - 9 * step_x - 3 * step_y - 1)
+    own_x = over(own, sizes[1] * sizes[2])
+    row = over(own, sizes[2])
+    near = near_of(
+        own_x + steps[0], row - own_x * sizes[1] + steps[1], own - row * sizes[2] + steps[2]
+    )
+    need = sum(
+        jnp.where(steps[axis] == 1, 1, jnp.where(steps[axis] == -1, 2, 0)) * (1 << (2 * axis))
+        for axis in range(3)
+    )
+    live = ramp((1, tiles), 1) < amount
+    near = jnp.where(live, near, 0)
+    near_ref[...] = near
+    word_ref[...] = near * 32 + jnp.where(live, kind, 0)
+    need_ref[...] = jnp.where(live, need, 64)
+    own_ref[...] = jnp.where(live, own, cells)
 
     radius = plane(6) + (radius_top + 1e-5)
     classes = jnp.zeros((span, lanes), jnp.float32)
@@ -87,21 +116,20 @@
         place = plane(axis)
         classes = classes + jnp.where(place < radius, 1.0 * (1 << (2 * axis)), 0.0)
         classes = classes + jnp.where(place > 1.0 - radius, 1.0 * (2 << (2 * axis)), 0.0)
-    class_ref[...] = jnp.zeros(class_ref.shape, jnp.float32)
+    if padded > span:
+        class_ref[...] = jnp.zeros(class_ref.shape, jnp.float32)
     class_ref[pl.ds(0, span), :] = classes
     codes = jnp.concatenate(
         [class_ref[pl.ds(at, lanes), :].T for at in range(0, padded, lanes)], axis=1
     ).astype(jnp.bfloat16)
     ones = jnp.ones((lanes, lanes), jnp.bfloat16)
     count_ref[...] = jnp.zeros(count_ref.shape, jnp.float32)
-
-    pair = 2 * wide
-    blocks = lax.div(amount_smem[0] + (pair - 1), pair)
+    blocks = lax.div(amount + (parts * wide - 1), parts * wide)
 
     def choose(block, unused):
         held = []
-        for half in range(2):
-            at = pl.ds(pl.multiple_of(block * pair + half * wide, wide), wide)
+        for part in range(parts):
+            at = pl.ds(pl.multiple_of((block * parts + part) * wide, wide), wide)
             hits = flag(ramp((padded, wide), 0) == near_ref[:, at])
             found = dot(codes, hits).astype(jnp.int32)
             need = need_ref[:, at]
@@ -110,7 +138,7 @@
             count = dot(ones, member.astype(jnp.bfloat16))
             mine = flag(ramp((cells, wide), 0) == own_ref[:, at])
             held.append(dot_lanes(mine, count.astype(jnp.bfloat16)))
-        count_ref[...] += held[0] + held[1]
+        count_ref[...] += (held[0] + held[1]) + (held[2] + held[3])
         return unused
 
     lax.fori_loop(0, blocks, choose, 0)
@@ -122,19 +150,17 @@
     upto = flag(ramp((cells, cells), 1) <= ramp((cells, cells), 0))
     ends = dot(upto, taken.astype(jnp.bfloat16))
     cell_ones = jnp.ones((8, cells), jnp.bfloat16)
-    group_blocks = cell_ref.shape[1] // lanes - 1
+    many = 8 * lanes
+    wide_ends = jnp.concatenate([ends] * 8, axis=1)
 
     def name_groups(block, unused):
-        group = (ramp((cells, lanes), 1) + block * lanes).astype(jnp.float32)
-        over = dot(cell_ones, flag(ends <= group))
-        at = pl.ds(pl.multiple_of(block * lanes, lanes), lanes)
-        cell_ref[:, at] = over[0:1].astype(jnp.int32)
+        group = (ramp((cells, many), 1) + block * many).astype(jnp.float32)
+        at = pl.ds(pl.multiple_of(block * many, many), many)
+        cell_ref[:, at] = dot(cell_ones, flag(wide_ends <= group))[0:1].astype(jnp.int32)
         return unused
 
-    used = jnp.max(ends).astype(jnp.int32)
-    needed = jnp.minimum((used >> (lanes.bit_length() - 1)) + 2, group_blocks)
-    lax.fori_loop(0, needed, name_groups, 0)
-    cell_ref[:, pl.ds(group_blocks * lanes, lanes)] = ends[cells - 1 : cells].astype(jnp.int32)
+    groups = jnp.max(ends).astype(jnp.int32)
+    lax.fori_loop(0, lax.div(groups + SLACK, many) + 1, name_groups, 0)
     before_cell = jnp.concatenate(
         [value.T[0:8] for value in (taken, high, low)], axis=0
     ).astype(jnp.bfloat16)
@@ -143,8 +169,9 @@
     earlier_tile = flag(ramp((wide, wide), 0) < ramp((wide, wide), 1))
 
     def place(block, done):
-        for half in range(2):
-            at = pl.ds(pl.multiple_of(block * pair + half * wide, wide), wide)
+        for part in range(parts):
+            first = pl.multiple_of((block * parts + part) * wide, wide)
+            at = pl.ds(first, wide)
             flags = member_ref[:, at].astype(jnp.bfloat16)
             count = dot(ones, flags)
             lower = flag(ramp((cells, wide), 0) < own_ref[:, at])
@@ -170,14 +197,14 @@
                 moved = jnp.concatenate([word[lanes - bit :], word[: lanes - bit]], axis=0)
                 word = jnp.where((turn & bit) != 0, moved, word)
                 bit *= 2
-            for part in range(wide // lanes):
-                first = block * pair + half * wide + part * lanes
-                rows = pl.ds(pl.multiple_of(first, lanes), lanes)
-                slots_ref[rows, :] = word[:, part * lanes : (part + 1) * lanes].T
+            for half in range(wide // lanes):
+                rows = pl.ds(pl.multiple_of(first + half * lanes, lanes), lanes)
+                slots_ref[rows, :] = word[:, half * lanes : (half + 1) * lanes].T
             done = done + jnp.sum(count[0:8], axis=1, keepdims=True)
         return done
 
     lax.fori_loop(0, blocks, place, jnp.zeros((8, 1), jnp.float32))
+    return groups
 
 
 def fill_lists(amount, where_smem, near_smem, table_ref, slots_ref, shift_ref, list_ref):
@@ -194,7 +221,7 @@
         last_chunk, last_new, last_held = carry
         units = range(FILL)
         where = [where_smem[0, block * FILL + unit] for unit in units]
-        near = [near_smem[block * FILL + unit] for unit in units]
+        near = [near_smem[0, block * FILL + unit] for unit in units]
         found = []
         for unit in units:
             slots = slots_ref[pl.ds(block * FILL + unit, 8, stride=0), :]
@@ -217,18 +244,16 @@
     lax.fori_loop(0, blocks, fill, (jnp.int32(0), absent, absent))
 
 
-def pair_forces(cell_smem, table_ref, list_ref, force_ref, even_ref, odd_ref):
+def pair_forces(groups, cell_smem, table_ref, list_ref, force_ref, even_ref, odd_ref):
     lanes = table_ref.shape[1]
     cells = table_ref.shape[0] // 8
     rows = even_ref.shape[0]
     chunks = rows // lanes
     units = rows // GROUP
-    groups = cell_smem[0, cell_smem.shape[1] - lanes]
     force_ref[...] = jnp.zeros(force_ref.shape, jnp.float32)
     part = lax.broadcasted_iota(jnp.int32, (32, 8 * lanes), 0)
     comp = lax.broadcasted_iota(jnp.int32, (32, 8 * lanes), 1) // lanes
     weights = jnp.where((part < 24) & (part % 8 == comp), 1.0, 0.0).astype(jnp.bfloat16)
-    column = 2 * lanes
 
     def turned(step):
         pieces = []
@@ -241,10 +266,8 @@
             pieces.append(parts.astype(jnp.bfloat16).T)
         return jnp.concatenate(pieces, axis=0)
 
-    def spread(rows_in, at, out_ref):
-        out_ref[:, at : at + column] = jnp.dot(
-            rows_in, weights[:, at : at + column], preferred_element_type=jnp.float32
-        )
+    def spread(step, out_ref):
+        out_ref[...] = jnp.dot(turned(step), weights, preferred_element_type=jnp.float32)
 
     def block_force(wide_ref, row, mine):
         other = [wide_ref[pl.ds(row, 8), pl.ds(value * lanes, lanes)] for value in range(8)]
@@ -266,10 +289,8 @@
 
     def pairs(step, wide_ref, next_ref, carry):
         last, running = carry
-        rows_in = turned(step + 1)
+        spread(step + 1, next_ref)
         for unit in range(units):
-            if unit % (units // 4) == 0:
-                spread(rows_in, unit // (units // 4) * column, next_ref)
             cell = cell_smem[0, step * units + unit]
             own = jnp.minimum(cell, cells - 1) * 8
             mine = [table_ref[pl.ds(own + value, 8, stride=0), :] for value in range(8)]
@@ -282,9 +303,7 @@
                 force_ref[cell, axis] = running[axis]
         return last, running
 
-    first = turned(0)
-    for at in range(0, 8 * lanes, column):
-        spread(first, at, even_ref)
+    spread(0, even_ref)
 
     def both(step, carry):
         carry = pairs(2 * step, even_ref, odd_ref, carry)
@@ -295,24 +314,41 @@
     lax.fori_loop(0, steps, both, (jnp.int32(-1), [zero] * 3))
 
 
-def inner_kernel(
-    amount_smem, where_smem, near_smem, cell_smem, table_ref, slots_ref,
-    force_ref, list_ref, even_ref, odd_ref, shift_ref,
+def forces(
+    amount, near_of, sizes, code_ref, table_ref, near_table_ref, force_ref,
+    slots_ref, where_ref, word_ref, cell_ref, where_smem, word_smem, cell_smem, sems,
+    class_ref, member_ref, count_ref, near_ref, need_ref, own_ref,
+    list_ref, even_ref, odd_ref, shift_ref,
 ):
-    cells = table_ref.shape[0]
-    fill_lists(amount_smem[0], where_smem, near_smem, table_ref, slots_ref, shift_ref, list_ref)
-    flat = table_ref.reshape(cells * 8, table_ref.shape[2])
-    pair_forces(cell_smem, flat, list_ref, force_ref, even_ref, odd_ref)
+    cells, _, lanes = table_ref.shape
+    groups = list_tiles(
+        amount, near_of, sizes, code_ref, near_table_ref, slots_ref, where_ref, word_ref, cell_ref,
+        class_ref, member_ref, count_ref, near_ref, need_ref, own_ref,
+    )
+    copies = [
+        pltpu.make_async_copy(where_ref, where_smem, sems.at[0]),
+        pltpu.make_async_copy(word_ref, word_smem, sems.at[1]),
+        pltpu.make_async_copy(cell_ref, cell_smem, sems.at[2]),
+    ]
+    for copy in copies:
+        copy.start()
+    for copy in copies:
+        copy.wait()
+    fill_lists(amount, where_smem, word_smem, near_table_ref, slots_ref, shift_ref, list_ref)
+    flat = table_ref.reshape(cells * 8, lanes)
+    pair_forces(groups, cell_smem, flat, list_ref, force_ref, even_ref, odd_ref)
+
+
+def inner_kernel(near_of, sizes, amount_smem, code_ref, table_ref, force_ref, *scratch):
+    forces(amount_smem[0], near_of, sizes, code_ref, table_ref, table_ref, force_ref, *scratch)
 
 
 def outer_kernel(
-    amount_smem, where_smem, near_smem, cell_smem, table_ref, halo_ref, slots_ref,
-    inner_ref, arms_ref, frag_ref, fixed_ref, out_ref, list_ref, even_ref, odd_ref,
-    shift_ref, force_ref, loads_ref,
+    near_of, sizes, amount_smem, code_ref, table_ref, halo_ref, inner_ref, arms_ref, frag_ref,
+    fixed_ref, out_ref, force_ref, loads_ref, *scratch,
 ):
     held = fixed_ref.shape[1] // 2
-    fill_lists(amount_smem[0], where_smem, near_smem, halo_ref, slots_ref, shift_ref, list_ref)
-    pair_forces(cell_smem, table_ref, list_ref, force_ref, even_ref, odd_ref)
+    forces(amount_smem[0], near_of, sizes, code_ref, table_ref, halo_ref, force_ref, *scratch)
     sums = fragment_sums(inner_ref, force_ref, arms_ref, frag_ref, loads_ref, held)
     out = fixed_ref[...] + jnp.concatenate([sums, jnp.zeros_like(sums)], axis=1)
     for brick in range(out_ref.shape[0]):
@@ -465,90 +501,67 @@
     starts += [starts[-1] + cells_y * span_z, starts[-1] + 2 * cells_y * span_z]
     starts += [starts[-1] + (cells_x + 2) * span_z]
 
-    def decode(codes):
-        own, offset = (codes // 27, codes % 27)
-        steps = (offset // 9 - 1, offset // 3 % 3 - 1, offset % 3 - 1)
-        x = own // (cells_y * cells_z) + steps[0]
-        y = own // cells_z % cells_y + steps[1]
-        z = own % cells_z + steps[2]
-        need = sum(
-            jnp.where(steps[axis] == 1, 1, jnp.where(steps[axis] == -1, 2, 0)) << (2 * axis)
-            for axis in range(3)
-        )
-        return own, offset, need, x, y, z
-
-    def inside(x, y, z):
+    def inside(codes):
+        own, kind = (codes // 27, codes % 27)
+        x = own // (cells_y * cells_z) + kind // 9 - 1
+        y = own // cells_z % cells_y + kind // 3 % 3 - 1
+        z = own % cells_z + kind % 3 - 1
         inner = (x >= 0) & (x < cells_x) & (y >= 0) & (y < cells_y)
         return inner & (z >= 0) & (z < cells_z)
 
+    def near_inside(x, y, z):
+        return (x * cells_y + y) * cells_z + z
+
+    def near_outside(x, y, z):
+        in_y = jnp.where(y < 0, starts[4], starts[5]) + (x + 1) * span_z + z + 1
+        in_x = jnp.where(x < 0, starts[2], starts[3]) + y * span_z + z + 1
+        in_z = jnp.where(z < 0, starts[0], starts[1]) + x * cells_y + y
+        in_x = jnp.where((x < 0) | (x >= cells_x), in_x, in_z)
+        return jnp.where((y < 0) | (y >= cells_y), in_y, in_x)
+
+    sizes = (cells_x, cells_y, cells_z)
     codes = tiles[0]
     total = codes.shape[0]
-    codes = jnp.sort(codes + jnp.where(inside(*decode(codes)[3:]), 0, outside))
-    inner_amount = jnp.sum((codes < outside).astype(jnp.int32))
-    order = jnp.arange(total, dtype=jnp.int32)
-
-    def listed(codes, amount, want_inside):
-        own, offset, need, x, y, z = decode(codes & (outside - 1))
-        if want_inside:
-            near = (x * cells_y + y) * cells_z + z
-        else:
-            in_y = jnp.where(y < 0, starts[4], starts[5]) + (x + 1) * span_z + z + 1
-            in_x = jnp.where(x < 0, starts[2], starts[3]) + y * span_z + z + 1
-            in_z = jnp.where(z < 0, starts[0], starts[1]) + x * cells_y + y
-            near = jnp.where(
-                (y < 0) | (y >= cells_y), in_y, jnp.where((x < 0) | (x >= cells_x), in_x, in_z)
-            )
-        live = order < amount
-        near = jnp.where(live, near, 0)
-        return (
-            near,
-            near * 32 + jnp.where(live, offset, 0),
-            jnp.where(live, need, 64),
-            jnp.where(live, own, cells),
-        )
-
-    chunks = -(-(total + cells * GROUP // lanes + 3 * SPREAD) // 16) * 16
-    group_top = chunks * (lanes // GROUP)
-
-    def lists(near, need, own, amount, source):
-        span = source.shape[0]
-        return pl.pallas_call(
-            list_kernel,
-            out_shape=(
-                jax.ShapeDtypeStruct((total, lanes), jnp.int32),
-                jax.ShapeDtypeStruct((1, total), jnp.int32),
-                jax.ShapeDtypeStruct((1, -(-group_top // lanes) * lanes + lanes), jnp.int32),
-            ),
-            in_specs=[smem] + [vmem] * 4,
-            out_specs=(vmem, vmem, vmem),
-            scratch_shapes=[
-                pltpu.VMEM((-(-span // lanes) * lanes, lanes), jnp.float32),
-                pltpu.VMEM((lanes, total), jnp.float32),
-                pltpu.VMEM((cells, lanes), jnp.float32),
-            ],
-            compiler_params=params,
-        )(amount[None], near[None], need[None], own[None], source.reshape(span * 8, lanes))
-
+    codes = codes + jnp.where(inside(codes), 0, outside)
+    chunks = total + cells * GROUP // lanes + 3 * SPREAD
+    group_top = -(-(chunks * (lanes // GROUP) + SLACK) // (8 * lanes)) * 8 * lanes + 8 * lanes
     force_shape = (cells + 8, 3, 8, lanes)
-    scratch = [
-        pltpu.VMEM((chunks, 8, lanes), jnp.float32),
-        pltpu.VMEM((SPREAD * lanes, 8 * lanes), jnp.float32),
-        pltpu.VMEM((SPREAD * lanes, 8 * lanes), jnp.float32),
-        pltpu.VMEM((27, 8, lanes), jnp.float32),
-    ]
-
-    near, word, need, own = listed(codes, inner_amount, True)
-    z_before, z_after, near, need, own = lax.optimization_barrier(
-        (z_before, z_after, near, need, own)
-    )
+
+    def scratch(span):
+        return [
+            pltpu.VMEM((total, lanes), jnp.int32),
+            pltpu.VMEM((1, total), jnp.int32),
+            pltpu.VMEM((1, total), jnp.int32),
+            pltpu.VMEM((1, group_top), jnp.int32),
+            pltpu.SMEM((1, total), jnp.int32),
+            pltpu.SMEM((1, total), jnp.int32),
+            pltpu.SMEM((1, group_top), jnp.int32),
+            pltpu.SemaphoreType.DMA((3,)),
+            pltpu.VMEM((-(-span // lanes) * lanes, lanes), jnp.float32),
+            pltpu.VMEM((lanes, total), jnp.float32),
+            pltpu.VMEM((cells, lanes), jnp.float32),
+            pltpu.VMEM((1, total), jnp.int32),
+            pltpu.VMEM((1, total), jnp.int32),
+            pltpu.VMEM((1, total), jnp.int32),
+            pltpu.VMEM((chunks, 8, lanes), jnp.float32),
+            pltpu.VMEM((SPREAD * lanes, 8 * lanes), jnp.float32),
+            pltpu.VMEM((SPREAD * lanes, 8 * lanes), jnp.float32),
+            pltpu.VMEM((27, 8, lanes), jnp.float32),
+        ]
+
+    z_before, z_after, codes = lax.optimization_barrier((z_before, z_after, codes))
     x_before, x_after = exchange(
         jnp.concatenate([z_before[-1:], grid[-1:], z_after[-1:]], axis=2),
         jnp.concatenate([z_before[:1], grid[:1], z_after[:1]], axis=2),
         "gx",
     )
-    slots, where, cell_of = lists(near, need, own, inner_amount, table)
-    x_before, x_after, slots, where, cell_of = lax.optimization_barrier(
-        (x_before, x_after, slots, where, cell_of)
+    codes = jnp.sort(codes)
+    inner_amount = jnp.sum((codes < outside).astype(jnp.int32))
+    outer_amount = total - inner_amount
+    outer_codes = lax.dynamic_slice(jnp.concatenate([codes, codes]), (inner_amount,), (total,))
+    outer_codes = outer_codes & (outside - 1)
+    x_before, x_after, codes, outer_codes = lax.optimization_barrier(
+        (x_before, x_after, codes, outer_codes)
     )
 
     def face(at):
@@ -557,17 +570,14 @@
 
     y_before, y_after = exchange(face(slice(-1, None)), face(slice(0, 1)), "gy")
     inner = pl.pallas_call(
-        inner_kernel,
+        functools.partial(inner_kernel, near_inside, sizes),
         out_shape=jax.ShapeDtypeStruct(force_shape, jnp.float32),
-        in_specs=[smem] * 4 + [vmem] * 2,
+        in_specs=[smem] + [vmem] * 2,
         out_specs=vmem,
-        scratch_shapes=scratch,
+        scratch_shapes=scratch(cells),
         compiler_params=params,
-    )(inner_amount[None], where, word, cell_of, table, slots)
-
-    outer_amount = total - inner_amount
-    codes = lax.dynamic_slice(jnp.concatenate([codes, codes]), (inner_amount,), (total,))
-    near, word, need, own = listed(codes, outer_amount, False)
+    )(inner_amount[None], (codes & (outside - 1))[None], table)
+
     halo = jnp.concatenate(
         [
             part.reshape(-1, 8, lanes)
@@ -575,29 +585,19 @@
         ],
         axis=0,
     )
-    slots, where, cell_of = lists(near, need, own, outer_amount, halo)
     bricks = lax.axis_size(names)
     known = pl.pallas_call(
-        outer_kernel,
+        functools.partial(outer_kernel, near_outside, sizes),
         out_shape=jax.ShapeDtypeStruct((bricks, 8, lanes), jnp.float32),
-        in_specs=[smem] * 4 + [vmem] * 7,
+        in_specs=[smem] + [vmem] * 7,
         out_specs=vmem,
-        scratch_shapes=scratch
-        + [pltpu.VMEM(force_shape, jnp.float32), pltpu.VMEM((16, 8, lanes), jnp.float32)],
+        scratch_shapes=[
+            pltpu.VMEM(force_shape, jnp.float32),
+            pltpu.VMEM((16, 8, lanes), jnp.float32),
+        ]
+        + scratch(halo.shape[0]),
         compiler_params=params,
-    )(
-        outer_amount[None],
-        where,
-        word,
-        cell_of,
-        table.reshape(cells * 8, lanes),
-        halo,
-        slots,
-        inner,
-        flat_arms,
-        flat_frag,
-        fixed,
-    )
+    )(outer_amount[None], outer_codes[None], table, halo, inner, flat_arms, flat_frag, fixed)
     known = lax.all_to_all(known, names, split_axis=0, concat_axis=0, tiled=True)
 
     brick = lax.axis_index(names)

time: 138 us -> 137 us (level)
  waiting for transfers between devices: 7.02 us -> 16 us
  Pallas kernels: 96.7 us -> 91.3 us
  starting transfers between devices: 16.9 us -> 12.6 us
    ppermute x6, waiting for transfers between devices: 0.02 us -> 9.02 us  [exchange(): return (lax.ppermute(last, axis, up), lax.ppermute(initial, axis, down))]
    pallas_call x4 -> x2, Pallas kernels: 88.7 us -> 83.4 us  [the longest x1 56.4 us: local(): pl.pallas_call(functools.partial(inner_kernel, near_inside, sizes), out_s...]
    all_to_all x1, starting transfers between devices: 7.77 us -> 4.92 us  [local(): lax.all_to_all(known, names, split_axis=0, concat_axis=0, tiled=True)]
    ppermute x6, starting transfers between devices: 9.1 us -> 7.66 us  [exchange(): return (lax.ppermute(last, axis, up), lax.ppermute(initial, axis, down))]
    add x2 -> x1, other arithmetic: 1.45 us -> 0.06 us  [local(): codes = codes + jnp.where(inside(codes), 0, outside)]
  transfers between devices with their start and end apart: 7 -> 7, of which waited for: 1 -> 5; matrix products, arithmetic and copies ran while one was open for 8% -> 3% of each run, Pallas kernels for 41% -> 41%
where the time goes in v9:
time: 137 us
  Pallas kernels  91.3 us (67%)
  waiting for transfers between devices  16 us (12%)
  starting transfers between devices  12.6 us (9%)
  other arithmetic  9.02 us (7%)
  local copies, waits for them, and re-layouts  4.91 us (4%)
  between operations  3.36 us (2%)
    pallas_call x1, Pallas kernels, local(): pl.pallas_call(functools.partial(inner_kernel, near_inside, sizes), out_s...  56.4 us
    pallas_call x1, Pallas kernels, local(): pl.pallas_call(functools.partial(outer_kernel, near_outside, sizes), out_...  27 us
    ppermute x6, waiting for transfers between devices, exchange(): return (lax.ppermute(last, axis, up), lax.ppermute(initial, axis, down))  9.02 us
    ppermute x6, starting transfers between devices, exchange(): return (lax.ppermute(last, axis, up), lax.ppermute(initial, axis, down))  7.66 us
    all_to_all x1, waiting for transfers between devices, local(): lax.all_to_all(known, names, split_axis=0, concat_axis=0, tiled=True)  7 us
    sort x1, other arithmetic, local(): codes = jnp.sort(codes)  5.04 us
    pallas_call x1, Pallas kernels, local(): pl.pallas_call(functools.partial(move_kernel, owned), out_shape=(jax.Shap...  5.03 us
    all_to_all x1, starting transfers between devices, local(): lax.all_to_all(known, names, split_axis=0, concat_axis=0, tiled=True)  4.92 us
  transfers between devices with their start and end apart: 7, of which 5 were waited for; matrix products, arithmetic and copies ran while one was open for 3% of the time, Pallas kernels for 41%

profile of v9, /device:TPU:0, one launch (start us, length us, event | category | flops | bytes accessed | tf_op | source)
XLA Modules:
  0.0 137.2 jit_solution(3794240341124047288)
XLA Ops:
  0.6 0.7 fusion.14
  1.3 0.5 pad_bitcast_fusion
  1.8 2.9 %shard_map.104.table_ref = f32[256,8,128]{2,1,0:T(8,128)} custom-call(f32[7,256,128]{2,1,0:T(8,128)} %bitcast.40, s32[256,128]{1,0:T(8,128)} %bitcast.44, f32[1,128]{1,0:T(1,128)} %get-tuple-element.41.key_ref), custom_call_target="tpu_custom_call" | custom-call | tf_op jit(solution)/shard_map/pallas_call | solution.py:488
  4.8 1.0 fusion.17
  5.7 3.0 %collective-permute-start = (f32[4,4,1,8,128]{4,3,2,0,1:T(8,128)S(1)}, f32[4,4,1,8,128]{4,3,2,0,1:T(8,128)S(1)}, u32[]{:S(2)}, u32[]{:S(2)}) collective-permute-start(f32[4,4,1,8,128]{4,3,2,0,1:T(8,128)S(1)} %copy.20), channel_id=1, source_target_pairs={{0,1},{1,0},{2,3},{3,2},{4,5},{5,4},{6,7},{7,6},{8,9},{9,8},{10,11... | collective-permute-start | bytes 196616 | tf_op jit(solution)/shard_map/ppermute | solution.py:51
  8.9 1.1 fusion.16
  10.2 0.7 maximum_maximum_fusion.fixed_ref
  11.2 1.9 %collective-permute-done.1 = f32[4,4,1,8,128]{4,3,2,0,1:T(8,128)S(1)} collective-permute-done((f32[4,4,1,8,128]{4,3,2,0,1:T(8,128)S(1)}, f32[4,4,1,8,128]{4,3,2,0,1:T(8,128)S(1)}, u32[]{:S(2)}, u32[]{:S(2)}) %collective-permute-start.1) | collective-permute-done | bytes 65568 | tf_op jit(solution)/shard_map/ppermute | solution.py:51
  13.1 5.0 %sort.15 = (s32[2048]{0:T(1024)S(1)}, s32[2048]{0:T(1024)}) sort(s32[2048]{0:T(1024)S(1)} %select_add_fusion, s32[2048]{0:T(1024)S(1)} %iota.11), dimensions={0}, to_apply=%region_0.1 | sort | flops 22528 | bytes 32768 | tf_op jit(solution)/shard_map/jit(sort)/sort | solution.py:558
  18.1 0.6 convert_reduce_fusion
  22.0 0.7 fusion.10
  22.7 4.4 %collective-permute-done.3 = f32[1,4,18,8,128]{4,3,2,0,1:T(8,128)S(1)} collective-permute-done((f32[1,4,18,8,128]{4,3,2,0,1:T(8,128)S(1)}, f32[1,4,18,8,128]{4,3,2,0,1:T(8,128)S(1)}, u32[]{:S(2)}, u32[]{:S(2)}) %collective-permute-start.3) | collective-permute-done | bytes 294944 | tf_op jit(solution)/shard_map/ppermute | solution.py:51
  27.1 2.4 %collective-permute-done.2 = f32[1,4,18,8,128]{4,3,2,0,1:T(8,128)S(1)} collective-permute-done((f32[1,4,18,8,128]{4,3,2,0,1:T(8,128)S(1)}, f32[1,4,18,8,128]{4,3,2,0,1:T(8,128)S(1)}, u32[]{:S(2)}, u32[]{:S(2)}) %collective-permute-start.2) | collective-permute-done | bytes 294944 | tf_op jit(solution)/shard_map/ppermute | solution.py:51
  29.5 1.6 %collective-permute-start.4 = (f32[6,1,18,8,128]{4,3,2,0,1:T(8,128)S(1)}, f32[6,1,18,8,128]{4,3,2,0,1:T(8,128)S(1)}, u32[]{:S(2)}, u32[]{:S(2)}) collective-permute-start(f32[6,1,18,8,128]{4,3,2,0,1:T(8,128)S(1)} %pad_maximum_fusion), channel_id=1, source_target_pairs={{0,2},{2,4},{4,6},{6,0},{1,3},{3,5},{5,7},{7,1},{8,10},{10,12},{12... | collective-permute-start | bytes 1327112 | tf_op jit(solution)/shard_map/ppermute | solution.py:51
  31.2 2.3 %collective-permute-start.5 = (f32[6,1,18,8,128]{4,3,2,0,1:T(8,128)S(1)}, f32[6,1,18,8,128]{4,3,2,0,1:T(8,128)S(1)}, u32[]{:S(2)}, u32[]{:S(2)}) collective-permute-start(f32[6,1,18,8,128]{4,3,2,0,1:T(8,128)S(1)} %pad_maximum_fusion.1), channel_id=1, source_target_pairs={{2,0},{4,2},{6,4},{0,6},{3,1},{5,3},{7,5},{1,7},{10,8},{12,10},{14... | collective-permute-start | bytes 1327112 | tf_op jit(solution)/shard_map/ppermute | solution.py:51
  33.5 0.6 broadcast_and_fusion
  34.1 56.4 %shard_map.105.inner_ref = f32[264,3,8,128]{3,2,1,0:T(8,128)} custom-call(s32[1]{0:T(128)} %bitcast.19.amount_smem, s32[1,2048]{1,0:T(1,128)} %bitcast.56, f32[256,8,128]{2,1,0:T(8,128)} %shard_map.104.table_ref), custom_call_target="tpu_custom_call" | custom-call | tf_op jit(solution)/shard_map/pallas_call | solution.py:572
  90.7 1.2 copy-done.1
  91.8 27.0 %shard_map.106 = f32[32,8,128]{2,1,0:T(8,128)} custom-call(s32[1]{0:T(128)} %bitcast.7.amount_smem, s32[1,2048]{1,0:T(1,128)} %bitcast.55, f32[256,8,128]{2,1,0:T(8,128)} %shard_map.104.table_ref, f32[392,8,128]{2,1,0:T(8,128)} %copy-done.1, f32[264,3,8,128]{3,2,1,0:T(8,128)} %shard_map.105.inner_ref, f32[3,256,128]{2,1,0:T(8,128)} %bitcast.42, ...), custom_call_target="tpu_custom_call" | custom-call | tf_op jit(solution)/shard_map/pallas_call | solution.py:589
  118.8 4.9 %all-to-all-start = ((f32[32,8,128]{2,1,0:T(8,128)}), f32[32,8,128]{2,1,0:T(8,128)S(1)}, u32[]{:S(2)}, u32[]{:S(2)}) async-start(f32[32,8,128]{2,1,0:T(8,128)} %shard_map.106), calls=%async_computation | async-start | bytes 262144 | tf_op jit(solution)/shard_map/all_to_all | solution.py:601
  123.8 0.7 copy.19.target_ref
  124.5 7.0 %all-to-all-done.known_ref = f32[32,8,128]{2,1,0:T(8,128)S(1)} async-done(((f32[32,8,128]{2,1,0:T(8,128)}), f32[32,8,128]{2,1,0:T(8,128)S(1)}, u32[]{:S(2)}, u32[]{:S(2)}) %all-to-all-start) | async-done | bytes 131104 | tf_op jit(solution)/shard_map/all_to_all | solution.py:601
  131.5 0.7 copy-done.2
  132.2 5.0 %shard_map.107 = (f32[6,256,128]{2,1,0:T(8,128)}, f32[6,128]{1,0:T(8,128)}) custom-call(f32[128,1]{1,0:T(8,128)} %copy.19.target_ref, f32[32,8,128]{2,1,0:T(8,128)} %copy-done.2, f32[7,256,128]{2,1,0:T(8,128)} %bitcast.41, f32[3,256,128]{2,1,0:T(8,128)} %bitcast.43, s32[256,128]{1,0:T(8,128)} %bitcast.46), custom_call_target="tpu_custom_call" | custom-call | tf_op jit(solution)/shard_map/pallas_call | solution.py:608
  (45 shorter events, 1.5 us)
Async XLA Ops:
  4.7 5.2 %copy-start = (f32[256,8,128]{2,1,0:T(8,128)S(1)}, f32[256,8,128]{2,1,0:T(8,128)}, u32[]{:S(2)}) copy-start(f32[256,8,128]{2,1,0:T(8,128)} %shard_map.104.table_ref) | copy-start | bytes 3145732
  4.7 5.3 %copy-start.3 = (s32[1,2048]{1,0:T(1,128)S(1)}, s32[1,2048]{1,0:T(1,128)}, u32[]{:S(2)}) copy-start(s32[1,2048]{1,0:T(1,128)} %param.14) | copy-start | bytes 24580
  4.7 5.4 %copy-start.4 = (f32[6,48]{1,0:T(8,128)S(1)}, f32[6,48]{1,0:T(8,128)}, u32[]{:S(2)}) copy-start(f32[6,48]{1,0:T(8,128)} %param.15) | copy-start | bytes 3460
  4.7 5.4 %copy-start.5 = (f32[48]{0:T(128)S(1)}, f32[48]{0:T(128)}, u32[]{:S(2)}) copy-start(f32[48]{0:T(128)} %param.17) | copy-start | bytes 580
  4.7 5.4 %copy-start.6 = (f32[48]{0:T(128)S(1)}, f32[48]{0:T(128)}, u32[]{:S(2)}) copy-start(f32[48]{0:T(128)} %param.16) | copy-start | bytes 580
  5.7 5.4 %collective-permute-start = (f32[4,4,1,8,128]{4,3,2,0,1:T(8,128)S(1)}, f32[4,4,1,8,128]{4,3,2,0,1:T(8,128)S(1)}, u32[]{:S(2)}, u32[]{:S(2)}) collective-permute-start(f32[4,4,1,8,128]{4,3,2,0,1:T(8,128)S(1)} %copy.20), channel_id=1, source_target_pairs={{0,1},{1,0},{2,3},{3,2},{4,5},{5,4},{6,7},{7,6},{8,9},{9,8},{10,11... | collective-permute-start | bytes 196616 | tf_op jit(solution)/shard_map/ppermute | solution.py:51
  8.8 4.3 %collective-permute-start.1 = (f32[4,4,1,8,128]{4,3,2,0,1:T(8,128)S(1)}, f32[4,4,1,8,128]{4,3,2,0,1:T(8,128)S(1)}, u32[]{:S(2)}, u32[]{:S(2)}) collective-permute-start(f32[4,4,1,8,128]{4,3,2,0,1:T(8,128)S(1)} %copy.21), channel_id=1, source_target_pairs={{1,0},{0,1},{3,2},{2,3},{5,4},{4,5},{7,6},{6,7},{9,8},{8,9},{11,10... | collective-permute-start | bytes 196616 | tf_op jit(solution)/shard_map/ppermute | solution.py:51
  20.1 7.0 %collective-permute-start.3 = (f32[1,4,18,8,128]{4,3,2,0,1:T(8,128)S(1)}, f32[1,4,18,8,128]{4,3,2,0,1:T(8,128)S(1)}, u32[]{:S(2)}, u32[]{:S(2)}) collective-permute-start(f32[1,4,18,8,128]{4,3,2,0,1:T(8,128)S(1)} %pad_maximum_fusion.3), channel_id=1, source_target_pairs={{8,0},{16,8},{24,16},{0,24},{9,1},{17,9},{25,17},{1,25},{10,2},{18... | collective-permute-start | bytes 884744 | tf_op jit(solution)/shard_map/ppermute | solution.py:51
  20.4 9.1 %collective-permute-start.2 = (f32[1,4,18,8,128]{4,3,2,0,1:T(8,128)S(1)}, f32[1,4,18,8,128]{4,3,2,0,1:T(8,128)S(1)}, u32[]{:S(2)}, u32[]{:S(2)}) collective-permute-start(f32[1,4,18,8,128]{4,3,2,0,1:T(8,128)S(1)} %pad_maximum_fusion.2), channel_id=1, source_target_pairs={{0,8},{8,16},{16,24},{24,0},{1,9},{9,17},{17,25},{25,1},{2,10},{10... | collective-permute-start | bytes 884744 | tf_op jit(solution)/shard_map/ppermute | solution.py:51
  29.5 61.0 %collective-permute-start.4 = (f32[6,1,18,8,128]{4,3,2,0,1:T(8,128)S(1)}, f32[6,1,18,8,128]{4,3,2,0,1:T(8,128)S(1)}, u32[]{:S(2)}, u32[]{:S(2)}) collective-permute-start(f32[6,1,18,8,128]{4,3,2,0,1:T(8,128)S(1)} %pad_maximum_fusion), channel_id=1, source_target_pairs={{0,2},{2,4},{4,6},{6,0},{1,3},{3,5},{5,7},{7,1},{8,10},{10,12},{12... | collective-permute-start | bytes 1327112 | tf_op jit(solution)/shard_map/ppermute | solution.py:51
  31.2 59.4 %collective-permute-start.5 = (f32[6,1,18,8,128]{4,3,2,0,1:T(8,128)S(1)}, f32[6,1,18,8,128]{4,3,2,0,1:T(8,128)S(1)}, u32[]{:S(2)}, u32[]{:S(2)}) collective-permute-start(f32[6,1,18,8,128]{4,3,2,0,1:T(8,128)S(1)} %pad_maximum_fusion.1), channel_id=1, source_target_pairs={{2,0},{4,2},{6,4},{0,6},{3,1},{5,3},{7,5},{1,7},{10,8},{12,10},{14... | collective-permute-start | bytes 1327112 | tf_op jit(solution)/shard_map/ppermute | solution.py:51
  90.7 1.2 copy-start.1
  118.8 12.7 %all-to-all-start = ((f32[32,8,128]{2,1,0:T(8,128)}), f32[32,8,128]{2,1,0:T(8,128)S(1)}, u32[]{:S(2)}, u32[]{:S(2)}) async-start(f32[32,8,128]{2,1,0:T(8,128)} %shard_map.106), calls=%async_computation | async-start | bytes 262144 | tf_op jit(solution)/shard_map/all_to_all | solution.py:601
  131.5 0.7 copy-start.2

commit v10 on v9

--- a/solution.py
+++ b/solution.py
@@ -51,14 +51,19 @@
     return lax.ppermute(last, axis, up), lax.ppermute(initial, axis, down)
 
 
-def pack_kernel(state_ref, frag_ref, key_ref, out_ref):
-    cells = frag_ref.shape[0]
+def pack_kernel(deep, state_ref, frag_ref, key_ref, out_ref, last_ref, first_ref):
+    cells, lanes = frag_ref.shape
+    held = key_ref.shape[1]
     for comp in range(7):
         out_ref[:, comp, :] = state_ref[comp]
-    keys = jnp.broadcast_to(key_ref[0:1, :], (8, key_ref.shape[1]))
+    keys = jnp.concatenate([key_ref[0:1, :], jnp.zeros((1, lanes - held), jnp.float32)], axis=1)
+    keys = jnp.broadcast_to(keys, (8, lanes))
     for block in range(cells // 8):
         rows = pl.ds(block * 8, 8)
         out_ref[rows, 7, :] = lanes_of(keys, frag_ref[rows, :])
+    for column in range(cells // deep):
+        first_ref[column] = out_ref[column * deep]
+        last_ref[column] = out_ref[column * deep + deep - 1]
 
 
 def list_tiles(
@@ -314,41 +319,55 @@
     lax.fori_loop(0, steps, both, (jnp.int32(-1), [zero] * 3))
 
 
-def forces(
-    amount, near_of, sizes, code_ref, table_ref, near_table_ref, force_ref,
-    slots_ref, where_ref, word_ref, cell_ref, where_smem, word_smem, cell_smem, sems,
-    class_ref, member_ref, count_ref, near_ref, need_ref, own_ref,
-    list_ref, even_ref, odd_ref, shift_ref,
-):
-    cells, _, lanes = table_ref.shape
-    groups = list_tiles(
-        amount, near_of, sizes, code_ref, near_table_ref, slots_ref, where_ref, word_ref, cell_ref,
-        class_ref, member_ref, count_ref, near_ref, need_ref, own_ref,
-    )
+def to_scalars(pairs, sems):
     copies = [
-        pltpu.make_async_copy(where_ref, where_smem, sems.at[0]),
-        pltpu.make_async_copy(word_ref, word_smem, sems.at[1]),
-        pltpu.make_async_copy(cell_ref, cell_smem, sems.at[2]),
+        pltpu.make_async_copy(source, target, sems.at[number])
+        for number, (source, target) in enumerate(pairs)
     ]
     for copy in copies:
         copy.start()
     for copy in copies:
         copy.wait()
-    fill_lists(amount, where_smem, word_smem, near_table_ref, slots_ref, shift_ref, list_ref)
+
+
+def list_kernel(
+    near_of, sizes, amount_smem, code_ref, table_ref, slots_ref, where_ref, word_ref, cell_ref,
+    groups_smem, *scratch,
+):
+    groups_smem[0] = list_tiles(
+        amount_smem[0], near_of, sizes, code_ref, table_ref, slots_ref, where_ref, word_ref,
+        cell_ref, *scratch,
+    )
+
+
+def inner_kernel(
+    amount_smem, where_smem, word_smem, cell_smem, groups_smem, table_ref, slots_ref, force_ref,
+    list_ref, even_ref, odd_ref, shift_ref,
+):
+    cells, _, lanes = table_ref.shape
+    fill_lists(amount_smem[0], where_smem, word_smem, table_ref, slots_ref, shift_ref, list_ref)
+    flat = table_ref.reshape(cells * 8, lanes)
+    pair_forces(groups_smem[0], cell_smem, flat, list_ref, force_ref, even_ref, odd_ref)
+
+
+def outer_kernel(
+    near_of, sizes, amount_smem, code_ref, table_ref, halo_ref, inner_ref, arms_ref, frag_ref,
+    fixed_ref, out_ref, force_ref, loads_ref, slots_ref, where_ref, word_ref, cell_ref,
+    where_smem, word_smem, cell_smem, sems, list_ref, even_ref, odd_ref, shift_ref, *scratch,
+):
+    cells, _, lanes = table_ref.shape
+    held = fixed_ref.shape[1] // 2
+    amount = amount_smem[0]
+    groups = list_tiles(
+        amount, near_of, sizes, code_ref, halo_ref, slots_ref, where_ref, word_ref, cell_ref,
+        *scratch,
+    )
+    to_scalars(
+        [(where_ref, where_smem), (word_ref, word_smem), (cell_ref, cell_smem)], sems
+    )
+    fill_lists(amount, where_smem, word_smem, halo_ref, slots_ref, shift_ref, list_ref)
     flat = table_ref.reshape(cells * 8, lanes)
     pair_forces(groups, cell_smem, flat, list_ref, force_ref, even_ref, odd_ref)
-
-
-def inner_kernel(near_of, sizes, amount_smem, code_ref, table_ref, force_ref, *scratch):
-    forces(amount_smem[0], near_of, sizes, code_ref, table_ref, table_ref, force_ref, *scratch)
-
-
-def outer_kernel(
-    near_of, sizes, amount_smem, code_ref, table_ref, halo_ref, inner_ref, arms_ref, frag_ref,
-    fixed_ref, out_ref, force_ref, loads_ref, *scratch,
-):
-    held = fixed_ref.shape[1] // 2
-    forces(amount_smem[0], near_of, sizes, code_ref, table_ref, halo_ref, force_ref, *scratch)
     sums = fragment_sums(inner_ref, force_ref, arms_ref, frag_ref, loads_ref, held)
     out = fixed_ref[...] + jnp.concatenate([sums, jnp.zeros_like(sums)], axis=1)
     for brick in range(out_ref.shape[0]):
@@ -359,13 +378,25 @@
     cells, lanes = frag_ref.shape
     tall = loads_ref.shape[0]
     label = lax.broadcasted_iota(jnp.int32, (held, lanes), 0)
+    parts = [
+        ref.reshape(ref.shape[0] * 24, lanes) for ref in (inner_ref, outer_ref)
+    ]
+
+    def total_force(block, axis):
+        halves = []
+        for half in range(tall // 8):
+            first = (block * tall + half * 8) * 24 + axis * 8
+            rows = [
+                ref[pl.ds(first + part, 8, stride=24), :] for ref in parts for part in range(8)
+            ]
+            while len(rows) > 1:
+                rows = [one + other for one, other in zip(rows[::2], rows[1::2])]
+            halves.append(rows[0])
+        return -damping * jnp.concatenate(halves, axis=0)
 
     def gather_sums(block, total):
         rows = pl.ds(pl.multiple_of(block * tall, tall), tall)
-        force = [
-            -damping * jnp.sum(inner_ref[rows, axis] + outer_ref[rows, axis], axis=1)
-            for axis in range(3)
-        ]
+        force = [total_force(block, axis) for axis in range(3)]
         lever = [arms_ref[axis, rows, :] for axis in range(3)]
         torque = [
             lever[1] * force[2] - lever[2] * force[1],
@@ -485,15 +516,20 @@
         axis=1,
     )
 
-    table = pl.pallas_call(
-        pack_kernel,
-        out_shape=jax.ShapeDtypeStruct((cells, 8, lanes), jnp.float32),
+    face_shape = jax.ShapeDtypeStruct((cells_x * cells_y, 8, lanes), jnp.float32)
+    table, z_last, z_first = pl.pallas_call(
+        functools.partial(pack_kernel, cells_z),
+        out_shape=(jax.ShapeDtypeStruct((cells, 8, lanes), jnp.float32), face_shape, face_shape),
         in_specs=[vmem] * 3,
-        out_specs=vmem,
+        out_specs=(vmem,) * 3,
         compiler_params=params,
-    )(flat_state, flat_frag, jnp.pad(frag_key, (0, lanes - held))[None])
+    )(flat_state, flat_frag, frag_key[None])
     grid = table.reshape(cells_x, cells_y, cells_z, 8, lanes)
-    z_before, z_after = exchange(grid[:, :, -1:], grid[:, :, :1], "gz")
+    z_before, z_after = exchange(
+        z_last.reshape(cells_x, cells_y, 1, 8, lanes),
+        z_first.reshape(cells_x, cells_y, 1, 8, lanes),
+        "gz",
+    )
 
     outside = 1 << 20
     span_z = cells_z + 2
@@ -527,41 +563,46 @@
     group_top = -(-(chunks * (lanes // GROUP) + SLACK) // (8 * lanes)) * 8 * lanes + 8 * lanes
     force_shape = (cells + 8, 3, 8, lanes)
 
-    def scratch(span):
+    list_shapes = [(total, lanes), (1, total), (1, total), (1, group_top)]
+
+    def list_scratch(span):
         return [
-            pltpu.VMEM((total, lanes), jnp.int32),
-            pltpu.VMEM((1, total), jnp.int32),
-            pltpu.VMEM((1, total), jnp.int32),
-            pltpu.VMEM((1, group_top), jnp.int32),
-            pltpu.SMEM((1, total), jnp.int32),
-            pltpu.SMEM((1, total), jnp.int32),
-            pltpu.SMEM((1, group_top), jnp.int32),
-            pltpu.SemaphoreType.DMA((3,)),
             pltpu.VMEM((-(-span // lanes) * lanes, lanes), jnp.float32),
             pltpu.VMEM((lanes, total), jnp.float32),
             pltpu.VMEM((cells, lanes), jnp.float32),
             pltpu.VMEM((1, total), jnp.int32),
             pltpu.VMEM((1, total), jnp.int32),
             pltpu.VMEM((1, total), jnp.int32),
-            pltpu.VMEM((chunks, 8, lanes), jnp.float32),
-            pltpu.VMEM((SPREAD * lanes, 8 * lanes), jnp.float32),
-            pltpu.VMEM((SPREAD * lanes, 8 * lanes), jnp.float32),
-            pltpu.VMEM((27, 8, lanes), jnp.float32),
         ]
 
-    z_before, z_after, codes = lax.optimization_barrier((z_before, z_after, codes))
+    pair_scratch = [
+        pltpu.VMEM((chunks, 8, lanes), jnp.float32),
+        pltpu.VMEM((SPREAD * lanes, 8 * lanes), jnp.float32),
+        pltpu.VMEM((SPREAD * lanes, 8 * lanes), jnp.float32),
+        pltpu.VMEM((27, 8, lanes), jnp.float32),
+    ]
+
+    codes = jnp.sort(codes)
+    inner_amount = jnp.sum((codes < outside).astype(jnp.int32))
+    outer_amount = total - inner_amount
+    z_before, z_after, codes, inner_amount = lax.optimization_barrier(
+        (z_before, z_after, codes, inner_amount)
+    )
     x_before, x_after = exchange(
         jnp.concatenate([z_before[-1:], grid[-1:], z_after[-1:]], axis=2),
         jnp.concatenate([z_before[:1], grid[:1], z_after[:1]], axis=2),
         "gx",
     )
-    codes = jnp.sort(codes)
-    inner_amount = jnp.sum((codes < outside).astype(jnp.int32))
-    outer_amount = total - inner_amount
-    outer_codes = lax.dynamic_slice(jnp.concatenate([codes, codes]), (inner_amount,), (total,))
-    outer_codes = outer_codes & (outside - 1)
-    x_before, x_after, codes, outer_codes = lax.optimization_barrier(
-        (x_before, x_after, codes, outer_codes)
+    slots, where, word, cell_of, groups = pl.pallas_call(
+        functools.partial(list_kernel, near_inside, sizes),
+        out_shape=tuple(jax.ShapeDtypeStruct(shape, jnp.int32) for shape in list_shapes + [(1,)]),
+        in_specs=[smem, vmem, vmem],
+        out_specs=(vmem,) * 4 + (smem,),
+        scratch_shapes=list_scratch(cells),
+        compiler_params=params,
+    )(inner_amount[None], (codes & (outside - 1))[None], table)
+    x_before, x_after, slots, where, word, cell_of, groups = lax.optimization_barrier(
+        (x_before, x_after, slots, where, word, cell_of, groups)
     )
 
     def face(at):
@@ -570,14 +611,16 @@
 
     y_before, y_after = exchange(face(slice(-1, None)), face(slice(0, 1)), "gy")
     inner = pl.pallas_call(
-        functools.partial(inner_kernel, near_inside, sizes),
+        inner_kernel,
         out_shape=jax.ShapeDtypeStruct(force_shape, jnp.float32),
-        in_specs=[smem] + [vmem] * 2,
+        in_specs=[smem] * 5 + [vmem] * 2,
         out_specs=vmem,
-        scratch_shapes=scratch(cells),
+        scratch_shapes=pair_scratch,
         compiler_params=params,
-    )(inner_amount[None], (codes & (outside - 1))[None], table)
-
+    )(inner_amount[None], where, word, cell_of, groups, table, slots)
+
+    outer_codes = lax.dynamic_slice(jnp.concatenate([codes, codes]), (inner_amount,), (total,))
+    outer_codes = outer_codes & (outside - 1)
     halo = jnp.concatenate(
         [
             part.reshape(-1, 8, lanes)
@@ -595,7 +638,11 @@
             pltpu.VMEM(force_shape, jnp.float32),
             pltpu.VMEM((16, 8, lanes), jnp.float32),
         ]
-        + scratch(halo.shape[0]),
+        + [pltpu.VMEM(shape, jnp.int32) for shape in list_shapes]
+        + [pltpu.SMEM(shape, jnp.int32) for shape in list_shapes[1:]]
+        + [pltpu.SemaphoreType.DMA((3,))]
+        + pair_scratch
+        + list_scratch(halo.shape[0]),
         compiler_params=params,
     )(outer_amount[None], outer_codes[None], table, halo, inner, flat_arms, flat_frag, fixed)
     known = lax.all_to_all(known, names, split_axis=0, concat_axis=0, tiled=True)

time: 137 us -> 133 us (0.971)
  waiting for transfers between devices: 16 us -> 6.95 us
  starting transfers between devices: 12.6 us -> 16.3 us
    ppermute x6, waiting for transfers between devices: 9.02 us -> 0.02 us  [exchange(): return (lax.ppermute(last, axis, up), lax.ppermute(initial, axis, down))]
    all_to_all x1, starting transfers between devices: 4.92 us -> 7.05 us  [local(): lax.all_to_all(known, names, split_axis=0, concat_axis=0, tiled=True)]
    reshape x0 -> x2, local copies, waits for them, and re-layouts: none -> 1.78 us  [the longest x1 0.93 us: local(): z_last.reshape(cells_x, cells_y, 1, 8, lanes)]
    ppermute x6, starting transfers between devices: 7.66 us -> 9.22 us  [exchange(): return (lax.ppermute(last, axis, up), lax.ppermute(initial, axis, down))]
    pallas_call x2 -> x3, Pallas kernels: 59.3 us -> 58.9 us  [the longest x1 46.7 us: local(): pl.pallas_call(inner_kernel, out_shape=jax.ShapeDtypeStruct(force_shape,...]
  transfers between devices with their start and end apart: 7 -> 7, of which waited for: 5 -> 1; matrix products, arithmetic and copies ran while one was open for 3% -> 8% of each run, Pallas kernels for 41% -> 42%
where the time goes in v10:
time: 133 us; the launch traced here: 134 us
  Pallas kernels  92 us (69%)
  starting transfers between devices  16.3 us (12%)
  other arithmetic  9.23 us (7%)
  waiting for transfers between devices  6.95 us (5%)
  local copies, waits for them, and re-layouts  5.71 us (4%)
  between operations  3.43 us (3%)
    pallas_call x1, Pallas kernels, local(): pl.pallas_call(inner_kernel, out_shape=jax.ShapeDtypeStruct(force_shape,...  46.7 us
    pallas_call x1, Pallas kernels, local(): pl.pallas_call(functools.partial(outer_kernel, near_outside, sizes), out_...  28.2 us
    pallas_call x1, Pallas kernels, local(): pl.pallas_call(functools.partial(list_kernel, near_inside, sizes), out_sh...  9.25 us
    ppermute x6, starting transfers between devices, exchange(): return (lax.ppermute(last, axis, up), lax.ppermute(initial, axis, down))  9.22 us
    all_to_all x1, starting transfers between devices, local(): lax.all_to_all(known, names, split_axis=0, concat_axis=0, tiled=True)  7.05 us
    all_to_all x1, waiting for transfers between devices, local(): lax.all_to_all(known, names, split_axis=0, concat_axis=0, tiled=True)  6.93 us
    sort x1, other arithmetic, local(): codes = jnp.sort(codes)  5.04 us
    pallas_call x1, Pallas kernels, local(): pl.pallas_call(functools.partial(move_kernel, owned), out_shape=(jax.Shap...  5.03 us
  transfers between devices with their start and end apart: 7, of which 1 were waited for; matrix products, arithmetic and copies ran while one was open for 8% of the time, Pallas kernels for 42%

profile of v10, /device:TPU:0, one launch (start us, length us, event | category | flops | bytes accessed | tf_op | source)
XLA Modules:
  0.0 133.6 jit_solution(8859765733235445114)
XLA Ops:
  0.6 1.2 fusion.14
  1.8 2.9 %shard_map.104 = (f32[256,8,128]{2,1,0:T(8,128)}, f32[16,8,128]{2,1,0:T(8,128)}, f32[16,8,128]{2,1,0:T(8,128)}) custom-call(f32[7,256,128]{2,1,0:T(8,128)} %bitcast.39, s32[256,128]{1,0:T(8,128)} %bitcast.43, f32[1,64]{1,0:T(1,128)} %bitcast.59), custom_call_target="tpu_custom_call" | custom-call | tf_op jit(solution)/shard_map/pallas_call | solution.py:520
  4.8 0.9 copy.11
  5.7 3.0 %collective-permute-start = (f32[4,4,1,8,128]{4,3,2,0,1:T(8,128)S(1)}, f32[4,4,1,8,128]{4,3,2,0,1:T(8,128)S(1)}, u32[]{:S(2)}, u32[]{:S(2)}) collective-permute-start(f32[4,4,1,8,128]{4,3,2,0,1:T(8,128)S(1)} %copy.11), channel_id=1, source_target_pairs={{0,1},{1,0},{2,3},{3,2},{4,5},{5,4},{6,7},{7,6},{8,9},{9,8},{10,11... | collective-permute-start | bytes 196616 | tf_op jit(solution)/shard_map/ppermute | solution.py:51
  8.7 0.8 copy.12
  9.5 0.8 select_add_fusion
  10.3 1.1 fusion.16
  11.4 5.0 %sort.15 = (s32[2048]{0:T(1024)S(1)}, s32[2048]{0:T(1024)}) sort(s32[2048]{0:T(1024)S(1)} %select_add_fusion, s32[2048]{0:T(1024)S(1)} %iota.11), dimensions={0}, to_apply=%region_0.1 | sort | flops 22528 | bytes 32768 | tf_op jit(solution)/shard_map/jit(sort)/sort | solution.py:585
  16.4 0.1 pad.6.clone
  16.5 0.7 maximum_maximum_fusion.fixed_ref
  17.2 0.7 convert_reduce_fusion
  20.0 1.8 %collective-permute-start.3 = (f32[1,4,18,8,128]{4,3,2,0,1:T(8,128)S(1)}, f32[1,4,18,8,128]{4,3,2,0,1:T(8,128)S(1)}, u32[]{:S(2)}, u32[]{:S(2)}) collective-permute-start(f32[1,4,18,8,128]{4,3,2,0,1:T(8,128)S(1)} %pad_maximum_fusion.3), channel_id=1, source_target_pairs={{8,0},{16,8},{24,16},{0,24},{9,1},{17,9},{25,17},{1,25},{10,2},{18... | collective-permute-start | bytes 884744 | tf_op jit(solution)/shard_map/ppermute | solution.py:51
  22.4 0.7 broadcast_and_fusion
  23.1 9.2 %shard_map.105 = (s32[2048,128]{1,0:T(8,128)}, s32[1,2048]{1,0:T(1,128)}, s32[1,2048]{1,0:T(1,128)}, s32[1,18432]{1,0:T(1,128)}, s32[1]{0:T(128)}) custom-call(s32[1]{0:T(128)} %bitcast.16.amount_smem, s32[1,2048]{1,0:T(1,128)} %bitcast.57, f32[256,8,128]{2,1,0:T(8,128)} %get-tuple-element.30.table_ref), custom_call_target="tpu_custom_call" | custom-call | tf_op jit(solution)/shard_map/pallas_call | solution.py:596
  32.5 2.3 %collective-permute-start.4 = (f32[6,1,18,8,128]{4,3,2,0,1:T(8,128)S(1)}, f32[6,1,18,8,128]{4,3,2,0,1:T(8,128)S(1)}, u32[]{:S(2)}, u32[]{:S(2)}) collective-permute-start(f32[6,1,18,8,128]{4,3,2,0,1:T(8,128)S(1)} %pad_maximum_fusion), channel_id=1, source_target_pairs={{0,2},{2,4},{4,6},{6,0},{1,3},{3,5},{5,7},{7,1},{8,10},{10,12},{12... | collective-permute-start | bytes 1327112 | tf_op jit(solution)/shard_map/ppermute | solution.py:51
  34.9 2.1 %collective-permute-start.5 = (f32[6,1,18,8,128]{4,3,2,0,1:T(8,128)S(1)}, f32[6,1,18,8,128]{4,3,2,0,1:T(8,128)S(1)}, u32[]{:S(2)}, u32[]{:S(2)}) collective-permute-start(f32[6,1,18,8,128]{4,3,2,0,1:T(8,128)S(1)} %pad_maximum_fusion.1), channel_id=1, source_target_pairs={{2,0},{4,2},{6,4},{0,6},{3,1},{5,3},{7,5},{1,7},{10,8},{12,10},{14... | collective-permute-start | bytes 1327112 | tf_op jit(solution)/shard_map/ppermute | solution.py:51
  37.0 46.7 %shard_map.106.inner_ref = f32[264,3,8,128]{3,2,1,0:T(8,128)} custom-call(s32[1]{0:T(128)} %bitcast.16.amount_smem, s32[1,2048]{1,0:T(1,128)} %get-tuple-element.40.where_smem, s32[1,2048]{1,0:T(1,128)} %get-tuple-element.41.word_smem, s32[1,18432]{1,0:T(1,128)} %get-tuple-element.42.cell_smem, s32[1]{0:T(128)} %get-tuple-element.43.groups_smem, ...), custom_call_target="tpu_custom_call" | custom-call | tf_op jit(solution)/shard_map/pallas_call | solution.py:613
  83.8 1.2 copy-done.1
  85.0 28.2 %shard_map.107 = f32[32,8,128]{2,1,0:T(8,128)} custom-call(s32[1]{0:T(128)} %bitcast.3.amount_smem, s32[1,2048]{1,0:T(1,128)} %bitcast.56, f32[256,8,128]{2,1,0:T(8,128)} %get-tuple-element.30.table_ref, f32[392,8,128]{2,1,0:T(8,128)} %copy-done.1, f32[264,3,8,128]{3,2,1,0:T(8,128)} %shard_map.106.inner_ref, f32[3,256,128]{2,1,0:T(8,128)} %bitcast.41, ...), custom_call_target="tpu_custom_call" | custom-call | tf_op jit(solution)/shard_map/pallas_call | solution.py:632
  113.1 7.0 %all-to-all-start = ((f32[32,8,128]{2,1,0:T(8,128)}), f32[32,8,128]{2,1,0:T(8,128)S(1)}, u32[]{:S(2)}, u32[]{:S(2)}) async-start(f32[32,8,128]{2,1,0:T(8,128)} %shard_map.107), calls=%async_computation | async-start | bytes 262144 | tf_op jit(solution)/shard_map/all_to_all | solution.py:648
  120.3 0.7 copy.19.target_ref
  121.0 6.9 %all-to-all-done.known_ref = f32[32,8,128]{2,1,0:T(8,128)S(1)} async-done(((f32[32,8,128]{2,1,0:T(8,128)}), f32[32,8,128]{2,1,0:T(8,128)S(1)}, u32[]{:S(2)}, u32[]{:S(2)}) %all-to-all-start) | async-done | bytes 131104 | tf_op jit(solution)/shard_map/all_to_all | solution.py:648
  127.9 0.7 copy-done.2
  128.6 5.0 %shard_map.108 = (f32[6,256,128]{2,1,0:T(8,128)}, f32[6,128]{1,0:T(8,128)}) custom-call(f32[128,1]{1,0:T(8,128)} %copy.19.target_ref, f32[32,8,128]{2,1,0:T(8,128)} %copy-done.2, f32[7,256,128]{2,1,0:T(8,128)} %bitcast.40, f32[3,256,128]{2,1,0:T(8,128)} %bitcast.42, s32[256,128]{1,0:T(8,128)} %bitcast.45), custom_call_target="tpu_custom_call" | custom-call | tf_op jit(solution)/shard_map/pallas_call | solution.py:655
  (44 shorter events, 0.5 us)
Async XLA Ops:
  1.8 14.7 %copy-start.3 = (f32[64]{0:T(128)S(1)}, f32[64]{0:T(128)}, u32[]{:S(2)}) copy-start(f32[64]{0:T(128)} %get-tuple-element.66) | copy-start | bytes 772
  1.8 14.7 %copy-start.4 = (f32[6,48]{1,0:T(8,128)S(1)}, f32[6,48]{1,0:T(8,128)}, u32[]{:S(2)}) copy-start(f32[6,48]{1,0:T(8,128)} %param.15) | copy-start | bytes 3460
  1.8 14.7 %copy-start.5 = (f32[48]{0:T(128)S(1)}, f32[48]{0:T(128)}, u32[]{:S(2)}) copy-start(f32[48]{0:T(128)} %param.17) | copy-start | bytes 580
  1.8 14.7 %copy-start.6 = (f32[48]{0:T(128)S(1)}, f32[48]{0:T(128)}, u32[]{:S(2)}) copy-start(f32[48]{0:T(128)} %param.16) | copy-start | bytes 580
  4.8 6.6 %copy-start = (f32[256,8,128]{2,1,0:T(8,128)S(1)}, f32[256,8,128]{2,1,0:T(8,128)}, u32[]{:S(2)}) copy-start(f32[256,8,128]{2,1,0:T(8,128)} %get-tuple-element.30.table_ref) | copy-start | bytes 3145732
  5.7 12.8 %collective-permute-start = (f32[4,4,1,8,128]{4,3,2,0,1:T(8,128)S(1)}, f32[4,4,1,8,128]{4,3,2,0,1:T(8,128)S(1)}, u32[]{:S(2)}, u32[]{:S(2)}) collective-permute-start(f32[4,4,1,8,128]{4,3,2,0,1:T(8,128)S(1)} %copy.11), channel_id=1, source_target_pairs={{0,1},{1,0},{2,3},{3,2},{4,5},{5,4},{6,7},{7,6},{8,9},{9,8},{10,11... | collective-permute-start | bytes 196616 | tf_op jit(solution)/shard_map/ppermute | solution.py:51
  9.5 9.0 %collective-permute-start.1 = (f32[4,4,1,8,128]{4,3,2,0,1:T(8,128)S(1)}, f32[4,4,1,8,128]{4,3,2,0,1:T(8,128)S(1)}, u32[]{:S(2)}, u32[]{:S(2)}) collective-permute-start(f32[4,4,1,8,128]{4,3,2,0,1:T(8,128)S(1)} %copy.12), channel_id=1, source_target_pairs={{1,0},{0,1},{3,2},{2,3},{5,4},{4,5},{7,6},{6,7},{9,8},{8,9},{11,10... | collective-permute-start | bytes 196616 | tf_op jit(solution)/shard_map/ppermute | solution.py:51
  19.9 12.5 %collective-permute-start.2 = (f32[1,4,18,8,128]{4,3,2,0,1:T(8,128)S(1)}, f32[1,4,18,8,128]{4,3,2,0,1:T(8,128)S(1)}, u32[]{:S(2)}, u32[]{:S(2)}) collective-permute-start(f32[1,4,18,8,128]{4,3,2,0,1:T(8,128)S(1)} %pad_maximum_fusion.2), channel_id=1, source_target_pairs={{0,8},{8,16},{16,24},{24,0},{1,9},{9,17},{17,25},{25,1},{2,10},{10... | collective-permute-start | bytes 884744 | tf_op jit(solution)/shard_map/ppermute | solution.py:51
  20.0 12.4 %collective-permute-start.3 = (f32[1,4,18,8,128]{4,3,2,0,1:T(8,128)S(1)}, f32[1,4,18,8,128]{4,3,2,0,1:T(8,128)S(1)}, u32[]{:S(2)}, u32[]{:S(2)}) collective-permute-start(f32[1,4,18,8,128]{4,3,2,0,1:T(8,128)S(1)} %pad_maximum_fusion.3), channel_id=1, source_target_pairs={{8,0},{16,8},{24,16},{0,24},{9,1},{17,9},{25,17},{1,25},{10,2},{18... | collective-permute-start | bytes 884744 | tf_op jit(solution)/shard_map/ppermute | solution.py:51
  32.5 51.2 %collective-permute-start.4 = (f32[6,1,18,8,128]{4,3,2,0,1:T(8,128)S(1)}, f32[6,1,18,8,128]{4,3,2,0,1:T(8,128)S(1)}, u32[]{:S(2)}, u32[]{:S(2)}) collective-permute-start(f32[6,1,18,8,128]{4,3,2,0,1:T(8,128)S(1)} %pad_maximum_fusion), channel_id=1, source_target_pairs={{0,2},{2,4},{4,6},{6,0},{1,3},{3,5},{5,7},{7,1},{8,10},{10,12},{12... | collective-permute-start | bytes 1327112 | tf_op jit(solution)/shard_map/ppermute | solution.py:51
  34.9 48.9 %collective-permute-start.5 = (f32[6,1,18,8,128]{4,3,2,0,1:T(8,128)S(1)}, f32[6,1,18,8,128]{4,3,2,0,1:T(8,128)S(1)}, u32[]{:S(2)}, u32[]{:S(2)}) collective-permute-start(f32[6,1,18,8,128]{4,3,2,0,1:T(8,128)S(1)} %pad_maximum_fusion.1), channel_id=1, source_target_pairs={{2,0},{4,2},{6,4},{0,6},{3,1},{5,3},{7,5},{1,7},{10,8},{12,10},{14... | collective-permute-start | bytes 1327112 | tf_op jit(solution)/shard_map/ppermute | solution.py:51
  83.8 1.2 copy-start.1
  113.1 14.8 %all-to-all-start = ((f32[32,8,128]{2,1,0:T(8,128)}), f32[32,8,128]{2,1,0:T(8,128)S(1)}, u32[]{:S(2)}, u32[]{:S(2)}) async-start(f32[32,8,128]{2,1,0:T(8,128)} %shard_map.107), calls=%async_computation | async-start | bytes 262144 | tf_op jit(solution)/shard_map/all_to_all | solution.py:648
  127.9 0.7 copy-start.2

commit v11 on v10

--- a/solution.py
+++ b/solution.py
@@ -14,7 +14,7 @@
 epsilon_sq = 1e-08
 radius_top = 0.14
 
-GROUP = 16
+GROUP = 32
 FILL = 32
 SLACK = 256
 SPREAD = 4
@@ -75,7 +75,7 @@
     padded = class_ref.shape[0]
     cells = count_ref.shape[0]
     wide = 256
-    parts = 4
+    parts = 2
     flat = table_ref.reshape(span * 8, lanes)
 
     def plane(comp):
@@ -142,13 +142,13 @@
             member_ref[:, at] = member
             count = dot(ones, member.astype(jnp.bfloat16))
             mine = flag(ramp((cells, wide), 0) == own_ref[:, at])
-            held.append(dot_lanes(mine, count.astype(jnp.bfloat16)))
-        count_ref[...] += (held[0] + held[1]) + (held[2] + held[3])
+            held.append(dot_lanes(mine, count[0:16].astype(jnp.bfloat16)))
+        count_ref[:, 0:16] += held[0] + held[1]
         return unused
 
     lax.fori_loop(0, blocks, choose, 0)
 
-    held = count_ref[...]
+    held = jnp.broadcast_to(count_ref[:, 0:1], count_ref.shape)
     high = jnp.floor(held * (1.0 / lanes))
     low = held - lanes * high
     taken = jnp.floor((held + (GROUP - 1)) * (1.0 / GROUP))
@@ -412,10 +412,10 @@
             for unit in range(tall)
         ]
         values = [split_rows(loads_ref[unit]) for unit in range(tall)]
-        return total + dot_lanes(jnp.concatenate(values, axis=1), jnp.concatenate(hits, axis=1))
-
-    total = lax.fori_loop(0, cells // tall, gather_sums, jnp.zeros((24, held), jnp.float32))
-    return joined_rows(total)
+        return total + dot_lanes(jnp.concatenate(hits, axis=1), jnp.concatenate(values, axis=1))
+
+    total = lax.fori_loop(0, cells // tall, gather_sums, jnp.zeros((held, 24), jnp.float32))
+    return joined_rows(total.T)
 
 
 def move_kernel(
@@ -437,14 +437,14 @@
             number = jnp.where(
                 (lane >= held) & (lane < held + owned), brick * owned + lane - held, -1
             ).astype(jnp.float32)
-            sums = sums + dot_lanes(values, (targets == key).astype(jnp.float32).astype(jnp.bfloat16))
-            base = base + dot_lanes(values, (targets == number).astype(jnp.float32).astype(jnp.bfloat16))
+            sums = sums + dot_lanes((targets == key).astype(jnp.float32).astype(jnp.bfloat16), values)
+            base = base + dot_lanes((targets == number).astype(jnp.float32).astype(jnp.bfloat16), values)
         return sums, base
 
-    zero = jnp.zeros((24, lanes), jnp.float32)
+    zero = jnp.zeros((lanes, 24), jnp.float32)
     sums, base = lax.fori_loop(0, bricks // 8, match, (zero, zero))
-    sums = joined_rows(sums)
-    base = joined_rows(base)
+    sums = joined_rows(sums.T)
+    base = joined_rows(base.T)
     rows = []
     for axis in range(3):
         pull = gravity if axis == 2 else 0.0

time: 133 us -> 136 us (1.023)
  Pallas kernels: 92 us -> 94.7 us
    pallas_call x1, Pallas kernels: 46.7 us -> 48.8 us  [local(): pl.pallas_call(inner_kernel, out_shape=jax.ShapeDtypeStruct(force_shape,...]
    pallas_call x1, Pallas kernels: 28.2 us -> 29.7 us  [local(): pl.pallas_call(functools.partial(outer_kernel, near_outside, sizes), out_...]
where the time goes in v11:
time: 136 us
  Pallas kernels  94.7 us (70%)
  starting transfers between devices  15.5 us (11%)
  other arithmetic  9.23 us (7%)
  waiting for transfers between devices  6.95 us (5%)
  local copies, waits for them, and re-layouts  5.71 us (4%)
  between operations  3.43 us (3%)
    pallas_call x1, Pallas kernels, local(): pl.pallas_call(inner_kernel, out_shape=jax.ShapeDtypeStruct(force_shape,...  48.8 us
    pallas_call x1, Pallas kernels, local(): pl.pallas_call(functools.partial(outer_kernel, near_outside, sizes), out_...  29.7 us
    ppermute x6, starting transfers between devices, exchange(): return (lax.ppermute(last, axis, up), lax.ppermute(initial, axis, down))  9.04 us
    pallas_call x1, Pallas kernels, local(): pl.pallas_call(functools.partial(list_kernel, near_inside, sizes), out_sh...  8.71 us
    all_to_all x1, waiting for transfers between devices, local(): lax.all_to_all(known, names, split_axis=0, concat_axis=0, tiled=True)  6.93 us
    all_to_all x1, starting transfers between devices, local(): lax.all_to_all(known, names, split_axis=0, concat_axis=0, tiled=True)  6.44 us
    sort x1, other arithmetic, local(): codes = jnp.sort(codes)  5.04 us
    pallas_call x1, Pallas kernels, local(): pl.pallas_call(functools.partial(move_kernel, owned), out_shape=(jax.Shap...  4.65 us
  transfers between devices with their start and end apart: 7, of which 1 were waited for; matrix products, arithmetic and copies ran while one was open for 8% of the time, Pallas kernels for 42%

profile of v11, /device:TPU:0, one launch (start us, length us, event | category | flops | bytes accessed | tf_op | source)
XLA Modules:
  0.0 135.5 jit_solution(1770360967945824128)
XLA Ops:
  0.6 1.2 fusion.14
  1.8 2.9 %shard_map.104 = (f32[256,8,128]{2,1,0:T(8,128)}, f32[16,8,128]{2,1,0:T(8,128)}, f32[16,8,128]{2,1,0:T(8,128)}) custom-call(f32[7,256,128]{2,1,0:T(8,128)} %bitcast.39, s32[256,128]{1,0:T(8,128)} %bitcast.43, f32[1,64]{1,0:T(1,128)} %bitcast.59), custom_call_target="tpu_custom_call" | custom-call | tf_op jit(solution)/shard_map/pallas_call | solution.py:520
  4.8 0.9 copy.11
  5.7 3.0 %collective-permute-start = (f32[4,4,1,8,128]{4,3,2,0,1:T(8,128)S(1)}, f32[4,4,1,8,128]{4,3,2,0,1:T(8,128)S(1)}, u32[]{:S(2)}, u32[]{:S(2)}) collective-permute-start(f32[4,4,1,8,128]{4,3,2,0,1:T(8,128)S(1)} %copy.11), channel_id=1, source_target_pairs={{0,1},{1,0},{2,3},{3,2},{4,5},{5,4},{6,7},{7,6},{8,9},{9,8},{10,11... | collective-permute-start | bytes 196616 | tf_op jit(solution)/shard_map/ppermute | solution.py:51
  8.7 0.8 copy.12
  9.5 0.8 select_add_fusion
  10.3 1.1 fusion.16
  11.4 5.0 %sort.15 = (s32[2048]{0:T(1024)S(1)}, s32[2048]{0:T(1024)}) sort(s32[2048]{0:T(1024)S(1)} %select_add_fusion, s32[2048]{0:T(1024)S(1)} %iota.11), dimensions={0}, to_apply=%region_0.1 | sort | flops 22528 | bytes 32768 | tf_op jit(solution)/shard_map/jit(sort)/sort | solution.py:585
  16.4 0.1 pad.6.clone
  16.5 0.7 maximum_maximum_fusion.fixed_ref
  17.2 0.7 convert_reduce_fusion
  20.0 1.8 %collective-permute-start.3 = (f32[1,4,18,8,128]{4,3,2,0,1:T(8,128)S(1)}, f32[1,4,18,8,128]{4,3,2,0,1:T(8,128)S(1)}, u32[]{:S(2)}, u32[]{:S(2)}) collective-permute-start(f32[1,4,18,8,128]{4,3,2,0,1:T(8,128)S(1)} %pad_maximum_fusion.3), channel_id=1, source_target_pairs={{8,0},{16,8},{24,16},{0,24},{9,1},{17,9},{25,17},{1,25},{10,2},{18... | collective-permute-start | bytes 884744 | tf_op jit(solution)/shard_map/ppermute | solution.py:51
  22.4 0.7 broadcast_and_fusion
  23.1 8.7 %shard_map.105 = (s32[2048,128]{1,0:T(8,128)}, s32[1,2048]{1,0:T(1,128)}, s32[1,2048]{1,0:T(1,128)}, s32[1,10240]{1,0:T(1,128)}, s32[1]{0:T(128)}) custom-call(s32[1]{0:T(128)} %bitcast.16.amount_smem, s32[1,2048]{1,0:T(1,128)} %bitcast.57, f32[256,8,128]{2,1,0:T(8,128)} %get-tuple-element.30.table_ref), custom_call_target="tpu_custom_call" | custom-call | tf_op jit(solution)/shard_map/pallas_call | solution.py:596
  31.9 2.1 %collective-permute-start.4 = (f32[6,1,18,8,128]{4,3,2,0,1:T(8,128)S(1)}, f32[6,1,18,8,128]{4,3,2,0,1:T(8,128)S(1)}, u32[]{:S(2)}, u32[]{:S(2)}) collective-permute-start(f32[6,1,18,8,128]{4,3,2,0,1:T(8,128)S(1)} %pad_maximum_fusion), channel_id=1, source_target_pairs={{0,2},{2,4},{4,6},{6,0},{1,3},{3,5},{5,7},{7,1},{8,10},{10,12},{12... | collective-permute-start | bytes 1327112 | tf_op jit(solution)/shard_map/ppermute | solution.py:51
  34.1 2.1 %collective-permute-start.5 = (f32[6,1,18,8,128]{4,3,2,0,1:T(8,128)S(1)}, f32[6,1,18,8,128]{4,3,2,0,1:T(8,128)S(1)}, u32[]{:S(2)}, u32[]{:S(2)}) collective-permute-start(f32[6,1,18,8,128]{4,3,2,0,1:T(8,128)S(1)} %pad_maximum_fusion.1), channel_id=1, source_target_pairs={{2,0},{4,2},{6,4},{0,6},{3,1},{5,3},{7,5},{1,7},{10,8},{12,10},{14... | collective-permute-start | bytes 1327112 | tf_op jit(solution)/shard_map/ppermute | solution.py:51
  36.2 48.8 %shard_map.106.inner_ref = f32[264,3,8,128]{3,2,1,0:T(8,128)} custom-call(s32[1]{0:T(128)} %bitcast.16.amount_smem, s32[1,2048]{1,0:T(1,128)} %get-tuple-element.40.where_smem, s32[1,2048]{1,0:T(1,128)} %get-tuple-element.41.word_smem, s32[1,10240]{1,0:T(1,128)} %get-tuple-element.42.cell_smem, s32[1]{0:T(128)} %get-tuple-element.43.groups_smem, ...), custom_call_target="tpu_custom_call" | custom-call | tf_op jit(solution)/shard_map/pallas_call | solution.py:613
  85.2 1.2 copy-done.1
  86.3 29.7 %shard_map.107 = f32[32,8,128]{2,1,0:T(8,128)} custom-call(s32[1]{0:T(128)} %bitcast.3.amount_smem, s32[1,2048]{1,0:T(1,128)} %bitcast.56, f32[256,8,128]{2,1,0:T(8,128)} %get-tuple-element.30.table_ref, f32[392,8,128]{2,1,0:T(8,128)} %copy-done.1, f32[264,3,8,128]{3,2,1,0:T(8,128)} %shard_map.106.inner_ref, f32[3,256,128]{2,1,0:T(8,128)} %bitcast.41, ...), custom_call_target="tpu_custom_call" | custom-call | tf_op jit(solution)/shard_map/pallas_call | solution.py:632
  116.0 6.4 %all-to-all-start = ((f32[32,8,128]{2,1,0:T(8,128)}), f32[32,8,128]{2,1,0:T(8,128)S(1)}, u32[]{:S(2)}, u32[]{:S(2)}) async-start(f32[32,8,128]{2,1,0:T(8,128)} %shard_map.107), calls=%async_computation | async-start | bytes 262144 | tf_op jit(solution)/shard_map/all_to_all | solution.py:648
  122.5 0.7 copy.19.target_ref
  123.3 6.9 %all-to-all-done.known_ref = f32[32,8,128]{2,1,0:T(8,128)S(1)} async-done(((f32[32,8,128]{2,1,0:T(8,128)}), f32[32,8,128]{2,1,0:T(8,128)S(1)}, u32[]{:S(2)}, u32[]{:S(2)}) %all-to-all-start) | async-done | bytes 131104 | tf_op jit(solution)/shard_map/all_to_all | solution.py:648
  130.2 0.7 copy-done.2
  130.9 4.7 %shard_map.108 = (f32[6,256,128]{2,1,0:T(8,128)}, f32[6,128]{1,0:T(8,128)}) custom-call(f32[128,1]{1,0:T(8,128)} %copy.19.target_ref, f32[32,8,128]{2,1,0:T(8,128)} %copy-done.2, f32[7,256,128]{2,1,0:T(8,128)} %bitcast.40, f32[3,256,128]{2,1,0:T(8,128)} %bitcast.42, s32[256,128]{1,0:T(8,128)} %bitcast.45), custom_call_target="tpu_custom_call" | custom-call | tf_op jit(solution)/shard_map/pallas_call | solution.py:655
  (44 shorter events, 0.5 us)
Async XLA Ops:
  1.8 14.7 %copy-start.3 = (f32[64]{0:T(128)S(1)}, f32[64]{0:T(128)}, u32[]{:S(2)}) copy-start(f32[64]{0:T(128)} %get-tuple-element.66) | copy-start | bytes 772
  1.8 14.7 %copy-start.4 = (f32[6,48]{1,0:T(8,128)S(1)}, f32[6,48]{1,0:T(8,128)}, u32[]{:S(2)}) copy-start(f32[6,48]{1,0:T(8,128)} %param.15) | copy-start | bytes 3460
  1.8 14.7 %copy-start.5 = (f32[48]{0:T(128)S(1)}, f32[48]{0:T(128)}, u32[]{:S(2)}) copy-start(f32[48]{0:T(128)} %param.17) | copy-start | bytes 580
  1.8 14.7 %copy-start.6 = (f32[48]{0:T(128)S(1)}, f32[48]{0:T(128)}, u32[]{:S(2)}) copy-start(f32[48]{0:T(128)} %param.16) | copy-start | bytes 580
  4.8 6.6 %copy-start = (f32[256,8,128]{2,1,0:T(8,128)S(1)}, f32[256,8,128]{2,1,0:T(8,128)}, u32[]{:S(2)}) copy-start(f32[256,8,128]{2,1,0:T(8,128)} %get-tuple-element.30.table_ref) | copy-start | bytes 3145732
  5.7 12.8 %collective-permute-start = (f32[4,4,1,8,128]{4,3,2,0,1:T(8,128)S(1)}, f32[4,4,1,8,128]{4,3,2,0,1:T(8,128)S(1)}, u32[]{:S(2)}, u32[]{:S(2)}) collective-permute-start(f32[4,4,1,8,128]{4,3,2,0,1:T(8,128)S(1)} %copy.11), channel_id=1, source_target_pairs={{0,1},{1,0},{2,3},{3,2},{4,5},{5,4},{6,7},{7,6},{8,9},{9,8},{10,11... | collective-permute-start | bytes 196616 | tf_op jit(solution)/shard_map/ppermute | solution.py:51
  9.5 9.0 %collective-permute-start.1 = (f32[4,4,1,8,128]{4,3,2,0,1:T(8,128)S(1)}, f32[4,4,1,8,128]{4,3,2,0,1:T(8,128)S(1)}, u32[]{:S(2)}, u32[]{:S(2)}) collective-permute-start(f32[4,4,1,8,128]{4,3,2,0,1:T(8,128)S(1)} %copy.12), channel_id=1, source_target_pairs={{1,0},{0,1},{3,2},{2,3},{5,4},{4,5},{7,6},{6,7},{9,8},{8,9},{11,10... | collective-permute-start | bytes 196616 | tf_op jit(solution)/shard_map/ppermute | solution.py:51
  19.9 11.9 %collective-permute-start.2 = (f32[1,4,18,8,128]{4,3,2,0,1:T(8,128)S(1)}, f32[1,4,18,8,128]{4,3,2,0,1:T(8,128)S(1)}, u32[]{:S(2)}, u32[]{:S(2)}) collective-permute-start(f32[1,4,18,8,128]{4,3,2,0,1:T(8,128)S(1)} %pad_maximum_fusion.2), channel_id=1, source_target_pairs={{0,8},{8,16},{16,24},{24,0},{1,9},{9,17},{17,25},{25,1},{2,10},{10... | collective-permute-start | bytes 884744 | tf_op jit(solution)/shard_map/ppermute | solution.py:51
  20.0 11.9 %collective-permute-start.3 = (f32[1,4,18,8,128]{4,3,2,0,1:T(8,128)S(1)}, f32[1,4,18,8,128]{4,3,2,0,1:T(8,128)S(1)}, u32[]{:S(2)}, u32[]{:S(2)}) collective-permute-start(f32[1,4,18,8,128]{4,3,2,0,1:T(8,128)S(1)} %pad_maximum_fusion.3), channel_id=1, source_target_pairs={{8,0},{16,8},{24,16},{0,24},{9,1},{17,9},{25,17},{1,25},{10,2},{18... | collective-permute-start | bytes 884744 | tf_op jit(solution)/shard_map/ppermute | solution.py:51
  31.9 53.1 %collective-permute-start.4 = (f32[6,1,18,8,128]{4,3,2,0,1:T(8,128)S(1)}, f32[6,1,18,8,128]{4,3,2,0,1:T(8,128)S(1)}, u32[]{:S(2)}, u32[]{:S(2)}) collective-permute-start(f32[6,1,18,8,128]{4,3,2,0,1:T(8,128)S(1)} %pad_maximum_fusion), channel_id=1, source_target_pairs={{0,2},{2,4},{4,6},{6,0},{1,3},{3,5},{5,7},{7,1},{8,10},{10,12},{12... | collective-permute-start | bytes 1327112 | tf_op jit(solution)/shard_map/ppermute | solution.py:51
  34.1 51.0 %collective-permute-start.5 = (f32[6,1,18,8,128]{4,3,2,0,1:T(8,128)S(1)}, f32[6,1,18,8,128]{4,3,2,0,1:T(8,128)S(1)}, u32[]{:S(2)}, u32[]{:S(2)}) collective-permute-start(f32[6,1,18,8,128]{4,3,2,0,1:T(8,128)S(1)} %pad_maximum_fusion.1), channel_id=1, source_target_pairs={{2,0},{4,2},{6,4},{0,6},{3,1},{5,3},{7,5},{1,7},{10,8},{12,10},{14... | collective-permute-start | bytes 1327112 | tf_op jit(solution)/shard_map/ppermute | solution.py:51
  85.2 1.2 copy-start.1
  116.0 14.2 %all-to-all-start = ((f32[32,8,128]{2,1,0:T(8,128)}), f32[32,8,128]{2,1,0:T(8,128)S(1)}, u32[]{:S(2)}, u32[]{:S(2)}) async-start(f32[32,8,128]{2,1,0:T(8,128)} %shard_map.107), calls=%async_computation | async-start | bytes 262144 | tf_op jit(solution)/shard_map/all_to_all | solution.py:648
  130.2 0.7 copy-start.2

commit v12 on v11

--- a/solution.py
+++ b/solution.py
@@ -14,8 +14,10 @@
 epsilon_sq = 1e-08
 radius_top = 0.14
 
-GROUP = 32
+INNER_GROUP = 32
+OUTER_GROUP = 16
 FILL = 32
+WORD_BITS = 16
 SLACK = 256
 SPREAD = 4
 VMEM = 56 * 1024 * 1024
@@ -67,13 +69,14 @@
 
 
 def list_tiles(
-    amount, near_of, sizes, code_ref, table_ref, slots_ref, where_ref, word_ref, cell_ref,
-    class_ref, member_ref, count_ref, near_ref, need_ref, own_ref,
+    group, amount, near_of, sizes, code_ref, table_ref, slots_ref, word_ref, cell_ref,
+    class_ref, member_ref, count_ref, near_ref, need_ref, own_ref, kind_ref,
 ):
     tiles, lanes = slots_ref.shape
     span = table_ref.shape[0]
     padded = class_ref.shape[0]
     cells = count_ref.shape[0]
+    lane_bits = lanes.bit_length() - 1
     wide = 256
     parts = 2
     flat = table_ref.reshape(span * 8, lanes)
@@ -111,7 +114,7 @@
     live = ramp((1, tiles), 1) < amount
     near = jnp.where(live, near, 0)
     near_ref[...] = near
-    word_ref[...] = near * 32 + jnp.where(live, kind, 0)
+    kind_ref[...] = near * 32 + jnp.where(live, kind, 0)
     need_ref[...] = jnp.where(live, need, 64)
     own_ref[...] = jnp.where(live, own, cells)
 
@@ -151,7 +154,7 @@
     held = jnp.broadcast_to(count_ref[:, 0:1], count_ref.shape)
     high = jnp.floor(held * (1.0 / lanes))
     low = held - lanes * high
-    taken = jnp.floor((held + (GROUP - 1)) * (1.0 / GROUP))
+    taken = jnp.floor((held + (group - 1)) * (1.0 / group))
     upto = flag(ramp((cells, cells), 1) <= ramp((cells, cells), 0))
     ends = dot(upto, taken.astype(jnp.bfloat16))
     cell_ones = jnp.ones((8, cells), jnp.bfloat16)
@@ -159,9 +162,9 @@
     wide_ends = jnp.concatenate([ends] * 8, axis=1)
 
     def name_groups(block, unused):
-        group = (ramp((cells, many), 1) + block * many).astype(jnp.float32)
+        number = (ramp((cells, many), 1) + block * many).astype(jnp.float32)
         at = pl.ds(pl.multiple_of(block * many, many), many)
-        cell_ref[:, at] = dot(cell_ones, flag(wide_ends <= group))[0:1].astype(jnp.int32)
+        cell_ref[:, at] = dot(cell_ones, flag(wide_ends <= number))[0:1].astype(jnp.int32)
         return unused
 
     groups = jnp.max(ends).astype(jnp.int32)
@@ -182,9 +185,10 @@
             lower = flag(ramp((cells, wide), 0) < own_ref[:, at])
             before = dot(before_cell, lower)
             so_far = dot(count[0:8].astype(jnp.bfloat16), earlier_tile) + done
-            start = GROUP * before[0:8] + so_far - (lanes * before[8:16] + before[16:24])
+            start = group * before[0:8] + so_far - (lanes * before[8:16] + before[16:24])
             start = start.astype(jnp.int32)[0:1]
-            where_ref[:, at] = start * 256 + count[0:1].astype(jnp.int32)
+            offset = jnp.broadcast_to(start & (lanes - 1), (8, wide))
+            word_ref[:, at] = (start >> lane_bits) * (1 << WORD_BITS) + kind_ref[:, at]
             rank = dot(earlier, flags)
             slot = ramp((lanes, wide), 0)
             moves = slot - rank.astype(jnp.int32)
@@ -196,26 +200,45 @@
                 word = keep | jnp.concatenate([gone[bit:], gone[:bit]], axis=0)
                 bit *= 2
             word = word & (lanes - 1)
-            turn = jnp.broadcast_to(start, (lanes, wide))
-            bit = 1
-            while bit < lanes:
-                moved = jnp.concatenate([word[lanes - bit :], word[: lanes - bit]], axis=0)
-                word = jnp.where((turn & bit) != 0, moved, word)
-                bit *= 2
+            line = ramp((8, wide), 0)
+            within = offset & 7
+            pick = (line - within) & 7
+            slabs = [
+                jnp.take_along_axis(
+                    word[at_row : at_row + 8], pick, axis=0, mode="promise_in_bounds"
+                )
+                for at_row in range(0, lanes, 8)
+            ]
+            slabs = [
+                jnp.where(line >= within, slabs[number], slabs[number - 1])
+                for number in range(len(slabs))
+            ]
+            hop = 1
+            while hop < len(slabs):
+                chosen = (offset & (8 * hop)) != 0
+                slabs = [
+                    jnp.where(chosen, slabs[number - hop], slabs[number])
+                    for number in range(len(slabs))
+                ]
+                hop *= 2
+            count = count[0:8].astype(jnp.int32)
+            for number in range(len(slabs)):
+                lead = line + 8 * number - offset
+                taken_lane = jnp.where((lead & (lanes - 1)) < count, lanes, 0)
+                slabs[number] = slabs[number] | taken_lane | jnp.where(lead < 0, 2 * lanes, 0)
+            word = jnp.concatenate(slabs, axis=0)
             for half in range(wide // lanes):
                 rows = pl.ds(pl.multiple_of(first + half * lanes, lanes), lanes)
                 slots_ref[rows, :] = word[:, half * lanes : (half + 1) * lanes].T
-            done = done + jnp.sum(count[0:8], axis=1, keepdims=True)
+            done = done + jnp.sum(count.astype(jnp.float32), axis=1, keepdims=True)
         return done
 
     lax.fori_loop(0, blocks, place, jnp.zeros((8, 1), jnp.float32))
     return groups
 
 
-def fill_lists(amount, where_smem, near_smem, table_ref, slots_ref, shift_ref, list_ref):
-    tiles, lanes = slots_ref.shape
-    lane_bits = lanes.bit_length() - 1
-    lane = lax.broadcasted_iota(jnp.int32, (8, lanes), 1)
+def fill_lists(amount, word_smem, near_table_ref, slots_ref, shift_ref, list_ref):
+    lanes = slots_ref.shape[1]
     row = lax.broadcasted_iota(jnp.int32, (8, lanes), 0)
     absent = jnp.where(row == 6, -10.0, 0.0)
     for kind in range(27):
@@ -224,22 +247,17 @@
 
     def fill(block, carry):
         last_chunk, last_new, last_held = carry
-        units = range(FILL)
-        where = [where_smem[0, block * FILL + unit] for unit in units]
-        near = [near_smem[0, block * FILL + unit] for unit in units]
-        found = []
-        for unit in units:
+        words = [word_smem[0, block * FILL + unit] for unit in range(FILL)]
+        for unit, word in enumerate(words):
             slots = slots_ref[pl.ds(block * FILL + unit, 8, stride=0), :]
-            cell = table_ref[near[unit] >> 5]
-            found.append(lanes_of(cell, slots) + shift_ref[near[unit] & 31])
-        for unit in units:
-            amount = where[unit] & 255
-            chunk = where[unit] >> (8 + lane_bits)
-            offset = (where[unit] >> 8) & (lanes - 1)
-            new = jnp.where(((lane - offset) & (lanes - 1)) < amount, found[unit], absent)
+            cell = near_table_ref[(word >> 5) & ((1 << (WORD_BITS - 5)) - 1)]
+            found = lanes_of(cell, slots & (lanes - 1)) + shift_ref[word & 31]
+            chunk = word >> WORD_BITS
+            new = jnp.where((slots & lanes) != 0, found, absent)
+            later = (slots & (2 * lanes)) != 0
             held_row = jnp.where(chunk != last_chunk, last_new, last_held)
-            held_row = jnp.where(lane >= offset, new, held_row)
-            new = jnp.where(lane >= offset, absent, new)
+            held_row = jnp.where(later, held_row, new)
+            new = jnp.where(later, new, absent)
             list_ref[chunk] = held_row
             list_ref[chunk + 1] = new
             last_chunk, last_new, last_held = chunk, new, held_row
@@ -249,12 +267,12 @@
     lax.fori_loop(0, blocks, fill, (jnp.int32(0), absent, absent))
 
 
-def pair_forces(groups, cell_smem, table_ref, list_ref, force_ref, even_ref, odd_ref):
+def pair_forces(group, groups, cell_smem, table_ref, list_ref, force_ref, even_ref, odd_ref):
     lanes = table_ref.shape[1]
     cells = table_ref.shape[0] // 8
     rows = even_ref.shape[0]
     chunks = rows // lanes
-    units = rows // GROUP
+    units = rows // group
     force_ref[...] = jnp.zeros(force_ref.shape, jnp.float32)
     part = lax.broadcasted_iota(jnp.int32, (32, 8 * lanes), 0)
     comp = lax.broadcasted_iota(jnp.int32, (32, 8 * lanes), 1) // lanes
@@ -300,8 +318,8 @@
             own = jnp.minimum(cell, cells - 1) * 8
             mine = [table_ref[pl.ds(own + value, 8, stride=0), :] for value in range(8)]
             running = [jnp.where(cell == last, running[axis], 0.0) for axis in range(3)]
-            for block in range(GROUP // 8):
-                force = block_force(wide_ref, unit * GROUP + block * 8, mine)
+            for block in range(group // 8):
+                force = block_force(wide_ref, unit * group + block * 8, mine)
                 running = [running[axis] + force[axis] for axis in range(3)]
             last = cell
             for axis in range(3):
@@ -331,43 +349,38 @@
 
 
 def list_kernel(
-    near_of, sizes, amount_smem, code_ref, table_ref, slots_ref, where_ref, word_ref, cell_ref,
+    near_of, sizes, amount_smem, code_ref, table_ref, slots_ref, word_ref, cell_ref,
     groups_smem, *scratch,
 ):
     groups_smem[0] = list_tiles(
-        amount_smem[0], near_of, sizes, code_ref, table_ref, slots_ref, where_ref, word_ref,
-        cell_ref, *scratch,
+        INNER_GROUP, amount_smem[0], near_of, sizes, code_ref, table_ref, slots_ref, word_ref, cell_ref, *scratch,
     )
 
 
 def inner_kernel(
-    amount_smem, where_smem, word_smem, cell_smem, groups_smem, table_ref, slots_ref, force_ref,
+    amount_smem, word_smem, cell_smem, groups_smem, table_ref, slots_ref, force_ref,
     list_ref, even_ref, odd_ref, shift_ref,
 ):
     cells, _, lanes = table_ref.shape
-    fill_lists(amount_smem[0], where_smem, word_smem, table_ref, slots_ref, shift_ref, list_ref)
+    fill_lists(amount_smem[0], word_smem, table_ref, slots_ref, shift_ref, list_ref)
     flat = table_ref.reshape(cells * 8, lanes)
-    pair_forces(groups_smem[0], cell_smem, flat, list_ref, force_ref, even_ref, odd_ref)
+    pair_forces(INNER_GROUP, groups_smem[0], cell_smem, flat, list_ref, force_ref, even_ref, odd_ref)
 
 
 def outer_kernel(
     near_of, sizes, amount_smem, code_ref, table_ref, halo_ref, inner_ref, arms_ref, frag_ref,
-    fixed_ref, out_ref, force_ref, loads_ref, slots_ref, where_ref, word_ref, cell_ref,
-    where_smem, word_smem, cell_smem, sems, list_ref, even_ref, odd_ref, shift_ref, *scratch,
+    fixed_ref, out_ref, force_ref, loads_ref, slots_ref, word_ref, cell_ref, word_smem, cell_smem, sems, list_ref, even_ref, odd_ref, shift_ref, *scratch,
 ):
     cells, _, lanes = table_ref.shape
     held = fixed_ref.shape[1] // 2
     amount = amount_smem[0]
     groups = list_tiles(
-        amount, near_of, sizes, code_ref, halo_ref, slots_ref, where_ref, word_ref, cell_ref,
-        *scratch,
-    )
-    to_scalars(
-        [(where_ref, where_smem), (word_ref, word_smem), (cell_ref, cell_smem)], sems
-    )
-    fill_lists(amount, where_smem, word_smem, halo_ref, slots_ref, shift_ref, list_ref)
+        OUTER_GROUP, amount, near_of, sizes, code_ref, halo_ref, slots_ref, word_ref, cell_ref, *scratch,
+    )
+    to_scalars([(word_ref, word_smem), (cell_ref, cell_smem)], sems)
+    fill_lists(amount, word_smem, halo_ref, slots_ref, shift_ref, list_ref)
     flat = table_ref.reshape(cells * 8, lanes)
-    pair_forces(groups, cell_smem, flat, list_ref, force_ref, even_ref, odd_ref)
+    pair_forces(OUTER_GROUP, groups, cell_smem, flat, list_ref, force_ref, even_ref, odd_ref)
     sums = fragment_sums(inner_ref, force_ref, arms_ref, frag_ref, loads_ref, held)
     out = fixed_ref[...] + jnp.concatenate([sums, jnp.zeros_like(sums)], axis=1)
     for brick in range(out_ref.shape[0]):
@@ -412,10 +425,10 @@
             for unit in range(tall)
         ]
         values = [split_rows(loads_ref[unit]) for unit in range(tall)]
-        return total + dot_lanes(jnp.concatenate(hits, axis=1), jnp.concatenate(values, axis=1))
-
-    total = lax.fori_loop(0, cells // tall, gather_sums, jnp.zeros((held, 24), jnp.float32))
-    return joined_rows(total.T)
+        return total + dot_lanes(jnp.concatenate(values, axis=1), jnp.concatenate(hits, axis=1))
+
+    total = lax.fori_loop(0, cells // tall, gather_sums, jnp.zeros((24, held), jnp.float32))
+    return joined_rows(total)
 
 
 def move_kernel(
@@ -559,11 +572,11 @@
     codes = tiles[0]
     total = codes.shape[0]
     codes = codes + jnp.where(inside(codes), 0, outside)
-    chunks = total + cells * GROUP // lanes + 3 * SPREAD
-    group_top = -(-(chunks * (lanes // GROUP) + SLACK) // (8 * lanes)) * 8 * lanes + 8 * lanes
+    chunks = total + cells * INNER_GROUP // lanes + 3 * SPREAD
+    group_top = -(-(chunks * (lanes // OUTER_GROUP) + SLACK) // (8 * lanes)) * 8 * lanes + 8 * lanes
     force_shape = (cells + 8, 3, 8, lanes)
 
-    list_shapes = [(total, lanes), (1, total), (1, total), (1, group_top)]
+    list_shapes = [(total, lanes), (1, total), (1, group_top)]
 
     def list_scratch(span):
         return [
@@ -573,6 +586,7 @@
             pltpu.VMEM((1, total), jnp.int32),
             pltpu.VMEM((1, total), jnp.int32),
             pltpu.VMEM((1, total), jnp.int32),
+            pltpu.VMEM((1, total), jnp.int32),
         ]
 
     pair_scratch = [
@@ -593,16 +607,16 @@
         jnp.concatenate([z_before[:1], grid[:1], z_after[:1]], axis=2),
         "gx",
     )
-    slots, where, word, cell_of, groups = pl.pallas_call(
+    slots, word, cell_of, groups = pl.pallas_call(
         functools.partial(list_kernel, near_inside, sizes),
         out_shape=tuple(jax.ShapeDtypeStruct(shape, jnp.int32) for shape in list_shapes + [(1,)]),
         in_specs=[smem, vmem, vmem],
-        out_specs=(vmem,) * 4 + (smem,),
+        out_specs=(vmem,) * 3 + (smem,),
         scratch_shapes=list_scratch(cells),
         compiler_params=params,
     )(inner_amount[None], (codes & (outside - 1))[None], table)
-    x_before, x_after, slots, where, word, cell_of, groups = lax.optimization_barrier(
-        (x_before, x_after, slots, where, word, cell_of, groups)
+    x_before, x_after, slots, word, cell_of, groups = lax.optimization_barrier(
+        (x_before, x_after, slots, word, cell_of, groups)
     )
 
     def face(at):
@@ -613,11 +627,11 @@
     inner = pl.pallas_call(
         inner_kernel,
         out_shape=jax.ShapeDtypeStruct(force_shape, jnp.float32),
-        in_specs=[smem] * 5 + [vmem] * 2,
+        in_specs=[smem] * 4 + [vmem] * 2,
         out_specs=vmem,
         scratch_shapes=pair_scratch,
         compiler_params=params,
-    )(inner_amount[None], where, word, cell_of, groups, table, slots)
+    )(inner_amount[None], word, cell_of, groups, table, slots)
 
     outer_codes = lax.dynamic_slice(jnp.concatenate([codes, codes]), (inner_amount,), (total,))
     outer_codes = outer_codes & (outside - 1)
@@ -640,7 +654,7 @@
         ]
         + [pltpu.VMEM(shape, jnp.int32) for shape in list_shapes]
         + [pltpu.SMEM(shape, jnp.int32) for shape in list_shapes[1:]]
-        + [pltpu.SemaphoreType.DMA((3,))]
+        + [pltpu.SemaphoreType.DMA((2,))]
         + pair_scratch
         + list_scratch(halo.shape[0]),
         compiler_params=params,

time: 136 us -> 132 us (0.971)
  Pallas kernels: 94.7 us -> 91.4 us
    pallas_call x1, Pallas kernels: 29.7 us -> 27.8 us  [local(): pl.pallas_call(functools.partial(outer_kernel, near_outside, sizes), out_...]
    pallas_call x1, Pallas kernels: 48.8 us -> 47.4 us  [local(): pl.pallas_call(inner_kernel, out_shape=jax.ShapeDtypeStruct(force_shape,...]
  transfers between devices with their start and end apart: 7 -> 7, of which waited for: 1 -> 1; matrix products, arithmetic and copies ran while one was open for 8% -> 8% of each run, Pallas kernels for 42% -> 43%
where the time goes in v12:
time: 132 us; the launch traced here: 131 us
  Pallas kernels  91.4 us (69%)
  starting transfers between devices  14.5 us (11%)
  other arithmetic  9.19 us (7%)
  waiting for transfers between devices  6.95 us (5%)
  local copies, waits for them, and re-layouts  5.71 us (4%)
  between operations  3.41 us (3%)
    pallas_call x1, Pallas kernels, local(): pl.pallas_call(inner_kernel, out_shape=jax.ShapeDtypeStruct(force_shape,...  47.4 us
    pallas_call x1, Pallas kernels, local(): pl.pallas_call(functools.partial(outer_kernel, near_outside, sizes), out_...  27.8 us
    ppermute x6, starting transfers between devices, exchange(): return (lax.ppermute(last, axis, up), lax.ppermute(initial, axis, down))  9.04 us
    pallas_call x1, Pallas kernels, local(): pl.pallas_call(functools.partial(list_kernel, near_inside, sizes), out_sh...  8.62 us
    all_to_all x1, waiting for transfers between devices, local(): lax.all_to_all(known, names, split_axis=0, concat_axis=0, tiled=True)  6.93 us
    all_to_all x1, starting transfers between devices, local(): lax.all_to_all(known, names, split_axis=0, concat_axis=0, tiled=True)  5.48 us
    sort x1, other arithmetic, local(): codes = jnp.sort(codes)  5.04 us
    pallas_call x1, Pallas kernels, local(): pl.pallas_call(functools.partial(move_kernel, owned), out_shape=(jax.Shap...  4.65 us
  transfers between devices with their start and end apart: 7, of which 1 were waited for; matrix products, arithmetic and copies ran while one was open for 8% of the time, Pallas kernels for 43%

profile of v12, /device:TPU:0, one launch (start us, length us, event | category | flops | bytes accessed | tf_op | source)
XLA Modules:
  0.0 131.2 jit_solution(1308669149191147567)
XLA Ops:
  0.6 1.2 fusion.14
  1.8 2.9 %shard_map.104 = (f32[256,8,128]{2,1,0:T(8,128)}, f32[16,8,128]{2,1,0:T(8,128)}, f32[16,8,128]{2,1,0:T(8,128)}) custom-call(f32[7,256,128]{2,1,0:T(8,128)} %bitcast.39, s32[256,128]{1,0:T(8,128)} %bitcast.43, f32[1,64]{1,0:T(1,128)} %bitcast.59), custom_call_target="tpu_custom_call" | custom-call | tf_op jit(solution)/shard_map/pallas_call | solution.py:533
  4.8 0.9 copy.11
  5.7 3.0 %collective-permute-start = (f32[4,4,1,8,128]{4,3,2,0,1:T(8,128)S(1)}, f32[4,4,1,8,128]{4,3,2,0,1:T(8,128)S(1)}, u32[]{:S(2)}, u32[]{:S(2)}) collective-permute-start(f32[4,4,1,8,128]{4,3,2,0,1:T(8,128)S(1)} %copy.11), channel_id=1, source_target_pairs={{0,1},{1,0},{2,3},{3,2},{4,5},{5,4},{6,7},{7,6},{8,9},{9,8},{10,11... | collective-permute-start | bytes 196616 | tf_op jit(solution)/shard_map/ppermute | solution.py:53
  8.7 0.8 copy.12
  9.5 0.8 select_add_fusion
  10.3 1.1 fusion.16
  11.4 5.0 %sort.15 = (s32[2048]{0:T(1024)S(1)}, s32[2048]{0:T(1024)}) sort(s32[2048]{0:T(1024)S(1)} %select_add_fusion, s32[2048]{0:T(1024)S(1)} %iota.11), dimensions={0}, to_apply=%region_0.1 | sort | flops 22528 | bytes 32768 | tf_op jit(solution)/shard_map/jit(sort)/sort | solution.py:599
  16.4 0.1 pad.6.clone
  16.5 0.7 maximum_maximum_fusion.fixed_ref
  17.2 0.6 convert_reduce_fusion
  19.9 1.8 %collective-permute-start.3 = (f32[1,4,18,8,128]{4,3,2,0,1:T(8,128)S(1)}, f32[1,4,18,8,128]{4,3,2,0,1:T(8,128)S(1)}, u32[]{:S(2)}, u32[]{:S(2)}) collective-permute-start(f32[1,4,18,8,128]{4,3,2,0,1:T(8,128)S(1)} %pad_maximum_fusion.3), channel_id=1, source_target_pairs={{8,0},{16,8},{24,16},{0,24},{9,1},{17,9},{25,17},{1,25},{10,2},{18... | collective-permute-start | bytes 884744 | tf_op jit(solution)/shard_map/ppermute | solution.py:53
  22.4 0.7 broadcast_and_fusion
  23.0 8.6 %shard_map.105 = (s32[2048,128]{1,0:T(8,128)}, s32[1,2048]{1,0:T(1,128)}, s32[1,18432]{1,0:T(1,128)}, s32[1]{0:T(128)}) custom-call(s32[1]{0:T(128)} %bitcast.16.amount_smem, s32[1,2048]{1,0:T(1,128)} %bitcast.57, f32[256,8,128]{2,1,0:T(8,128)} %get-tuple-element.28.table_ref), custom_call_target="tpu_custom_call" | custom-call | tf_op jit(solution)/shard_map/pallas_call | solution.py:610
  31.8 2.1 %collective-permute-start.4 = (f32[6,1,18,8,128]{4,3,2,0,1:T(8,128)S(1)}, f32[6,1,18,8,128]{4,3,2,0,1:T(8,128)S(1)}, u32[]{:S(2)}, u32[]{:S(2)}) collective-permute-start(f32[6,1,18,8,128]{4,3,2,0,1:T(8,128)S(1)} %pad_maximum_fusion), channel_id=1, source_target_pairs={{0,2},{2,4},{4,6},{6,0},{1,3},{3,5},{5,7},{7,1},{8,10},{10,12},{12... | collective-permute-start | bytes 1327112 | tf_op jit(solution)/shard_map/ppermute | solution.py:53
  34.0 2.1 %collective-permute-start.5 = (f32[6,1,18,8,128]{4,3,2,0,1:T(8,128)S(1)}, f32[6,1,18,8,128]{4,3,2,0,1:T(8,128)S(1)}, u32[]{:S(2)}, u32[]{:S(2)}) collective-permute-start(f32[6,1,18,8,128]{4,3,2,0,1:T(8,128)S(1)} %pad_maximum_fusion.1), channel_id=1, source_target_pairs={{2,0},{4,2},{6,4},{0,6},{3,1},{5,3},{7,5},{1,7},{10,8},{12,10},{14... | collective-permute-start | bytes 1327112 | tf_op jit(solution)/shard_map/ppermute | solution.py:53
  36.1 47.4 %shard_map.106.inner_ref = f32[264,3,8,128]{3,2,1,0:T(8,128)} custom-call(s32[1]{0:T(128)} %bitcast.16.amount_smem, s32[1,2048]{1,0:T(1,128)} %get-tuple-element.37.word_smem, s32[1,18432]{1,0:T(1,128)} %get-tuple-element.38.cell_smem, s32[1]{0:T(128)} %get-tuple-element.39.groups_smem, f32[256,8,128]{2,1,0:T(8,128)} %get-tuple-element.28.table_ref, ...), custom_call_target="tpu_custom_call" | custom-call | tf_op jit(solution)/shard_map/pallas_call | solution.py:627
  83.6 1.2 copy-done.1
  84.8 27.8 %shard_map.107 = f32[32,8,128]{2,1,0:T(8,128)} custom-call(s32[1]{0:T(128)} %bitcast.3.amount_smem, s32[1,2048]{1,0:T(1,128)} %bitcast.56, f32[256,8,128]{2,1,0:T(8,128)} %get-tuple-element.28.table_ref, f32[392,8,128]{2,1,0:T(8,128)} %copy-done.1, f32[264,3,8,128]{3,2,1,0:T(8,128)} %shard_map.106.inner_ref, f32[3,256,128]{2,1,0:T(8,128)} %bitcast.41, ...), custom_call_target="tpu_custom_call" | custom-call | tf_op jit(solution)/shard_map/pallas_call | solution.py:646
  112.6 5.5 %all-to-all-start = ((f32[32,8,128]{2,1,0:T(8,128)}), f32[32,8,128]{2,1,0:T(8,128)S(1)}, u32[]{:S(2)}, u32[]{:S(2)}) async-start(f32[32,8,128]{2,1,0:T(8,128)} %shard_map.107), calls=%async_computation | async-start | bytes 262144 | tf_op jit(solution)/shard_map/all_to_all | solution.py:662
  118.2 0.7 copy.19.target_ref
  118.9 6.9 %all-to-all-done.known_ref = f32[32,8,128]{2,1,0:T(8,128)S(1)} async-done(((f32[32,8,128]{2,1,0:T(8,128)}), f32[32,8,128]{2,1,0:T(8,128)S(1)}, u32[]{:S(2)}, u32[]{:S(2)}) %all-to-all-start) | async-done | bytes 131104 | tf_op jit(solution)/shard_map/all_to_all | solution.py:662
  125.9 0.7 copy-done.2
  126.5 4.7 %shard_map.108 = (f32[6,256,128]{2,1,0:T(8,128)}, f32[6,128]{1,0:T(8,128)}) custom-call(f32[128,1]{1,0:T(8,128)} %copy.19.target_ref, f32[32,8,128]{2,1,0:T(8,128)} %copy-done.2, f32[7,256,128]{2,1,0:T(8,128)} %bitcast.40, f32[3,256,128]{2,1,0:T(8,128)} %bitcast.42, s32[256,128]{1,0:T(8,128)} %bitcast.45), custom_call_target="tpu_custom_call" | custom-call | tf_op jit(solution)/shard_map/pallas_call | solution.py:669
  (44 shorter events, 0.5 us)
Async XLA Ops:
  1.8 14.7 %copy-start.3 = (f32[64]{0:T(128)S(1)}, f32[64]{0:T(128)}, u32[]{:S(2)}) copy-start(f32[64]{0:T(128)} %get-tuple-element.62) | copy-start | bytes 772
  1.8 14.7 %copy-start.4 = (f32[6,48]{1,0:T(8,128)S(1)}, f32[6,48]{1,0:T(8,128)}, u32[]{:S(2)}) copy-start(f32[6,48]{1,0:T(8,128)} %param.15) | copy-start | bytes 3460
  1.8 14.7 %copy-start.5 = (f32[48]{0:T(128)S(1)}, f32[48]{0:T(128)}, u32[]{:S(2)}) copy-start(f32[48]{0:T(128)} %param.17) | copy-start | bytes 580
  1.8 14.7 %copy-start.6 = (f32[48]{0:T(128)S(1)}, f32[48]{0:T(128)}, u32[]{:S(2)}) copy-start(f32[48]{0:T(128)} %param.16) | copy-start | bytes 580
  4.8 6.6 %copy-start = (f32[256,8,128]{2,1,0:T(8,128)S(1)}, f32[256,8,128]{2,1,0:T(8,128)}, u32[]{:S(2)}) copy-start(f32[256,8,128]{2,1,0:T(8,128)} %get-tuple-element.28.table_ref) | copy-start | bytes 3145732
  5.7 12.8 %collective-permute-start = (f32[4,4,1,8,128]{4,3,2,0,1:T(8,128)S(1)}, f32[4,4,1,8,128]{4,3,2,0,1:T(8,128)S(1)}, u32[]{:S(2)}, u32[]{:S(2)}) collective-permute-start(f32[4,4,1,8,128]{4,3,2,0,1:T(8,128)S(1)} %copy.11), channel_id=1, source_target_pairs={{0,1},{1,0},{2,3},{3,2},{4,5},{5,4},{6,7},{7,6},{8,9},{9,8},{10,11... | collective-permute-start | bytes 196616 | tf_op jit(solution)/shard_map/ppermute | solution.py:53
  9.5 9.0 %collective-permute-start.1 = (f32[4,4,1,8,128]{4,3,2,0,1:T(8,128)S(1)}, f32[4,4,1,8,128]{4,3,2,0,1:T(8,128)S(1)}, u32[]{:S(2)}, u32[]{:S(2)}) collective-permute-start(f32[4,4,1,8,128]{4,3,2,0,1:T(8,128)S(1)} %copy.12), channel_id=1, source_target_pairs={{1,0},{0,1},{3,2},{2,3},{5,4},{4,5},{7,6},{6,7},{9,8},{8,9},{11,10... | collective-permute-start | bytes 196616 | tf_op jit(solution)/shard_map/ppermute | solution.py:53
  19.9 11.9 %collective-permute-start.2 = (f32[1,4,18,8,128]{4,3,2,0,1:T(8,128)S(1)}, f32[1,4,18,8,128]{4,3,2,0,1:T(8,128)S(1)}, u32[]{:S(2)}, u32[]{:S(2)}) collective-permute-start(f32[1,4,18,8,128]{4,3,2,0,1:T(8,128)S(1)} %pad_maximum_fusion.2), channel_id=1, source_target_pairs={{0,8},{8,16},{16,24},{24,0},{1,9},{9,17},{17,25},{25,1},{2,10},{10... | collective-permute-start | bytes 884744 | tf_op jit(solution)/shard_map/ppermute | solution.py:53
  19.9 11.8 %collective-permute-start.3 = (f32[1,4,18,8,128]{4,3,2,0,1:T(8,128)S(1)}, f32[1,4,18,8,128]{4,3,2,0,1:T(8,128)S(1)}, u32[]{:S(2)}, u32[]{:S(2)}) collective-permute-start(f32[1,4,18,8,128]{4,3,2,0,1:T(8,128)S(1)} %pad_maximum_fusion.3), channel_id=1, source_target_pairs={{8,0},{16,8},{24,16},{0,24},{9,1},{17,9},{25,17},{1,25},{10,2},{18... | collective-permute-start | bytes 884744 | tf_op jit(solution)/shard_map/ppermute | solution.py:53
  31.8 51.7 %collective-permute-start.4 = (f32[6,1,18,8,128]{4,3,2,0,1:T(8,128)S(1)}, f32[6,1,18,8,128]{4,3,2,0,1:T(8,128)S(1)}, u32[]{:S(2)}, u32[]{:S(2)}) collective-permute-start(f32[6,1,18,8,128]{4,3,2,0,1:T(8,128)S(1)} %pad_maximum_fusion), channel_id=1, source_target_pairs={{0,2},{2,4},{4,6},{6,0},{1,3},{3,5},{5,7},{7,1},{8,10},{10,12},{12... | collective-permute-start | bytes 1327112 | tf_op jit(solution)/shard_map/ppermute | solution.py:53
  34.0 49.6 %collective-permute-start.5 = (f32[6,1,18,8,128]{4,3,2,0,1:T(8,128)S(1)}, f32[6,1,18,8,128]{4,3,2,0,1:T(8,128)S(1)}, u32[]{:S(2)}, u32[]{:S(2)}) collective-permute-start(f32[6,1,18,8,128]{4,3,2,0,1:T(8,128)S(1)} %pad_maximum_fusion.1), channel_id=1, source_target_pairs={{2,0},{4,2},{6,4},{0,6},{3,1},{5,3},{7,5},{1,7},{10,8},{12,10},{14... | collective-permute-start | bytes 1327112 | tf_op jit(solution)/shard_map/ppermute | solution.py:53
  83.6 1.2 copy-start.1
  112.6 13.2 %all-to-all-start = ((f32[32,8,128]{2,1,0:T(8,128)}), f32[32,8,128]{2,1,0:T(8,128)S(1)}, u32[]{:S(2)}, u32[]{:S(2)}) async-start(f32[32,8,128]{2,1,0:T(8,128)} %shard_map.107), calls=%async_computation | async-start | bytes 262144 | tf_op jit(solution)/shard_map/all_to_all | solution.py:662
  125.9 0.7 copy-start.2

commit v13 on v12

--- a/solution.py
+++ b/solution.py
@@ -16,7 +16,8 @@
 
 INNER_GROUP = 32
 OUTER_GROUP = 16
-FILL = 32
+FILL = 64
+OUTSIDE = 1 << 20
 WORD_BITS = 16
 SLACK = 256
 SPREAD = 4
@@ -57,7 +58,7 @@
     cells, lanes = frag_ref.shape
     held = key_ref.shape[1]
     for comp in range(7):
-        out_ref[:, comp, :] = state_ref[comp]
+        out_ref[:, comp, :] = state_ref[comp] * (damping / stiffness if 3 <= comp < 6 else 1.0)
     keys = jnp.concatenate([key_ref[0:1, :], jnp.zeros((1, lanes - held), jnp.float32)], axis=1)
     keys = jnp.broadcast_to(keys, (8, lanes))
     for block in range(cells // 8):
@@ -96,7 +97,7 @@
     def over(value, by):
         return jnp.floor((value.astype(jnp.float32) + 0.5) * (1.0 / by)).astype(jnp.int32)
 
-    code = code_ref[...]
+    code = code_ref[...] & (OUTSIDE - 1)
     own = over(code, 27)
     kind = code - 27 * own
     step_x = over(kind, 9)
@@ -307,7 +308,7 @@
         )
         scaled = overlap * (other[6] * mine[6])
         root = scaled * lax.rsqrt(jnp.maximum(scaled * reach, 1e-30))
-        factor = root * inverse * (stiffness / damping * overlap - closing * inverse)
+        factor = root * inverse * (overlap - closing * inverse)
         return [factor * apart[axis] for axis in range(3)]
 
     def pairs(step, wide_ref, next_ref, carry):
@@ -358,21 +359,37 @@
 
 
 def inner_kernel(
-    amount_smem, word_smem, cell_smem, groups_smem, table_ref, slots_ref, force_ref,
+    amount_smem, word_smem, cell_smem, groups_smem, table_ref, slots_ref, sums_ref, force_ref,
     list_ref, even_ref, odd_ref, shift_ref,
 ):
     cells, _, lanes = table_ref.shape
     fill_lists(amount_smem[0], word_smem, table_ref, slots_ref, shift_ref, list_ref)
     flat = table_ref.reshape(cells * 8, lanes)
     pair_forces(INNER_GROUP, groups_smem[0], cell_smem, flat, list_ref, force_ref, even_ref, odd_ref)
+    parts = force_ref.reshape(force_ref.shape[0] * 24, lanes)
+
+    def store_sums(block, unused):
+        for half in range(4):
+            at = pl.multiple_of(block * 32 + half * 8, 8)
+            for axis in range(3):
+                sums_ref[axis, pl.ds(at, 8), :] = sublane_sums(parts, at, axis)
+        return unused
+
+    lax.fori_loop(0, cells // 32, store_sums, 0)
 
 
 def outer_kernel(
     near_of, sizes, amount_smem, code_ref, table_ref, halo_ref, inner_ref, arms_ref, frag_ref,
-    fixed_ref, out_ref, force_ref, loads_ref, slots_ref, word_ref, cell_ref, word_smem, cell_smem, sems, list_ref, even_ref, odd_ref, shift_ref, *scratch,
+    key_ref, motion_ref, mass_ref, moment_ref, out_ref, fixed_ref, force_ref, loads_ref, slots_ref, word_ref, cell_ref, word_smem, cell_smem, sems, list_ref, even_ref, odd_ref, shift_ref, *scratch,
 ):
     cells, _, lanes = table_ref.shape
-    held = fixed_ref.shape[1] // 2
+    held = key_ref.shape[1]
+    owned = mass_ref.shape[1]
+    fixed_ref[...] = jnp.zeros(fixed_ref.shape, jnp.float32)
+    fixed_ref[6:7, 0:held] = key_ref[...]
+    fixed_ref[0:6, held : held + owned] = motion_ref[...]
+    fixed_ref[6:7, held : held + owned] = mass_ref[...]
+    fixed_ref[7:8, held : held + owned] = moment_ref[...]
     amount = amount_smem[0]
     groups = list_tiles(
         OUTER_GROUP, amount, near_of, sizes, code_ref, halo_ref, slots_ref, word_ref, cell_ref, *scratch,
@@ -387,25 +404,25 @@
         out_ref[brick] = out
 
 
+def sublane_sums(parts_ref, first, axis):
+    rows = [parts_ref[pl.ds(first * 24 + axis * 8 + part, 8, stride=24), :] for part in range(8)]
+    while len(rows) > 1:
+        rows = [one + other for one, other in zip(rows[::2], rows[1::2])]
+    return rows[0]
+
+
 def fragment_sums(inner_ref, outer_ref, arms_ref, frag_ref, loads_ref, held):
     cells, lanes = frag_ref.shape
     tall = loads_ref.shape[0]
     label = lax.broadcasted_iota(jnp.int32, (held, lanes), 0)
-    parts = [
-        ref.reshape(ref.shape[0] * 24, lanes) for ref in (inner_ref, outer_ref)
-    ]
+    parts = outer_ref.reshape(outer_ref.shape[0] * 24, lanes)
 
     def total_force(block, axis):
         halves = []
         for half in range(tall // 8):
-            first = (block * tall + half * 8) * 24 + axis * 8
-            rows = [
-                ref[pl.ds(first + part, 8, stride=24), :] for ref in parts for part in range(8)
-            ]
-            while len(rows) > 1:
-                rows = [one + other for one, other in zip(rows[::2], rows[1::2])]
-            halves.append(rows[0])
-        return -damping * jnp.concatenate(halves, axis=0)
+            at = pl.multiple_of(block * tall + half * 8, 8)
+            halves.append(sublane_sums(parts, at, axis) + inner_ref[axis, pl.ds(at, 8), :])
+        return -stiffness * jnp.concatenate(halves, axis=0)
 
     def gather_sums(block, total):
         rows = pl.ds(pl.multiple_of(block * tall, tall), tall)
@@ -520,15 +537,6 @@
     flat_arms = arms.reshape(3, cells, lanes)
     flat_frag = sphere_frag.reshape(cells, lanes)
 
-    fixed = jnp.concatenate(
-        [
-            jnp.concatenate([jnp.zeros((6, held)), frag_key[None], jnp.zeros((1, held))], axis=0),
-            jnp.concatenate([clump_motion, inv_mass[None], inv_moment[None]], axis=0),
-            jnp.zeros((8, lanes - held - owned)),
-        ],
-        axis=1,
-    )
-
     face_shape = jax.ShapeDtypeStruct((cells_x * cells_y, 8, lanes), jnp.float32)
     table, z_last, z_first = pl.pallas_call(
         functools.partial(pack_kernel, cells_z),
@@ -538,13 +546,8 @@
         compiler_params=params,
     )(flat_state, flat_frag, frag_key[None])
     grid = table.reshape(cells_x, cells_y, cells_z, 8, lanes)
-    z_before, z_after = exchange(
-        z_last.reshape(cells_x, cells_y, 1, 8, lanes),
-        z_first.reshape(cells_x, cells_y, 1, 8, lanes),
-        "gz",
-    )
-
-    outside = 1 << 20
+    z_before, z_after = exchange(z_last, z_first, "gz")
+
     span_z = cells_z + 2
     starts = [0, cells_x * cells_y, 2 * cells_x * cells_y]
     starts += [starts[-1] + cells_y * span_z, starts[-1] + 2 * cells_y * span_z]
@@ -571,7 +574,7 @@
     sizes = (cells_x, cells_y, cells_z)
     codes = tiles[0]
     total = codes.shape[0]
-    codes = codes + jnp.where(inside(codes), 0, outside)
+    codes = codes + jnp.where(inside(codes), 0, OUTSIDE)
     chunks = total + cells * INNER_GROUP // lanes + 3 * SPREAD
     group_top = -(-(chunks * (lanes // OUTER_GROUP) + SLACK) // (8 * lanes)) * 8 * lanes + 8 * lanes
     force_shape = (cells + 8, 3, 8, lanes)
@@ -597,10 +600,13 @@
     ]
 
     codes = jnp.sort(codes)
-    inner_amount = jnp.sum((codes < outside).astype(jnp.int32))
+    inner_amount = jnp.sum((codes < OUTSIDE).astype(jnp.int32))
     outer_amount = total - inner_amount
     z_before, z_after, codes, inner_amount = lax.optimization_barrier(
         (z_before, z_after, codes, inner_amount)
+    )
+    z_before, z_after = (
+        part.reshape(cells_x, cells_y, 1, 8, lanes) for part in (z_before, z_after)
     )
     x_before, x_after = exchange(
         jnp.concatenate([z_before[-1:], grid[-1:], z_after[-1:]], axis=2),
@@ -614,7 +620,7 @@
         out_specs=(vmem,) * 3 + (smem,),
         scratch_shapes=list_scratch(cells),
         compiler_params=params,
-    )(inner_amount[None], (codes & (outside - 1))[None], table)
+    )(inner_amount[None], codes[None], table)
     x_before, x_after, slots, word, cell_of, groups = lax.optimization_barrier(
         (x_before, x_after, slots, word, cell_of, groups)
     )
@@ -626,15 +632,14 @@
     y_before, y_after = exchange(face(slice(-1, None)), face(slice(0, 1)), "gy")
     inner = pl.pallas_call(
         inner_kernel,
-        out_shape=jax.ShapeDtypeStruct(force_shape, jnp.float32),
+        out_shape=jax.ShapeDtypeStruct((3, cells, lanes), jnp.float32),
         in_specs=[smem] * 4 + [vmem] * 2,
         out_specs=vmem,
-        scratch_shapes=pair_scratch,
+        scratch_shapes=[pltpu.VMEM(force_shape, jnp.float32)] + pair_scratch,
         compiler_params=params,
     )(inner_amount[None], word, cell_of, groups, table, slots)
 
     outer_codes = lax.dynamic_slice(jnp.concatenate([codes, codes]), (inner_amount,), (total,))
-    outer_codes = outer_codes & (outside - 1)
     halo = jnp.concatenate(
         [
             part.reshape(-1, 8, lanes)
@@ -646,9 +651,10 @@
     known = pl.pallas_call(
         functools.partial(outer_kernel, near_outside, sizes),
         out_shape=jax.ShapeDtypeStruct((bricks, 8, lanes), jnp.float32),
-        in_specs=[smem] + [vmem] * 7,
+        in_specs=[smem] + [vmem] * 10,
         out_specs=vmem,
         scratch_shapes=[
+            pltpu.VMEM((8, lanes), jnp.float32),
             pltpu.VMEM(force_shape, jnp.float32),
             pltpu.VMEM((16, 8, lanes), jnp.float32),
         ]
@@ -658,7 +664,8 @@
         + pair_scratch
         + list_scratch(halo.shape[0]),
         compiler_params=params,
-    )(outer_amount[None], outer_codes[None], table, halo, inner, flat_arms, flat_frag, fixed)
+    )(outer_amount[None], outer_codes[None], table, halo, inner, flat_arms, flat_frag,
+        frag_key[None], clump_motion, inv_mass[None], inv_moment[None])
     known = lax.all_to_all(known, names, split_axis=0, concat_axis=0, tiled=True)
 
     brick = lax.axis_index(names)

time: 132 us -> 127 us (0.962)
  Pallas kernels: 91.4 us -> 88.8 us
    reshape x2 -> x0, local copies, waits for them, and re-layouts: 1.78 us -> none  [the longest x1 0.93 us: local(): z_last.reshape(cells_x, cells_y, 1, 8, lanes)]
    pallas_call x1, Pallas kernels: 27.8 us -> 26.3 us  [local(): pl.pallas_call(functools.partial(outer_kernel, near_outside, sizes), out_...]
    unnamed x20 -> x18, local copies, waits for them, and re-layouts: 1.96 us -> 3.01 us
where the time goes in v13:
time: 127 us
  Pallas kernels  88.8 us (70%)
  starting transfers between devices  14.5 us (11%)
  other arithmetic  8.52 us (7%)
  waiting for transfers between devices  6.93 us (5%)
  local copies, waits for them, and re-layouts  4.88 us (4%)
  between operations  3.4 us (3%)
    pallas_call x1, Pallas kernels, local(): pl.pallas_call(inner_kernel, out_shape=jax.ShapeDtypeStruct((3, cells, la...  46.3 us
    pallas_call x1, Pallas kernels, local(): pl.pallas_call(functools.partial(outer_kernel, near_outside, sizes), out_...  26.3 us
    ppermute x6, starting transfers between devices, exchange(): return (lax.ppermute(last, axis, up), lax.ppermute(initial, axis, down))  9.03 us
    pallas_call x1, Pallas kernels, local(): pl.pallas_call(functools.partial(list_kernel, near_inside, sizes), out_sh...  8.64 us
    all_to_all x1, waiting for transfers between devices, local(): lax.all_to_all(known, names, split_axis=0, concat_axis=0, tiled=True)  6.91 us
    all_to_all x1, starting transfers between devices, local(): lax.all_to_all(known, names, split_axis=0, concat_axis=0, tiled=True)  5.42 us
    sort x1, other arithmetic, local(): codes = jnp.sort(codes)  5.03 us
    pallas_call x1, Pallas kernels, local(): pl.pallas_call(functools.partial(move_kernel, owned), out_shape=(jax.Shap...  4.65 us
  transfers between devices with their start and end apart: 7, of which 1 were waited for; matrix products, arithmetic and copies ran while one was open for 8% of the time, Pallas kernels for 43%

profile of v13, /device:TPU:0, one launch (start us, length us, event | category | flops | bytes accessed | tf_op | source)
XLA Modules:
  0.0 127.0 jit_solution(12663438105328113964)
XLA Ops:
  0.6 1.2 fusion.13
  1.8 2.9 %shard_map.104 = (f32[256,8,128]{2,1,0:T(8,128)}, f32[16,8,128]{2,1,0:T(8,128)}, f32[16,8,128]{2,1,0:T(8,128)}) custom-call(f32[7,256,128]{2,1,0:T(8,128)} %bitcast.61, s32[256,128]{1,0:T(8,128)} %bitcast.65, f32[1,64]{1,0:T(1,128)} %bitcast.79), custom_call_target="tpu_custom_call" | custom-call | tf_op jit(solution)/shard_map/pallas_call | solution.py:541
  4.7 3.0 %collective-permute-start = (f32[16,8,128]{2,1,0:T(8,128)}, f32[16,8,128]{2,1,0:T(8,128)S(1)}, u32[]{:S(2)}, u32[]{:S(2)}) collective-permute-start(f32[16,8,128]{2,1,0:T(8,128)} %get-tuple-element.24), channel_id=1, source_target_pairs={{0,1},{1,0},{2,3},{3,2},{4,5},{5,4},{6,7},{7,6},{8,9},{9,8},{10,11... | collective-permute-start | bytes 196616 | tf_op jit(solution)/shard_map/ppermute | solution.py:54
  7.7 0.0 collective-permute-start.1
  7.7 0.8 select_add_fusion
  8.5 1.1 fusion.15
  9.6 1.1 slice_bitcast_fusion
  10.6 5.0 %sort.15 = (s32[2048]{0:T(1024)S(1)}, s32[2048]{0:T(1024)}) sort(s32[2048]{0:T(1024)S(1)} %select_add_fusion, s32[2048]{0:T(1024)S(1)} %iota.11), dimensions={0}, to_apply=%region_0.1 | sort | flops 22528 | bytes 32768 | tf_op jit(solution)/shard_map/jit(sort)/sort | solution.py:602
  15.7 0.7 convert_reduce_fusion
  17.1 0.1 collective-permute-start.2
  17.2 1.8 %collective-permute-start.3 = (f32[1,4,18,8,128]{4,3,2,0,1:T(8,128)S(1)}, f32[1,4,18,8,128]{4,3,2,0,1:T(8,128)S(1)}, u32[]{:S(2)}, u32[]{:S(2)}) collective-permute-start(f32[1,4,18,8,128]{4,3,2,0,1:T(8,128)S(1)} %pad_maximum_fusion.3), channel_id=1, source_target_pairs={{8,0},{16,8},{24,16},{0,24},{9,1},{17,9},{25,17},{1,25},{10,2},{18... | collective-permute-start | bytes 884744 | tf_op jit(solution)/shard_map/ppermute | solution.py:54
  20.2 8.6 %shard_map.105 = (s32[2048,128]{1,0:T(8,128)}, s32[1,2048]{1,0:T(1,128)}, s32[1,18432]{1,0:T(1,128)}, s32[1]{0:T(128)}) custom-call(s32[1]{0:T(128)} %bitcast.20.amount_smem, s32[1,2048]{1,0:T(1,128)} %bitcast.76, f32[256,8,128]{2,1,0:T(8,128)} %get-tuple-element.28.table_ref), custom_call_target="tpu_custom_call" | custom-call | tf_op jit(solution)/shard_map/pallas_call | solution.py:616
  29.6 2.1 %collective-permute-start.4 = (f32[6,1,18,8,128]{4,3,2,0,1:T(8,128)S(1)}, f32[6,1,18,8,128]{4,3,2,0,1:T(8,128)S(1)}, u32[]{:S(2)}, u32[]{:S(2)}) collective-permute-start(f32[6,1,18,8,128]{4,3,2,0,1:T(8,128)S(1)} %pad_maximum_fusion), channel_id=1, source_target_pairs={{0,2},{2,4},{4,6},{6,0},{1,3},{3,5},{5,7},{7,1},{8,10},{10,12},{12... | collective-permute-start | bytes 1327112 | tf_op jit(solution)/shard_map/ppermute | solution.py:54
  31.8 2.1 %collective-permute-start.5 = (f32[6,1,18,8,128]{4,3,2,0,1:T(8,128)S(1)}, f32[6,1,18,8,128]{4,3,2,0,1:T(8,128)S(1)}, u32[]{:S(2)}, u32[]{:S(2)}) collective-permute-start(f32[6,1,18,8,128]{4,3,2,0,1:T(8,128)S(1)} %pad_maximum_fusion.1), channel_id=1, source_target_pairs={{2,0},{4,2},{6,4},{0,6},{3,1},{5,3},{7,5},{1,7},{10,8},{12,10},{14... | collective-permute-start | bytes 1327112 | tf_op jit(solution)/shard_map/ppermute | solution.py:54
  33.9 0.7 fusion.9
  34.6 46.3 %shard_map.106.inner_ref = f32[3,256,128]{2,1,0:T(8,128)} custom-call(s32[1]{0:T(128)} %bitcast.20.amount_smem, s32[1,2048]{1,0:T(1,128)} %get-tuple-element.37.word_smem, s32[1,18432]{1,0:T(1,128)} %get-tuple-element.38.cell_smem, s32[1]{0:T(128)} %get-tuple-element.39.groups_smem, f32[256,8,128]{2,1,0:T(8,128)} %get-tuple-element.28.table_ref, ...), custom_call_target="tpu_custom_call" | custom-call | tf_op jit(solution)/shard_map/pallas_call | solution.py:633
  81.1 1.2 copy-done
  82.2 26.3 %shard_map.107 = f32[32,8,128]{2,1,0:T(8,128)} custom-call(s32[1]{0:T(128)} %bitcast.3.amount_smem, s32[1,2048]{1,0:T(1,128)} %bitcast.77, f32[256,8,128]{2,1,0:T(8,128)} %get-tuple-element.28.table_ref, f32[392,8,128]{2,1,0:T(8,128)} %copy-done, f32[3,256,128]{2,1,0:T(8,128)} %shard_map.106.inner_ref, f32[3,256,128]{2,1,0:T(8,128)} %bitcast.63, ...), custom_call_target="tpu_custom_call" | custom-call | tf_op jit(solution)/shard_map/pallas_call | solution.py:651
  108.5 5.4 %all-to-all-start = ((f32[32,8,128]{2,1,0:T(8,128)}), f32[32,8,128]{2,1,0:T(8,128)S(1)}, u32[]{:S(2)}, u32[]{:S(2)}) async-start(f32[32,8,128]{2,1,0:T(8,128)} %shard_map.107), calls=%async_computation | async-start | bytes 262144 | tf_op jit(solution)/shard_map/all_to_all | solution.py:669
  114.0 0.1 maximum_bitcast_fusion
  114.0 0.7 copy.23.target_ref
  114.8 6.9 %all-to-all-done.known_ref = f32[32,8,128]{2,1,0:T(8,128)S(1)} async-done(((f32[32,8,128]{2,1,0:T(8,128)}), f32[32,8,128]{2,1,0:T(8,128)S(1)}, u32[]{:S(2)}, u32[]{:S(2)}) %all-to-all-start) | async-done | bytes 131104 | tf_op jit(solution)/shard_map/all_to_all | solution.py:669
  121.7 0.6 copy-done.1
  122.3 4.7 %shard_map.108 = (f32[6,256,128]{2,1,0:T(8,128)}, f32[6,128]{1,0:T(8,128)}) custom-call(f32[128,1]{1,0:T(8,128)} %copy.23.target_ref, f32[32,8,128]{2,1,0:T(8,128)} %copy-done.1, f32[7,256,128]{2,1,0:T(8,128)} %bitcast.62, f32[3,256,128]{2,1,0:T(8,128)} %bitcast.64, s32[256,128]{1,0:T(8,128)} %bitcast.67), custom_call_target="tpu_custom_call" | custom-call | tf_op jit(solution)/shard_map/pallas_call | solution.py:676
  (31 shorter events, 0.3 us)
Async XLA Ops:
  4.7 12.3 %collective-permute-start = (f32[16,8,128]{2,1,0:T(8,128)}, f32[16,8,128]{2,1,0:T(8,128)S(1)}, u32[]{:S(2)}, u32[]{:S(2)}) collective-permute-start(f32[16,8,128]{2,1,0:T(8,128)} %get-tuple-element.24), channel_id=1, source_target_pairs={{0,1},{1,0},{2,3},{3,2},{4,5},{5,4},{6,7},{7,6},{8,9},{9,8},{10,11... | collective-permute-start | bytes 196616 | tf_op jit(solution)/shard_map/ppermute | solution.py:54
  7.7 9.3 %collective-permute-start.1 = (f32[16,8,128]{2,1,0:T(8,128)}, f32[16,8,128]{2,1,0:T(8,128)S(1)}, u32[]{:S(2)}, u32[]{:S(2)}) collective-permute-start(f32[16,8,128]{2,1,0:T(8,128)} %get-tuple-element.25), channel_id=1, source_target_pairs={{1,0},{0,1},{3,2},{2,3},{5,4},{4,5},{7,6},{6,7},{9,8},{8,9},{11,10... | collective-permute-start | bytes 196616 | tf_op jit(solution)/shard_map/ppermute | solution.py:54
  15.7 4.5 %copy-start.2 = (s32[2048]{0:T(1024)}, s32[2048]{0:T(1024)S(1)}, u32[]{:S(2)}) copy-start(s32[2048]{0:T(1024)S(1)} %get-tuple-element.26) | copy-start | bytes 24580
  17.1 12.5 %collective-permute-start.2 = (f32[1,4,18,8,128]{4,3,2,0,1:T(8,128)S(1)}, f32[1,4,18,8,128]{4,3,2,0,1:T(8,128)S(1)}, u32[]{:S(2)}, u32[]{:S(2)}) collective-permute-start(f32[1,4,18,8,128]{4,3,2,0,1:T(8,128)S(1)} %pad_maximum_fusion.2), channel_id=1, source_target_pairs={{0,8},{8,16},{16,24},{24,0},{1,9},{9,17},{17,25},{25,1},{2,10},{10... | collective-permute-start | bytes 884744 | tf_op jit(solution)/shard_map/ppermute | solution.py:54
  17.2 12.4 %collective-permute-start.3 = (f32[1,4,18,8,128]{4,3,2,0,1:T(8,128)S(1)}, f32[1,4,18,8,128]{4,3,2,0,1:T(8,128)S(1)}, u32[]{:S(2)}, u32[]{:S(2)}) collective-permute-start(f32[1,4,18,8,128]{4,3,2,0,1:T(8,128)S(1)} %pad_maximum_fusion.3), channel_id=1, source_target_pairs={{8,0},{16,8},{24,16},{0,24},{9,1},{17,9},{25,17},{1,25},{10,2},{18... | collective-permute-start | bytes 884744 | tf_op jit(solution)/shard_map/ppermute | solution.py:54
  28.9 5.0 %copy-start.3 = (s32[2048]{0:T(1024)S(1)}, s32[2048]{0:T(1024)}, u32[]{:S(2)}) copy-start(s32[2048]{0:T(1024)} %copy-done.2) | copy-start | bytes 24580
  29.6 51.3 %collective-permute-start.4 = (f32[6,1,18,8,128]{4,3,2,0,1:T(8,128)S(1)}, f32[6,1,18,8,128]{4,3,2,0,1:T(8,128)S(1)}, u32[]{:S(2)}, u32[]{:S(2)}) collective-permute-start(f32[6,1,18,8,128]{4,3,2,0,1:T(8,128)S(1)} %pad_maximum_fusion), channel_id=1, source_target_pairs={{0,2},{2,4},{4,6},{6,0},{1,3},{3,5},{5,7},{7,1},{8,10},{10,12},{12... | collective-permute-start | bytes 1327112 | tf_op jit(solution)/shard_map/ppermute | solution.py:54
  31.8 49.2 %collective-permute-start.5 = (f32[6,1,18,8,128]{4,3,2,0,1:T(8,128)S(1)}, f32[6,1,18,8,128]{4,3,2,0,1:T(8,128)S(1)}, u32[]{:S(2)}, u32[]{:S(2)}) collective-permute-start(f32[6,1,18,8,128]{4,3,2,0,1:T(8,128)S(1)} %pad_maximum_fusion.1), channel_id=1, source_target_pairs={{2,0},{4,2},{6,4},{0,6},{3,1},{5,3},{7,5},{1,7},{10,8},{12,10},{14... | collective-permute-start | bytes 1327112 | tf_op jit(solution)/shard_map/ppermute | solution.py:54
  81.1 1.2 copy-start
  82.2 31.7 %copy-start.4 = (f32[64]{0:T(128)S(1)}, f32[64]{0:T(128)}, u32[]{:S(2)}) copy-start(f32[64]{0:T(128)} %get-tuple-element.60) | copy-start | bytes 772
  108.5 13.2 %all-to-all-start = ((f32[32,8,128]{2,1,0:T(8,128)}), f32[32,8,128]{2,1,0:T(8,128)S(1)}, u32[]{:S(2)}, u32[]{:S(2)}) async-start(f32[32,8,128]{2,1,0:T(8,128)} %shard_map.107), calls=%async_computation | async-start | bytes 262144 | tf_op jit(solution)/shard_map/all_to_all | solution.py:669
  121.7 0.7 copy-start.1

commit v14 on v13

--- a/solution.py
+++ b/solution.py
@@ -16,7 +16,9 @@
 
 INNER_GROUP = 32
 OUTER_GROUP = 16
-FILL = 64
+FILL = 16
+INNER_FILL = 48
+OUTER_FILL = 88
 OUTSIDE = 1 << 20
 WORD_BITS = 16
 SLACK = 256
@@ -238,19 +240,28 @@
     return groups
 
 
-def fill_lists(amount, word_smem, near_table_ref, slots_ref, shift_ref, list_ref):
-    lanes = slots_ref.shape[1]
+def pair_forces(
+    group, beside, amount, groups, word_smem, cell_smem, table_ref, near_table_ref, slots_ref,
+    shift_ref, list_ref, force_ref, even_ref, odd_ref,
+):
+    lanes = table_ref.shape[1]
+    cells = table_ref.shape[0] // 8
+    rows = even_ref.shape[0]
+    chunks = rows // lanes
+    units = rows // group
     row = lax.broadcasted_iota(jnp.int32, (8, lanes), 0)
     absent = jnp.where(row == 6, -10.0, 0.0)
     for kind in range(27):
         steps = (kind // 9 - 1.0, kind // 3 % 3 - 1.0, kind % 3 - 1.0)
         shift_ref[kind] = sum(jnp.where(row == axis, steps[axis], 0.0) for axis in range(3))
-
-    def fill(block, carry):
-        last_chunk, last_new, last_held = carry
-        words = [word_smem[0, block * FILL + unit] for unit in range(FILL)]
-        for unit, word in enumerate(words):
-            slots = slots_ref[pl.ds(block * FILL + unit, 8, stride=0), :]
+    last_tile = jnp.maximum(amount - 1, 0)
+
+    def fill(count, state):
+        tile, _, last_chunk, last_new, last_held = state
+        places = [jnp.minimum(tile + unit, last_tile) for unit in range(count + 1)]
+        words = [word_smem[0, place] for place in places]
+        for place, word in zip(places[:count], words):
+            slots = slots_ref[pl.ds(place, 8, stride=0), :]
             cell = near_table_ref[(word >> 5) & ((1 << (WORD_BITS - 5)) - 1)]
             found = lanes_of(cell, slots & (lanes - 1)) + shift_ref[word & 31]
             chunk = word >> WORD_BITS
@@ -262,18 +273,13 @@
             list_ref[chunk] = held_row
             list_ref[chunk + 1] = new
             last_chunk, last_new, last_held = chunk, new, held_row
-        return last_chunk, last_new, last_held
-
-    blocks = lax.div(amount + (FILL - 1), FILL)
-    lax.fori_loop(0, blocks, fill, (jnp.int32(0), absent, absent))
-
-
-def pair_forces(group, groups, cell_smem, table_ref, list_ref, force_ref, even_ref, odd_ref):
-    lanes = table_ref.shape[1]
-    cells = table_ref.shape[0] // 8
-    rows = even_ref.shape[0]
-    chunks = rows // lanes
-    units = rows // group
+        return tile + count, words[count] >> WORD_BITS, last_chunk, last_new, last_held
+
+    def catch_up(limit, state):
+        return lax.while_loop(
+            lambda state: (state[0] < amount) & (state[1] <= limit), functools.partial(fill, FILL), state
+        )
+
     force_ref[...] = jnp.zeros(force_ref.shape, jnp.float32)
     part = lax.broadcasted_iota(jnp.int32, (32, 8 * lanes), 0)
     comp = lax.broadcasted_iota(jnp.int32, (32, 8 * lanes), 1) // lanes
@@ -311,9 +317,8 @@
         factor = root * inverse * (overlap - closing * inverse)
         return [factor * apart[axis] for axis in range(3)]
 
-    def pairs(step, wide_ref, next_ref, carry):
+    def pairs(step, wide_ref, carry):
         last, running = carry
-        spread(step + 1, next_ref)
         for unit in range(units):
             cell = cell_smem[0, step * units + unit]
             own = jnp.minimum(cell, cells - 1) * 8
@@ -327,15 +332,20 @@
                 force_ref[cell, axis] = running[axis]
         return last, running
 
+    def both(step, carry):
+        state, carry = carry
+        state = catch_up((2 * step + 3) * chunks - 1, state)
+        spread(2 * step + 1, odd_ref)
+        state = fill(beside, state)
+        carry = pairs(2 * step, even_ref, carry)
+        spread(2 * step + 2, even_ref)
+        return state, pairs(2 * step + 1, odd_ref, carry)
+
+    zero = jnp.zeros((8, lanes), jnp.float32)
+    state = catch_up(3 * chunks - 1, (jnp.int32(0), jnp.int32(0), jnp.int32(0), absent, absent))
     spread(0, even_ref)
-
-    def both(step, carry):
-        carry = pairs(2 * step, even_ref, odd_ref, carry)
-        return pairs(2 * step + 1, odd_ref, even_ref, carry)
-
-    zero = jnp.zeros((8, lanes), jnp.float32)
     steps = lax.div(groups + (2 * units - 1), 2 * units)
-    lax.fori_loop(0, steps, both, (jnp.int32(-1), [zero] * 3))
+    lax.fori_loop(0, steps, both, (state, (jnp.int32(-1), [zero] * 3)))
 
 
 def to_scalars(pairs, sems):
@@ -363,9 +373,11 @@
     list_ref, even_ref, odd_ref, shift_ref,
 ):
     cells, _, lanes = table_ref.shape
-    fill_lists(amount_smem[0], word_smem, table_ref, slots_ref, shift_ref, list_ref)
-    flat = table_ref.reshape(cells * 8, lanes)
-    pair_forces(INNER_GROUP, groups_smem[0], cell_smem, flat, list_ref, force_ref, even_ref, odd_ref)
+    pair_forces(
+        INNER_GROUP, INNER_FILL, amount_smem[0], groups_smem[0], word_smem, cell_smem,
+        table_ref.reshape(cells * 8, lanes), table_ref, slots_ref, shift_ref, list_ref, force_ref,
+        even_ref, odd_ref,
+    )
     parts = force_ref.reshape(force_ref.shape[0] * 24, lanes)
 
     def store_sums(block, unused):
@@ -395,9 +407,11 @@
         OUTER_GROUP, amount, near_of, sizes, code_ref, halo_ref, slots_ref, word_ref, cell_ref, *scratch,
     )
     to_scalars([(word_ref, word_smem), (cell_ref, cell_smem)], sems)
-    fill_lists(amount, word_smem, halo_ref, slots_ref, shift_ref, list_ref)
-    flat = table_ref.reshape(cells * 8, lanes)
-    pair_forces(OUTER_GROUP, groups, cell_smem, flat, list_ref, force_ref, even_ref, odd_ref)
+    pair_forces(
+        OUTER_GROUP, OUTER_FILL, amount, groups, word_smem, cell_smem,
+        table_ref.reshape(cells * 8, lanes), halo_ref, slots_ref, shift_ref, list_ref, force_ref,
+        even_ref, odd_ref,
+    )
     sums = fragment_sums(inner_ref, force_ref, arms_ref, frag_ref, loads_ref, held)
     out = fixed_ref[...] + jnp.concatenate([sums, jnp.zeros_like(sums)], axis=1)
     for brick in range(out_ref.shape[0]):

time: 127 us -> 129 us (1.016)
  no operation moved by 1% of the time
where the time goes in v14:
time: 129 us
  Pallas kernels  89.9 us (70%)
  starting transfers between devices  14.9 us (12%)
  other arithmetic  8.52 us (7%)
  waiting for transfers between devices  6.93 us (5%)
  local copies, waits for them, and re-layouts  4.88 us (4%)
  between operations  3.4 us (3%)
    pallas_call x1, Pallas kernels, local(): pl.pallas_call(inner_kernel, out_shape=jax.ShapeDtypeStruct((3, cells, la...  46.3 us
    pallas_call x1, Pallas kernels, local(): pl.pallas_call(functools.partial(outer_kernel, near_outside, sizes), out_...  27.3 us
    ppermute x6, starting transfers between devices, exchange(): return (lax.ppermute(last, axis, up), lax.ppermute(initial, axis, down))  9.03 us
    pallas_call x1, Pallas kernels, local(): pl.pallas_call(functools.partial(list_kernel, near_inside, sizes), out_sh...  8.64 us
    all_to_all x1, waiting for transfers between devices, local(): lax.all_to_all(known, names, split_axis=0, concat_axis=0, tiled=True)  6.91 us
    all_to_all x1, starting transfers between devices, local(): lax.all_to_all(known, names, split_axis=0, concat_axis=0, tiled=True)  5.86 us
    sort x1, other arithmetic, local(): codes = jnp.sort(codes)  5.03 us
    pallas_call x1, Pallas kernels, local(): pl.pallas_call(functools.partial(move_kernel, owned), out_shape=(jax.Shap...  4.66 us
  transfers between devices with their start and end apart: 7, of which 1 were waited for; matrix products, arithmetic and copies ran while one was open for 8% of the time, Pallas kernels for 43%

profile of v14, /device:TPU:0, one launch (start us, length us, event | category | flops | bytes accessed | tf_op | source)
XLA Modules:
  0.0 128.5 jit_solution(6472678296880611433)
XLA Ops:
  0.6 1.2 fusion.13
  1.8 2.9 %shard_map.104 = (f32[256,8,128]{2,1,0:T(8,128)}, f32[16,8,128]{2,1,0:T(8,128)}, f32[16,8,128]{2,1,0:T(8,128)}) custom-call(f32[7,256,128]{2,1,0:T(8,128)} %bitcast.61, s32[256,128]{1,0:T(8,128)} %bitcast.65, f32[1,64]{1,0:T(1,128)} %bitcast.79), custom_call_target="tpu_custom_call" | custom-call | tf_op jit(solution)/shard_map/pallas_call | solution.py:555
  4.7 3.0 %collective-permute-start = (f32[16,8,128]{2,1,0:T(8,128)}, f32[16,8,128]{2,1,0:T(8,128)S(1)}, u32[]{:S(2)}, u32[]{:S(2)}) collective-permute-start(f32[16,8,128]{2,1,0:T(8,128)} %get-tuple-element.24), channel_id=1, source_target_pairs={{0,1},{1,0},{2,3},{3,2},{4,5},{5,4},{6,7},{7,6},{8,9},{9,8},{10,11... | collective-permute-start | bytes 196616 | tf_op jit(solution)/shard_map/ppermute | solution.py:56
  7.7 0.0 collective-permute-start.1
  7.7 0.8 select_add_fusion
  8.5 1.1 fusion.15
  9.6 1.1 slice_bitcast_fusion
  10.6 5.0 %sort.15 = (s32[2048]{0:T(1024)S(1)}, s32[2048]{0:T(1024)}) sort(s32[2048]{0:T(1024)S(1)} %select_add_fusion, s32[2048]{0:T(1024)S(1)} %iota.11), dimensions={0}, to_apply=%region_0.1 | sort | flops 22528 | bytes 32768 | tf_op jit(solution)/shard_map/jit(sort)/sort | solution.py:616
  15.7 0.7 convert_reduce_fusion
  17.1 0.1 collective-permute-start.2
  17.2 1.8 %collective-permute-start.3 = (f32[1,4,18,8,128]{4,3,2,0,1:T(8,128)S(1)}, f32[1,4,18,8,128]{4,3,2,0,1:T(8,128)S(1)}, u32[]{:S(2)}, u32[]{:S(2)}) collective-permute-start(f32[1,4,18,8,128]{4,3,2,0,1:T(8,128)S(1)} %pad_maximum_fusion.3), channel_id=1, source_target_pairs={{8,0},{16,8},{24,16},{0,24},{9,1},{17,9},{25,17},{1,25},{10,2},{18... | collective-permute-start | bytes 884744 | tf_op jit(solution)/shard_map/ppermute | solution.py:56
  20.2 8.6 %shard_map.105 = (s32[2048,128]{1,0:T(8,128)}, s32[1,2048]{1,0:T(1,128)}, s32[1,18432]{1,0:T(1,128)}, s32[1]{0:T(128)}) custom-call(s32[1]{0:T(128)} %bitcast.20.amount_smem, s32[1,2048]{1,0:T(1,128)} %bitcast.76, f32[256,8,128]{2,1,0:T(8,128)} %get-tuple-element.28.table_ref), custom_call_target="tpu_custom_call" | custom-call | tf_op jit(solution)/shard_map/pallas_call | solution.py:630
  29.6 2.1 %collective-permute-start.4 = (f32[6,1,18,8,128]{4,3,2,0,1:T(8,128)S(1)}, f32[6,1,18,8,128]{4,3,2,0,1:T(8,128)S(1)}, u32[]{:S(2)}, u32[]{:S(2)}) collective-permute-start(f32[6,1,18,8,128]{4,3,2,0,1:T(8,128)S(1)} %pad_maximum_fusion), channel_id=1, source_target_pairs={{0,2},{2,4},{4,6},{6,0},{1,3},{3,5},{5,7},{7,1},{8,10},{10,12},{12... | collective-permute-start | bytes 1327112 | tf_op jit(solution)/shard_map/ppermute | solution.py:56
  31.8 2.1 %collective-permute-start.5 = (f32[6,1,18,8,128]{4,3,2,0,1:T(8,128)S(1)}, f32[6,1,18,8,128]{4,3,2,0,1:T(8,128)S(1)}, u32[]{:S(2)}, u32[]{:S(2)}) collective-permute-start(f32[6,1,18,8,128]{4,3,2,0,1:T(8,128)S(1)} %pad_maximum_fusion.1), channel_id=1, source_target_pairs={{2,0},{4,2},{6,4},{0,6},{3,1},{5,3},{7,5},{1,7},{10,8},{12,10},{14... | collective-permute-start | bytes 1327112 | tf_op jit(solution)/shard_map/ppermute | solution.py:56
  33.9 0.7 fusion.9
  34.6 46.3 %shard_map.106.inner_ref = f32[3,256,128]{2,1,0:T(8,128)} custom-call(s32[1]{0:T(128)} %bitcast.20.amount_smem, s32[1,2048]{1,0:T(1,128)} %get-tuple-element.37.word_smem, s32[1,18432]{1,0:T(1,128)} %get-tuple-element.38.cell_smem, s32[1]{0:T(128)} %get-tuple-element.39.groups_smem, f32[256,8,128]{2,1,0:T(8,128)} %get-tuple-element.28.table_ref, ...), custom_call_target="tpu_custom_call" | custom-call | tf_op jit(solution)/shard_map/pallas_call | solution.py:647
  81.1 1.2 copy-done
  82.2 27.3 %shard_map.107 = f32[32,8,128]{2,1,0:T(8,128)} custom-call(s32[1]{0:T(128)} %bitcast.3.amount_smem, s32[1,2048]{1,0:T(1,128)} %bitcast.77, f32[256,8,128]{2,1,0:T(8,128)} %get-tuple-element.28.table_ref, f32[392,8,128]{2,1,0:T(8,128)} %copy-done, f32[3,256,128]{2,1,0:T(8,128)} %shard_map.106.inner_ref, f32[3,256,128]{2,1,0:T(8,128)} %bitcast.63, ...), custom_call_target="tpu_custom_call" | custom-call | tf_op jit(solution)/shard_map/pallas_call | solution.py:665
  109.6 5.9 %all-to-all-start = ((f32[32,8,128]{2,1,0:T(8,128)}), f32[32,8,128]{2,1,0:T(8,128)S(1)}, u32[]{:S(2)}, u32[]{:S(2)}) async-start(f32[32,8,128]{2,1,0:T(8,128)} %shard_map.107), calls=%async_computation | async-start | bytes 262144 | tf_op jit(solution)/shard_map/all_to_all | solution.py:683
  115.5 0.1 maximum_bitcast_fusion
  115.5 0.7 copy.23.target_ref
  116.3 6.9 %all-to-all-done.known_ref = f32[32,8,128]{2,1,0:T(8,128)S(1)} async-done(((f32[32,8,128]{2,1,0:T(8,128)}), f32[32,8,128]{2,1,0:T(8,128)S(1)}, u32[]{:S(2)}, u32[]{:S(2)}) %all-to-all-start) | async-done | bytes 131104 | tf_op jit(solution)/shard_map/all_to_all | solution.py:683
  123.2 0.6 copy-done.1
  123.8 4.7 %shard_map.108 = (f32[6,256,128]{2,1,0:T(8,128)}, f32[6,128]{1,0:T(8,128)}) custom-call(f32[128,1]{1,0:T(8,128)} %copy.23.target_ref, f32[32,8,128]{2,1,0:T(8,128)} %copy-done.1, f32[7,256,128]{2,1,0:T(8,128)} %bitcast.62, f32[3,256,128]{2,1,0:T(8,128)} %bitcast.64, s32[256,128]{1,0:T(8,128)} %bitcast.67), custom_call_target="tpu_custom_call" | custom-call | tf_op jit(solution)/shard_map/pallas_call | solution.py:690
  (31 shorter events, 0.3 us)
Async XLA Ops:
  4.7 12.3 %collective-permute-start = (f32[16,8,128]{2,1,0:T(8,128)}, f32[16,8,128]{2,1,0:T(8,128)S(1)}, u32[]{:S(2)}, u32[]{:S(2)}) collective-permute-start(f32[16,8,128]{2,1,0:T(8,128)} %get-tuple-element.24), channel_id=1, source_target_pairs={{0,1},{1,0},{2,3},{3,2},{4,5},{5,4},{6,7},{7,6},{8,9},{9,8},{10,11... | collective-permute-start | bytes 196616 | tf_op jit(solution)/shard_map/ppermute | solution.py:56
  7.7 9.3 %collective-permute-start.1 = (f32[16,8,128]{2,1,0:T(8,128)}, f32[16,8,128]{2,1,0:T(8,128)S(1)}, u32[]{:S(2)}, u32[]{:S(2)}) collective-permute-start(f32[16,8,128]{2,1,0:T(8,128)} %get-tuple-element.25), channel_id=1, source_target_pairs={{1,0},{0,1},{3,2},{2,3},{5,4},{4,5},{7,6},{6,7},{9,8},{8,9},{11,10... | collective-permute-start | bytes 196616 | tf_op jit(solution)/shard_map/ppermute | solution.py:56
  15.7 4.5 %copy-start.2 = (s32[2048]{0:T(1024)}, s32[2048]{0:T(1024)S(1)}, u32[]{:S(2)}) copy-start(s32[2048]{0:T(1024)S(1)} %get-tuple-element.26) | copy-start | bytes 24580
  17.1 12.5 %collective-permute-start.2 = (f32[1,4,18,8,128]{4,3,2,0,1:T(8,128)S(1)}, f32[1,4,18,8,128]{4,3,2,0,1:T(8,128)S(1)}, u32[]{:S(2)}, u32[]{:S(2)}) collective-permute-start(f32[1,4,18,8,128]{4,3,2,0,1:T(8,128)S(1)} %pad_maximum_fusion.2), channel_id=1, source_target_pairs={{0,8},{8,16},{16,24},{24,0},{1,9},{9,17},{17,25},{25,1},{2,10},{10... | collective-permute-start | bytes 884744 | tf_op jit(solution)/shard_map/ppermute | solution.py:56
  17.2 12.4 %collective-permute-start.3 = (f32[1,4,18,8,128]{4,3,2,0,1:T(8,128)S(1)}, f32[1,4,18,8,128]{4,3,2,0,1:T(8,128)S(1)}, u32[]{:S(2)}, u32[]{:S(2)}) collective-permute-start(f32[1,4,18,8,128]{4,3,2,0,1:T(8,128)S(1)} %pad_maximum_fusion.3), channel_id=1, source_target_pairs={{8,0},{16,8},{24,16},{0,24},{9,1},{17,9},{25,17},{1,25},{10,2},{18... | collective-permute-start | bytes 884744 | tf_op jit(solution)/shard_map/ppermute | solution.py:56
  28.9 5.0 %copy-start.3 = (s32[2048]{0:T(1024)S(1)}, s32[2048]{0:T(1024)}, u32[]{:S(2)}) copy-start(s32[2048]{0:T(1024)} %copy-done.2) | copy-start | bytes 24580
  29.6 51.3 %collective-permute-start.4 = (f32[6,1,18,8,128]{4,3,2,0,1:T(8,128)S(1)}, f32[6,1,18,8,128]{4,3,2,0,1:T(8,128)S(1)}, u32[]{:S(2)}, u32[]{:S(2)}) collective-permute-start(f32[6,1,18,8,128]{4,3,2,0,1:T(8,128)S(1)} %pad_maximum_fusion), channel_id=1, source_target_pairs={{0,2},{2,4},{4,6},{6,0},{1,3},{3,5},{5,7},{7,1},{8,10},{10,12},{12... | collective-permute-start | bytes 1327112 | tf_op jit(solution)/shard_map/ppermute | solution.py:56
  31.8 49.2 %collective-permute-start.5 = (f32[6,1,18,8,128]{4,3,2,0,1:T(8,128)S(1)}, f32[6,1,18,8,128]{4,3,2,0,1:T(8,128)S(1)}, u32[]{:S(2)}, u32[]{:S(2)}) collective-permute-start(f32[6,1,18,8,128]{4,3,2,0,1:T(8,128)S(1)} %pad_maximum_fusion.1), channel_id=1, source_target_pairs={{2,0},{4,2},{6,4},{0,6},{3,1},{5,3},{7,5},{1,7},{10,8},{12,10},{14... | collective-permute-start | bytes 1327112 | tf_op jit(solution)/shard_map/ppermute | solution.py:56
  81.1 1.2 copy-start
  82.2 33.2 %copy-start.4 = (f32[64]{0:T(128)S(1)}, f32[64]{0:T(128)}, u32[]{:S(2)}) copy-start(f32[64]{0:T(128)} %get-tuple-element.60) | copy-start | bytes 772
  109.6 13.6 %all-to-all-start = ((f32[32,8,128]{2,1,0:T(8,128)}), f32[32,8,128]{2,1,0:T(8,128)S(1)}, u32[]{:S(2)}, u32[]{:S(2)}) async-start(f32[32,8,128]{2,1,0:T(8,128)} %shard_map.107), calls=%async_computation | async-start | bytes 262144 | tf_op jit(solution)/shard_map/all_to_all | solution.py:683
  123.2 0.7 copy-start.1

commit v15 on v13

--- a/solution.py
+++ b/solution.py
@@ -39,6 +39,10 @@
 def joined_rows(stacked):
     rows = stacked.shape[0] // 3
     return stacked[0:rows] + stacked[rows : 2 * rows] + stacked[2 * rows :]
+
+
+def inverse_root(values):
+    return jnp.exp2(-0.5 * jnp.log2(values))
 
 
 def dot_lanes(first, second):
@@ -297,7 +301,7 @@
         other = [wide_ref[pl.ds(row, 8), pl.ds(value * lanes, lanes)] for value in range(8)]
         apart = [other[axis] - mine[axis] for axis in range(3)]
         square = apart[0] * apart[0] + apart[1] * apart[1] + apart[2] * apart[2] + epsilon_sq
-        inverse = lax.rsqrt(square)
+        inverse = inverse_root(square)
         reach = other[6] + mine[6]
         overlap = jnp.maximum(reach - square * inverse, 0.0)
         overlap = jnp.where(other[7] != mine[7], overlap, 0.0)
@@ -307,7 +311,7 @@
             + (other[5] - mine[5]) * apart[2]
         )
         scaled = overlap * (other[6] * mine[6])
-        root = scaled * lax.rsqrt(jnp.maximum(scaled * reach, 1e-30))
+        root = scaled * inverse_root(jnp.maximum(scaled * reach, 1e-30))
         factor = root * inverse * (overlap - closing * inverse)
         return [factor * apart[axis] for axis in range(3)]
 

time: 127 us -> 130 us (1.024)
  Pallas kernels: 88.8 us -> 92 us
    pallas_call x1, Pallas kernels: 46.3 us -> 50 us  [local(): pl.pallas_call(inner_kernel, out_shape=jax.ShapeDtypeStruct((3, cells, la...]
  transfers between devices with their start and end apart: 7 -> 7, of which waited for: 1 -> 1; matrix products, arithmetic and copies ran while one was open for 8% -> 8% of each run, Pallas kernels for 43% -> 45%
where the time goes in v15:
time: 130 us
  Pallas kernels  92 us (71%)
  starting transfers between devices  13.8 us (11%)
  other arithmetic  8.52 us (7%)
  waiting for transfers between devices  6.93 us (5%)
  local copies, waits for them, and re-layouts  4.88 us (4%)
  between operations  3.4 us (3%)
    pallas_call x1, Pallas kernels, local(): pl.pallas_call(inner_kernel, out_shape=jax.ShapeDtypeStruct((3, cells, la...  50 us
    pallas_call x1, Pallas kernels, local(): pl.pallas_call(functools.partial(outer_kernel, near_outside, sizes), out_...  25.8 us
    ppermute x6, starting transfers between devices, exchange(): return (lax.ppermute(last, axis, up), lax.ppermute(initial, axis, down))  9.03 us
    pallas_call x1, Pallas kernels, local(): pl.pallas_call(functools.partial(list_kernel, near_inside, sizes), out_sh...  8.64 us
    all_to_all x1, waiting for transfers between devices, local(): lax.all_to_all(known, names, split_axis=0, concat_axis=0, tiled=True)  6.91 us
    sort x1, other arithmetic, local(): codes = jnp.sort(codes)  5.03 us
    all_to_all x1, starting transfers between devices, local(): lax.all_to_all(known, names, split_axis=0, concat_axis=0, tiled=True)  4.81 us
    pallas_call x1, Pallas kernels, local(): pl.pallas_call(functools.partial(move_kernel, owned), out_shape=(jax.Shap...  4.67 us
  transfers between devices with their start and end apart: 7, of which 1 were waited for; matrix products, arithmetic and copies ran while one was open for 8% of the time, Pallas kernels for 45%

profile of v15, /device:TPU:0, one launch (start us, length us, event | category | flops | bytes accessed | tf_op | source)
XLA Modules:
  0.0 129.5 jit_solution(16499306305637898505)
XLA Ops:
  0.6 1.2 fusion.13
  1.8 2.9 %shard_map.104 = (f32[256,8,128]{2,1,0:T(8,128)}, f32[16,8,128]{2,1,0:T(8,128)}, f32[16,8,128]{2,1,0:T(8,128)}) custom-call(f32[7,256,128]{2,1,0:T(8,128)} %bitcast.61, s32[256,128]{1,0:T(8,128)} %bitcast.65, f32[1,64]{1,0:T(1,128)} %bitcast.79), custom_call_target="tpu_custom_call" | custom-call | tf_op jit(solution)/shard_map/pallas_call | solution.py:545
  4.7 3.0 %collective-permute-start = (f32[16,8,128]{2,1,0:T(8,128)}, f32[16,8,128]{2,1,0:T(8,128)S(1)}, u32[]{:S(2)}, u32[]{:S(2)}) collective-permute-start(f32[16,8,128]{2,1,0:T(8,128)} %get-tuple-element.24), channel_id=1, source_target_pairs={{0,1},{1,0},{2,3},{3,2},{4,5},{5,4},{6,7},{7,6},{8,9},{9,8},{10,11... | collective-permute-start | bytes 196616 | tf_op jit(solution)/shard_map/ppermute | solution.py:58
  7.7 0.0 collective-permute-start.1
  7.7 0.8 select_add_fusion
  8.5 1.1 fusion.15
  9.6 1.1 slice_bitcast_fusion
  10.6 5.0 %sort.15 = (s32[2048]{0:T(1024)S(1)}, s32[2048]{0:T(1024)}) sort(s32[2048]{0:T(1024)S(1)} %select_add_fusion, s32[2048]{0:T(1024)S(1)} %iota.11), dimensions={0}, to_apply=%region_0.1 | sort | flops 22528 | bytes 32768 | tf_op jit(solution)/shard_map/jit(sort)/sort | solution.py:606
  15.7 0.7 convert_reduce_fusion
  17.1 0.1 collective-permute-start.2
  17.2 1.8 %collective-permute-start.3 = (f32[1,4,18,8,128]{4,3,2,0,1:T(8,128)S(1)}, f32[1,4,18,8,128]{4,3,2,0,1:T(8,128)S(1)}, u32[]{:S(2)}, u32[]{:S(2)}) collective-permute-start(f32[1,4,18,8,128]{4,3,2,0,1:T(8,128)S(1)} %pad_maximum_fusion.3), channel_id=1, source_target_pairs={{8,0},{16,8},{24,16},{0,24},{9,1},{17,9},{25,17},{1,25},{10,2},{18... | collective-permute-start | bytes 884744 | tf_op jit(solution)/shard_map/ppermute | solution.py:58
  20.2 8.6 %shard_map.105 = (s32[2048,128]{1,0:T(8,128)}, s32[1,2048]{1,0:T(1,128)}, s32[1,18432]{1,0:T(1,128)}, s32[1]{0:T(128)}) custom-call(s32[1]{0:T(128)} %bitcast.20.amount_smem, s32[1,2048]{1,0:T(1,128)} %bitcast.76, f32[256,8,128]{2,1,0:T(8,128)} %get-tuple-element.28.table_ref), custom_call_target="tpu_custom_call" | custom-call | tf_op jit(solution)/shard_map/pallas_call | solution.py:620
  29.6 2.1 %collective-permute-start.4 = (f32[6,1,18,8,128]{4,3,2,0,1:T(8,128)S(1)}, f32[6,1,18,8,128]{4,3,2,0,1:T(8,128)S(1)}, u32[]{:S(2)}, u32[]{:S(2)}) collective-permute-start(f32[6,1,18,8,128]{4,3,2,0,1:T(8,128)S(1)} %pad_maximum_fusion), channel_id=1, source_target_pairs={{0,2},{2,4},{4,6},{6,0},{1,3},{3,5},{5,7},{7,1},{8,10},{10,12},{12... | collective-permute-start | bytes 1327112 | tf_op jit(solution)/shard_map/ppermute | solution.py:58
  31.8 2.1 %collective-permute-start.5 = (f32[6,1,18,8,128]{4,3,2,0,1:T(8,128)S(1)}, f32[6,1,18,8,128]{4,3,2,0,1:T(8,128)S(1)}, u32[]{:S(2)}, u32[]{:S(2)}) collective-permute-start(f32[6,1,18,8,128]{4,3,2,0,1:T(8,128)S(1)} %pad_maximum_fusion.1), channel_id=1, source_target_pairs={{2,0},{4,2},{6,4},{0,6},{3,1},{5,3},{7,5},{1,7},{10,8},{12,10},{14... | collective-permute-start | bytes 1327112 | tf_op jit(solution)/shard_map/ppermute | solution.py:58
  33.9 0.7 fusion.9
  34.6 50.0 %shard_map.106.inner_ref = f32[3,256,128]{2,1,0:T(8,128)} custom-call(s32[1]{0:T(128)} %bitcast.20.amount_smem, s32[1,2048]{1,0:T(1,128)} %get-tuple-element.37.word_smem, s32[1,18432]{1,0:T(1,128)} %get-tuple-element.38.cell_smem, s32[1]{0:T(128)} %get-tuple-element.39.groups_smem, f32[256,8,128]{2,1,0:T(8,128)} %get-tuple-element.28.table_ref, ...), custom_call_target="tpu_custom_call" | custom-call | tf_op jit(solution)/shard_map/pallas_call | solution.py:637
  84.7 1.2 copy-done
  85.9 25.8 %shard_map.107 = f32[32,8,128]{2,1,0:T(8,128)} custom-call(s32[1]{0:T(128)} %bitcast.3.amount_smem, s32[1,2048]{1,0:T(1,128)} %bitcast.77, f32[256,8,128]{2,1,0:T(8,128)} %get-tuple-element.28.table_ref, f32[392,8,128]{2,1,0:T(8,128)} %copy-done, f32[3,256,128]{2,1,0:T(8,128)} %shard_map.106.inner_ref, f32[3,256,128]{2,1,0:T(8,128)} %bitcast.63, ...), custom_call_target="tpu_custom_call" | custom-call | tf_op jit(solution)/shard_map/pallas_call | solution.py:655
  111.6 4.8 %all-to-all-start = ((f32[32,8,128]{2,1,0:T(8,128)}), f32[32,8,128]{2,1,0:T(8,128)S(1)}, u32[]{:S(2)}, u32[]{:S(2)}) async-start(f32[32,8,128]{2,1,0:T(8,128)} %shard_map.107), calls=%async_computation | async-start | bytes 262144 | tf_op jit(solution)/shard_map/all_to_all | solution.py:673
  116.5 0.1 maximum_bitcast_fusion
  116.5 0.7 copy.23.target_ref
  117.3 6.9 %all-to-all-done.known_ref = f32[32,8,128]{2,1,0:T(8,128)S(1)} async-done(((f32[32,8,128]{2,1,0:T(8,128)}), f32[32,8,128]{2,1,0:T(8,128)S(1)}, u32[]{:S(2)}, u32[]{:S(2)}) %all-to-all-start) | async-done | bytes 131104 | tf_op jit(solution)/shard_map/all_to_all | solution.py:673
  124.2 0.6 copy-done.1
  124.9 4.7 %shard_map.108 = (f32[6,256,128]{2,1,0:T(8,128)}, f32[6,128]{1,0:T(8,128)}) custom-call(f32[128,1]{1,0:T(8,128)} %copy.23.target_ref, f32[32,8,128]{2,1,0:T(8,128)} %copy-done.1, f32[7,256,128]{2,1,0:T(8,128)} %bitcast.62, f32[3,256,128]{2,1,0:T(8,128)} %bitcast.64, s32[256,128]{1,0:T(8,128)} %bitcast.67), custom_call_target="tpu_custom_call" | custom-call | tf_op jit(solution)/shard_map/pallas_call | solution.py:680
  (31 shorter events, 0.3 us)
Async XLA Ops:
  4.7 12.3 %collective-permute-start = (f32[16,8,128]{2,1,0:T(8,128)}, f32[16,8,128]{2,1,0:T(8,128)S(1)}, u32[]{:S(2)}, u32[]{:S(2)}) collective-permute-start(f32[16,8,128]{2,1,0:T(8,128)} %get-tuple-element.24), channel_id=1, source_target_pairs={{0,1},{1,0},{2,3},{3,2},{4,5},{5,4},{6,7},{7,6},{8,9},{9,8},{10,11... | collective-permute-start | bytes 196616 | tf_op jit(solution)/shard_map/ppermute | solution.py:58
  7.7 9.3 %collective-permute-start.1 = (f32[16,8,128]{2,1,0:T(8,128)}, f32[16,8,128]{2,1,0:T(8,128)S(1)}, u32[]{:S(2)}, u32[]{:S(2)}) collective-permute-start(f32[16,8,128]{2,1,0:T(8,128)} %get-tuple-element.25), channel_id=1, source_target_pairs={{1,0},{0,1},{3,2},{2,3},{5,4},{4,5},{7,6},{6,7},{9,8},{8,9},{11,10... | collective-permute-start | bytes 196616 | tf_op jit(solution)/shard_map/ppermute | solution.py:58
  15.7 4.5 %copy-start.2 = (s32[2048]{0:T(1024)}, s32[2048]{0:T(1024)S(1)}, u32[]{:S(2)}) copy-start(s32[2048]{0:T(1024)S(1)} %get-tuple-element.26) | copy-start | bytes 24580
  17.1 12.5 %collective-permute-start.2 = (f32[1,4,18,8,128]{4,3,2,0,1:T(8,128)S(1)}, f32[1,4,18,8,128]{4,3,2,0,1:T(8,128)S(1)}, u32[]{:S(2)}, u32[]{:S(2)}) collective-permute-start(f32[1,4,18,8,128]{4,3,2,0,1:T(8,128)S(1)} %pad_maximum_fusion.2), channel_id=1, source_target_pairs={{0,8},{8,16},{16,24},{24,0},{1,9},{9,17},{17,25},{25,1},{2,10},{10... | collective-permute-start | bytes 884744 | tf_op jit(solution)/shard_map/ppermute | solution.py:58
  17.2 12.4 %collective-permute-start.3 = (f32[1,4,18,8,128]{4,3,2,0,1:T(8,128)S(1)}, f32[1,4,18,8,128]{4,3,2,0,1:T(8,128)S(1)}, u32[]{:S(2)}, u32[]{:S(2)}) collective-permute-start(f32[1,4,18,8,128]{4,3,2,0,1:T(8,128)S(1)} %pad_maximum_fusion.3), channel_id=1, source_target_pairs={{8,0},{16,8},{24,16},{0,24},{9,1},{17,9},{25,17},{1,25},{10,2},{18... | collective-permute-start | bytes 884744 | tf_op jit(solution)/shard_map/ppermute | solution.py:58
  28.9 5.0 %copy-start.3 = (s32[2048]{0:T(1024)S(1)}, s32[2048]{0:T(1024)}, u32[]{:S(2)}) copy-start(s32[2048]{0:T(1024)} %copy-done.2) | copy-start | bytes 24580
  29.6 54.9 %collective-permute-start.4 = (f32[6,1,18,8,128]{4,3,2,0,1:T(8,128)S(1)}, f32[6,1,18,8,128]{4,3,2,0,1:T(8,128)S(1)}, u32[]{:S(2)}, u32[]{:S(2)}) collective-permute-start(f32[6,1,18,8,128]{4,3,2,0,1:T(8,128)S(1)} %pad_maximum_fusion), channel_id=1, source_target_pairs={{0,2},{2,4},{4,6},{6,0},{1,3},{3,5},{5,7},{7,1},{8,10},{10,12},{12... | collective-permute-start | bytes 1327112 | tf_op jit(solution)/shard_map/ppermute | solution.py:58
  31.8 52.8 %collective-permute-start.5 = (f32[6,1,18,8,128]{4,3,2,0,1:T(8,128)S(1)}, f32[6,1,18,8,128]{4,3,2,0,1:T(8,128)S(1)}, u32[]{:S(2)}, u32[]{:S(2)}) collective-permute-start(f32[6,1,18,8,128]{4,3,2,0,1:T(8,128)S(1)} %pad_maximum_fusion.1), channel_id=1, source_target_pairs={{2,0},{4,2},{6,4},{0,6},{3,1},{5,3},{7,5},{1,7},{10,8},{12,10},{14... | collective-permute-start | bytes 1327112 | tf_op jit(solution)/shard_map/ppermute | solution.py:58
  84.7 1.2 copy-start
  85.9 30.6 %copy-start.4 = (f32[64]{0:T(128)S(1)}, f32[64]{0:T(128)}, u32[]{:S(2)}) copy-start(f32[64]{0:T(128)} %get-tuple-element.60) | copy-start | bytes 772
  111.6 12.6 %all-to-all-start = ((f32[32,8,128]{2,1,0:T(8,128)}), f32[32,8,128]{2,1,0:T(8,128)S(1)}, u32[]{:S(2)}, u32[]{:S(2)}) async-start(f32[32,8,128]{2,1,0:T(8,128)} %shard_map.107), calls=%async_computation | async-start | bytes 262144 | tf_op jit(solution)/shard_map/all_to_all | solution.py:673
  124.2 0.7 copy-start.1

commit v16 on v13

--- a/solution.py
+++ b/solution.py
@@ -19,6 +19,7 @@
 FILL = 64
 OUTSIDE = 1 << 20
 WORD_BITS = 16
+VALUES = 9
 SLACK = 256
 SPREAD = 4
 VMEM = 56 * 1024 * 1024
@@ -54,7 +55,29 @@
     return lax.ppermute(last, axis, up), lax.ppermute(initial, axis, down)
 
 
-def pack_kernel(deep, state_ref, frag_ref, key_ref, out_ref, last_ref, first_ref):
+def decode(code, sizes):
+    def over(value, by):
+        return jnp.floor((value.astype(jnp.float32) + 0.5) * (1.0 / by)).astype(jnp.int32)
+
+    own = over(code, 27)
+    kind = code - 27 * own
+    step_x = over(kind, 9)
+    step_y = over(kind, 3) - 3 * step_x
+    steps = (step_x - 1, step_y - 1, kind - 9 * step_x - 3 * step_y - 1)
+    own_x = over(own, sizes[1] * sizes[2])
+    row = over(own, sizes[2])
+    place = (own_x + steps[0], row - own_x * sizes[1] + steps[1], own - row * sizes[2] + steps[2])
+    return own, kind, steps, place
+
+
+def pack_kernel(
+    sizes, state_ref, frag_ref, key_ref, code_ref, out_ref, last_ref, first_ref, marked_ref
+):
+    deep = sizes[2]
+    code = code_ref[...]
+    place = decode(code, sizes)[3]
+    within = [(place[axis] >= 0) & (place[axis] < sizes[axis]) for axis in range(3)]
+    marked_ref[...] = jnp.where(within[0] & within[1] & within[2], code, code + OUTSIDE)
     cells, lanes = frag_ref.shape
     held = key_ref.shape[1]
     for comp in range(7):
@@ -94,20 +117,9 @@
     def ramp(shape, axis):
         return lax.broadcasted_iota(jnp.int32, shape, axis)
 
-    def over(value, by):
-        return jnp.floor((value.astype(jnp.float32) + 0.5) * (1.0 / by)).astype(jnp.int32)
-
     code = code_ref[...] & (OUTSIDE - 1)
-    own = over(code, 27)
-    kind = code - 27 * own
-    step_x = over(kind, 9)
-    step_y = over(kind, 3) - 3 * step_x
-    steps = (step_x - 1, step_y - 1, kind - 9 * step_x - 3 * step_y - 1)
-    own_x = over(own, sizes[1] * sizes[2])
-    row = over(own, sizes[2])
-    near = near_of(
-        own_x + steps[0], row - own_x * sizes[1] + steps[1], own - row * sizes[2] + steps[2]
-    )
+    own, kind, steps, place = decode(code, sizes)
+    near = near_of(*place)
     need = sum(
         jnp.where(steps[axis] == 1, 1, jnp.where(steps[axis] == -1, 2, 0)) * (1 << (2 * axis))
         for axis in range(3)
@@ -275,9 +287,11 @@
     chunks = rows // lanes
     units = rows // group
     force_ref[...] = jnp.zeros(force_ref.shape, jnp.float32)
-    part = lax.broadcasted_iota(jnp.int32, (32, 8 * lanes), 0)
-    comp = lax.broadcasted_iota(jnp.int32, (32, 8 * lanes), 1) // lanes
-    weights = jnp.where((part < 24) & (part % 8 == comp), 1.0, 0.0).astype(jnp.bfloat16)
+    part = lax.broadcasted_iota(jnp.int32, (32, VALUES * lanes), 0)
+    comp = lax.broadcasted_iota(jnp.int32, (32, VALUES * lanes), 1) // lanes
+    chosen = ((part < 24) & (part % 8 == comp)) | ((part >= 24) & (part < 27) & (comp == 8))
+    weights = jnp.where(chosen, 1.0, 0.0).astype(jnp.bfloat16)
+    line = lax.broadcasted_iota(jnp.int32, (8, lanes), 0)
 
     def turned(step):
         pieces = []
@@ -286,7 +300,13 @@
             high = values.astype(jnp.bfloat16).astype(jnp.float32)
             rest = values - high
             middle = rest.astype(jnp.bfloat16).astype(jnp.float32)
-            parts = jnp.concatenate([high, middle, rest - middle, jnp.zeros_like(values)], axis=0)
+            over = 1.0 / jnp.broadcast_to(values[6:7], (8, lanes))
+            over_high = over.astype(jnp.bfloat16).astype(jnp.float32)
+            over_rest = over - over_high
+            over_middle = over_rest.astype(jnp.bfloat16).astype(jnp.float32)
+            over = jnp.where(line == 2, over_rest - over_middle, 0.0)
+            over = jnp.where(line == 1, over_middle, jnp.where(line == 0, over_high, over))
+            parts = jnp.concatenate([high, middle, rest - middle, over], axis=0)
             pieces.append(parts.astype(jnp.bfloat16).T)
         return jnp.concatenate(pieces, axis=0)
 
@@ -294,7 +314,7 @@
         out_ref[...] = jnp.dot(turned(step), weights, preferred_element_type=jnp.float32)
 
     def block_force(wide_ref, row, mine):
-        other = [wide_ref[pl.ds(row, 8), pl.ds(value * lanes, lanes)] for value in range(8)]
+        other = [wide_ref[pl.ds(row, 8), pl.ds(value * lanes, lanes)] for value in range(VALUES)]
         apart = [other[axis] - mine[axis] for axis in range(3)]
         square = apart[0] * apart[0] + apart[1] * apart[1] + apart[2] * apart[2] + epsilon_sq
         inverse = lax.rsqrt(square)
@@ -306,8 +326,7 @@
             + (other[4] - mine[4]) * apart[1]
             + (other[5] - mine[5]) * apart[2]
         )
-        scaled = overlap * (other[6] * mine[6])
-        root = scaled * lax.rsqrt(jnp.maximum(scaled * reach, 1e-30))
+        root = overlap * lax.rsqrt(jnp.maximum(overlap * (other[8] + mine[8]), 1e-30))
         factor = root * inverse * (overlap - closing * inverse)
         return [factor * apart[axis] for axis in range(3)]
 
@@ -318,6 +337,7 @@
             cell = cell_smem[0, step * units + unit]
             own = jnp.minimum(cell, cells - 1) * 8
             mine = [table_ref[pl.ds(own + value, 8, stride=0), :] for value in range(8)]
+            mine.append(1.0 / mine[6])
             running = [jnp.where(cell == last, running[axis], 0.0) for axis in range(3)]
             for block in range(group // 8):
                 force = block_force(wide_ref, unit * group + block * 8, mine)
@@ -538,13 +558,20 @@
     flat_frag = sphere_frag.reshape(cells, lanes)
 
     face_shape = jax.ShapeDtypeStruct((cells_x * cells_y, 8, lanes), jnp.float32)
-    table, z_last, z_first = pl.pallas_call(
-        functools.partial(pack_kernel, cells_z),
-        out_shape=(jax.ShapeDtypeStruct((cells, 8, lanes), jnp.float32), face_shape, face_shape),
-        in_specs=[vmem] * 3,
-        out_specs=(vmem,) * 3,
+    sizes = (cells_x, cells_y, cells_z)
+    total = tiles.shape[1]
+    table, z_last, z_first, codes = pl.pallas_call(
+        functools.partial(pack_kernel, sizes),
+        out_shape=(
+            jax.ShapeDtypeStruct((cells, 8, lanes), jnp.float32),
+            face_shape,
+            face_shape,
+            jax.ShapeDtypeStruct((1, total), jnp.int32),
+        ),
+        in_specs=[vmem] * 4,
+        out_specs=(vmem,) * 4,
         compiler_params=params,
-    )(flat_state, flat_frag, frag_key[None])
+    )(flat_state, flat_frag, frag_key[None], tiles)
     grid = table.reshape(cells_x, cells_y, cells_z, 8, lanes)
     z_before, z_after = exchange(z_last, z_first, "gz")
 
@@ -552,14 +579,6 @@
     starts = [0, cells_x * cells_y, 2 * cells_x * cells_y]
     starts += [starts[-1] + cells_y * span_z, starts[-1] + 2 * cells_y * span_z]
     starts += [starts[-1] + (cells_x + 2) * span_z]
-
-    def inside(codes):
-        own, kind = (codes // 27, codes % 27)
-        x = own // (cells_y * cells_z) + kind // 9 - 1
-        y = own // cells_z % cells_y + kind // 3 % 3 - 1
-        z = own % cells_z + kind % 3 - 1
-        inner = (x >= 0) & (x < cells_x) & (y >= 0) & (y < cells_y)
-        return inner & (z >= 0) & (z < cells_z)
 
     def near_inside(x, y, z):
         return (x * cells_y + y) * cells_z + z
@@ -571,10 +590,6 @@
         in_x = jnp.where((x < 0) | (x >= cells_x), in_x, in_z)
         return jnp.where((y < 0) | (y >= cells_y), in_y, in_x)
 
-    sizes = (cells_x, cells_y, cells_z)
-    codes = tiles[0]
-    total = codes.shape[0]
-    codes = codes + jnp.where(inside(codes), 0, OUTSIDE)
     chunks = total + cells * INNER_GROUP // lanes + 3 * SPREAD
     group_top = -(-(chunks * (lanes // OUTER_GROUP) + SLACK) // (8 * lanes)) * 8 * lanes + 8 * lanes
     force_shape = (cells + 8, 3, 8, lanes)
@@ -594,12 +609,12 @@
 
     pair_scratch = [
         pltpu.VMEM((chunks, 8, lanes), jnp.float32),
-        pltpu.VMEM((SPREAD * lanes, 8 * lanes), jnp.float32),
-        pltpu.VMEM((SPREAD * lanes, 8 * lanes), jnp.float32),
+        pltpu.VMEM((SPREAD * lanes, VALUES * lanes), jnp.float32),
+        pltpu.VMEM((SPREAD * lanes, VALUES * lanes), jnp.float32),
         pltpu.VMEM((27, 8, lanes), jnp.float32),
     ]
 
-    codes = jnp.sort(codes)
+    codes = jnp.sort(codes, axis=1)
     inner_amount = jnp.sum((codes < OUTSIDE).astype(jnp.int32))
     outer_amount = total - inner_amount
     z_before, z_after, codes, inner_amount = lax.optimization_barrier(
@@ -620,7 +635,7 @@
         out_specs=(vmem,) * 3 + (smem,),
         scratch_shapes=list_scratch(cells),
         compiler_params=params,
-    )(inner_amount[None], codes[None], table)
+    )(inner_amount[None], codes, table)
     x_before, x_after, slots, word, cell_of, groups = lax.optimization_barrier(
         (x_before, x_after, slots, word, cell_of, groups)
     )
@@ -639,7 +654,9 @@
         compiler_params=params,
     )(inner_amount[None], word, cell_of, groups, table, slots)
 
-    outer_codes = lax.dynamic_slice(jnp.concatenate([codes, codes]), (inner_amount,), (total,))
+    outer_codes = lax.dynamic_slice(
+        jnp.concatenate([codes, codes], axis=1), (jnp.int32(0), inner_amount), (1, total)
+    )
     halo = jnp.concatenate(
         [
             part.reshape(-1, 8, lanes)
@@ -664,7 +681,7 @@
         + pair_scratch
         + list_scratch(halo.shape[0]),
         compiler_params=params,
-    )(outer_amount[None], outer_codes[None], table, halo, inner, flat_arms, flat_frag,
+    )(outer_amount[None], outer_codes, table, halo, inner, flat_arms, flat_frag,
         frag_key[None], clump_motion, inv_mass[None], inv_moment[None])
     known = lax.all_to_all(known, names, split_axis=0, concat_axis=0, tiled=True)
 

time: 127 us -> 138 us (1.087)
  between operations: 3.4 us -> 16.7 us
  other arithmetic: 8.52 us -> 3.55 us
  Pallas kernels: 88.8 us -> 90.8 us
    sort x1 -> x0, other arithmetic: 5.03 us -> none  [local(): codes = jnp.sort(codes)]
    pallas_call x1, Pallas kernels: 46.3 us -> 48.1 us  [local(): pl.pallas_call(inner_kernel, out_shape=jax.ShapeDtypeStruct((3, cells, la...]
    unnamed x18 -> x17, local copies, waits for them, and re-layouts: 3.01 us -> 3 us
  transfers between devices with their start and end apart: 7 -> 7, of which waited for: 1 -> 1; matrix products, arithmetic and copies ran while one was open for 8% -> 4% of each run, Pallas kernels for 43% -> 41%
where the time goes in v16:
time: 138 us; the launch traced here: 139 us
  Pallas kernels  90.8 us (66%)
  between operations  16.7 us (12%)
  starting transfers between devices  14.4 us (10%)
  waiting for transfers between devices  6.94 us (5%)
  local copies, waits for them, and re-layouts  6.15 us (4%)
  other arithmetic  3.55 us (3%)
    pallas_call x1, Pallas kernels, local(): pl.pallas_call(inner_kernel, out_shape=jax.ShapeDtypeStruct((3, cells, la...  48.1 us
    pallas_call x1, Pallas kernels, local(): pl.pallas_call(functools.partial(outer_kernel, near_outside, sizes), out_...  26.5 us
    ppermute x6, starting transfers between devices, exchange(): return (lax.ppermute(last, axis, up), lax.ppermute(initial, axis, down))  10.1 us
    pallas_call x1, Pallas kernels, local(): pl.pallas_call(functools.partial(list_kernel, near_inside, sizes), out_sh...  8.69 us
    all_to_all x1, waiting for transfers between devices, local(): lax.all_to_all(known, names, split_axis=0, concat_axis=0, tiled=True)  6.92 us
    pallas_call x1, Pallas kernels, local(): pl.pallas_call(functools.partial(move_kernel, owned), out_shape=(jax.Shap...  4.63 us
    all_to_all x1, starting transfers between devices, local(): lax.all_to_all(known, names, split_axis=0, concat_axis=0, tiled=True)  4.26 us
    unnamed x17, local copies, waits for them, and re-layouts  3 us
  transfers between devices with their start and end apart: 7, of which 1 were waited for; matrix products, arithmetic and copies ran while one was open for 4% of the time, Pallas kernels for 41%

profile of v16, /device:TPU:0, one launch (start us, length us, event | category | flops | bytes accessed | tf_op | source)
XLA Modules:
  0.0 138.5 jit_solution(12825731501921150998)
XLA Ops:
  7.2 0.0 sort.10.cloned.1.call-start
  7.2 1.2 fusion.2
  8.4 2.9 %shard_map.104 = (f32[256,8,128]{2,1,0:T(8,128)}, f32[16,8,128]{2,1,0:T(8,128)}, f32[16,8,128]{2,1,0:T(8,128)}, s32[1,2048]{1,0:T(1,128)}) custom-call(f32[7,256,128]{2,1,0:T(8,128)} %bitcast.58, s32[256,128]{1,0:T(8,128)} %bitcast.62, f32[1,64]{1,0:T(1,128)} %bitcast.73, s32[1,2048]{1,0:T(1,128)} %code_ref.1), custom_call_target="tpu_custom_call" | custom-call | tf_op jit(solution)/shard_map/pallas_call | solution.py:563
  11.3 3.0 %collective-permute-start = (f32[16,8,128]{2,1,0:T(8,128)}, f32[16,8,128]{2,1,0:T(8,128)S(1)}, u32[]{:S(2)}, u32[]{:S(2)}) collective-permute-start(f32[16,8,128]{2,1,0:T(8,128)} %get-tuple-element.23), channel_id=1, source_target_pairs={{0,1},{1,0},{2,3},{3,2},{4,5},{5,4},{6,7},{7,6},{8,9},{9,8},{10,11... | collective-permute-start | bytes 196616 | tf_op jit(solution)/shard_map/ppermute | solution.py:55
  14.3 0.1 collective-permute-start.1
  14.4 1.1 fusion.4
  15.5 1.1 slice_bitcast_fusion
  16.6 1.3 sort.10.cloned.1.call-done.code_ref
  17.8 1.4 %fusion.1 = s32[]{:T(128)} fusion(s32[1,2048]{1,0:T(1,128)} %sort.10.cloned.1.call-done.code_ref), kind=kLoop, calls=%fused_computation.24 | loop fusion | flops 6143 | bytes 8196 | tf_op jit(solution)/shard_map/reduce_sum | solution.py:618
  20.0 0.5 collective-permute-start.2
  20.5 2.0 %collective-permute-start.3 = (f32[1,4,18,8,128]{4,3,2,0,1:T(8,128)S(1)}, f32[1,4,18,8,128]{4,3,2,0,1:T(8,128)S(1)}, u32[]{:S(2)}, u32[]{:S(2)}) collective-permute-start(f32[1,4,18,8,128]{4,3,2,0,1:T(8,128)S(1)} %pad_maximum_fusion.3), channel_id=1, source_target_pairs={{8,0},{16,8},{24,16},{0,24},{9,1},{17,9},{25,17},{1,25},{10,2},{18... | collective-permute-start | bytes 884744 | tf_op jit(solution)/shard_map/ppermute | solution.py:55
  23.7 8.7 %shard_map.105 = (s32[2048,128]{1,0:T(8,128)}, s32[1,2048]{1,0:T(1,128)}, s32[1,18432]{1,0:T(1,128)}, s32[1]{0:T(128)}) custom-call(s32[1]{0:T(128)} %bitcast.18.amount_smem, s32[1,2048]{1,0:T(1,128)} %sort.10.cloned.1.call-done.code_ref, f32[256,8,128]{2,1,0:T(8,128)} %get-tuple-element.27.table_ref), custom_call_target="tpu_custom_call" | custom-call | tf_op jit(solution)/shard_map/pallas_call | solution.py:631
  33.1 0.7 fusion.code_ref
  33.9 2.4 %collective-permute-start.4 = (f32[6,1,18,8,128]{4,3,2,0,1:T(8,128)S(1)}, f32[6,1,18,8,128]{4,3,2,0,1:T(8,128)S(1)}, u32[]{:S(2)}, u32[]{:S(2)}) collective-permute-start(f32[6,1,18,8,128]{4,3,2,0,1:T(8,128)S(1)} %pad_maximum_fusion), channel_id=1, source_target_pairs={{0,2},{2,4},{4,6},{6,0},{1,3},{3,5},{5,7},{7,1},{8,10},{10,12},{12... | collective-permute-start | bytes 1327112 | tf_op jit(solution)/shard_map/ppermute | solution.py:55
  36.4 2.1 %collective-permute-start.5 = (f32[6,1,18,8,128]{4,3,2,0,1:T(8,128)S(1)}, f32[6,1,18,8,128]{4,3,2,0,1:T(8,128)S(1)}, u32[]{:S(2)}, u32[]{:S(2)}) collective-permute-start(f32[6,1,18,8,128]{4,3,2,0,1:T(8,128)S(1)} %pad_maximum_fusion.1), channel_id=1, source_target_pairs={{2,0},{4,2},{6,4},{0,6},{3,1},{5,3},{7,5},{1,7},{10,8},{12,10},{14... | collective-permute-start | bytes 1327112 | tf_op jit(solution)/shard_map/ppermute | solution.py:55
  38.5 48.1 %shard_map.106.inner_ref = f32[3,256,128]{2,1,0:T(8,128)} custom-call(s32[1]{0:T(128)} %bitcast.18.amount_smem, s32[1,2048]{1,0:T(1,128)} %get-tuple-element.36.word_smem, s32[1,18432]{1,0:T(1,128)} %get-tuple-element.37.cell_smem, s32[1]{0:T(128)} %get-tuple-element.38.groups_smem, f32[256,8,128]{2,1,0:T(8,128)} %get-tuple-element.27.table_ref, ...), custom_call_target="tpu_custom_call" | custom-call | tf_op jit(solution)/shard_map/pallas_call | solution.py:648
  86.7 1.2 copy-done
  87.9 26.5 %shard_map.107 = f32[32,8,128]{2,1,0:T(8,128)} custom-call(s32[1]{0:T(128)} %bitcast.5.amount_smem, s32[1,2048]{1,0:T(1,128)} %fusion.code_ref, f32[256,8,128]{2,1,0:T(8,128)} %get-tuple-element.27.table_ref, f32[392,8,128]{2,1,0:T(8,128)} %copy-done, f32[3,256,128]{2,1,0:T(8,128)} %shard_map.106.inner_ref, f32[3,256,128]{2,1,0:T(8,128)} %bitcast.60, ...), custom_call_target="tpu_custom_call" | custom-call | tf_op jit(solution)/shard_map/pallas_call | solution.py:668
  114.4 4.3 %all-to-all-start = ((f32[32,8,128]{2,1,0:T(8,128)}), f32[32,8,128]{2,1,0:T(8,128)S(1)}, u32[]{:S(2)}, u32[]{:S(2)}) async-start(f32[32,8,128]{2,1,0:T(8,128)} %shard_map.107), calls=%async_computation | async-start | bytes 262144 | tf_op jit(solution)/shard_map/all_to_all | solution.py:686
  118.7 0.1 maximum_bitcast_fusion
  118.8 0.7 copy.23.target_ref
  119.5 6.9 %all-to-all-done.known_ref = f32[32,8,128]{2,1,0:T(8,128)S(1)} async-done(((f32[32,8,128]{2,1,0:T(8,128)}), f32[32,8,128]{2,1,0:T(8,128)S(1)}, u32[]{:S(2)}, u32[]{:S(2)}) %all-to-all-start) | async-done | bytes 131104 | tf_op jit(solution)/shard_map/all_to_all | solution.py:686
  126.4 0.6 copy-done.1
  127.1 4.6 %shard_map.108 = (f32[6,256,128]{2,1,0:T(8,128)}, f32[6,128]{1,0:T(8,128)}) custom-call(f32[128,1]{1,0:T(8,128)} %copy.23.target_ref, f32[32,8,128]{2,1,0:T(8,128)} %copy-done.1, f32[7,256,128]{2,1,0:T(8,128)} %bitcast.59, f32[3,256,128]{2,1,0:T(8,128)} %bitcast.61, s32[256,128]{1,0:T(8,128)} %bitcast.64), custom_call_target="tpu_custom_call" | custom-call | tf_op jit(solution)/shard_map/pallas_call | solution.py:693
  (29 shorter events, 0.3 us)
Async XLA Ops:
  7.2 10.7 %sort.10.cloned.1.call-start = ((), (), s32[]{:S(2)}) async-start(), calls=%async_computation.1 | async-start | bytes 24608 | tf_op jit(solution)/shard_map/jit(sort)/sort | solution.py:617
  11.3 8.6 %collective-permute-start = (f32[16,8,128]{2,1,0:T(8,128)}, f32[16,8,128]{2,1,0:T(8,128)S(1)}, u32[]{:S(2)}, u32[]{:S(2)}) collective-permute-start(f32[16,8,128]{2,1,0:T(8,128)} %get-tuple-element.23), channel_id=1, source_target_pairs={{0,1},{1,0},{2,3},{3,2},{4,5},{5,4},{6,7},{7,6},{8,9},{9,8},{10,11... | collective-permute-start | bytes 196616 | tf_op jit(solution)/shard_map/ppermute | solution.py:55
  14.3 5.6 %collective-permute-start.1 = (f32[16,8,128]{2,1,0:T(8,128)}, f32[16,8,128]{2,1,0:T(8,128)S(1)}, u32[]{:S(2)}, u32[]{:S(2)}) collective-permute-start(f32[16,8,128]{2,1,0:T(8,128)} %get-tuple-element.24), channel_id=1, source_target_pairs={{1,0},{0,1},{3,2},{2,3},{5,4},{4,5},{7,6},{6,7},{9,8},{8,9},{11,10... | collective-permute-start | bytes 196616 | tf_op jit(solution)/shard_map/ppermute | solution.py:55
  17.8 15.2 %copy-start.2 = (s32[1,2048]{1,0:T(1,128)S(1)}, s32[1,2048]{1,0:T(1,128)}, u32[]{:S(2)}) copy-start(s32[1,2048]{1,0:T(1,128)} %sort.10.cloned.1.call-done.code_ref) | copy-start | bytes 24580
  20.0 13.9 %collective-permute-start.2 = (f32[1,4,18,8,128]{4,3,2,0,1:T(8,128)S(1)}, f32[1,4,18,8,128]{4,3,2,0,1:T(8,128)S(1)}, u32[]{:S(2)}, u32[]{:S(2)}) collective-permute-start(f32[1,4,18,8,128]{4,3,2,0,1:T(8,128)S(1)} %pad_maximum_fusion.2), channel_id=1, source_target_pairs={{0,8},{8,16},{16,24},{24,0},{1,9},{9,17},{17,25},{25,1},{2,10},{10... | collective-permute-start | bytes 884744 | tf_op jit(solution)/shard_map/ppermute | solution.py:55
  20.5 13.3 %collective-permute-start.3 = (f32[1,4,18,8,128]{4,3,2,0,1:T(8,128)S(1)}, f32[1,4,18,8,128]{4,3,2,0,1:T(8,128)S(1)}, u32[]{:S(2)}, u32[]{:S(2)}) collective-permute-start(f32[1,4,18,8,128]{4,3,2,0,1:T(8,128)S(1)} %pad_maximum_fusion.3), channel_id=1, source_target_pairs={{8,0},{16,8},{24,16},{0,24},{9,1},{17,9},{25,17},{1,25},{10,2},{18... | collective-permute-start | bytes 884744 | tf_op jit(solution)/shard_map/ppermute | solution.py:55
  33.9 52.7 %collective-permute-start.4 = (f32[6,1,18,8,128]{4,3,2,0,1:T(8,128)S(1)}, f32[6,1,18,8,128]{4,3,2,0,1:T(8,128)S(1)}, u32[]{:S(2)}, u32[]{:S(2)}) collective-permute-start(f32[6,1,18,8,128]{4,3,2,0,1:T(8,128)S(1)} %pad_maximum_fusion), channel_id=1, source_target_pairs={{0,2},{2,4},{4,6},{6,0},{1,3},{3,5},{5,7},{7,1},{8,10},{10,12},{12... | collective-permute-start | bytes 1327112 | tf_op jit(solution)/shard_map/ppermute | solution.py:55
  36.4 50.3 %collective-permute-start.5 = (f32[6,1,18,8,128]{4,3,2,0,1:T(8,128)S(1)}, f32[6,1,18,8,128]{4,3,2,0,1:T(8,128)S(1)}, u32[]{:S(2)}, u32[]{:S(2)}) collective-permute-start(f32[6,1,18,8,128]{4,3,2,0,1:T(8,128)S(1)} %pad_maximum_fusion.1), channel_id=1, source_target_pairs={{2,0},{4,2},{6,4},{0,6},{3,1},{5,3},{7,5},{1,7},{10,8},{12,10},{14... | collective-permute-start | bytes 1327112 | tf_op jit(solution)/shard_map/ppermute | solution.py:55
  86.7 1.2 copy-start
  87.9 30.8 %copy-start.3 = (f32[64]{0:T(128)S(1)}, f32[64]{0:T(128)}, u32[]{:S(2)}) copy-start(f32[64]{0:T(128)} %get-tuple-element.59) | copy-start | bytes 772
  114.4 12.0 %all-to-all-start = ((f32[32,8,128]{2,1,0:T(8,128)}), f32[32,8,128]{2,1,0:T(8,128)S(1)}, u32[]{:S(2)}, u32[]{:S(2)}) async-start(f32[32,8,128]{2,1,0:T(8,128)} %shard_map.107), calls=%async_computation | async-start | bytes 262144 | tf_op jit(solution)/shard_map/all_to_all | solution.py:686
  126.4 0.6 copy-start.1
Sparse Core Ops, SparseCore 0:
  11.4 6.1 sort.12.cloned.1.call-done
  (1 shorter events, 0.0 us)

commit v17 on v16

--- a/solution.py
+++ b/solution.py
@@ -614,7 +614,7 @@
         pltpu.VMEM((27, 8, lanes), jnp.float32),
     ]
 
-    codes = jnp.sort(codes, axis=1)
+    codes = jnp.sort(codes[0])
     inner_amount = jnp.sum((codes < OUTSIDE).astype(jnp.int32))
     outer_amount = total - inner_amount
     z_before, z_after, codes, inner_amount = lax.optimization_barrier(
@@ -635,7 +635,7 @@
         out_specs=(vmem,) * 3 + (smem,),
         scratch_shapes=list_scratch(cells),
         compiler_params=params,
-    )(inner_amount[None], codes, table)
+    )(inner_amount[None], codes[None], table)
     x_before, x_after, slots, word, cell_of, groups = lax.optimization_barrier(
         (x_before, x_after, slots, word, cell_of, groups)
     )
@@ -654,9 +654,7 @@
         compiler_params=params,
     )(inner_amount[None], word, cell_of, groups, table, slots)
 
-    outer_codes = lax.dynamic_slice(
-        jnp.concatenate([codes, codes], axis=1), (jnp.int32(0), inner_amount), (1, total)
-    )
+    outer_codes = lax.dynamic_slice(jnp.concatenate([codes, codes]), (inner_amount,), (total,))
     halo = jnp.concatenate(
         [
             part.reshape(-1, 8, lanes)
@@ -681,7 +679,7 @@
         + pair_scratch
         + list_scratch(halo.shape[0]),
         compiler_params=params,
-    )(outer_amount[None], outer_codes, table, halo, inner, flat_arms, flat_frag,
+    )(outer_amount[None], outer_codes[None], table, halo, inner, flat_arms, flat_frag,
         frag_key[None], clump_motion, inv_mass[None], inv_moment[None])
     known = lax.all_to_all(known, names, split_axis=0, concat_axis=0, tiled=True)
 

time: 138 us -> 127 us (0.920)
  between operations: 16.7 us -> 3.45 us
  other arithmetic: 3.55 us -> 7.73 us
    sort x0 -> x1, other arithmetic: none -> 5.03 us  [local(): codes = jnp.sort(codes[0])]
    unnamed x17 -> x20, local copies, waits for them, and re-layouts: 3 us -> 3.02 us
  transfers between devices with their start and end apart: 7 -> 7, of which waited for: 1 -> 1; matrix products, arithmetic and copies ran while one was open for 4% -> 7% of each run, Pallas kernels for 41% -> 44%
where the time goes in v17:
time: 127 us
  Pallas kernels  89.6 us (71%)
  starting transfers between devices  14.5 us (11%)
  other arithmetic  7.73 us (6%)
  waiting for transfers between devices  6.93 us (5%)
  local copies, waits for them, and re-layouts  4.88 us (4%)
  between operations  3.45 us (3%)
    pallas_call x1, Pallas kernels, local(): pl.pallas_call(inner_kernel, out_shape=jax.ShapeDtypeStruct((3, cells, la...  46.9 us
    pallas_call x1, Pallas kernels, local(): pl.pallas_call(functools.partial(outer_kernel, near_outside, sizes), out_...  26.5 us
    ppermute x6, starting transfers between devices, exchange(): return (lax.ppermute(last, axis, up), lax.ppermute(initial, axis, down))  9.03 us
    pallas_call x1, Pallas kernels, local(): pl.pallas_call(functools.partial(list_kernel, near_inside, sizes), out_sh...  8.67 us
    all_to_all x1, waiting for transfers between devices, local(): lax.all_to_all(known, names, split_axis=0, concat_axis=0, tiled=True)  6.92 us
    all_to_all x1, starting transfers between devices, local(): lax.all_to_all(known, names, split_axis=0, concat_axis=0, tiled=True)  5.47 us
    sort x1, other arithmetic, local(): codes = jnp.sort(codes[0])  5.03 us
    pallas_call x1, Pallas kernels, local(): pl.pallas_call(functools.partial(move_kernel, owned), out_shape=(jax.Shap...  4.63 us
  transfers between devices with their start and end apart: 7, of which 1 were waited for; matrix products, arithmetic and copies ran while one was open for 7% of the time, Pallas kernels for 44%

profile of v17, /device:TPU:0, one launch (start us, length us, event | category | flops | bytes accessed | tf_op | source)
XLA Modules:
  0.0 127.1 jit_solution(18014550740454329391)
XLA Ops:
  0.6 1.2 fusion.1
  1.8 2.9 %shard_map.104 = (f32[256,8,128]{2,1,0:T(8,128)}, f32[16,8,128]{2,1,0:T(8,128)}, f32[16,8,128]{2,1,0:T(8,128)}, s32[1,2048]{1,0:T(1,128)}) custom-call(f32[7,256,128]{2,1,0:T(8,128)} %bitcast.61, s32[256,128]{1,0:T(8,128)} %bitcast.65, f32[1,64]{1,0:T(1,128)} %bitcast.79, s32[1,2048]{1,0:T(1,128)} %code_ref.1), custom_call_target="tpu_custom_call" | custom-call | tf_op jit(solution)/shard_map/pallas_call | solution.py:563
  4.7 3.0 %collective-permute-start = (f32[16,8,128]{2,1,0:T(8,128)}, f32[16,8,128]{2,1,0:T(8,128)S(1)}, u32[]{:S(2)}, u32[]{:S(2)}) collective-permute-start(f32[16,8,128]{2,1,0:T(8,128)} %get-tuple-element.26), channel_id=1, source_target_pairs={{0,1},{1,0},{2,3},{3,2},{4,5},{5,4},{6,7},{7,6},{8,9},{9,8},{10,11... | collective-permute-start | bytes 196616 | tf_op jit(solution)/shard_map/ppermute | solution.py:55
  7.7 0.1 collective-permute-start.1
  7.8 1.1 fusion.3
  8.8 1.1 slice_bitcast_fusion
  9.9 5.0 %sort.15 = (s32[2048]{0:T(1024)S(1)}, s32[2048]{0:T(1024)}) sort(s32[2048]{0:T(1024)S(1)} %bitcast.78, s32[2048]{0:T(1024)S(1)} %iota.11), dimensions={0}, to_apply=%region_0.0 | sort | flops 22528 | bytes 32768 | tf_op jit(solution)/shard_map/jit(sort)/sort | solution.py:617
  15.0 0.7 convert_reduce_fusion
  16.3 0.0 collective-permute-done
  16.4 0.1 collective-permute-start.2
  16.4 1.8 %collective-permute-start.3 = (f32[1,4,18,8,128]{4,3,2,0,1:T(8,128)S(1)}, f32[1,4,18,8,128]{4,3,2,0,1:T(8,128)S(1)}, u32[]{:S(2)}, u32[]{:S(2)}) collective-permute-start(f32[1,4,18,8,128]{4,3,2,0,1:T(8,128)S(1)} %pad_maximum_fusion.3), channel_id=1, source_target_pairs={{8,0},{16,8},{24,16},{0,24},{9,1},{17,9},{25,17},{1,25},{10,2},{18... | collective-permute-start | bytes 884744 | tf_op jit(solution)/shard_map/ppermute | solution.py:55
  19.5 8.7 %shard_map.105 = (s32[2048,128]{1,0:T(8,128)}, s32[1,2048]{1,0:T(1,128)}, s32[1,18432]{1,0:T(1,128)}, s32[1]{0:T(128)}) custom-call(s32[1]{0:T(128)} %bitcast.20.amount_smem, s32[1,2048]{1,0:T(1,128)} %bitcast.76, f32[256,8,128]{2,1,0:T(8,128)} %get-tuple-element.30.table_ref), custom_call_target="tpu_custom_call" | custom-call | tf_op jit(solution)/shard_map/pallas_call | solution.py:631
  29.0 2.1 %collective-permute-start.4 = (f32[6,1,18,8,128]{4,3,2,0,1:T(8,128)S(1)}, f32[6,1,18,8,128]{4,3,2,0,1:T(8,128)S(1)}, u32[]{:S(2)}, u32[]{:S(2)}) collective-permute-start(f32[6,1,18,8,128]{4,3,2,0,1:T(8,128)S(1)} %pad_maximum_fusion), channel_id=1, source_target_pairs={{0,2},{2,4},{4,6},{6,0},{1,3},{3,5},{5,7},{7,1},{8,10},{10,12},{12... | collective-permute-start | bytes 1327112 | tf_op jit(solution)/shard_map/ppermute | solution.py:55
  31.1 2.1 %collective-permute-start.5 = (f32[6,1,18,8,128]{4,3,2,0,1:T(8,128)S(1)}, f32[6,1,18,8,128]{4,3,2,0,1:T(8,128)S(1)}, u32[]{:S(2)}, u32[]{:S(2)}) collective-permute-start(f32[6,1,18,8,128]{4,3,2,0,1:T(8,128)S(1)} %pad_maximum_fusion.1), channel_id=1, source_target_pairs={{2,0},{4,2},{6,4},{0,6},{3,1},{5,3},{7,5},{1,7},{10,8},{12,10},{14... | collective-permute-start | bytes 1327112 | tf_op jit(solution)/shard_map/ppermute | solution.py:55
  33.2 0.7 fusion
  33.8 46.9 %shard_map.106.inner_ref = f32[3,256,128]{2,1,0:T(8,128)} custom-call(s32[1]{0:T(128)} %bitcast.20.amount_smem, s32[1,2048]{1,0:T(1,128)} %get-tuple-element.39.word_smem, s32[1,18432]{1,0:T(1,128)} %get-tuple-element.40.cell_smem, s32[1]{0:T(128)} %get-tuple-element.41.groups_smem, f32[256,8,128]{2,1,0:T(8,128)} %get-tuple-element.30.table_ref, ...), custom_call_target="tpu_custom_call" | custom-call | tf_op jit(solution)/shard_map/pallas_call | solution.py:648
  80.9 1.2 copy-done
  82.1 26.5 %shard_map.107 = f32[32,8,128]{2,1,0:T(8,128)} custom-call(s32[1]{0:T(128)} %bitcast.6.amount_smem, s32[1,2048]{1,0:T(1,128)} %bitcast.77, f32[256,8,128]{2,1,0:T(8,128)} %get-tuple-element.30.table_ref, f32[392,8,128]{2,1,0:T(8,128)} %copy-done, f32[3,256,128]{2,1,0:T(8,128)} %shard_map.106.inner_ref, f32[3,256,128]{2,1,0:T(8,128)} %bitcast.63, ...), custom_call_target="tpu_custom_call" | custom-call | tf_op jit(solution)/shard_map/pallas_call | solution.py:666
  108.6 5.5 %all-to-all-start = ((f32[32,8,128]{2,1,0:T(8,128)}), f32[32,8,128]{2,1,0:T(8,128)S(1)}, u32[]{:S(2)}, u32[]{:S(2)}) async-start(f32[32,8,128]{2,1,0:T(8,128)} %shard_map.107), calls=%async_computation | async-start | bytes 262144 | tf_op jit(solution)/shard_map/all_to_all | solution.py:684
  114.1 0.1 maximum_bitcast_fusion
  114.2 0.7 copy.23.target_ref
  114.9 6.9 %all-to-all-done.known_ref = f32[32,8,128]{2,1,0:T(8,128)S(1)} async-done(((f32[32,8,128]{2,1,0:T(8,128)}), f32[32,8,128]{2,1,0:T(8,128)S(1)}, u32[]{:S(2)}, u32[]{:S(2)}) %all-to-all-start) | async-done | bytes 131104 | tf_op jit(solution)/shard_map/all_to_all | solution.py:684
  121.8 0.7 copy-done.1
  122.5 4.6 %shard_map.108 = (f32[6,256,128]{2,1,0:T(8,128)}, f32[6,128]{1,0:T(8,128)}) custom-call(f32[128,1]{1,0:T(8,128)} %copy.23.target_ref, f32[32,8,128]{2,1,0:T(8,128)} %copy-done.1, f32[7,256,128]{2,1,0:T(8,128)} %bitcast.62, f32[3,256,128]{2,1,0:T(8,128)} %bitcast.64, s32[256,128]{1,0:T(8,128)} %bitcast.67), custom_call_target="tpu_custom_call" | custom-call | tf_op jit(solution)/shard_map/pallas_call | solution.py:691
  (32 shorter events, 0.3 us)
Async XLA Ops:
  4.7 5.2 %copy-start.4 = (s32[1,2048]{1,0:T(1,128)S(1)}, s32[1,2048]{1,0:T(1,128)}, u32[]{:S(2)}) copy-start(s32[1,2048]{1,0:T(1,128)} %get-tuple-element.24) | copy-start | bytes 24580
  4.7 11.5 %collective-permute-start = (f32[16,8,128]{2,1,0:T(8,128)}, f32[16,8,128]{2,1,0:T(8,128)S(1)}, u32[]{:S(2)}, u32[]{:S(2)}) collective-permute-start(f32[16,8,128]{2,1,0:T(8,128)} %get-tuple-element.26), channel_id=1, source_target_pairs={{0,1},{1,0},{2,3},{3,2},{4,5},{5,4},{6,7},{7,6},{8,9},{9,8},{10,11... | collective-permute-start | bytes 196616 | tf_op jit(solution)/shard_map/ppermute | solution.py:55
  7.7 8.6 %collective-permute-start.1 = (f32[16,8,128]{2,1,0:T(8,128)}, f32[16,8,128]{2,1,0:T(8,128)S(1)}, u32[]{:S(2)}, u32[]{:S(2)}) collective-permute-start(f32[16,8,128]{2,1,0:T(8,128)} %get-tuple-element.27), channel_id=1, source_target_pairs={{1,0},{0,1},{3,2},{2,3},{5,4},{4,5},{7,6},{6,7},{9,8},{8,9},{11,10... | collective-permute-start | bytes 196616 | tf_op jit(solution)/shard_map/ppermute | solution.py:55
  15.0 4.5 %copy-start.2 = (s32[2048]{0:T(1024)}, s32[2048]{0:T(1024)S(1)}, u32[]{:S(2)}) copy-start(s32[2048]{0:T(1024)S(1)} %get-tuple-element.28) | copy-start | bytes 24580
  16.4 12.5 %collective-permute-start.2 = (f32[1,4,18,8,128]{4,3,2,0,1:T(8,128)S(1)}, f32[1,4,18,8,128]{4,3,2,0,1:T(8,128)S(1)}, u32[]{:S(2)}, u32[]{:S(2)}) collective-permute-start(f32[1,4,18,8,128]{4,3,2,0,1:T(8,128)S(1)} %pad_maximum_fusion.2), channel_id=1, source_target_pairs={{0,8},{8,16},{16,24},{24,0},{1,9},{9,17},{17,25},{25,1},{2,10},{10... | collective-permute-start | bytes 884744 | tf_op jit(solution)/shard_map/ppermute | solution.py:55
  16.4 12.4 %collective-permute-start.3 = (f32[1,4,18,8,128]{4,3,2,0,1:T(8,128)S(1)}, f32[1,4,18,8,128]{4,3,2,0,1:T(8,128)S(1)}, u32[]{:S(2)}, u32[]{:S(2)}) collective-permute-start(f32[1,4,18,8,128]{4,3,2,0,1:T(8,128)S(1)} %pad_maximum_fusion.3), channel_id=1, source_target_pairs={{8,0},{16,8},{24,16},{0,24},{9,1},{17,9},{25,17},{1,25},{10,2},{18... | collective-permute-start | bytes 884744 | tf_op jit(solution)/shard_map/ppermute | solution.py:55
  28.2 5.0 %copy-start.3 = (s32[2048]{0:T(1024)S(1)}, s32[2048]{0:T(1024)}, u32[]{:S(2)}) copy-start(s32[2048]{0:T(1024)} %copy-done.2) | copy-start | bytes 24580
  29.0 51.9 %collective-permute-start.4 = (f32[6,1,18,8,128]{4,3,2,0,1:T(8,128)S(1)}, f32[6,1,18,8,128]{4,3,2,0,1:T(8,128)S(1)}, u32[]{:S(2)}, u32[]{:S(2)}) collective-permute-start(f32[6,1,18,8,128]{4,3,2,0,1:T(8,128)S(1)} %pad_maximum_fusion), channel_id=1, source_target_pairs={{0,2},{2,4},{4,6},{6,0},{1,3},{3,5},{5,7},{7,1},{8,10},{10,12},{12... | collective-permute-start | bytes 1327112 | tf_op jit(solution)/shard_map/ppermute | solution.py:55
  31.1 49.8 %collective-permute-start.5 = (f32[6,1,18,8,128]{4,3,2,0,1:T(8,128)S(1)}, f32[6,1,18,8,128]{4,3,2,0,1:T(8,128)S(1)}, u32[]{:S(2)}, u32[]{:S(2)}) collective-permute-start(f32[6,1,18,8,128]{4,3,2,0,1:T(8,128)S(1)} %pad_maximum_fusion.1), channel_id=1, source_target_pairs={{2,0},{4,2},{6,4},{0,6},{3,1},{5,3},{7,5},{1,7},{10,8},{12,10},{14... | collective-permute-start | bytes 1327112 | tf_op jit(solution)/shard_map/ppermute | solution.py:55
  80.9 1.2 copy-start
  82.1 32.0 %copy-start.5 = (f32[64]{0:T(128)S(1)}, f32[64]{0:T(128)}, u32[]{:S(2)}) copy-start(f32[64]{0:T(128)} %get-tuple-element.62) | copy-start | bytes 772
  108.6 13.2 %all-to-all-start = ((f32[32,8,128]{2,1,0:T(8,128)}), f32[32,8,128]{2,1,0:T(8,128)S(1)}, u32[]{:S(2)}, u32[]{:S(2)}) async-start(f32[32,8,128]{2,1,0:T(8,128)} %shard_map.107), calls=%async_computation | async-start | bytes 262144 | tf_op jit(solution)/shard_map/all_to_all | solution.py:684
  121.8 0.7 copy-start.1

commit v18 on v17

--- a/solution.py
+++ b/solution.py
@@ -506,7 +506,7 @@
         rows.append(base[axis : axis + 1] + time_step * sums[axis : axis + 1] * base[7:8])
     for comp in range(6):
         clumps_ref[comp : comp + 1, :] = rows[comp]
-    tall = 32
+    tall = 64
     wide = [jnp.broadcast_to(value, (tall, lanes)) for value in rows]
 
     def cross(first, second):
@@ -671,7 +671,7 @@
         scratch_shapes=[
             pltpu.VMEM((8, lanes), jnp.float32),
             pltpu.VMEM(force_shape, jnp.float32),
-            pltpu.VMEM((16, 8, lanes), jnp.float32),
+            pltpu.VMEM((32, 8, lanes), jnp.float32),
         ]
         + [pltpu.VMEM(shape, jnp.int32) for shape in list_shapes]
         + [pltpu.SMEM(shape, jnp.int32) for shape in list_shapes[1:]]

time: 127 us -> 126 us (level); the launches traced: 127 us -> 125 us
  Pallas kernels: 89.6 us -> 87.4 us
    pallas_call x1, Pallas kernels: 46.9 us -> 45.6 us  [local(): pl.pallas_call(inner_kernel, out_shape=jax.ShapeDtypeStruct((3, cells, la...]
  transfers between devices with their start and end apart: 7 -> 7, of which waited for: 1 -> 1; matrix products, arithmetic and copies ran while one was open for 7% -> 8% of each run, Pallas kernels for 44% -> 43%
where the time goes in v18:
time: 126 us; the launch traced here: 125 us
  Pallas kernels  87.4 us (69%)
  starting transfers between devices  14.5 us (12%)
  other arithmetic  7.73 us (6%)
  waiting for transfers between devices  6.93 us (6%)
  local copies, waits for them, and re-layouts  4.88 us (4%)
  between operations  3.45 us (3%)
    pallas_call x1, Pallas kernels, local(): pl.pallas_call(inner_kernel, out_shape=jax.ShapeDtypeStruct((3, cells, la...  45.6 us
    pallas_call x1, Pallas kernels, local(): pl.pallas_call(functools.partial(outer_kernel, near_outside, sizes), out_...  25.7 us
    ppermute x6, starting transfers between devices, exchange(): return (lax.ppermute(last, axis, up), lax.ppermute(initial, axis, down))  9.03 us
    pallas_call x1, Pallas kernels, local(): pl.pallas_call(functools.partial(list_kernel, near_inside, sizes), out_sh...  8.67 us
    all_to_all x1, waiting for transfers between devices, local(): lax.all_to_all(known, names, split_axis=0, concat_axis=0, tiled=True)  6.92 us
    all_to_all x1, starting transfers between devices, local(): lax.all_to_all(known, names, split_axis=0, concat_axis=0, tiled=True)  5.46 us
    sort x1, other arithmetic, local(): codes = jnp.sort(codes[0])  5.03 us
    pallas_call x1, Pallas kernels, local(): pl.pallas_call(functools.partial(move_kernel, owned), out_shape=(jax.Shap...  4.49 us
  transfers between devices with their start and end apart: 7, of which 1 were waited for; matrix products, arithmetic and copies ran while one was open for 8% of the time, Pallas kernels for 43%

profile of v18, /device:TPU:0, one launch (start us, length us, event | category | flops | bytes accessed | tf_op | source)
XLA Modules:
  0.0 124.8 jit_solution(8704705123505853036)
XLA Ops:
  0.6 1.2 fusion.1
  1.8 2.9 %shard_map.104 = (f32[256,8,128]{2,1,0:T(8,128)}, f32[16,8,128]{2,1,0:T(8,128)}, f32[16,8,128]{2,1,0:T(8,128)}, s32[1,2048]{1,0:T(1,128)}) custom-call(f32[7,256,128]{2,1,0:T(8,128)} %bitcast.61, s32[256,128]{1,0:T(8,128)} %bitcast.65, f32[1,64]{1,0:T(1,128)} %bitcast.79, s32[1,2048]{1,0:T(1,128)} %code_ref.1), custom_call_target="tpu_custom_call" | custom-call | tf_op jit(solution)/shard_map/pallas_call | solution.py:563
  4.7 3.0 %collective-permute-start = (f32[16,8,128]{2,1,0:T(8,128)}, f32[16,8,128]{2,1,0:T(8,128)S(1)}, u32[]{:S(2)}, u32[]{:S(2)}) collective-permute-start(f32[16,8,128]{2,1,0:T(8,128)} %get-tuple-element.26), channel_id=1, source_target_pairs={{0,1},{1,0},{2,3},{3,2},{4,5},{5,4},{6,7},{7,6},{8,9},{9,8},{10,11... | collective-permute-start | bytes 196616 | tf_op jit(solution)/shard_map/ppermute | solution.py:55
  7.7 0.1 collective-permute-start.1
  7.8 1.1 fusion.3
  8.8 1.1 slice_bitcast_fusion
  9.9 5.0 %sort.15 = (s32[2048]{0:T(1024)S(1)}, s32[2048]{0:T(1024)}) sort(s32[2048]{0:T(1024)S(1)} %bitcast.78, s32[2048]{0:T(1024)S(1)} %iota.11), dimensions={0}, to_apply=%region_0.0 | sort | flops 22528 | bytes 32768 | tf_op jit(solution)/shard_map/jit(sort)/sort | solution.py:617
  15.0 0.7 convert_reduce_fusion
  16.3 0.0 collective-permute-done
  16.4 0.1 collective-permute-start.2
  16.4 1.8 %collective-permute-start.3 = (f32[1,4,18,8,128]{4,3,2,0,1:T(8,128)S(1)}, f32[1,4,18,8,128]{4,3,2,0,1:T(8,128)S(1)}, u32[]{:S(2)}, u32[]{:S(2)}) collective-permute-start(f32[1,4,18,8,128]{4,3,2,0,1:T(8,128)S(1)} %pad_maximum_fusion.3), channel_id=1, source_target_pairs={{8,0},{16,8},{24,16},{0,24},{9,1},{17,9},{25,17},{1,25},{10,2},{18... | collective-permute-start | bytes 884744 | tf_op jit(solution)/shard_map/ppermute | solution.py:55
  19.5 8.7 %shard_map.105 = (s32[2048,128]{1,0:T(8,128)}, s32[1,2048]{1,0:T(1,128)}, s32[1,18432]{1,0:T(1,128)}, s32[1]{0:T(128)}) custom-call(s32[1]{0:T(128)} %bitcast.20.amount_smem, s32[1,2048]{1,0:T(1,128)} %bitcast.76, f32[256,8,128]{2,1,0:T(8,128)} %get-tuple-element.30.table_ref), custom_call_target="tpu_custom_call" | custom-call | tf_op jit(solution)/shard_map/pallas_call | solution.py:631
  29.0 2.1 %collective-permute-start.4 = (f32[6,1,18,8,128]{4,3,2,0,1:T(8,128)S(1)}, f32[6,1,18,8,128]{4,3,2,0,1:T(8,128)S(1)}, u32[]{:S(2)}, u32[]{:S(2)}) collective-permute-start(f32[6,1,18,8,128]{4,3,2,0,1:T(8,128)S(1)} %pad_maximum_fusion), channel_id=1, source_target_pairs={{0,2},{2,4},{4,6},{6,0},{1,3},{3,5},{5,7},{7,1},{8,10},{10,12},{12... | collective-permute-start | bytes 1327112 | tf_op jit(solution)/shard_map/ppermute | solution.py:55
  31.1 2.1 %collective-permute-start.5 = (f32[6,1,18,8,128]{4,3,2,0,1:T(8,128)S(1)}, f32[6,1,18,8,128]{4,3,2,0,1:T(8,128)S(1)}, u32[]{:S(2)}, u32[]{:S(2)}) collective-permute-start(f32[6,1,18,8,128]{4,3,2,0,1:T(8,128)S(1)} %pad_maximum_fusion.1), channel_id=1, source_target_pairs={{2,0},{4,2},{6,4},{0,6},{3,1},{5,3},{7,5},{1,7},{10,8},{12,10},{14... | collective-permute-start | bytes 1327112 | tf_op jit(solution)/shard_map/ppermute | solution.py:55
  33.2 0.7 fusion
  33.8 45.6 %shard_map.106.inner_ref = f32[3,256,128]{2,1,0:T(8,128)} custom-call(s32[1]{0:T(128)} %bitcast.20.amount_smem, s32[1,2048]{1,0:T(1,128)} %get-tuple-element.39.word_smem, s32[1,18432]{1,0:T(1,128)} %get-tuple-element.40.cell_smem, s32[1]{0:T(128)} %get-tuple-element.41.groups_smem, f32[256,8,128]{2,1,0:T(8,128)} %get-tuple-element.30.table_ref, ...), custom_call_target="tpu_custom_call" | custom-call | tf_op jit(solution)/shard_map/pallas_call | solution.py:648
  79.6 1.2 copy-done
  80.7 25.7 %shard_map.107 = f32[32,8,128]{2,1,0:T(8,128)} custom-call(s32[1]{0:T(128)} %bitcast.6.amount_smem, s32[1,2048]{1,0:T(1,128)} %bitcast.77, f32[256,8,128]{2,1,0:T(8,128)} %get-tuple-element.30.table_ref, f32[392,8,128]{2,1,0:T(8,128)} %copy-done, f32[3,256,128]{2,1,0:T(8,128)} %shard_map.106.inner_ref, f32[3,256,128]{2,1,0:T(8,128)} %bitcast.63, ...), custom_call_target="tpu_custom_call" | custom-call | tf_op jit(solution)/shard_map/pallas_call | solution.py:666
  106.5 5.5 %all-to-all-start = ((f32[32,8,128]{2,1,0:T(8,128)}), f32[32,8,128]{2,1,0:T(8,128)S(1)}, u32[]{:S(2)}, u32[]{:S(2)}) async-start(f32[32,8,128]{2,1,0:T(8,128)} %shard_map.107), calls=%async_computation | async-start | bytes 262144 | tf_op jit(solution)/shard_map/all_to_all | solution.py:684
  111.9 0.1 maximum_bitcast_fusion
  112.0 0.7 copy.23.target_ref
  112.8 6.9 %all-to-all-done.known_ref = f32[32,8,128]{2,1,0:T(8,128)S(1)} async-done(((f32[32,8,128]{2,1,0:T(8,128)}), f32[32,8,128]{2,1,0:T(8,128)S(1)}, u32[]{:S(2)}, u32[]{:S(2)}) %all-to-all-start) | async-done | bytes 131104 | tf_op jit(solution)/shard_map/all_to_all | solution.py:684
  119.7 0.7 copy-done.1
  120.3 4.5 %shard_map.108 = (f32[6,256,128]{2,1,0:T(8,128)}, f32[6,128]{1,0:T(8,128)}) custom-call(f32[128,1]{1,0:T(8,128)} %copy.23.target_ref, f32[32,8,128]{2,1,0:T(8,128)} %copy-done.1, f32[7,256,128]{2,1,0:T(8,128)} %bitcast.62, f32[3,256,128]{2,1,0:T(8,128)} %bitcast.64, s32[256,128]{1,0:T(8,128)} %bitcast.67), custom_call_target="tpu_custom_call" | custom-call | tf_op jit(solution)/shard_map/pallas_call | solution.py:691
  (32 shorter events, 0.3 us)
Async XLA Ops:
  4.7 5.2 %copy-start.4 = (s32[1,2048]{1,0:T(1,128)S(1)}, s32[1,2048]{1,0:T(1,128)}, u32[]{:S(2)}) copy-start(s32[1,2048]{1,0:T(1,128)} %get-tuple-element.24) | copy-start | bytes 24580
  4.7 11.5 %collective-permute-start = (f32[16,8,128]{2,1,0:T(8,128)}, f32[16,8,128]{2,1,0:T(8,128)S(1)}, u32[]{:S(2)}, u32[]{:S(2)}) collective-permute-start(f32[16,8,128]{2,1,0:T(8,128)} %get-tuple-element.26), channel_id=1, source_target_pairs={{0,1},{1,0},{2,3},{3,2},{4,5},{5,4},{6,7},{7,6},{8,9},{9,8},{10,11... | collective-permute-start | bytes 196616 | tf_op jit(solution)/shard_map/ppermute | solution.py:55
  7.7 8.6 %collective-permute-start.1 = (f32[16,8,128]{2,1,0:T(8,128)}, f32[16,8,128]{2,1,0:T(8,128)S(1)}, u32[]{:S(2)}, u32[]{:S(2)}) collective-permute-start(f32[16,8,128]{2,1,0:T(8,128)} %get-tuple-element.27), channel_id=1, source_target_pairs={{1,0},{0,1},{3,2},{2,3},{5,4},{4,5},{7,6},{6,7},{9,8},{8,9},{11,10... | collective-permute-start | bytes 196616 | tf_op jit(solution)/shard_map/ppermute | solution.py:55
  15.0 4.5 %copy-start.2 = (s32[2048]{0:T(1024)}, s32[2048]{0:T(1024)S(1)}, u32[]{:S(2)}) copy-start(s32[2048]{0:T(1024)S(1)} %get-tuple-element.28) | copy-start | bytes 24580
  16.4 12.5 %collective-permute-start.2 = (f32[1,4,18,8,128]{4,3,2,0,1:T(8,128)S(1)}, f32[1,4,18,8,128]{4,3,2,0,1:T(8,128)S(1)}, u32[]{:S(2)}, u32[]{:S(2)}) collective-permute-start(f32[1,4,18,8,128]{4,3,2,0,1:T(8,128)S(1)} %pad_maximum_fusion.2), channel_id=1, source_target_pairs={{0,8},{8,16},{16,24},{24,0},{1,9},{9,17},{17,25},{25,1},{2,10},{10... | collective-permute-start | bytes 884744 | tf_op jit(solution)/shard_map/ppermute | solution.py:55
  16.4 12.4 %collective-permute-start.3 = (f32[1,4,18,8,128]{4,3,2,0,1:T(8,128)S(1)}, f32[1,4,18,8,128]{4,3,2,0,1:T(8,128)S(1)}, u32[]{:S(2)}, u32[]{:S(2)}) collective-permute-start(f32[1,4,18,8,128]{4,3,2,0,1:T(8,128)S(1)} %pad_maximum_fusion.3), channel_id=1, source_target_pairs={{8,0},{16,8},{24,16},{0,24},{9,1},{17,9},{25,17},{1,25},{10,2},{18... | collective-permute-start | bytes 884744 | tf_op jit(solution)/shard_map/ppermute | solution.py:55
  28.2 5.0 %copy-start.3 = (s32[2048]{0:T(1024)S(1)}, s32[2048]{0:T(1024)}, u32[]{:S(2)}) copy-start(s32[2048]{0:T(1024)} %copy-done.2) | copy-start | bytes 24580
  29.0 50.5 %collective-permute-start.4 = (f32[6,1,18,8,128]{4,3,2,0,1:T(8,128)S(1)}, f32[6,1,18,8,128]{4,3,2,0,1:T(8,128)S(1)}, u32[]{:S(2)}, u32[]{:S(2)}) collective-permute-start(f32[6,1,18,8,128]{4,3,2,0,1:T(8,128)S(1)} %pad_maximum_fusion), channel_id=1, source_target_pairs={{0,2},{2,4},{4,6},{6,0},{1,3},{3,5},{5,7},{7,1},{8,10},{10,12},{12... | collective-permute-start | bytes 1327112 | tf_op jit(solution)/shard_map/ppermute | solution.py:55
  31.1 48.4 %collective-permute-start.5 = (f32[6,1,18,8,128]{4,3,2,0,1:T(8,128)S(1)}, f32[6,1,18,8,128]{4,3,2,0,1:T(8,128)S(1)}, u32[]{:S(2)}, u32[]{:S(2)}) collective-permute-start(f32[6,1,18,8,128]{4,3,2,0,1:T(8,128)S(1)} %pad_maximum_fusion.1), channel_id=1, source_target_pairs={{2,0},{4,2},{6,4},{0,6},{3,1},{5,3},{7,5},{1,7},{10,8},{12,10},{14... | collective-permute-start | bytes 1327112 | tf_op jit(solution)/shard_map/ppermute | solution.py:55
  79.5 1.2 copy-start
  80.7 31.2 %copy-start.5 = (f32[64]{0:T(128)S(1)}, f32[64]{0:T(128)}, u32[]{:S(2)}) copy-start(f32[64]{0:T(128)} %get-tuple-element.62) | copy-start | bytes 772
  106.5 13.2 %all-to-all-start = ((f32[32,8,128]{2,1,0:T(8,128)}), f32[32,8,128]{2,1,0:T(8,128)S(1)}, u32[]{:S(2)}, u32[]{:S(2)}) async-start(f32[32,8,128]{2,1,0:T(8,128)} %shard_map.107), calls=%async_computation | async-start | bytes 262144 | tf_op jit(solution)/shard_map/all_to_all | solution.py:684
  119.7 0.7 copy-start.1
